TPU v7x, 128 devices: a whole 4x4x4 slice. The times are simulated.
128 devices in a mesh: section: 2 (over core), ctx: 16 (over x, y), fsdp: 4 (over z).
Axes of the slice: x: 4, y: 4, z: 4, core: 2. Of those that a mesh axis runs over, the one named last changes fastest.
Arguments:
- tokens: float32 [2, 4, 2048, 896], P(None, 'fsdp', 'ctx'), may hold values from -6 to 6
- cotangent: float32 [2, 4, 2048, 896], P(None, 'fsdp', 'ctx'), may hold values from -6 to 6
- pair_of: int32 [16], P('ctx'), may hold values from 0 to 15, each once
- attn_gain: bfloat16 [2, 896], P('section', 'fsdp'), may hold values from 0.099609375 to 1.8984375
- ffn_gain: bfloat16 [2, 896], P('section', 'fsdp'), may hold values from 0.099609375 to 1.8984375
- qkv_weight: bfloat16 [2, 896, 1152], P('section', 'fsdp'), may hold values from -0.1875 to 0.1875
- qkv_bias: bfloat16 [2, 1152], P('section', 'fsdp'), may hold values from -2 to 2
- out_weight: bfloat16 [2, 896, 896], P('section', 'fsdp'), may hold values from -1.5 to 1.5
- gate_weight: bfloat16 [2, 896, 4864], P('section', 'fsdp'), may hold values from -0.1875 to 0.1875
- up_weight: bfloat16 [2, 896, 4864], P('section', 'fsdp'), may hold values from -0.1875 to 0.1875
- down_weight: bfloat16 [2, 4864, 896], P('section', 'fsdp'), may hold values from -0.078125 to 0.078125
Outputs:
- layer_out: float32 [2, 2, 4, 2048, 896], P('section', None, 'fsdp', 'ctx')
- input_grad: float32 [2, 2, 4, 2048, 896], P('section', None, 'fsdp', 'ctx')
- attn_gain_grad: float32 [2, 896], P('section', 'fsdp')
- ffn_gain_grad: float32 [2, 896], P('section', 'fsdp')
- qkv_weight_grad: float32 [2, 896, 1152], P('section', 'fsdp')
- qkv_bias_grad: float32 [2, 1152], P('section', 'fsdp')
- out_weight_grad: float32 [2, 896, 896], P('section', 'fsdp')
- gate_weight_grad: float32 [2, 896, 4864], P('section', 'fsdp')
- up_weight_grad: float32 [2, 896, 4864], P('section', 'fsdp')
- down_weight_grad: float32 [2, 4864, 896], P('section', 'fsdp')
Inputs may be any that keep to these rules, and one draw needn't show every extreme that they name: pair_of is a permutation of the ctx ranks: rank r holds the causal blocks pair_of[r] and 31 - pair_of[r] of each sequence, 64 tokens each.
All inputs are finite; a program needn't handle non-finite values.
Results may differ from a plain program's by a relative error of at most 0.02.
Values may be sent and summed in bfloat16 or wider, within the bound.
A program may use at most 320 MiB of HBM per device.

v0:
```python
import jax
import jax.numpy as jnp
from jax import lax
from jax.sharding import PartitionSpec as P

HEADS = 14
KV_HEADS = 2
HEAD_DIM = 64


EPS = 1e-06
THETA = 1000000.0


def passed_along(value, axis, by):
    devices = lax.axis_size(axis)
    pairs = [(i, i + by) for i in range(devices) if 0 <= i + by < devices]
    return lax.ppermute(value, axis, pairs)


def shortened(value):
    return jax.tree.map(lambda a: a.astype(jnp.bfloat16) if a.dtype == jnp.float32 else a, value)


def dealt_positions(chosen_pair, block_len, ctx_count):
    within = jnp.arange(2 * block_len, dtype=jnp.int32)
    first = chosen_pair * block_len + within
    second = (2 * ctx_count - 1 - chosen_pair) * block_len + within - block_len
    return jnp.where(within < block_len, first, second)


def rope_tables(positions):
    freq_index = jnp.arange(HEAD_DIM // 2, dtype=jnp.float32)
    inverse = THETA ** (-2.0 * freq_index / HEAD_DIM)
    angles = positions.astype(jnp.float32)[:, None] * inverse[None, :]
    angles = jnp.concatenate([angles, angles], -1)
    return (jnp.cos(angles), jnp.sin(angles))


def turn_half(field):
    half_width = HEAD_DIM // 2
    return jnp.concatenate([-field[..., half_width:], field[..., :half_width]], -1)


def rotate(field, cosine, sine):
    return field * cosine[:, None, :] + turn_half(field) * sine[:, None, :]


def unrotate(field, cosine, sine):
    return field * cosine[:, None, :] - turn_half(field) * sine[:, None, :]


def norm_back(grad_normed, source, factor, gain):
    unit = source * factor
    gain_grad = jnp.sum(grad_normed * unit, axis=(0, 1))
    scaled = grad_normed * gain
    grad_source = factor * (scaled - unit * jnp.mean(scaled * unit, -1, keepdims=True))
    return (grad_source, gain_grad)


def masked_scores(queries_b, keys_four, allowed):
    scores = jnp.einsum(
        "sqgjd,skgd->sgjqk", queries_b, keys_four, preferred_element_type=jnp.float32
    ) * HEAD_DIM ** (-0.5)
    return jnp.where(allowed, scores, -1e30)


def forward(inputs, params, tables):
    gain_one, gain_two, qkv_w, qkv_b, out_w, gate_w, up_w, down_w = params
    cosine, sine, allowed = tables
    seqs_here, tok_local = (inputs.shape[0], inputs.shape[1])
    group_size = HEADS // KV_HEADS
    width_query = HEADS * HEAD_DIM
    width_key = KV_HEADS * HEAD_DIM
    factor_one = lax.rsqrt(jnp.mean(inputs * inputs, -1, keepdims=True) + EPS)
    normed = (inputs * factor_one * gain_one).astype(jnp.bfloat16)
    linear = jnp.einsum(
        "std,de->ste", normed, qkv_w, preferred_element_type=jnp.float32
    ) + qkv_b.astype(jnp.float32)
    queries = rotate(
        linear[..., :width_query].reshape(seqs_here, tok_local, HEADS, HEAD_DIM), cosine, sine
    )
    queries_b = queries.astype(jnp.bfloat16).reshape(
        seqs_here, tok_local, KV_HEADS, group_size, HEAD_DIM
    )
    keys_own = rotate(
        linear[..., width_query : width_query + width_key].reshape(
            seqs_here, tok_local, KV_HEADS, HEAD_DIM
        ),
        cosine,
        sine,
    )
    keys_own = keys_own.astype(jnp.bfloat16).reshape(seqs_here, tok_local, width_key)
    values_own = linear[..., width_query + width_key :].astype(jnp.bfloat16)
    keys_all, values_all = (
        lax.all_gather(keys_own, "ctx", axis=1, tiled=True),
        lax.all_gather(values_own, "ctx", axis=1, tiled=True),
    )
    keys_four = keys_all.reshape(seqs_here, -1, KV_HEADS, HEAD_DIM)
    values_four = values_all.reshape(seqs_here, -1, KV_HEADS, HEAD_DIM)
    scores = masked_scores(queries_b, keys_four, allowed)
    top_score = jnp.max(scores, -1, keepdims=True)
    weights = jnp.exp(scores - top_score)
    total_weight = jnp.sum(weights, -1, keepdims=True)
    probs = weights / total_weight
    log_total = top_score + jnp.log(total_weight)
    mixed = jnp.einsum(
        "sgjqk,skgd->sqgjd",
        probs.astype(jnp.bfloat16),
        values_four,
        preferred_element_type=jnp.float32,
    )
    attended_b = mixed.reshape(seqs_here, tok_local, width_query).astype(jnp.bfloat16)
    middle = inputs + jnp.einsum(
        "sti,id->std", attended_b, out_w, preferred_element_type=jnp.float32
    )
    factor_two = lax.rsqrt(jnp.mean(middle * middle, -1, keepdims=True) + EPS)
    normed_two = (middle * factor_two * gain_two).astype(jnp.bfloat16)
    gate = jnp.einsum("std,df->stf", normed_two, gate_w, preferred_element_type=jnp.float32)
    up_part = jnp.einsum("std,df->stf", normed_two, up_w, preferred_element_type=jnp.float32)
    hidden_b = (jax.nn.silu(gate) * up_part).astype(jnp.bfloat16)
    result = middle + jnp.einsum(
        "stf,fd->std", hidden_b, down_w, preferred_element_type=jnp.float32
    )
    saved = (
        inputs,
        factor_one,
        normed,
        queries_b,
        keys_four,
        values_four,
        log_total,
        attended_b,
        middle,
        factor_two,
        normed_two,
        gate,
        up_part,
        hidden_b,
    )
    return (result, saved)


def backward(upstream, saved, params, tables):
    gain_one, gain_two, qkv_w, qkv_b, out_w, gate_w, up_w, down_w = params
    cosine, sine, allowed = tables
    (
        inputs,
        factor_one,
        normed,
        queries_b,
        keys_four,
        values_four,
        log_total,
        attended_b,
        middle,
        factor_two,
        normed_two,
        gate,
        up_part,
        hidden_b,
    ) = saved
    seqs_here, tok_local = (inputs.shape[0], inputs.shape[1])
    scale_factor = HEAD_DIM ** (-0.5)
    upstream_b = upstream.astype(jnp.bfloat16)
    grad_down = jnp.einsum("stf,std->fd", hidden_b, upstream_b, preferred_element_type=jnp.float32)
    grad_hidden = jnp.einsum("std,fd->stf", upstream_b, down_w, preferred_element_type=jnp.float32)
    sigma = jax.nn.sigmoid(gate)
    grad_gate = (grad_hidden * up_part * sigma * (1.0 + gate * (1.0 - sigma))).astype(jnp.bfloat16)
    grad_up = (grad_hidden * gate * sigma).astype(jnp.bfloat16)
    grad_gate_w = jnp.einsum(
        "std,stf->df", normed_two, grad_gate, preferred_element_type=jnp.float32
    )
    grad_up_w = jnp.einsum("std,stf->df", normed_two, grad_up, preferred_element_type=jnp.float32)
    grad_normed_two = jnp.einsum(
        "stf,df->std", grad_gate, gate_w, preferred_element_type=jnp.float32
    )
    grad_normed_two = grad_normed_two + jnp.einsum(
        "stf,df->std", grad_up, up_w, preferred_element_type=jnp.float32
    )
    middle_part, gain_two_grad = norm_back(grad_normed_two, middle, factor_two, gain_two)
    grad_middle = upstream + middle_part
    branch_b = grad_middle.astype(jnp.bfloat16)
    grad_out_w = jnp.einsum("sti,std->id", attended_b, branch_b, preferred_element_type=jnp.float32)
    grad_attended = jnp.einsum(
        "std,id->sti", branch_b, out_w, preferred_element_type=jnp.float32
    ).astype(jnp.bfloat16)
    grad_attended = grad_attended.reshape(queries_b.shape)
    probs = jnp.exp(masked_scores(queries_b, keys_four, allowed) - log_total)
    grad_probs = jnp.einsum(
        "sqgjd,skgd->sgjqk", grad_attended, values_four, preferred_element_type=jnp.float32
    )
    grad_values = jnp.einsum(
        "sgjqk,sqgjd->skgd",
        probs.astype(jnp.bfloat16),
        grad_attended,
        preferred_element_type=jnp.float32,
    )
    delta = jnp.sum(grad_probs * probs, -1, keepdims=True)
    grad_scores = (probs * (grad_probs - delta)).astype(jnp.bfloat16)
    grad_queries = (
        jnp.einsum("sgjqk,skgd->sqgjd", grad_scores, keys_four, preferred_element_type=jnp.float32)
        * scale_factor
    )
    grad_keys = (
        jnp.einsum("sgjqk,sqgjd->skgd", grad_scores, queries_b, preferred_element_type=jnp.float32)
        * scale_factor
    )
    width_key = KV_HEADS * HEAD_DIM
    key_share, value_share = (
        lax.psum_scatter(
            grad_keys.reshape(seqs_here, -1, width_key).astype(jnp.bfloat16),
            "ctx",
            scatter_dimension=1,
            tiled=True,
        ).astype(jnp.float32),
        lax.psum_scatter(
            grad_values.reshape(seqs_here, -1, width_key).astype(jnp.bfloat16),
            "ctx",
            scatter_dimension=1,
            tiled=True,
        ).astype(jnp.float32),
    )
    query_part = unrotate(
        grad_queries.reshape(seqs_here, tok_local, HEADS, HEAD_DIM), cosine, sine
    ).reshape(seqs_here, tok_local, HEADS * HEAD_DIM)
    key_part = unrotate(
        key_share.reshape(seqs_here, tok_local, KV_HEADS, HEAD_DIM), cosine, sine
    ).reshape(seqs_here, tok_local, width_key)
    grad_linear = jnp.concatenate([query_part, key_part, value_share], -1).astype(jnp.bfloat16)
    grad_bias = jnp.sum(grad_linear.astype(jnp.float32), axis=(0, 1))
    grad_qkv_w = jnp.einsum("std,ste->de", normed, grad_linear, preferred_element_type=jnp.float32)
    grad_normed = jnp.einsum("ste,de->std", grad_linear, qkv_w, preferred_element_type=jnp.float32)
    input_part, gain_one_grad = norm_back(grad_normed, inputs, factor_one, gain_one)
    grad_inputs = grad_middle + input_part
    return (
        grad_inputs,
        (
            gain_one_grad,
            gain_two_grad,
            grad_qkv_w,
            grad_bias,
            grad_out_w,
            grad_gate_w,
            grad_up_w,
            grad_down,
        ),
    )


def local(
    tokens,
    cotangent,
    pair_of,
    attn_gain,
    ffn_gain,
    qkv_weight,
    qkv_bias,
    out_weight,
    gate_weight,
    up_weight,
    down_weight,
):
    section_index = lax.axis_index("section")
    ctx_count = lax.axis_size("ctx")
    micro = tokens.shape[0]
    tok_local = tokens.shape[2]
    block_len = tok_local // 2
    all_pairs = lax.all_gather(pair_of, "ctx", axis=0, tiled=True)
    own_pos = dealt_positions(pair_of[0], block_len, ctx_count)
    key_pos = jax.vmap(lambda chosen_pair: dealt_positions(chosen_pair, block_len, ctx_count))(
        all_pairs
    ).reshape(-1)
    cosine, sine = rope_tables(own_pos)
    allowed = key_pos[None, :] <= own_pos[:, None]
    tables = (cosine, sine, allowed)
    gathered = (
        lax.all_gather(attn_gain, "fsdp", axis=1, tiled=True),
        lax.all_gather(ffn_gain, "fsdp", axis=1, tiled=True),
        lax.all_gather(qkv_weight, "fsdp", axis=1, tiled=True),
        lax.all_gather(qkv_bias, "fsdp", axis=1, tiled=True),
        lax.all_gather(out_weight, "fsdp", axis=1, tiled=True),
        lax.all_gather(gate_weight, "fsdp", axis=1, tiled=True),
        lax.all_gather(up_weight, "fsdp", axis=1, tiled=True),
        lax.all_gather(down_weight, "fsdp", axis=1, tiled=True),
    )
    gain_one = gathered[0][0].astype(jnp.float32)
    gain_two = gathered[1][0].astype(jnp.float32)
    params = (
        gain_one,
        gain_two,
        gathered[2][0],
        gathered[3][0],
        gathered[4][0],
        gathered[5][0],
        gathered[6][0],
        gathered[7][0],
    )
    empty_rows = jnp.zeros_like(tokens[0])
    received = empty_rows.astype(jnp.bfloat16)
    stash = []
    results = []
    for tick in range(micro + 1):
        fresh = tokens[tick] if tick < micro else empty_rows
        inputs = jnp.where(section_index == 0, fresh, received.astype(jnp.float32))
        result, saved = forward(inputs, params, tables)
        stash.append(saved)
        results.append(result)
        if tick < micro:
            received = passed_along(result.astype(jnp.bfloat16), "section", 1)
    layer_out = jnp.stack(
        [
            jnp.where(section_index == 0, results[index_mb], results[index_mb + 1])
            for index_mb in range(micro)
        ]
    )
    returned = empty_rows.astype(jnp.bfloat16)
    totals = None
    grad_ticks = []
    for tick in range(micro + 1):
        index_mb = micro - 1 - tick
        fresh = cotangent[index_mb] if index_mb >= 0 else empty_rows
        upstream = jnp.where(section_index == 1, fresh, returned.astype(jnp.float32))
        grad_inputs, grads = backward(upstream, stash[micro - tick], params, tables)
        totals = (
            grads if totals is None else tuple((total + part for total, part in zip(totals, grads)))
        )
        grad_ticks.append(grad_inputs)
        if tick < micro:
            returned = passed_along(grad_inputs.astype(jnp.bfloat16), "section", -1)
    input_grad = jnp.stack(
        [
            jnp.where(
                section_index == 0, grad_ticks[micro - index_mb], grad_ticks[micro - 1 - index_mb]
            )
            for index_mb in range(micro)
        ]
    )
    full_grads = tuple((item[None] for item in totals))
    shares = jax.tree.map(
        lambda part: part.astype(jnp.float32),
        lax.psum_scatter(shortened(full_grads), "fsdp", scatter_dimension=1, tiled=True),
    )
    finals = jax.tree.map(lambda part: part.astype(jnp.float32), lax.psum(shortened(shares), "ctx"))
    return (
        layer_out[None],
        input_grad[None],
        finals[0],
        finals[1],
        finals[2],
        finals[3],
        finals[4],
        finals[5],
        finals[6],
        finals[7],
    )


def solution(mesh):
    return jax.shard_map(
        local,
        mesh=mesh,
        in_specs=(
            P(None, "fsdp", "ctx", None),
            P(None, "fsdp", "ctx", None),
            P("ctx"),
            P("section", "fsdp"),
            P("section", "fsdp"),
            P("section", "fsdp", None),
            P("section", "fsdp"),
            P("section", "fsdp", None),
            P("section", "fsdp", None),
            P("section", "fsdp", None),
            P("section", "fsdp", None),
        ),
        out_specs=(
            P("section", None, "fsdp", "ctx", None),
            P("section", None, "fsdp", "ctx", None),
            P("section", "fsdp"),
            P("section", "fsdp"),
            P("section", "fsdp", None),
            P("section", "fsdp"),
            P("section", "fsdp", None),
            P("section", "fsdp", None),
            P("section", "fsdp", None),
            P("section", "fsdp", None),
        ),
        check_vma=False,
    )
```

profile of v0, /device:TPU:0, one launch (start us, length us, event | category | flops | bytes accessed | tf_op | source)
XLA Modules:
  0.0 1646.9 jit_solution(8176089642849476900)
XLA Ops:
  12.7 16.5 %all-reduce.2 = s32[16]{0:T(128)S(1)} all-reduce(s32[16]{0:T(128)S(1)} %dynamic-update-slice.2), channel_id=1, replica_groups=mesh['section'=2,'ctx'=16,'fsdp'=4] {'ctx'}, use_global_device_ids=true, to_apply=%add.2 | all-reduce | flops 16 | bytes 128
  31.9 11.9 all-reduce.6
  47.8 24.5 %all_gather.48 = bf16[1,2048,128]{2,1,0:T(8,128)(2,1)} all-gather(bf16[1,128,128]{2,1,0:T(8,128)(2,1)S(1)} %slice.238), channel_id=1, replica_groups=mesh['section'=2,'ctx'=16,'fsdp'=4] {'ctx'}, dimensions={1}, use_global_device_ids=true | all-gather | bytes 557056 | tf_op jit(solution)/shard_map/all_gather | solution.py:97
  73.9 25.3 %all_gather.50 = bf16[1,2048,128]{2,1,0:T(8,128)(2,1)} all-gather(bf16[1,128,128]{2,1,0:T(8,128)(2,1)S(1)} %add_convert_fusion.6), channel_id=1, replica_groups=mesh['section'=2,'ctx'=16,'fsdp'=4] {'ctx'}, dimensions={1}, use_global_device_ids=true | all-gather | bytes 557056 | tf_op jit(solution)/shard_map/all_gather | solution.py:96
  124.6 34.7 %all-gather.10.cloned.1.call-done = bf16[1,896,4864]{2,1,0:T(8,128)(2,1)} async-done(((bf16[1,224,4864]{2,1,0:T(8,128)(2,1)}), bf16[1,896,4864]{2,1,0:T(8,128)(2,1)}) %all-gather.10.cloned.1.call-update) | async-done | bytes 8716304 | tf_op jit(solution)/shard_map/all_gather | solution.py:283
  165.7 82.1 %all-gather.12.cloned.1.call-done = bf16[1,896,4864]{2,1,0:T(8,128)(2,1)} async-done(((bf16[1,224,4864]{2,1,0:T(8,128)(2,1)}), bf16[1,896,4864]{2,1,0:T(8,128)(2,1)}) %all-gather.12.cloned.1.call-update) | async-done | bytes 8716304 | tf_op jit(solution)/shard_map/all_gather | solution.py:284
  255.1 81.2 %all-gather.14.cloned.1.call-done = bf16[1,4864,896]{2,1,0:T(8,128)(2,1)} async-done(((bf16[1,1216,896]{2,1,0:T(8,128)(2,1)}), bf16[1,4864,896]{2,1,0:T(8,128)(2,1)}) %all-gather.14.cloned.1.call-update) | async-done | bytes 8716304 | tf_op jit(solution)/shard_map/all_gather | solution.py:285
  347.6 24.2 %all_gather.56 = bf16[1,2048,128]{2,1,0:T(8,128)(2,1)S(1)} all-gather(bf16[1,128,128]{2,1,0:T(8,128)(2,1)S(1)} %slice.237), channel_id=1, replica_groups=mesh['section'=2,'ctx'=16,'fsdp'=4] {'ctx'}, dimensions={1}, use_global_device_ids=true | all-gather | bytes 557056 | tf_op jit(solution)/shard_map/all_gather | solution.py:97
  373.1 23.2 %all_gather.57 = bf16[1,2048,128]{2,1,0:T(8,128)(2,1)S(1)} all-gather(bf16[1,128,128]{2,1,0:T(8,128)(2,1)S(1)} %add_convert_fusion.5), channel_id=1, replica_groups=mesh['section'=2,'ctx'=16,'fsdp'=4] {'ctx'}, dimensions={1}, use_global_device_ids=true | all-gather | bytes 557056 | tf_op jit(solution)/shard_map/all_gather | solution.py:96
  434.8 22.1 %all_gather.58 = bf16[1,2048,128]{2,1,0:T(8,128)(2,1)S(1)} all-gather(bf16[1,128,128]{2,1,0:T(8,128)(2,1)S(1)} %slice.236), channel_id=1, replica_groups=mesh['section'=2,'ctx'=16,'fsdp'=4] {'ctx'}, dimensions={1}, use_global_device_ids=true | all-gather | bytes 557056 | tf_op jit(solution)/shard_map/all_gather | solution.py:97
  458.2 23.0 %all_gather.59 = bf16[1,2048,128]{2,1,0:T(8,128)(2,1)S(1)} all-gather(bf16[1,128,128]{2,1,0:T(8,128)(2,1)S(1)} %add_convert_fusion.4), channel_id=1, replica_groups=mesh['section'=2,'ctx'=16,'fsdp'=4] {'ctx'}, dimensions={1}, use_global_device_ids=true | all-gather | bytes 557056 | tf_op jit(solution)/shard_map/all_gather | solution.py:96
  517.8 13.6 fusion.6
  565.3 54.2 %reduce-scatter.43.cloned.1.call-done = bf16[128,128]{1,0:T(8,128)(2,1)} async-done(((bf16[2048,128]{1,0:T(8,128)(2,1)}), bf16[128,128]{1,0:T(8,128)(2,1)}) %reduce-scatter.43.cloned.1.call-update) | async-done | bytes 32784
  620.5 74.7 %reduce-scatter.45.cloned.1.call-done = bf16[128,128]{1,0:T(8,128)(2,1)} async-done(((bf16[2048,128]{1,0:T(8,128)(2,1)}), bf16[128,128]{1,0:T(8,128)(2,1)}) %reduce-scatter.45.cloned.1.call-update) | async-done | bytes 32784
  703.5 9.3 multiply_convert_fusion.3
  722.6 13.3 fusion.3
  773.1 52.7 %reduce-scatter.47.cloned.1.call-done = bf16[128,128]{1,0:T(8,128)(2,1)} async-done(((bf16[2048,128]{1,0:T(8,128)(2,1)}), bf16[128,128]{1,0:T(8,128)(2,1)}) %reduce-scatter.47.cloned.1.call-update) | async-done | bytes 32784
  826.8 74.8 %reduce-scatter.49.cloned.1.call-done = bf16[128,128]{1,0:T(8,128)(2,1)} async-done(((bf16[2048,128]{1,0:T(8,128)(2,1)}), bf16[128,128]{1,0:T(8,128)(2,1)}) %reduce-scatter.49.cloned.1.call-update) | async-done | bytes 32784
  928.0 13.5 fusion
  979.7 48.7 %reduce-scatter.51.cloned.1.call-done = bf16[128,128]{1,0:T(8,128)(2,1)} async-done(((bf16[2048,128]{1,0:T(8,128)(2,1)}), bf16[128,128]{1,0:T(8,128)(2,1)}) %reduce-scatter.51.cloned.1.call-update) | async-done | bytes 32784
  1029.4 74.7 %reduce-scatter.53.cloned.1.call-done = bf16[128,128]{1,0:T(8,128)(2,1)} async-done(((bf16[2048,128]{1,0:T(8,128)(2,1)}), bf16[128,128]{1,0:T(8,128)(2,1)}) %reduce-scatter.53.cloned.1.call-update) | async-done | bytes 32784
  1127.1 16.1 fusion.51
  1161.6 16.0 fusion.52
  1195.2 16.4 fusion.53
  1221.8 28.4 %reduce-scatter.37.cloned.1.call-done = bf16[1,224,4864]{2,1,0:T(8,128)(2,1)} async-done(((bf16[1,896,4864]{2,1,0:T(8,128)(2,1)}), bf16[1,224,4864]{2,1,0:T(8,128)(2,1)}) %reduce-scatter.37.cloned.1.call-update) | async-done | bytes 2179088 | tf_op jit(solution)/shard_map/reduce_scatter | solution.py:342
  1250.2 85.3 %reduce-scatter.39.cloned.1.call-done = bf16[1,224,4864]{2,1,0:T(8,128)(2,1)} async-done(((bf16[1,896,4864]{2,1,0:T(8,128)(2,1)}), bf16[1,224,4864]{2,1,0:T(8,128)(2,1)}) %reduce-scatter.39.cloned.1.call-update) | async-done | bytes 2179088 | tf_op jit(solution)/shard_map/reduce_scatter | solution.py:342
  1335.5 85.5 %reduce-scatter.41.cloned.1.call-done = bf16[1,1216,896]{2,1,0:T(8,128)(2,1)} async-done(((bf16[1,4864,896]{2,1,0:T(8,128)(2,1)}), bf16[1,1216,896]{2,1,0:T(8,128)(2,1)}) %reduce-scatter.41.cloned.1.call-update) | async-done | bytes 2179088 | tf_op jit(solution)/shard_map/reduce_scatter | solution.py:342
  1426.8 16.8 %reduce-scatter.57.cloned.1.call-done = bf16[224,1]{1,0:T(8,128)(2,1)} async-done(((bf16[896,1]{1,0:T(8,128)(2,1)}), bf16[224,1]{1,0:T(8,128)(2,1)}) %reduce-scatter.57.cloned.1.call-update) | async-done | bytes 464
  1448.8 17.6 %reduce-scatter.55.cloned.1.call-done = bf16[224,1]{1,0:T(8,128)(2,1)} async-done(((bf16[896,1]{1,0:T(8,128)(2,1)}), bf16[224,1]{1,0:T(8,128)(2,1)}) %reduce-scatter.55.cloned.1.call-update) | async-done | bytes 464
  1467.3 22.7 %reduce-scatter.59.cloned.1.call-done = bf16[288,1]{1,0:T(8,128)(2,1)} async-done(((bf16[1152,1]{1,0:T(8,128)(2,1)}), bf16[288,1]{1,0:T(8,128)(2,1)}) %reduce-scatter.59.cloned.1.call-update) | async-done | bytes 592
  1491.0 41.7 %all-reduce.4 = (bf16[1,224]{1,0:T(2,128)(2,1)S(1)}, bf16[1,224]{1,0:T(2,128)(2,1)S(1)}, bf16[1,288]{1,0:T(2,128)(2,1)S(1)}) all-reduce(bf16[1,224]{1,0:T(2,128)(2,1)S(1)} %copy.192, bf16[1,224]{1,0:T(2,128)(2,1)S(1)} %copy.194, bf16[1,288]{1,0:T(2,128)(2,1)S(1)} %copy.196), channel_id=1, replica_groups=mesh['section'=2,'ctx'=16,'fsdp'=4] {'ctx'}, use_global_device_ids=true, to_apply=%region_31.32 | all-reduce | flops 736 | bytes 2944 | tf_op jit(solution)/shard_map/psum | solution.py:344
  1534.4 92.5 %all-reduce.9.cloned.1.call-done = (bf16[1,224,1152]{2,1,0:T(8,128)(2,1)}, bf16[1,224,896]{2,1,0:T(8,128)(2,1)}, bf16[1,224,4864]{2,1,0:T(8,128)(2,1)}, bf16[1,2...) async-done(((bf16[1,224,1152]{2,1,0:T(8,128)(2,1)}, bf16[1,224,896]{2,1,0:T(8,128)(2,1)}, bf16[1,224,4864]{2,1,0:T(8,128)(2,1)}, bf16[1,224,4864]{2,1,0:T(8,128)(2,1)}, ...) | async-done | bytes 7454736 | tf_op jit(solution)/shard_map/psum | solution.py:344
  (603 shorter events, 390.4 us)
Async XLA Ops:
  7.2 37.6 %all-gather.6.cloned.1.call-start = ((), (), s32[]{:S(2)}) async-start(), calls=%async_computation.14 | async-start | bytes 2580480 | tf_op jit(solution)/shard_map/all_gather | solution.py:280
  8.0 114.4 %all-gather.8.cloned.1.call-start = ((), (), s32[]{:S(2)}) async-start(), calls=%async_computation.15 | async-start | bytes 2007040 | tf_op jit(solution)/shard_map/all_gather | solution.py:282
  8.7 150.6 %all-gather.10.cloned.1.call-start = ((), (), s32[]{:S(2)}) async-start(), calls=%async_computation.16 | async-start | bytes 10895360 | tf_op jit(solution)/shard_map/all_gather | solution.py:283
  9.5 238.3 %all-gather.12.cloned.1.call-start = ((), (), s32[]{:S(2)}) async-start(), calls=%async_computation.17 | async-start | bytes 10895360 | tf_op jit(solution)/shard_map/all_gather | solution.py:284
  10.0 326.2 %all-gather.14.cloned.1.call-start = ((), (), s32[]{:S(2)}) async-start(), calls=%async_computation.18 | async-start | bytes 10895360 | tf_op jit(solution)/shard_map/all_gather | solution.py:285
  10.6 608.9 %reduce-scatter.43.cloned.1.call-start = ((), (), s32[]{:S(2)}) async-start(), calls=%async_computation.24 | async-start | bytes 557056
  44.2 329.0 %copy-start.77 = (f32[1,128,128]{2,1,0:T(8,128)}, f32[1,128,128]{2,1,0:T(8,128)S(1)}, u32[]{:S(2)}) copy-start(f32[1,128,128]{2,1,0:T(8,128)S(1)} %copy.115) | copy-start | bytes 196612
  124.4 211.8 %copy-start.12 = (f32[128,896]{1,0:T(8,128)}, f32[128,896]{1,0:T(8,128)S(1)}, u32[]{:S(2)}) copy-start(f32[128,896]{1,0:T(8,128)S(1)} %get-tuple-element.105) | copy-start | bytes 1376260
  341.3 2.8 collective-permute-start
  427.0 5.8 collective-permute-start.1
  432.8 539.4 %copy-start.26 = (bf16[1,128,896]{2,1,0:T(8,128)(2,1)}, bf16[1,128,896]{2,1,0:T(8,128)(2,1)S(1)}, u32[]{:S(2)}) copy-start(bf16[1,128,896]{2,1,0:T(8,128)(2,1)S(1)} %collective-permute-done.1) | copy-start | bytes 688132
  516.9 182.4 %copy-start.9 = (f32[1,128,896]{2,1,0:T(8,128)}, f32[1,128,896]{2,1,0:T(8,128)S(1)}, u32[]{:S(2)}) copy-start(f32[1,128,896]{2,1,0:T(8,128)S(1)} %fusion.218) | copy-start | bytes 1376260
  548.7 146.4 %reduce-scatter.45.cloned.1.call-start = ((), (), s32[]{:S(2)}) async-start(), calls=%async_computation.25 | async-start | bytes 557056
  560.6 140.6 %copy-start.91 = (f32[2,7,128]{2,1,0:T(8,128)S(1)}, f32[2,7,128]{2,1,0:T(8,128)}, u32[]{:S(2)}) copy-start(f32[2,7,128]{2,1,0:T(8,128)} %copy-done.90) | copy-start | bytes 21508
  560.7 265.2 %reduce-scatter.47.cloned.1.call-start = ((), (), s32[]{:S(2)}) async-start(), calls=%async_computation.26 | async-start | bytes 557056
  700.0 3.5 collective-permute-start.2
  721.7 183.4 %copy-start.29 = (f32[1,128,896]{2,1,0:T(8,128)}, f32[1,128,896]{2,1,0:T(8,128)S(1)}, u32[]{:S(2)}) copy-start(f32[1,128,896]{2,1,0:T(8,128)S(1)} %fusion.212) | copy-start | bytes 1376260
  754.1 147.4 %reduce-scatter.49.cloned.1.call-start = ((), (), s32[]{:S(2)}) async-start(), calls=%async_computation.27 | async-start | bytes 557056
  768.4 260.1 %reduce-scatter.51.cloned.1.call-start = ((), (), s32[]{:S(2)}) async-start(), calls=%async_computation.28 | async-start | bytes 557056
  906.1 3.5 collective-permute-start.3
  956.7 147.4 %reduce-scatter.53.cloned.1.call-start = ((), (), s32[]{:S(2)}) async-start(), calls=%async_computation.29 | async-start | bytes 557056
  966.3 255.4 %reduce-scatter.35.cloned.1.call-start = ((), (), s32[]{:S(2)}) async-start(), calls=%async_computation.20 | async-start | bytes 2007040 | tf_op jit(solution)/shard_map/reduce_scatter | solution.py:342
  972.1 249.6 %reduce-scatter.33.cloned.1.call-start = ((), (), s32[]{:S(2)}) async-start(), calls=%async_computation.19 | async-start | bytes 2580480 | tf_op jit(solution)/shard_map/reduce_scatter | solution.py:342
  1109.6 140.5 %reduce-scatter.37.cloned.1.call-start = ((), (), s32[]{:S(2)}) async-start(), calls=%async_computation.21 | async-start | bytes 10895360 | tf_op jit(solution)/shard_map/reduce_scatter | solution.py:342
  1143.2 192.2 %reduce-scatter.39.cloned.1.call-start = ((), (), s32[]{:S(2)}) async-start(), calls=%async_computation.22 | async-start | bytes 10895360 | tf_op jit(solution)/shard_map/reduce_scatter | solution.py:342
  1177.7 243.3 %reduce-scatter.41.cloned.1.call-start = ((), (), s32[]{:S(2)}) async-start(), calls=%async_computation.23 | async-start | bytes 10895360 | tf_op jit(solution)/shard_map/reduce_scatter | solution.py:342
  1211.7 209.3 %copy-start.17 = (f32[1,128,896]{2,1,0:T(8,128)S(1)}, f32[1,128,896]{2,1,0:T(8,128)}, u32[]{:S(2)}) copy-start(f32[1,128,896]{2,1,0:T(8,128)} %copy-done.16) | copy-start | bytes 1376260
  1211.7 231.9 %reduce-scatter.57.cloned.1.call-start = ((), (), s32[]{:S(2)}) async-start(), calls=%async_computation.31 | async-start | bytes 286720
  1215.2 251.3 %reduce-scatter.55.cloned.1.call-start = ((), (), s32[]{:S(2)}) async-start(), calls=%async_computation.30 | async-start | bytes 286720
  1217.8 203.2 %copy-start.21 = (bf16[128,4864]{1,0:T(8,128)(2,1)S(1)}, bf16[128,4864]{1,0:T(8,128)(2,1)}, u32[]{:S(2)}) copy-start(bf16[128,4864]{1,0:T(8,128)(2,1)} %get-tuple-element.74) | copy-start | bytes 3735556
  1220.6 269.4 %reduce-scatter.59.cloned.1.call-start = ((), (), s32[]{:S(2)}) async-start(), calls=%async_computation.32 | async-start | bytes 368640
  1221.7 405.2 %all-reduce.9.cloned.1.call-start = ((), (), s32[]{:S(2)}) async-start(), calls=%async_computation.33 | async-start | bytes 14909440 | tf_op jit(solution)/shard_map/psum | solution.py:344
  (146 other events, 3110.8 us)
Sparse Core Ops, SparseCore 0:
  9.7 33.5 all-gather.5
  45.0 26.7 all-gather.7
  73.4 85.8 all-gather.9
  160.8 86.9 all-gather.11
  249.3 86.9 all-gather.13
  548.8 70.6 reduce-scatter.42
  623.6 71.4 reduce-scatter.44
  754.3 71.5 reduce-scatter.46
  829.9 71.5 reduce-scatter.48
  956.8 71.6 reduce-scatter.50
  1032.5 71.5 reduce-scatter.52
  1106.9 25.4 reduce-scatter.34
  1135.4 29.2 reduce-scatter.32
  1167.2 82.9 reduce-scatter.36
  1252.5 82.9 reduce-scatter.38
  1338.0 82.9 reduce-scatter.40
  1423.2 20.4 reduce-scatter.56
  1446.0 20.4 reduce-scatter.54
  1469.4 20.5 reduce-scatter.58
  1493.9 132.8 all-reduce.8
where the time goes:
time: 1650 us
  waiting for transfers between devices  935 us (57%)
  matrix products  335 us (20%)
  blocking collectives  212 us (13%)
  other arithmetic  76.2 us (5%)
  local copies, waits for them, and re-layouts  61 us (4%)
  between operations  19.2 us (1%)
    unnamed x29, waiting for transfers between devices  440 us
    reduce_scatter x5, waiting for transfers between devices, local(): lax.psum_scatter(shortened(full_grads), 'fsdp', scatter_dimension=1, tile...  199 us
    psum x1, waiting for transfers between devices, local(): lax.psum(shortened(shares), 'ctx')  92.5 us
    all_gather x1, waiting for transfers between devices, local(): lax.all_gather(up_weight, 'fsdp', axis=1, tiled=True)  82.1 us
    all_gather x1, waiting for transfers between devices, local(): lax.all_gather(down_weight, 'fsdp', axis=1, tiled=True)  81.2 us
    all_gather x3, blocking collectives, forward(): lax.all_gather(keys_own, 'ctx', axis=1, tiled=True)  71.5 us
    all_gather x3, blocking collectives, forward(): lax.all_gather(values_own, 'ctx', axis=1, tiled=True)  70.9 us
    unnamed x348, local copies, waits for them, and re-layouts  50.1 us
  transfers between devices with their start and end apart: 24, of which 19 were waited for; matrix products, arithmetic and copies ran while one was open for 15% of the time, Pallas kernels for 0%

commit v1 on v0

v1 whole, which is shorter than its diff:
```python
import functools

import jax
import jax.numpy as jnp
from jax import lax
from jax.experimental import pallas as pl
from jax.experimental.pallas import tpu as pltpu
from jax.sharding import PartitionSpec as P

D = 896
HEADS = 14
KV_HEADS = 2
HEAD_DIM = 64
GROUP = HEADS // KV_HEADS
FF = 4864
QKV = 1152
EPS = 1e-06
THETA = 1000000.0
LANES = 128
TILES = D // LANES
WIN = 1280
NEG = -1e30
F32 = jnp.float32
BF16 = jnp.bfloat16
MESH = pl.DeviceIdType.MESH
VMEM_LIMIT = 56 * 2**20


def mm(a, b):
    return jnp.dot(a, b, preferred_element_type=F32)


def mm_nt(a, b):
    return lax.dot_general(a, b, (((1,), (1,)), ((), ())), preferred_element_type=F32)


def greet(axis, n):
    me = lax.axis_index(axis)
    bar = pltpu.get_barrier_semaphore()

    def one(k, c):
        pl.semaphore_signal(
            bar, inc=1, device_id={axis: lax.rem(me + k, n)}, device_id_type=MESH
        )
        return c

    lax.fori_loop(1, n, one, 0)
    return bar


def push(src, dst, ssem, rsem, axis, to):
    return pltpu.make_async_remote_copy(
        src_ref=src,
        dst_ref=dst,
        send_sem=ssem,
        recv_sem=rsem,
        device_id={axis: to},
        device_id_type=MESH,
    )


def rope(u, cos, sa, sb):
    return u * cos + pltpu.roll(u, 96, 1) * sa + pltpu.roll(u, 32, 1) * sb


def unrope(u, cos, sa, sb):
    return u * cos - pltpu.roll(u, 96, 1) * sa - pltpu.roll(u, 32, 1) * sb


def spread(ref, t, tile_t):
    half = HEAD_DIM
    zero = jnp.zeros((half, LANES), BF16)
    for j in range(2):
        h = 2 * t + j
        slab = tile_t[j * half : (j + 1) * half, :].astype(BF16)
        both = [slab, zero] if h // GROUP == 0 else [zero, slab]
        ref[:, h * LANES : (h + 1) * LANES] = jnp.concatenate(both, 0)


def gathered_tile(wide, t):
    half = HEAD_DIM
    rows = []
    for j in range(2):
        g = (2 * t + j) // GROUP
        rows.append(wide[g * half : (g + 1) * half, j * LANES : (j + 1) * LANES])
    return jnp.concatenate(rows, 0).T


def attn_fwd_kernel(
    n, x_ref, g1_ref, g2_ref, wqkv_ref, bias_ref, cos_ref, sa_ref, sb_ref, kpos_ref, qpos_ref, wout_ref,
    mid_ref, n2_ref, n1_ref, qst_ref, kv_ref, lse_ref, att_ref,
    m_s, l_s, acc_s, ssem, rsem,
):
    me = lax.axis_index("ctx")
    bar = greet("ctx", n)
    x = x_ref[...]
    r1 = lax.rsqrt(jnp.mean(x * x, -1, keepdims=True) + EPS)
    n1 = (x * r1 * g1_ref[...]).astype(BF16)
    n1_ref[...] = n1
    cos, sa, sb = cos_ref[...], sa_ref[...], sb_ref[...]
    lin = mm(n1, wqkv_ref[:, D:]) + bias_ref[:, D:]
    kv_ref[me] = jnp.concatenate(
        [rope(lin[:, :LANES], cos, sa, sb), lin[:, LANES:]], 1
    ).astype(BF16)
    pl.semaphore_wait(bar, n - 1)

    def start(k, c):
        push(kv_ref.at[me], kv_ref.at[me], ssem.at[k], rsem.at[k], "ctx", lax.rem(me + k, n)).start()
        return c

    lax.fori_loop(1, n, start, 0)
    linq = mm(n1, wqkv_ref[:, :D]) + bias_ref[:, :D]
    for t in range(TILES):
        q = rope(linq[:, t * LANES : (t + 1) * LANES], cos, sa, sb) * HEAD_DIM ** (-0.5)
        spread(qst_ref, t, q.T)
    m_s[...] = jnp.full_like(m_s, NEG)
    l_s[...] = jnp.zeros_like(l_s)
    acc_s[...] = jnp.zeros_like(acc_s)
    qpos = qpos_ref[...]

    def block(src):
        keys = kv_ref[src, :, :LANES]
        vals_t = kv_ref[src, :, LANES:].astype(F32).T.astype(BF16)
        hide = jnp.where(kpos_ref[src] <= qpos, 0.0, NEG)
        hide = jnp.concatenate([hide, hide], 1)
        for t in range(TILES):
            cols = slice(2 * t * LANES, 2 * (t + 1) * LANES)
            s = mm(keys, qst_ref[:, cols]) + hide
            m_old = m_s[:, cols]
            m_new = jnp.maximum(m_old, jnp.max(s, 0, keepdims=True))
            p = jnp.exp(s - m_new)
            alpha = jnp.exp(m_old - m_new)
            m_s[:, cols] = m_new
            l_s[:, cols] = l_s[:, cols] * alpha + jnp.sum(p, 0, keepdims=True)
            acc_s[:, cols] = acc_s[:, cols] * alpha + mm(vals_t, p.astype(BF16))

    block(me)

    def step(k, c):
        src = lax.rem(me + n - k, n)
        push(kv_ref.at[src], kv_ref.at[src], ssem.at[k], rsem.at[k], "ctx", lax.rem(me + k, n)).wait_recv()
        block(src)
        return c

    lax.fori_loop(1, n, step, 0)
    lse_ref[...] = m_s[...] + jnp.log(l_s[...])
    for t in range(TILES):
        cols = slice(2 * t * LANES, 2 * (t + 1) * LANES)
        wide = acc_s[:, cols] / l_s[:, cols]
        att_ref[:, t * LANES : (t + 1) * LANES] = gathered_tile(wide, t).astype(BF16)
    mid = x + mm(att_ref[...], wout_ref[...])
    mid_ref[...] = mid
    r2 = lax.rsqrt(jnp.mean(mid * mid, -1, keepdims=True) + EPS)
    n2_ref[...] = (mid * r2 * g2_ref[...]).astype(BF16)

    def done(k, c):
        push(kv_ref.at[me], kv_ref.at[me], ssem.at[k], rsem.at[k], "ctx", lax.rem(me + k, n)).wait_send()
        return c

    lax.fori_loop(1, n, done, 0)


def attn_bwd_kernel(
    n, gm_ref, x_ref, g1_ref, wqkv_ref, wout_ref, qst_ref, kv_ref, lse_ref, att_ref,
    cos_ref, sa_ref, sb_ref, kpos_ref, qpos_ref,
    gx_ref, glin_ref, gmb_ref, dg1_ref,
    gst_s, delta_s, gq_s, send_s, land_s, ssem, rsem,
):
    me = lax.axis_index("ctx")
    bar = greet("ctx", n)
    half = HEAD_DIM
    gm = gm_ref[...]
    gmb = gm.astype(BF16)
    gmb_ref[...] = gmb
    ga = mm_nt(gmb, wout_ref[...])
    for t in range(TILES):
        tile = slice(t * LANES, (t + 1) * LANES)
        ga_t = ga[:, tile].T
        spread(gst_s, t, ga_t)
        prod = ga_t * att_ref[:, tile].astype(F32).T
        delta_s[:, 2 * t * LANES : (2 * t + 1) * LANES] = jnp.sum(prod[:half], 0, keepdims=True)
        delta_s[:, (2 * t + 1) * LANES : (2 * t + 2) * LANES] = jnp.sum(prod[half:], 0, keepdims=True)
    gq_s[...] = jnp.zeros_like(gq_s)
    qpos = qpos_ref[...]
    pl.semaphore_wait(bar, n - 1)

    def block(src):
        keys = kv_ref[src, :, :LANES]
        vals = kv_ref[src, :, LANES:]
        keys_t = keys.astype(F32).T.astype(BF16)
        hide = jnp.where(kpos_ref[src] <= qpos, 0.0, NEG)
        hide = jnp.concatenate([hide, hide], 1)
        gk = jnp.zeros((LANES, LANES), F32)
        gv = jnp.zeros((LANES, LANES), F32)
        for t in range(TILES):
            cols = slice(2 * t * LANES, 2 * (t + 1) * LANES)
            qs, gs = qst_ref[:, cols], gst_s[:, cols]
            p = jnp.exp(mm(keys, qs) + hide - lse_ref[:, cols])
            ds = (p * (mm(vals, gs) - delta_s[:, cols])).astype(BF16)
            gv = gv + mm_nt(p.astype(BF16), gs)
            gk = gk + mm_nt(ds, qs)
            gq_s[:, cols] += mm(keys_t, ds)
        return jnp.concatenate([gk, gv], 1)

    def step(k, c):
        to = lax.rem(me + k, n)
        send_s[k] = block(to).astype(BF16)
        push(send_s.at[k], land_s.at[k], ssem.at[k], rsem.at[k], "ctx", to).start()
        return c

    lax.fori_loop(1, n, step, 0)
    own = block(me)

    def take(k, total):
        push(send_s.at[k], land_s.at[k], ssem.at[k], rsem.at[k], "ctx", lax.rem(me + k, n)).wait_recv()
        return total + land_s[k].astype(F32)

    own = lax.fori_loop(1, n, take, own)
    cos, sa, sb = cos_ref[...], sa_ref[...], sb_ref[...]
    for t in range(TILES):
        wide = gq_s[:, 2 * t * LANES : 2 * (t + 1) * LANES]
        gq = gathered_tile(wide, t) * HEAD_DIM ** (-0.5)
        glin_ref[:, t * LANES : (t + 1) * LANES] = unrope(gq, cos, sa, sb).astype(BF16)
    glin_ref[:, D : D + LANES] = unrope(own[:, :LANES], cos, sa, sb).astype(BF16)
    glin_ref[:, D + LANES :] = own[:, LANES:].astype(BF16)
    gn1 = mm_nt(glin_ref[...], wqkv_ref[...])
    x = x_ref[...]
    r1 = lax.rsqrt(jnp.mean(x * x, -1, keepdims=True) + EPS)
    unit = x * r1
    dg1_ref[...] = jnp.sum(gn1 * unit, 0, keepdims=True)
    dz = gn1 * g1_ref[...]
    gx_ref[...] = gm + r1 * (dz - unit * jnp.mean(dz * unit, -1, keepdims=True))

    def done(k, c):
        push(send_s.at[k], land_s.at[k], ssem.at[k], rsem.at[k], "ctx", lax.rem(me + k, n)).wait_send()
        return c

    lax.fori_loop(1, n, done, 0)


def ffn_fwd_kernel(
    n, n2_ref, mid_ref, wg_ref, wu_ref, wd_ref,
    y_ref, all_ref, gate_ref, up_ref,
    send_s, land_s, ssem, rsem, ssem2, rsem2,
):
    me = lax.axis_index("fsdp")
    bar = greet("fsdp", n)
    all_ref[me] = n2_ref[...]
    order = [k for k in (1, 3, 2) if k < n]
    pl.semaphore_wait(bar, n - 1)

    def first(k):
        return push(all_ref.at[me], all_ref.at[me], ssem.at[k], rsem.at[k], "fsdp", lax.rem(me + k, n))

    def second(k):
        return push(send_s.at[k], land_s.at[k], ssem2.at[k], rsem2.at[k], "fsdp", lax.rem(me + n - k, n))

    for k in order:
        first(k).start()

    def block(src):
        a = all_ref[src]
        gate = mm(a, wg_ref[...])
        up = mm(a, wu_ref[...])
        gate_ref[src] = gate
        up_ref[src] = up
        hidden = (gate * jax.nn.sigmoid(gate) * up).astype(BF16)
        return mm(hidden, wd_ref[...])

    y_ref[...] = mid_ref[...] + block(me)
    for k in order:
        first(k).wait_recv()
        send_s[k] = block(lax.rem(me + n - k, n)).astype(BF16)
        second(k).start()
    for k in order:
        second(k).wait_recv()
        y_ref[...] += land_s[k].astype(F32)
    for k in order:
        first(k).wait_send()
        second(k).wait_send()


def ffn_bwd_kernel(
    n, gy_ref, mid_ref, g2_ref, wg_ref, wu_ref, wd_ref, gate_ref, up_ref,
    gm_ref, all_ref, hid_ref, ggate_ref, gup_ref, dg2_ref,
    own_s, send_s, land_s, ssem, rsem, ssem2, rsem2,
):
    me = lax.axis_index("fsdp")
    bar = greet("fsdp", n)
    all_ref[me] = gy_ref[...].astype(BF16)
    order = [k for k in (1, 3, 2) if k < n]
    pl.semaphore_wait(bar, n - 1)

    def first(k):
        return push(all_ref.at[me], all_ref.at[me], ssem.at[k], rsem.at[k], "fsdp", lax.rem(me + k, n))

    def second(k):
        return push(send_s.at[k], land_s.at[k], ssem2.at[k], rsem2.at[k], "fsdp", lax.rem(me + n - k, n))

    for k in order:
        first(k).start()

    def block(src):
        gh = mm_nt(all_ref[src], wd_ref[...])
        gate, up = gate_ref[src], up_ref[src]
        sg = jax.nn.sigmoid(gate)
        act = gate * sg
        hid_ref[src] = (act * up).astype(BF16)
        ggate = (gh * up * sg * (1.0 + gate * (1.0 - sg))).astype(BF16)
        gup = (gh * act).astype(BF16)
        ggate_ref[src] = ggate
        gup_ref[src] = gup
        return mm_nt(ggate, wg_ref[...]) + mm_nt(gup, wu_ref[...])

    own_s[...] = block(me)
    for k in order:
        first(k).wait_recv()
        send_s[k] = block(lax.rem(me + n - k, n)).astype(BF16)
        second(k).start()
    for k in order:
        second(k).wait_recv()
        own_s[...] += land_s[k].astype(F32)
    gn2 = own_s[...]
    mid = mid_ref[...]
    r2 = lax.rsqrt(jnp.mean(mid * mid, -1, keepdims=True) + EPS)
    unit = mid * r2
    dg2_ref[...] = jnp.sum(gn2 * unit, 0, keepdims=True)
    dz = gn2 * g2_ref[...]
    gm_ref[...] = gy_ref[...] + r2 * (dz - unit * jnp.mean(dz * unit, -1, keepdims=True))
    for k in order:
        first(k).wait_send()
        second(k).wait_send()


def call(kernel, n, ins, outs, scratch, cid, name, flops):
    vm = pl.BlockSpec(memory_space=pltpu.VMEM)
    moved = sum(a.size * a.dtype.itemsize for a in ins)
    return pl.pallas_call(
        functools.partial(kernel, n),
        out_shape=[jax.ShapeDtypeStruct(s, t) for s, t in outs],
        in_specs=[vm] * len(ins),
        out_specs=[vm] * len(outs),
        scratch_shapes=scratch,
        compiler_params=pltpu.CompilerParams(
            collective_id=cid, has_side_effects=True, vmem_limit_bytes=VMEM_LIMIT
        ),
        cost_estimate=pl.CostEstimate(flops=flops, bytes_accessed=moved, transcendentals=0),
        name=name,
    )(*ins)


def attn_fwd(x, g1, g2, wqkv, bias, tabs, wout):
    n = lax.axis_size("ctx")
    tok = x.shape[0]
    wide = HEADS * LANES
    cos, sa, sb, kpos, qpos = tabs
    dma = pltpu.SemaphoreType.DMA
    return call(
        attn_fwd_kernel, n,
        (x, g1, g2, wqkv, bias, cos, sa, sb, kpos, qpos, wout),
        [((tok, D), F32), ((tok, D), BF16), ((tok, D), BF16), ((LANES, wide), BF16),
         ((n, tok, 2 * LANES), BF16), ((1, wide), F32), ((tok, D), BF16)],
        [pltpu.VMEM((1, wide), F32), pltpu.VMEM((1, wide), F32), pltpu.VMEM((LANES, wide), F32), dma((n,)), dma((n,))],
        1, "attn_fwd", 10 * 10**9,
    )


def attn_bwd(gm, x, g1, wqkv, wout, saved, tabs):
    n = lax.axis_size("ctx")
    tok = x.shape[0]
    wide = HEADS * LANES
    cos, sa, sb, kpos, qpos = tabs
    qst, kv, lse, att = saved
    dma = pltpu.SemaphoreType.DMA
    return call(
        attn_bwd_kernel, n,
        (gm, x, g1, wqkv, wout, qst, kv, lse, att, cos, sa, sb, kpos, qpos),
        [((tok, D), F32), ((tok, QKV), BF16), ((tok, D), BF16), ((1, D), F32)],
        [pltpu.VMEM((LANES, wide), BF16), pltpu.VMEM((1, wide), F32), pltpu.VMEM((LANES, wide), F32),
         pltpu.VMEM((n, tok, 2 * LANES), BF16), pltpu.VMEM((n, tok, 2 * LANES), BF16), dma((n,)), dma((n,))],
        2, "attn_bwd", 20 * 10**9,
    )


def ffn_fwd(n2, mid, wg, wu, wd):
    n = lax.axis_size("fsdp")
    tok = n2.shape[0]
    dma = pltpu.SemaphoreType.DMA
    return call(
        ffn_fwd_kernel, n, (n2, mid, wg, wu, wd),
        [((tok, D), F32), ((n, tok, D), BF16), ((n, tok, WIN), F32), ((n, tok, WIN), F32)],
        [pltpu.VMEM((n, tok, D), BF16), pltpu.VMEM((n, tok, D), BF16), dma((n,)), dma((n,)), dma((n,)), dma((n,))],
        3, "ffn_fwd", 10 * 10**9,
    )


def ffn_bwd(gy, mid, g2, wg, wu, wd, gate, up):
    n = lax.axis_size("fsdp")
    tok = gy.shape[0]
    dma = pltpu.SemaphoreType.DMA
    return call(
        ffn_bwd_kernel, n, (gy, mid, g2, wg, wu, wd, gate, up),
        [((tok, D), F32), ((n, tok, D), BF16), ((n, tok, WIN), BF16), ((n, tok, WIN), BF16),
         ((n, tok, WIN), BF16), ((1, D), F32)],
        [pltpu.VMEM((tok, D), F32), pltpu.VMEM((n, tok, D), BF16), pltpu.VMEM((n, tok, D), BF16),
         dma((n,)), dma((n,)), dma((n,)), dma((n,))],
        4, "ffn_bwd", 20 * 10**9,
    )


def dealt_positions(chosen_pair, block_len, ctx_count):
    within = jnp.arange(2 * block_len, dtype=jnp.int32)
    first = chosen_pair * block_len + within
    second = (2 * ctx_count - 1 - chosen_pair) * block_len + within - block_len
    return jnp.where(within < block_len, first, second)


def tables(pair_of):
    n = lax.axis_size("ctx")
    block_len = 64
    all_pairs = lax.all_gather(pair_of, "ctx", axis=0, tiled=True)
    own = dealt_positions(pair_of[0], block_len, n)
    kpos = jax.vmap(lambda p: dealt_positions(p, block_len, n))(all_pairs)
    freq = jnp.arange(HEAD_DIM // 2, dtype=F32)
    inverse = THETA ** (-2.0 * freq / HEAD_DIM)
    angles = own.astype(F32)[:, None] * inverse[None, :]
    cos, sin = jnp.cos(angles), jnp.sin(angles)
    zero = jnp.zeros_like(sin)
    return (
        jnp.concatenate([cos] * 4, -1),
        jnp.concatenate([-sin, zero] * 2, -1),
        jnp.concatenate([zero, sin] * 2, -1),
        kpos[:, :, None],
        own[None, :],
    )


def window_starts():
    n = lax.axis_size("fsdp")
    share = FF // n
    return [(i * share // LANES) * LANES for i in range(n)]


def local(
    tokens, cotangent, pair_of, attn_gain, ffn_gain, qkv_weight, qkv_bias, out_weight, gate_weight, up_weight, down_weight,
):
    s = lax.axis_index("section")
    z = lax.axis_index("fsdp")
    nz = lax.axis_size("fsdp")
    share = FF // nz
    starts = window_starts()
    tabs = tables(pair_of)
    both = ("section", "fsdp")

    small = jnp.concatenate([attn_gain[0], ffn_gain[0], qkv_bias[0]])
    small = lax.all_gather(small, both, axis=0, tiled=False).reshape(2, nz, -1)
    qd = D // nz
    gain1 = small[:, :, :qd].reshape(2, 1, D).astype(F32)
    gain2 = small[:, :, qd : 2 * qd].reshape(2, 1, D).astype(F32)
    bias = small[:, :, 2 * qd :].reshape(2, 1, QKV).astype(F32)
    wqkv = lax.all_gather(qkv_weight[0], both, axis=0).reshape(2, D, QKV)
    wout = lax.all_gather(out_weight[0], both, axis=0).reshape(2, D, D)

    def windows(w):
        return jnp.stack([w[:, a : a + WIN] for a in starts])

    gu = jnp.stack([windows(gate_weight[0]), windows(up_weight[0])], 1)
    gu = lax.all_to_all(gu, "fsdp", 0, 0)
    gu = gu.transpose(1, 0, 2, 3).reshape(2, D, WIN)
    gu = lax.all_gather(gu, "section", axis=0)
    pad = (WIN - share) * lax.rem(z, 2)
    down = jnp.pad(down_weight[0], ((WIN - share, WIN - share), (0, 0)))
    down = lax.dynamic_slice_in_dim(down, WIN - share - pad, WIN, 0)
    wd = lax.all_gather(down, "section", axis=0)

    x = jnp.where(s == 0, tokens[0, 0], tokens[1, 0])
    saved = []
    outs = []
    for l in range(2):
        mid, n2, n1, qst, kv, lse, att = attn_fwd(x, gain1[l], gain2[l], wqkv[l], bias[l], tabs, wout[l])
        y, n2_all, gate, up = ffn_fwd(n2, mid, gu[l, 0], gu[l, 1], wd[l])
        saved.append((x, mid, n1, (qst, kv, lse, att), n2_all, gate, up))
        outs.append(y)
        x = y.astype(BF16).astype(F32)

    gy = jnp.where(s == 0, cotangent[0, 0], cotangent[1, 0])
    grads = [None, None]
    gxs = [None, None]
    for l in (1, 0):
        x, mid, n1, attn_saved, n2_all, gate, up = saved[l]
        gm, gy_all, hid, ggate, gup, dg2 = ffn_bwd(gy, mid, gain2[l], gu[l, 0], gu[l, 1], wd[l], gate, up)
        gx, glin, gmb, dg1 = attn_bwd(gm, x, gain1[l], wqkv[l], wout[l], attn_saved, tabs)
        gxs[l] = gx
        gy = gx.astype(BF16).astype(F32)
        ddown = jnp.einsum("stf,std->fd", hid, gy_all, preferred_element_type=F32)
        dgate = jnp.einsum("std,stf->df", n2_all, ggate, preferred_element_type=F32)
        dup = jnp.einsum("std,stf->df", n2_all, gup, preferred_element_type=F32)
        dqkv = jnp.einsum("td,te->de", n1, glin, preferred_element_type=F32)
        dout = jnp.einsum("td,te->de", attn_saved[3], gmb, preferred_element_type=F32)
        dbias = jnp.sum(glin.astype(F32), 0)
        ddown = lax.dynamic_slice_in_dim(ddown, pad, share, 0)
        grads[l] = (ddown, dgate, dup, dqkv, dout, dg1[0], dg2[0], dbias)

    def over_sections(index):
        pair = jnp.stack([grads[0][index], grads[1][index]]).astype(BF16)
        return lax.psum_scatter(pair, "section", scatter_dimension=0, tiled=False)

    ddown, dgate, dup, dqkv, dout = (over_sections(i) for i in range(5))
    ddown = lax.psum(ddown, "ctx").astype(F32)
    dqkv = lax.psum_scatter(dqkv, "fsdp", scatter_dimension=0, tiled=True)
    dout = lax.psum_scatter(dout, "fsdp", scatter_dimension=0, tiled=True)
    dqkv, dout = lax.psum((dqkv, dout), "ctx")
    gu_grad = jnp.concatenate([dgate.reshape(nz, qd, WIN), dup.reshape(nz, qd, WIN)], 2)
    gu_grad = lax.psum_scatter(gu_grad, "ctx", scatter_dimension=2, tiled=True)
    gu_grad = lax.all_to_all(gu_grad, "fsdp", 0, 0)
    gu_grad = lax.all_gather(gu_grad, "ctx", axis=2, tiled=True).astype(F32)

    def assembled(w):
        total = jnp.zeros((qd, FF), F32)
        for i, a in enumerate(starts):
            total = total.at[:, a : a + WIN].add(w[i])
        return total

    small_grad = jnp.stack(
        [jnp.concatenate([g[5].reshape(nz, -1), g[6].reshape(nz, -1), g[7].reshape(nz, -1)], 1) for g in grads]
    )
    small_grad = lax.psum(small_grad, ("section", "ctx", "fsdp"))
    small_grad = lax.dynamic_slice(small_grad, (s, z, 0), (1, 1, small_grad.shape[2]))[0, 0]

    def by_layer(pair):
        theirs = jnp.where(s == 0, pair[1], pair[0])
        mine = jnp.where(s == 0, pair[0], pair[1])
        got = lax.ppermute(theirs, "section", [(0, 1), (1, 0)])
        return jnp.where(s == 0, jnp.stack([mine, got]), jnp.stack([got, mine]))[None, :, None]

    return (
        by_layer(outs),
        by_layer(gxs),
        small_grad[None, :qd],
        small_grad[None, qd : 2 * qd],
        dqkv.astype(F32)[None],
        small_grad[None, 2 * qd :],
        dout.astype(F32)[None],
        assembled(gu_grad[:, :, :WIN])[None],
        assembled(gu_grad[:, :, WIN:])[None],
        ddown[None],
    )


def solution(mesh):
    return jax.shard_map(
        local,
        mesh=mesh,
        in_specs=(
            P(None, "fsdp", "ctx", None),
            P(None, "fsdp", "ctx", None),
            P("ctx"),
            P("section", "fsdp"),
            P("section", "fsdp"),
            P("section", "fsdp", None),
            P("section", "fsdp"),
            P("section", "fsdp", None),
            P("section", "fsdp", None),
            P("section", "fsdp", None),
            P("section", "fsdp", None),
        ),
        out_specs=(
            P("section", None, "fsdp", "ctx", None),
            P("section", None, "fsdp", "ctx", None),
            P("section", "fsdp"),
            P("section", "fsdp"),
            P("section", "fsdp", None),
            P("section", "fsdp"),
            P("section", "fsdp", None),
            P("section", "fsdp", None),
            P("section", "fsdp", None),
            P("section", "fsdp", None),
        ),
        check_vma=False,
    )
```

time: 1650 us -> 849 us (0.51)
  waiting for transfers between devices: 935 us -> 252 us
  matrix products: 335 us -> 12.3 us
  Pallas kernels: 0 us -> 255 us
  other arithmetic: 76.2 us -> 51.5 us
  blocking collectives: 212 us -> 188 us
    unnamed x29 -> x13, waiting for transfers between devices: 440 us -> 2.05 us
    dot_general x63 -> x10, matrix products: 335 us -> 12.3 us  [the longest x2 3.11 us: local(): ddown = jnp.einsum('stf,std->fd', hid, gy_all, preferred_element_type=F32)]
    pallas_call x0 -> x8, Pallas kernels: none -> 255 us  [call(): pl.pallas_call(functools.partial(kernel, n), out_shape=[jax.ShapeDtypeStr...]
    all_gather x5, waiting for transfers between devices: 198 us -> 0.03 us  [the longest x1 0.02 us: local(): gu = lax.all_gather(gu, 'section', axis=0)]
    all_gather x6 -> x0, blocking collectives: 142 us -> none  [the longest x3 71.5 us: forward(): lax.all_gather(keys_own, 'ctx', axis=1, tiled=True)]
    reduce_scatter x5 -> x7, waiting for transfers between devices: 199 us -> 105 us  [the longest x5 43.5 us: over_sections(): return lax.psum_scatter(pair, 'section', scatter_dimension=0, tiled=False)]
    all_to_all x0 -> x2, blocking collectives: none -> 82.5 us  [the longest x1 71.1 us: local(): gu = lax.all_to_all(gu, 'fsdp', 0, 0)]
    psum x1, waiting for transfers between devices: 92.5 us -> 145 us  [local(): dqkv, dout = lax.psum((dqkv, dout), 'ctx')]
  transfers between devices with their start and end apart: 24 -> 15, of which waited for: 19 -> 7; matrix products, arithmetic and copies ran while one was open for 15% -> 10% of each run, Pallas kernels for 0% -> 4%
where the time goes in v1:
time: 849 us; the launch traced here: 845 us
  Pallas kernels  255 us (30%)
  waiting for transfers between devices  252 us (30%)
  blocking collectives  188 us (22%)
  local copies, waits for them, and re-layouts  67.7 us (8%)
  other arithmetic  51.5 us (6%)
  between operations  17 us (2%)
  matrix products  12.3 us (1%)
    pallas_call x8, Pallas kernels, call(): pl.pallas_call(functools.partial(kernel, n), out_shape=[jax.ShapeDtypeStr...  255 us
    psum x1, waiting for transfers between devices, local(): dqkv, dout = lax.psum((dqkv, dout), 'ctx')  145 us
    all_to_all x1, blocking collectives, local(): gu = lax.all_to_all(gu, 'fsdp', 0, 0)  71.1 us
    psum x1, blocking collectives, local(): small_grad = lax.psum(small_grad, ('section', 'ctx', 'fsdp'))  64.1 us
    reduce_scatter x5, waiting for transfers between devices, over_sections(): return lax.psum_scatter(pair, 'section', scatter_dimension=0, tiled=False)  43.5 us
    unnamed x2, blocking collectives  41.2 us
    reduce_scatter x1, waiting for transfers between devices, local(): dqkv = lax.psum_scatter(dqkv, 'fsdp', scatter_dimension=0, tiled=True)  31.8 us
    reduce_scatter x1, waiting for transfers between devices, local(): dout = lax.psum_scatter(dout, 'fsdp', scatter_dimension=0, tiled=True)  29.9 us
  transfers between devices with their start and end apart: 15, of which 7 were waited for; matrix products, arithmetic and copies ran while one was open for 10% of the time, Pallas kernels for 4%

profile of v1, /device:TPU:0, one launch (start us, length us, event | category | flops | bytes accessed | tf_op | source)
XLA Modules:
  0.0 844.6 jit_solution(2164186807226745994)
XLA Ops:
  7.2 3.2 pad_dynamic-slice_fusion
  14.9 71.1 %all_to_all.10 = bf16[4,2,224,1280]{3,2,1,0:T(8,128)(2,1)S(1)} all-to-all(bf16[4,2,224,1280]{3,2,1,0:T(8,128)(2,1)S(1)} %pad_maximum_fusion.1), channel_id=1, replica_groups=mesh['section'=2,'ctx'=16,'fsdp'=4] {'fsdp'}, dimensions={0} | all-to-all | bytes 9175040 | tf_op jit(solution)/shard_map/all_to_all | solution.py:468
  90.7 16.4 %all-reduce.4 = s32[16]{0:T(128)S(1)} all-reduce(s32[16]{0:T(128)S(1)} %dynamic-update-slice.27), channel_id=1, replica_groups=mesh['section'=2,'ctx'=16,'fsdp'=4] {'ctx'}, use_global_device_ids=true, to_apply=%add.4 | all-reduce | flops 16 | bytes 128
  108.8 24.8 %all-reduce.3 = bf16[5888]{0:T(1024)(128)(2,1)S(1)} all-reduce(bf16[5888]{0:T(1024)(128)(2,1)S(1)} %dynamic-update-slice.26), channel_id=2, replica_groups=mesh['section'=2,'ctx'=16,'fsdp'=4] {'section','fsdp'}, use_global_device_ids=true, to_apply=%add.3 | all-reduce | flops 5888 | bytes 23552
  143.3 4.8 fusion.24
  148.1 3.8 fusion.26
  151.9 4.5 fusion.25
  156.4 30.8 %attn_fwd.2 = (f32[128,896]{1,0:T(8,128)}, bf16[128,896]{1,0:T(8,128)(2,1)}, bf16[128,896]{1,0:T(8,128)(2,1)}, bf16[128,1792]{1,0:T(8,128)(2,1)}, bf16[16,128,25...) custom-call(f32[128,896]{1,0:T(8,128)} %select_bitcast_fusion.3.x_ref, f32[1,896]{1,0:T(1,128)} %squeeze.47.g1_ref, ...), custom_call_target="tpu_custom_call" | custom-call | flops 10000000000 | bytes 4345856 | tf_op jit(solution)/shard_map/attn_fwd/pallas_call | solution.py:338
  187.3 6.7 slice_bitcast_fusion
  194.0 29.1 %ffn_fwd.2 = (f32[128,896]{1,0:T(8,128)}, bf16[4,128,896]{2,1,0:T(8,128)(2,1)}, f32[4,128,1280]{2,1,0:T(8,128)}, f32[4,128,1280]{2,1,0:T(8,128)}) custom-call(bf16[128,896]{1,0:T(8,128)(2,1)} %get-tuple-element.148.n2_ref, f32[128,896]{1,0:T(8,128)} %get-tuple-element.149.mid_ref, bf16[896,1280]{1,0:T(8,128)(2,1)} %get-tuple-element.215.wg_ref, ...), custom_call_target="tpu_custom_call" | custom-call | flops 10000000000 | bytes 7569408 | tf_op jit(solution)/shard_map/ffn_fwd/pallas_call | solution.py:338
  225.0 25.2 %attn_fwd.3 = (f32[128,896]{1,0:T(8,128)}, bf16[128,896]{1,0:T(8,128)(2,1)}, bf16[128,896]{1,0:T(8,128)(2,1)}, bf16[128,1792]{1,0:T(8,128)(2,1)}, bf16[16,128,25...) custom-call(f32[128,896]{1,0:T(8,128)} %convert_convert_fusion.1.x_ref, f32[1,896]{1,0:T(1,128)} %squeeze.108.g1_ref, ...), custom_call_target="tpu_custom_call" | custom-call | flops 10000000000 | bytes 4345856 | tf_op jit(solution)/shard_map/attn_fwd/pallas_call | solution.py:338
  250.1 30.7 %ffn_fwd.3 = (f32[128,896]{1,0:T(8,128)}, bf16[4,128,896]{2,1,0:T(8,128)(2,1)}, f32[4,128,1280]{2,1,0:T(8,128)}, f32[4,128,1280]{2,1,0:T(8,128)}) custom-call(bf16[128,896]{1,0:T(8,128)(2,1)} %get-tuple-element.151.n2_ref, f32[128,896]{1,0:T(8,128)} %get-tuple-element.152.mid_ref, bf16[896,1280]{1,0:T(8,128)(2,1)} %get-tuple-element.213.wg_ref, ...), custom_call_target="tpu_custom_call" | custom-call | flops 10000000000 | bytes 7569408 | tf_op jit(solution)/shard_map/ffn_fwd/pallas_call | solution.py:338
  280.8 27.9 %ffn_bwd.2 = (f32[128,896]{1,0:T(8,128)}, bf16[4,128,896]{2,1,0:T(8,128)(2,1)}, bf16[4,128,1280]{2,1,0:T(8,128)(2,1)}, bf16[4,128,1280]{2,1,0:T(8,128)(2,1)}, bf...) custom-call(f32[128,896]{1,0:T(8,128)} %select_bitcast_fusion.1.gy_ref, f32[128,896]{1,0:T(8,128)} %get-tuple-element.152.mid_ref, ...), custom_call_target="tpu_custom_call" | custom-call | flops 20000000000 | bytes 13045248 | tf_op jit(solution)/shard_map/ffn_bwd/pallas_call | solution.py:338
  308.7 42.7 %attn_bwd.2 = (f32[128,896]{1,0:T(8,128)}, bf16[128,1152]{1,0:T(8,128)(2,1)}, bf16[128,896]{1,0:T(8,128)(2,1)}, f32[1,896]{1,0:T(1,128)}) custom-call(f32[128,896]{1,0:T(8,128)} %get-tuple-element.156.gm_ref, f32[128,896]{1,0:T(8,128)} %convert_convert_fusion.1.x_ref, f32[1,896]{1,0:T(1,128)} %squeeze.108.g1_ref, bf16[896,1152]{1,0:T(8,128)(2,1)} %bitcast.187, ...), custom_call_target="tpu_custom_call" | custom-call | flops 20000000000 | bytes 6540288 | tf_op jit(solution)/shard_map/attn_bwd/pallas_call | solution.py:338
  353.3 30.6 %ffn_bwd.3 = (f32[128,896]{1,0:T(8,128)}, bf16[4,128,896]{2,1,0:T(8,128)(2,1)}, bf16[4,128,1280]{2,1,0:T(8,128)(2,1)}, bf16[4,128,1280]{2,1,0:T(8,128)(2,1)}, bf...) custom-call(f32[128,896]{1,0:T(8,128)} %convert_convert_fusion.gy_ref, f32[128,896]{1,0:T(8,128)} %get-tuple-element.149.mid_ref, ...), custom_call_target="tpu_custom_call" | custom-call | flops 20000000000 | bytes 13045248 | tf_op jit(solution)/shard_map/ffn_bwd/pallas_call | solution.py:338
  383.9 37.8 %attn_bwd.3 = (f32[128,896]{1,0:T(8,128)}, bf16[128,1152]{1,0:T(8,128)(2,1)}, bf16[128,896]{1,0:T(8,128)(2,1)}, f32[1,896]{1,0:T(1,128)}) custom-call(f32[128,896]{1,0:T(8,128)} %get-tuple-element.164.gm_ref, f32[128,896]{1,0:T(8,128)} %select_bitcast_fusion.3.x_ref, f32[1,896]{1,0:T(1,128)} %squeeze.47.g1_ref, bf16[896,1152]{1,0:T(8,128)(2,1)} %bitcast.185, ...), custom_call_target="tpu_custom_call" | custom-call | flops 20000000000 | bytes 6540288 | tf_op jit(solution)/shard_map/attn_bwd/pallas_call | solution.py:338
  435.5 2.5 pad_maximum_fusion.2
  442.5 2.5 pad_maximum_fusion.3
  454.7 5.7 reduce-scatter.8.cloned.1.call-done
  460.7 18.8 %reduce-scatter.16.cloned.1.call-done = bf16[1,896,1280]{2,1,0:T(8,128)(2,1)} async-done(((bf16[2,896,1280]{2,1,0:T(8,128)(2,1)}), bf16[1,896,1280]{2,1,0:T(8,128)(2,1)}) %reduce-scatter.16.cloned.1.call-update) | async-done | bytes 2293776 | tf_op jit(solution)/shard_map/reduce_scatter | solution.py:506
  479.5 4.0 copy.51
  483.5 15.0 %reduce-scatter.18.cloned.1.call-done = bf16[1,896,1280]{2,1,0:T(8,128)(2,1)} async-done(((bf16[2,896,1280]{2,1,0:T(8,128)(2,1)}), bf16[1,896,1280]{2,1,0:T(8,128)(2,1)}) %reduce-scatter.18.cloned.1.call-update) | async-done | bytes 2293776 | tf_op jit(solution)/shard_map/reduce_scatter | solution.py:506
  498.5 5.2 copy.52
  503.6 10.4 %pad_maximum_fusion = bf16[4,224,2560]{1,0,2:T(4,128)(2,1)} fusion(bf16[4,224,1280]{1,0,2:T(4,128)(2,1)} %copy.52, bf16[4,224,1280]{1,0,2:T(4,128)(2,1)S(1)} %copy.51), kind=kLoop, calls=%fused_computation | loop fusion | flops 2293760 | bytes 9175040 | tf_op jit(solution)/shard_map/concatenate | solution.py:513
  514.0 4.0 reduce-scatter.20.cloned.1.call-done
  518.0 29.9 %reduce-scatter.14.cloned.1.call-done = bf16[224,896]{1,0:T(8,128)(2,1)} async-done(((bf16[896,896]{1,0:T(8,128)(2,1)}), bf16[224,896]{1,0:T(8,128)(2,1)}) %reduce-scatter.14.cloned.1.call-update) | async-done | bytes 401424 | tf_op jit(solution)/shard_map/reduce_scatter | solution.py:511
  547.8 31.8 %reduce-scatter.10.cloned.1.call-done = bf16[224,1152]{1,0:T(8,128)(2,1)} async-done(((bf16[896,1152]{1,0:T(8,128)(2,1)}), bf16[224,1152]{1,0:T(8,128)(2,1)}) %reduce-scatter.10.cloned.1.call-update) | async-done | bytes 516112 | tf_op jit(solution)/shard_map/reduce_scatter | solution.py:510
  580.4 144.8 %all-reduce.9.cloned.1.call-done = (bf16[1,224,1152]{2,1,0:T(8,128)(2,1)}, bf16[1,224,896]{2,1,0:T(8,128)(2,1)}, bf16[4,224,2560]{1,0,2:T(4,128)(2,1)}, bf16[1,1216,896]{2,1,0:T(8,128)(2,1)}) async-done(((bf16[1,224,1152]{2,1,0:T(8,128)(2,1)}, bf16[1,224,896]{2,1,0:T(8,128)(2,1)}, bf16[4,224,2560]{1,0,2:T(4,128)(2,1)}, bf16[1,1216,896]{2,1,0:T(8,128)(2,1)}), (bf16[1,224,1152]{2,1,0:T(8,128)(2,1)}, ...) | async-done | bytes 7684112 | tf_op jit(solution)/shard_map/psum | solution.py:512
  726.3 11.4 %all_to_all.11 = bf16[4,224,160]{1,2,0:T(8,128)(2,1)S(1)} all-to-all(bf16[4,224,160]{1,2,0:T(8,128)(2,1)S(1)} %copy.53), channel_id=1, replica_groups=mesh['section'=2,'ctx'=16,'fsdp'=4] {'fsdp'}, dimensions={0} | all-to-all | bytes 573440 | tf_op jit(solution)/shard_map/all_to_all | solution.py:515
  743.1 64.1 %psum.28 = f32[2,4,736]{2,1,0:T(4,128)S(1)} all-reduce(f32[2,4,736]{2,1,0:T(4,128)S(1)} %pad_maximum_fusion.10), channel_id=1, replica_groups=mesh['section'=2,'ctx'=16,'fsdp'=4] {'section','ctx','fsdp'}, use_global_device_ids=true, to_apply=%region_2.3 | all-reduce | flops 5888 | bytes 47104 | tf_op jit(solution)/shard_map/psum | solution.py:527
  817.1 9.0 %copy.55 = bf16[4,224,2560]{2,1,0:T(8,128)(2,1)} copy(bf16[4,224,2560]{1,0,2:T(4,128)(2,1)} %all-gather.14.cloned.1.call-done) | data formatting | bytes 9175040 | tf_op jit(solution)/shard_map/all_gather | solution.py:516
  826.1 3.5 convert_element_type.84
  (208 shorter events, 74.8 us)
Async XLA Ops:
  7.2 136.1 %all-gather.16.cloned.1.call-start = ((), (), s32[]{:S(2)}) async-start(), calls=%async_computation.20 | async-start | bytes 6881280 | tf_op jit(solution)/shard_map/all_gather | solution.py:474
  10.5 137.7 %all-gather.10.cloned.1.call-start = ((), (), s32[]{:S(2)}) async-start(), calls=%async_computation.10 | async-start | bytes 3612672 | tf_op jit(solution)/shard_map/all_gather | solution.py:462
  11.2 140.7 %all-gather.8.cloned.1.call-start = ((), (), s32[]{:S(2)}) async-start(), calls=%async_computation.9 | async-start | bytes 4644864 | tf_op jit(solution)/shard_map/all_gather | solution.py:461
  11.9 175.4 %all-gather.12.cloned.1.call-start = ((), (), s32[]{:S(2)}) async-start(), calls=%async_computation.11 | async-start | bytes 13762560 | tf_op jit(solution)/shard_map/all_gather | solution.py:470
  88.5 18.7 %copy-start.28 = (u32[128]{0:T(128)S(1)}, u32[128]{0:T(128)}, u32[]{:S(2)}) copy-start(u32[128]{0:T(128)} %constant.259) | copy-start | bytes 1540
  88.5 19.3 %copy-start.25 = (bf16[1,288]{1,0:T(2,128)(2,1)S(1)}, bf16[1,288]{1,0:T(2,128)(2,1)}, u32[]{:S(2)}) copy-start(bf16[1,288]{1,0:T(2,128)(2,1)} %param.33) | copy-start | bytes 1732
  88.5 19.3 %copy-start.26 = (bf16[1,224]{1,0:T(2,128)(2,1)S(1)}, bf16[1,224]{1,0:T(2,128)(2,1)}, u32[]{:S(2)}) copy-start(bf16[1,224]{1,0:T(2,128)(2,1)} %param.30) | copy-start | bytes 1348
  88.5 19.3 %copy-start.27 = (bf16[1,224]{1,0:T(2,128)(2,1)S(1)}, bf16[1,224]{1,0:T(2,128)(2,1)}, u32[]{:S(2)}) copy-start(bf16[1,224]{1,0:T(2,128)(2,1)} %param.31) | copy-start | bytes 1348
  88.5 51.8 %copy-start.9 = (f32[2,1,128,896]{3,2,1,0:T(8,128)S(1)}, f32[2,1,128,896]{3,2,1,0:T(8,128)}, u32[]{:S(2)}) copy-start(f32[2,1,128,896]{3,2,1,0:T(8,128)} %param.27) | copy-start | bytes 2752516
  88.5 52.6 %copy-start.10 = (f32[2,1,128,896]{3,2,1,0:T(8,128)S(1)}, f32[2,1,128,896]{3,2,1,0:T(8,128)}, u32[]{:S(2)}) copy-start(f32[2,1,128,896]{3,2,1,0:T(8,128)} %param.28) | copy-start | bytes 2752516
  88.6 365.6 %reduce-scatter.12.cloned.1.call-start = ((), (), s32[]{:S(2)}) async-start(), calls=%async_computation.14 | async-start | bytes 4816896 | tf_op jit(solution)/shard_map/reduce_scatter | solution.py:506
  383.9 37.9 %copy-start.17 = (bf16[128,896]{1,0:T(8,128)(2,1)S(1)}, bf16[128,896]{1,0:T(8,128)(2,1)}, u32[]{:S(2)}) copy-start(bf16[128,896]{1,0:T(8,128)(2,1)} %get-tuple-element.168.att_ref) | copy-start | bytes 688132
  383.9 39.4 %copy-start.18 = (bf16[128,896]{1,0:T(8,128)(2,1)S(1)}, bf16[128,896]{1,0:T(8,128)(2,1)}, u32[]{:S(2)}) copy-start(bf16[128,896]{1,0:T(8,128)(2,1)} %get-tuple-element.160.att_ref) | copy-start | bytes 688132
  383.9 39.4 %copy-start.19 = (bf16[128,896]{1,0:T(8,128)(2,1)S(1)}, bf16[128,896]{1,0:T(8,128)(2,1)}, u32[]{:S(2)}) copy-start(bf16[128,896]{1,0:T(8,128)(2,1)} %get-tuple-element.179) | copy-start | bytes 688132
  426.0 34.4 %reduce-scatter.8.cloned.1.call-start = ((), (), s32[]{:S(2)}) async-start(), calls=%async_computation.12 | async-start | bytes 6193152 | tf_op jit(solution)/shard_map/reduce_scatter | solution.py:506
  431.0 48.6 %reduce-scatter.16.cloned.1.call-start = ((), (), s32[]{:S(2)}) async-start(), calls=%async_computation.16 | async-start | bytes 6881280 | tf_op jit(solution)/shard_map/reduce_scatter | solution.py:506
  438.0 60.4 %reduce-scatter.18.cloned.1.call-start = ((), (), s32[]{:S(2)}) async-start(), calls=%async_computation.17 | async-start | bytes 6881280 | tf_op jit(solution)/shard_map/reduce_scatter | solution.py:506
  445.1 72.9 %reduce-scatter.20.cloned.1.call-start = ((), (), s32[]{:S(2)}) async-start(), calls=%async_computation.19 | async-start | bytes 6537216 | tf_op jit(solution)/shard_map/reduce_scatter | solution.py:506
  454.1 93.8 %reduce-scatter.14.cloned.1.call-start = ((), (), s32[]{:S(2)}) async-start(), calls=%async_computation.15 | async-start | bytes 2007040 | tf_op jit(solution)/shard_map/reduce_scatter | solution.py:511
  454.7 125.0 %reduce-scatter.10.cloned.1.call-start = ((), (), s32[]{:S(2)}) async-start(), calls=%async_computation.13 | async-start | bytes 2580480 | tf_op jit(solution)/shard_map/reduce_scatter | solution.py:510
  460.4 264.8 %all-reduce.9.cloned.1.call-start = ((), (), s32[]{:S(2)}) async-start(), calls=%async_computation.21 | async-start | bytes 16678912 | tf_op jit(solution)/shard_map/psum | solution.py:512
  579.7 160.5 %copy-start.23 = (f32[1,896]{1,0:T(1,128)S(1)}, f32[1,896]{1,0:T(1,128)}, u32[]{:S(2)}) copy-start(f32[1,896]{1,0:T(1,128)} %get-tuple-element.170) | copy-start | bytes 10756
  579.7 160.6 %copy-start.22 = (f32[1,896]{1,0:T(1,128)S(1)}, f32[1,896]{1,0:T(1,128)}, u32[]{:S(2)}) copy-start(f32[1,896]{1,0:T(1,128)} %get-tuple-element.171) | copy-start | bytes 10756
  579.7 160.7 %copy-start.6 = (f32[128,896]{1,0:T(8,128)S(1)}, f32[128,896]{1,0:T(8,128)}, u32[]{:S(2)}) copy-start(f32[128,896]{1,0:T(8,128)} %get-tuple-element.161) | copy-start | bytes 1376260
  579.7 160.7 %copy-start.13 = (f32[128,896]{1,0:T(8,128)S(1)}, f32[128,896]{1,0:T(8,128)}, u32[]{:S(2)}) copy-start(f32[128,896]{1,0:T(8,128)} %get-tuple-element.169) | copy-start | bytes 1376260
  579.7 237.4 %all-gather.14.cloned.1.call-start = ((), (), s32[]{:S(2)}) async-start(), calls=%async_computation.18 | async-start | bytes 5570560 | tf_op jit(solution)/shard_map/all_gather | solution.py:516
  726.3 14.9 %copy-start.5 = (f32[128,896]{1,0:T(8,128)S(1)}, f32[128,896]{1,0:T(8,128)}, u32[]{:S(2)}) copy-start(f32[128,896]{1,0:T(8,128)} %get-tuple-element.150) | copy-start | bytes 1376260
  726.3 14.9 %copy-start.12 = (f32[128,896]{1,0:T(8,128)S(1)}, f32[128,896]{1,0:T(8,128)}, u32[]{:S(2)}) copy-start(f32[128,896]{1,0:T(8,128)} %get-tuple-element.153) | copy-start | bytes 1376260
  738.7 4.2 copy-start.20
  741.2 67.2 %collective-permute-start.1 = (f32[128,896]{1,0:T(8,128)}, f32[128,896]{1,0:T(8,128)}, u32[]{:S(2)}, u32[]{:S(2)}) collective-permute-start(f32[128,896]{1,0:T(8,128)} %get-tuple-element.231), channel_id=1, source_target_pairs={{0,64},{64,0},{1,65},{65,1},{2,66},{66,2},{3,67},{67,3},{4,68},{68... | collective-permute-start | bytes 1376264 | tf_op jit(solution)/shard_map/ppermute | solution.py:533
  742.0 70.7 %copy-start.4 = (bf16[1,1216,896]{2,1,0:T(8,128)(2,1)S(1)}, bf16[1,1216,896]{2,1,0:T(8,128)(2,1)}, u32[]{:S(2)}) copy-start(bf16[1,1216,896]{2,1,0:T(8,128)(2,1)} %get-tuple-element.203) | copy-start | bytes 6537220
  742.0 68.5 %collective-permute-start = (f32[128,896]{1,0:T(8,128)}, f32[128,896]{1,0:T(8,128)}, u32[]{:S(2)}, u32[]{:S(2)}) collective-permute-start(f32[128,896]{1,0:T(8,128)} %get-tuple-element.233), channel_id=1, source_target_pairs={{0,64},{64,0},{1,65},{65,1},{2,66},{66,2},{3,67},{67,3},{4,68},{68... | collective-permute-start | bytes 1376264 | tf_op jit(solution)/shard_map/ppermute | solution.py:533
  (23 other events, 41.2 us)
Sparse Core Ops, SparseCore 0:
  10.6 19.3 all-gather.15
  31.7 54.5 all-gather.9
  88.0 31.6 all-gather.7
  121.3 24.1 all-gather.11
  426.2 14.9 reduce-scatter.11
  444.2 16.1 reduce-scatter.7
  463.0 16.5 reduce-scatter.15
  481.9 16.4 reduce-scatter.17
  501.6 16.3 reduce-scatter.19
  520.4 27.4 reduce-scatter.13
  550.4 29.1 reduce-scatter.9
  583.6 141.5 all-reduce.8
  738.8 54.3 all-gather.13

commit v2 on v1

--- a/solution.py
+++ b/solution.py
@@ -24,6 +24,12 @@
 BF16 = jnp.bfloat16
 MESH = pl.DeviceIdType.MESH
 VMEM_LIMIT = 56 * 2**20
+UNIT = 16
+SIDE = 4
+GATE_PER = (5, 4)
+DOWN_PER = (8, 9)
+Q_PER = (4, 4)
+Q_ROWS = 16 * sum(Q_PER) * UNIT
 
 
 def mm(a, b):
@@ -32,6 +38,10 @@
 
 def mm_nt(a, b):
     return lax.dot_general(a, b, (((1,), (1,)), ((), ())), preferred_element_type=F32)
+
+
+def mm_tn(a, b):
+    return lax.dot_general(a, b, (((0,), (0,)), ((), ())), preferred_element_type=F32)
 
 
 def greet(axis, n):
@@ -162,16 +172,15 @@
 
 def attn_bwd_kernel(
     n, gm_ref, x_ref, g1_ref, wqkv_ref, wout_ref, qst_ref, kv_ref, lse_ref, att_ref,
-    cos_ref, sa_ref, sb_ref, kpos_ref, qpos_ref,
-    gx_ref, glin_ref, gmb_ref, dg1_ref,
-    gst_s, delta_s, gq_s, send_s, land_s, ssem, rsem,
+    cos_ref, sa_ref, sb_ref, kpos_ref, qpos_ref, n1_ref, dg2_ref,
+    gx_ref, q_ref,
+    gst_s, delta_s, gq_s, glin_ref, small_s, send_s, land_s, ssem, rsem,
 ):
     me = lax.axis_index("ctx")
     bar = greet("ctx", n)
     half = HEAD_DIM
     gm = gm_ref[...]
     gmb = gm.astype(BF16)
-    gmb_ref[...] = gmb
     ga = mm_nt(gmb, wout_ref[...])
     for t in range(TILES):
         tile = slice(t * LANES, (t + 1) * LANES)
@@ -227,9 +236,32 @@
     x = x_ref[...]
     r1 = lax.rsqrt(jnp.mean(x * x, -1, keepdims=True) + EPS)
     unit = x * r1
-    dg1_ref[...] = jnp.sum(gn1 * unit, 0, keepdims=True)
+    dg1 = jnp.sum(gn1 * unit, 0, keepdims=True)
     dz = gn1 * g1_ref[...]
     gx_ref[...] = gm + r1 * (dz - unit * jnp.mean(dz * unit, -1, keepdims=True))
+    dbias = jnp.sum(glin_ref[...].astype(F32), 0, keepdims=True)
+    small_s[...] = jnp.zeros_like(small_s)
+    row = 0
+    for part in (dg1, dg2_ref[...], dbias):
+        for t in range(part.shape[1] // LANES):
+            small_s[row : row + 1, :] = part[:, t * LANES : (t + 1) * LANES]
+            row += 1
+    small = small_s[...].astype(BF16)
+    parts = q_ref.shape[1]
+    share = D // parts
+    for j in range(0, QKV // LANES + TILES, 8):
+        for t in range(j, j + 8):
+            if t < QKV // LANES:
+                d = mm_tn(n1_ref[...], glin_ref[:, t * LANES : (t + 1) * LANES])
+            else:
+                u = t - QKV // LANES
+                d = mm_tn(att_ref[...], gmb[:, u * LANES : (u + 1) * LANES])
+            d = d.astype(BF16)
+            for i in range(parts):
+                q_ref[j // 8, i, (t % 8) * share : (t % 8 + 1) * share, :] = d[i * share : (i + 1) * share, :]
+        for i in range(parts):
+            q_ref[j // 8, i, 8 * share : 8 * share + 2 * UNIT, :] = small if j == 0 else jnp.zeros_like(small)
+            q_ref[j // 8, i, 8 * share + 2 * UNIT :, :] = jnp.zeros((Q_ROWS - 8 * share - 2 * UNIT, LANES), BF16)
 
     def done(k, c):
         push(send_s.at[k], land_s.at[k], ssem.at[k], rsem.at[k], "ctx", lax.rem(me + k, n)).wait_send()
@@ -280,19 +312,48 @@
         second(k).wait_send()
 
 
+def dealt(a_per, b_per):
+    where = [(0, u // a_per, u % a_per) for u in range(16 * a_per)]
+    return where + [(1, v // b_per, v % b_per) for v in range(16 * b_per)]
+
+
+def unit_runs(first, count, per):
+    where = dealt(*per)
+    found = []
+    for i in range(count):
+        part, piece, slot = where[first + i]
+        if found and found[-1][0] == part and found[-1][1] == piece:
+            found[-1][4] += 1
+        else:
+            found.append([part, piece, slot, i, 1])
+    return found
+
+
+def put_units(refs, section, base, per, first, rows):
+    for part, piece, slot, i, m in unit_runs(first, rows.shape[0] // UNIT, per):
+        at = base[part] + slot * UNIT
+        refs[part][section, piece // SIDE, piece % SIDE, at : at + m * UNIT, :] = rows[i * UNIT : (i + m) * UNIT, :]
+
+
 def ffn_bwd_kernel(
-    n, gy_ref, mid_ref, g2_ref, wg_ref, wu_ref, wd_ref, gate_ref, up_ref,
-    gm_ref, all_ref, hid_ref, ggate_ref, gup_ref, dg2_ref,
-    own_s, send_s, land_s, ssem, rsem, ssem2, rsem2,
+    n, gy_ref, mid_ref, g2_ref, wg_ref, wu_ref, wd_ref, gate_ref, up_ref, n2_ref,
+    gm_ref, dg2_ref, fa_ref, fb_ref,
+    all_s, hid_s, ggate_s, gup_s, down_s, own_s, send_s, land_s, ssem, rsem, ssem2, rsem2,
 ):
     me = lax.axis_index("fsdp")
     bar = greet("fsdp", n)
-    all_ref[me] = gy_ref[...].astype(BF16)
+    tok = gy_ref.shape[0]
     order = [k for k in (1, 3, 2) if k < n]
+
+    def rows_of(i):
+        return pl.ds(pl.multiple_of(i * tok, tok), tok)
+
+    all_s[rows_of(me), :] = gy_ref[...].astype(BF16)
     pl.semaphore_wait(bar, n - 1)
 
     def first(k):
-        return push(all_ref.at[me], all_ref.at[me], ssem.at[k], rsem.at[k], "fsdp", lax.rem(me + k, n))
+        mine = all_s.at[rows_of(me), :]
+        return push(mine, mine, ssem.at[k], rsem.at[k], "fsdp", lax.rem(me + k, n))
 
     def second(k):
         return push(send_s.at[k], land_s.at[k], ssem2.at[k], rsem2.at[k], "fsdp", lax.rem(me + n - k, n))
@@ -301,15 +362,16 @@
         first(k).start()
 
     def block(src):
-        gh = mm_nt(all_ref[src], wd_ref[...])
+        rows = rows_of(src)
+        gh = mm_nt(all_s[rows, :], wd_ref[...])
         gate, up = gate_ref[src], up_ref[src]
         sg = jax.nn.sigmoid(gate)
         act = gate * sg
-        hid_ref[src] = (act * up).astype(BF16)
+        hid_s[rows, :] = (act * up).astype(BF16)
         ggate = (gh * up * sg * (1.0 + gate * (1.0 - sg))).astype(BF16)
         gup = (gh * act).astype(BF16)
-        ggate_ref[src] = ggate
-        gup_ref[src] = gup
+        ggate_s[rows, :] = ggate
+        gup_s[rows, :] = gup
         return mm_nt(ggate, wg_ref[...]) + mm_nt(gup, wu_ref[...])
 
     own_s[...] = block(me)
@@ -317,6 +379,37 @@
         first(k).wait_recv()
         send_s[k] = block(lax.rem(me + n - k, n)).astype(BF16)
         second(k).start()
+
+    refs = (fa_ref, fb_ref)
+    share = D // n
+    normed = jnp.concatenate([n2_ref[i] for i in range(n)], 0)
+    for section, part in ((0, ggate_s), (1, gup_s)):
+        for j in range(WIN // (2 * LANES)):
+            d = mm_tn(normed, part[:, 2 * j * LANES : 2 * (j + 1) * LANES]).astype(BF16)
+            for t in (2 * j, 2 * j + 1):
+                tile = d[:, (t % 2) * LANES : (t % 2 + 1) * LANES]
+                for i in range(n):
+                    base = [i * per * UNIT for per in GATE_PER]
+                    put_units(refs, section, base, GATE_PER, t * (share // UNIT), tile[i * share : (i + 1) * share, :])
+        used = WIN // LANES * (share // UNIT)
+        extra = 16 * sum(GATE_PER) - used
+        for i in range(n):
+            base = [i * per * UNIT for per in GATE_PER]
+            put_units(refs, section, base, GATE_PER, used, jnp.zeros((extra * UNIT, LANES), BF16))
+    for j in range(WIN // (2 * LANES)):
+        cols = slice(2 * j * LANES, 2 * (j + 1) * LANES)
+        down_s[cols, :] = mm_tn(hid_s[:, cols], all_s[...]).astype(BF16)
+    pad = (WIN - FF // n) * lax.rem(me, 2)
+    half = FF // n // 2
+    base = [n * per * UNIT for per in GATE_PER]
+    for section in range(2):
+        rows = down_s[pl.ds(pl.multiple_of(pad + section * half, UNIT), half), :]
+        for t in range(TILES):
+            put_units(refs, section, base, DOWN_PER, t * (half // UNIT), rows[:, t * LANES : (t + 1) * LANES])
+        used = TILES * (half // UNIT)
+        extra = 16 * sum(DOWN_PER) - used
+        put_units(refs, section, base, DOWN_PER, used, jnp.zeros((extra * UNIT, LANES), BF16))
+
     for k in order:
         second(k).wait_recv()
         own_s[...] += land_s[k].astype(F32)
@@ -330,6 +423,337 @@
     for k in order:
         first(k).wait_send()
         second(k).wait_send()
+
+
+class Stages:
+    def __init__(self, ssem, rsem):
+        self.s = lax.axis_index("section")
+        c = lax.axis_index("ctx")
+        self.x, self.y = c // SIDE, lax.rem(c, SIDE)
+        self.z = lax.axis_index("fsdp")
+        self.nz = lax.axis_size("fsdp")
+        self.ssem, self.rsem = ssem, rsem
+        self.used = 0
+        self.sent = []
+
+    def along(self, axis, k):
+        own, n = {"x": (self.x, SIDE), "y": (self.y, SIDE), "z": (self.z, self.nz)}[axis]
+        return lax.rem(own + k, n)
+
+    def peer(self, axis, k, section=None):
+        if axis == "s":
+            return {"section": 1 - self.s}
+        if axis == "z":
+            return {"fsdp": self.along("z", k)}
+        to = self.along("x", k) * SIDE + self.y if axis == "x" else self.x * SIDE + self.along("y", k)
+        return {"ctx": to} if section is None else {"ctx": to, "section": section}
+
+    def greet(self, owners):
+        ids = [self.peer("s", 0)]
+        for k in range(1, SIDE):
+            for axis in ("x", "y"):
+                ids.append(self.peer(axis, k))
+                if owners:
+                    ids.append(self.peer(axis, k, 1 - self.s))
+        ids += [self.peer("z", k) for k in range(1, self.nz)]
+        bar = pltpu.get_barrier_semaphore()
+        for i in ids:
+            pl.semaphore_signal(bar, inc=1, device_id=i, device_id_type=MESH)
+        pl.semaphore_wait(bar, len(ids))
+
+    def take(self, count):
+        self.used += count
+        return self.used - count
+
+    def copy(self, src, dst, at, to, recv_at=None):
+        return pltpu.make_async_remote_copy(
+            src_ref=src,
+            dst_ref=dst,
+            send_sem=self.ssem.at[at],
+            recv_sem=self.rsem.at[at if recv_at is None else recv_at],
+            device_id=to,
+            device_id_type=MESH,
+        )
+
+    def begin(self, copies):
+        for c in copies:
+            c.start()
+        self.sent += copies
+        return copies
+
+    def drain(self):
+        for c in self.sent:
+            c.wait_send()
+
+    def swap(self, src, land):
+        return self.begin([self.copy(src.at[1 - self.s], land, self.take(1), self.peer("s", 0))])
+
+    def scatter(self, axis, src, land, peers=None):
+        at = self.take(SIDE - 1)
+        return self.begin(
+            [self.copy(src.at[self.along(axis, k)], land.at[k - 1], at + k - 1, self.peer(axis, k)) for k in range(1, SIDE)]
+        )
+
+    def gather(self, axis, ref):
+        at = self.take(SIDE - 1)
+        mine = ref.at[self.along(axis, 0)]
+        return self.begin([self.copy(mine, mine, at + k - 1, self.peer(axis, k)) for k in range(1, SIDE)])
+
+    def deal(self, src, dst, rows):
+        at = self.take(self.nz - 1)
+        mine = dst.at[self.block(self.z, rows), :]
+        return self.begin(
+            [
+                self.copy(src.at[self.block(self.along("z", k), rows), :], mine, at + k - 1, self.peer("z", k))
+                for k in range(1, self.nz)
+            ]
+        )
+
+    def block(self, i, rows):
+        return pl.ds(pl.multiple_of(i * rows, UNIT), rows)
+
+    def hand_over(self, axis, src, dst, layer):
+        at = self.take(2 * SIDE)
+        mine = dst.at[self.s, self.along(axis, 0)]
+        copies = self.begin(
+            [
+                self.copy(src, mine, at + k, self.peer(axis, k, layer), at + self.s * SIDE + k)
+                for k in range(1, SIDE)
+            ]
+        )
+        beside = self.copy(src, mine, at, {"section": layer}, at + self.s * SIDE)
+
+        @pl.when(self.s != layer)
+        def _():
+            beside.start()
+
+        @pl.when(self.s == layer)
+        def _():
+            mine[...] = src[...]
+
+        def finish():
+            @pl.when(self.s == layer)
+            def _():
+                for half in range(2):
+                    for k in range(0 if half != layer else 1, SIDE):
+                        self.copy(src, mine, at, {"section": layer}, at + half * SIDE + k).wait_recv()
+
+            @pl.when(self.s != layer)
+            def _():
+                beside.wait_send()
+
+        return finish
+
+
+def arrived(copies):
+    for c in copies:
+        c.wait_recv()
+
+
+def add_into(dst, parts):
+    def one(i, c):
+        total = parts[0][i].astype(F32)
+        for p in parts[1:]:
+            total = total + p[i].astype(F32)
+        dst[i] = total.astype(dst.dtype)
+        return c
+
+    lax.fori_loop(0, dst.shape[0], one, 0)
+
+
+def add_rows(dst, parts):
+    total = parts[0][...].astype(F32)
+    for p in parts[1:]:
+        total = total + p[...].astype(F32)
+    dst[...] = total.astype(dst.dtype)
+
+
+AXES = (("x", "y"), ("y", "x"))
+
+
+def reduce_kernel(
+    layer, fa_ref, fb_ref, q_ref,
+    ga_ref, gb_ref, qa_ref, qb_ref,
+    sa, sb, l1a, l1b, l2a, l2b, t2a, t2b, g1a, g1b,
+    sq, zq, qpa, qpb, q1a, q1b, q2a, q2b, qga, qgb, ssem, rsem,
+):
+    st = Stages(ssem, rsem)
+    st.greet(True)
+    f, sl, l1, l2, t2, g1, out = (fa_ref, fb_ref), (sa, sb), (l1a, l1b), (l2a, l2b), (t2a, t2b), (g1a, g1b), (ga_ref, gb_ref)
+    qp, q1, q2, qg, qout = (qpa, qpb), (q1a, q1b), (q2a, q2b), (qga, qgb), (qa_ref, qb_ref)
+    both = range(2)
+    swaps = [st.swap(f[h], sl[h]) for h in both]
+    qswap = st.swap(q_ref, sq)
+    r1 = [None, None]
+    for h in both:
+        arrived(swaps[h])
+        for i in range(SIDE):
+            add_into(sl[h].at[i], [f[h].at[st.s, i], sl[h].at[i]])
+        r1[h] = st.scatter(AXES[h][0], sl[h], l1[h])
+    arrived(qswap)
+    add_into(sq, [q_ref.at[st.s], sq])
+    at = st.take(st.nz - 1)
+    zr = st.begin([st.copy(sq.at[st.along("z", k)], zq.at[k - 1], at + k - 1, st.peer("z", k)) for k in range(1, st.nz)])
+    r2 = [None, None]
+    for h in both:
+        arrived(r1[h])
+        own = sl[h].at[st.along(AXES[h][0], 0)]
+        add_into(own, [own] + [l1[h].at[k] for k in range(SIDE - 1)])
+        r2[h] = st.scatter(AXES[h][1], own, l2[h])
+    arrived(zr)
+    parts = [sq.at[st.z]] + [zq.at[k] for k in range(st.nz - 1)]
+    rows = Q_ROWS // 2 // 16
+    qr1 = [None, None]
+    for h in both:
+        for i in range(16):
+            total = jnp.zeros((rows, LANES), F32)
+            for p in parts:
+                total = total + p[h * Q_ROWS // 2 + i * rows : h * Q_ROWS // 2 + (i + 1) * rows, :].astype(F32)
+            qp[h][i // SIDE, i % SIDE] = total.astype(BF16)
+        qr1[h] = st.scatter(AXES[h][0], qp[h], q1[h])
+    zs = [None, None]
+    for h in both:
+        arrived(r2[h])
+        own = sl[h].at[st.along(AXES[h][0], 0), st.along(AXES[h][1], 0)]
+        add_rows(t2[h], [own] + [l2[h].at[k] for k in range(SIDE - 1)])
+        per = GATE_PER[h] * UNIT
+        mine = g1[h].at[st.along(AXES[h][1], 0)]
+        zs[h] = st.deal(t2[h], mine, per)
+        mine[st.block(st.z, per), :] = t2[h][st.block(st.z, per), :]
+        mine[st.nz * per :, :] = t2[h][st.nz * per :, :]
+    qr2 = [None, None]
+    for h in both:
+        arrived(qr1[h])
+        own = qp[h].at[st.along(AXES[h][0], 0)]
+        add_into(own, [own] + [q1[h].at[k] for k in range(SIDE - 1)])
+        qr2[h] = st.scatter(AXES[h][1], own, q2[h])
+    ag = [None, None]
+    for h in both:
+        arrived(zs[h])
+        ag[h] = st.gather(AXES[h][1], g1[h])
+    qag = [None, None]
+    for h in both:
+        arrived(qr2[h])
+        own = qp[h].at[st.along(AXES[h][0], 0), st.along(AXES[h][1], 0)]
+        add_rows(qg[h].at[st.along(AXES[h][1], 0)], [own] + [q2[h].at[k] for k in range(SIDE - 1)])
+        qag[h] = st.gather(AXES[h][1], qg[h])
+    last = []
+    for h in both:
+        arrived(ag[h])
+        last.append(st.hand_over(AXES[h][0], g1[h], out[h], layer))
+    for h in both:
+        arrived(qag[h])
+        last.append(st.hand_over(AXES[h][0], qg[h], qout[h], layer))
+    for finish in last:
+        finish()
+    st.drain()
+
+
+def reduce_gradients(fa, fb, q, layer):
+    ra, rb = fa.shape[3], fb.shape[3]
+    rq = Q_ROWS // 2 // 16
+    vm = pl.BlockSpec(memory_space=pltpu.VMEM)
+    dma = pltpu.SemaphoreType.DMA
+
+    def buf(*shape):
+        return pltpu.VMEM(shape + (LANES,), BF16)
+
+    sides = (SIDE, SIDE)
+    nz = lax.axis_size("fsdp")
+    return pl.pallas_call(
+        functools.partial(reduce_kernel, layer),
+        out_shape=[
+            jax.ShapeDtypeStruct((2,) + sides + (r, LANES), BF16) for r in (ra, rb, rq, rq)
+        ],
+        in_specs=[vm] * 3,
+        out_specs=[vm] * 4,
+        scratch_shapes=[
+            buf(*sides, ra), buf(*sides, rb),
+            buf(SIDE - 1, SIDE, ra), buf(SIDE - 1, SIDE, rb),
+            buf(SIDE - 1, ra), buf(SIDE - 1, rb),
+            buf(ra), buf(rb),
+            buf(SIDE, ra), buf(SIDE, rb),
+            buf(nz, Q_ROWS), buf(nz - 1, Q_ROWS),
+            buf(*sides, rq), buf(*sides, rq),
+            buf(SIDE - 1, SIDE, rq), buf(SIDE - 1, SIDE, rq),
+            buf(SIDE - 1, rq), buf(SIDE - 1, rq),
+            buf(SIDE, rq), buf(SIDE, rq),
+            dma((80,)), dma((80,)),
+        ],
+        compiler_params=pltpu.CompilerParams(
+            collective_id=5 + layer, has_side_effects=True, vmem_limit_bytes=VMEM_LIMIT
+        ),
+        cost_estimate=pl.CostEstimate(flops=10**9, bytes_accessed=40 * 2**20, transcendentals=0),
+        name=f"reduce_{layer}",
+    )(fa, fb, q)
+
+
+def assemble_kernel(nz, *refs):
+    given, outs, held, sem = (refs[:4], refs[4:8]), refs[8:14], refs[14:18], refs[18]
+    s = lax.axis_index("section")
+    for layer in range(2):
+        @pl.when(s == layer)
+        def _():
+            copies = [pltpu.make_async_copy(a, b, sem.at[i]) for i, (a, b) in enumerate(zip(given[layer], held))]
+            for c in copies:
+                c.start()
+            for c in copies:
+                c.wait()
+
+    gate_ref, up_ref, down_ref, qkv_ref, out_ref, small_ref = outs
+    share = D // nz
+    starts = window_starts(nz)
+
+    def units(refs, section, base, per, first, count):
+        rows = []
+        for part, piece, slot, _, m in unit_runs(first, count, per):
+            at = base[part] + slot * UNIT
+            rows.append(refs[part][section, piece // SIDE, piece % SIDE, at : at + m * UNIT, :].astype(F32))
+        return jnp.concatenate(rows, 0) if len(rows) > 1 else rows[0]
+
+    for section, ref in ((0, gate_ref), (1, up_ref)):
+        tiles = {}
+        for w, a in enumerate(starts):
+            for t in range(WIN // LANES):
+                tiles.setdefault(a // LANES + t, []).append((w, t))
+        for col, sources in tiles.items():
+            total = None
+            for w, t in sources:
+                base = [w * per * UNIT for per in GATE_PER]
+                got = units(held[:2], section, base, GATE_PER, t * (share // UNIT), share // UNIT)
+                total = got if total is None else total + got
+            ref[:, col * LANES : (col + 1) * LANES] = total
+    base = [nz * per * UNIT for per in GATE_PER]
+    half = FF // nz // 2
+    for section in range(2):
+        for t in range(TILES):
+            got = units(held[:2], section, base, DOWN_PER, t * (half // UNIT), half // UNIT)
+            down_ref[section * half : (section + 1) * half, t * LANES : (t + 1) * LANES] = got
+    for t in range(QKV // LANES + TILES):
+        got = units(held[2:], t // 8, (0, 0), Q_PER, (t % 8) * (share // UNIT), share // UNIT)
+        if t < QKV // LANES:
+            qkv_ref[:, t * LANES : (t + 1) * LANES] = got
+        else:
+            u = t - QKV // LANES
+            out_ref[:, u * LANES : (u + 1) * LANES] = got
+    small_ref[...] = units(held[2:], 0, (0, 0), Q_PER, 8 * (share // UNIT), 2)
+
+
+def assemble(given):
+    nz = lax.axis_size("fsdp")
+    vm = pl.BlockSpec(memory_space=pltpu.VMEM)
+    share = D // nz
+    shapes = [(share, FF), (share, FF), (FF // nz, D), (share, QKV), (share, D), (2 * UNIT, LANES)]
+    flat = [a for one in given for a in one]
+    return pl.pallas_call(
+        functools.partial(assemble_kernel, nz),
+        out_shape=[jax.ShapeDtypeStruct(a, F32) for a in shapes],
+        in_specs=[pl.BlockSpec(memory_space=pl.ANY)] * len(flat),
+        out_specs=[vm] * len(shapes),
+        scratch_shapes=[pltpu.VMEM(a.shape, a.dtype) for a in given[0]] + [pltpu.SemaphoreType.DMA((4,))],
+        compiler_params=pltpu.CompilerParams(vmem_limit_bytes=VMEM_LIMIT),
+        name="assemble",
+    )(*flat)
 
 
 def call(kernel, n, ins, outs, scratch, cid, name, flops):
@@ -365,8 +789,9 @@
     )
 
 
-def attn_bwd(gm, x, g1, wqkv, wout, saved, tabs):
+def attn_bwd(gm, x, g1, wqkv, wout, saved, tabs, n1, dg2):
     n = lax.axis_size("ctx")
+    nz = lax.axis_size("fsdp")
     tok = x.shape[0]
     wide = HEADS * LANES
     cos, sa, sb, kpos, qpos = tabs
@@ -374,9 +799,10 @@
     dma = pltpu.SemaphoreType.DMA
     return call(
         attn_bwd_kernel, n,
-        (gm, x, g1, wqkv, wout, qst, kv, lse, att, cos, sa, sb, kpos, qpos),
-        [((tok, D), F32), ((tok, QKV), BF16), ((tok, D), BF16), ((1, D), F32)],
+        (gm, x, g1, wqkv, wout, qst, kv, lse, att, cos, sa, sb, kpos, qpos, n1, dg2),
+        [((tok, D), F32), ((2, nz, Q_ROWS, LANES), BF16)],
         [pltpu.VMEM((LANES, wide), BF16), pltpu.VMEM((1, wide), F32), pltpu.VMEM((LANES, wide), F32),
+         pltpu.VMEM((tok, QKV), BF16), pltpu.VMEM((2 * UNIT, LANES), F32),
          pltpu.VMEM((n, tok, 2 * LANES), BF16), pltpu.VMEM((n, tok, 2 * LANES), BF16), dma((n,)), dma((n,))],
         2, "attn_bwd", 20 * 10**9,
     )
@@ -394,15 +820,17 @@
     )
 
 
-def ffn_bwd(gy, mid, g2, wg, wu, wd, gate, up):
+def ffn_bwd(gy, mid, g2, wg, wu, wd, gate, up, n2_all):
     n = lax.axis_size("fsdp")
     tok = gy.shape[0]
     dma = pltpu.SemaphoreType.DMA
+    rows = [(n * g + d) * UNIT for g, d in zip(GATE_PER, DOWN_PER)]
     return call(
-        ffn_bwd_kernel, n, (gy, mid, g2, wg, wu, wd, gate, up),
-        [((tok, D), F32), ((n, tok, D), BF16), ((n, tok, WIN), BF16), ((n, tok, WIN), BF16),
-         ((n, tok, WIN), BF16), ((1, D), F32)],
-        [pltpu.VMEM((tok, D), F32), pltpu.VMEM((n, tok, D), BF16), pltpu.VMEM((n, tok, D), BF16),
+        ffn_bwd_kernel, n, (gy, mid, g2, wg, wu, wd, gate, up, n2_all),
+        [((tok, D), F32), ((1, D), F32), ((2, SIDE, SIDE, rows[0], LANES), BF16), ((2, SIDE, SIDE, rows[1], LANES), BF16)],
+        [pltpu.VMEM((n * tok, D), BF16), pltpu.VMEM((n * tok, WIN), BF16), pltpu.VMEM((n * tok, WIN), BF16),
+         pltpu.VMEM((n * tok, WIN), BF16), pltpu.VMEM((WIN, D), BF16),
+         pltpu.VMEM((tok, D), F32), pltpu.VMEM((n, tok, D), BF16), pltpu.VMEM((n, tok, D), BF16),
          dma((n,)), dma((n,)), dma((n,)), dma((n,))],
         4, "ffn_bwd", 20 * 10**9,
     )
@@ -435,8 +863,7 @@
     )
 
 
-def window_starts():
-    n = lax.axis_size("fsdp")
+def window_starts(n):
     share = FF // n
     return [(i * share // LANES) * LANES for i in range(n)]
 
@@ -448,7 +875,7 @@
     z = lax.axis_index("fsdp")
     nz = lax.axis_size("fsdp")
     share = FF // nz
-    starts = window_starts()
+    starts = window_starts(nz)
     tabs = tables(pair_of)
     both = ("section", "fsdp")
 
@@ -484,48 +911,20 @@
         x = y.astype(BF16).astype(F32)
 
     gy = jnp.where(s == 0, cotangent[0, 0], cotangent[1, 0])
-    grads = [None, None]
+    given = [None, None]
     gxs = [None, None]
     for l in (1, 0):
         x, mid, n1, attn_saved, n2_all, gate, up = saved[l]
-        gm, gy_all, hid, ggate, gup, dg2 = ffn_bwd(gy, mid, gain2[l], gu[l, 0], gu[l, 1], wd[l], gate, up)
-        gx, glin, gmb, dg1 = attn_bwd(gm, x, gain1[l], wqkv[l], wout[l], attn_saved, tabs)
+        gm, dg2, fa, fb = ffn_bwd(gy, mid, gain2[l], gu[l, 0], gu[l, 1], wd[l], gate, up, n2_all)
+        gx, q = attn_bwd(gm, x, gain1[l], wqkv[l], wout[l], attn_saved, tabs, n1, dg2)
         gxs[l] = gx
         gy = gx.astype(BF16).astype(F32)
-        ddown = jnp.einsum("stf,std->fd", hid, gy_all, preferred_element_type=F32)
-        dgate = jnp.einsum("std,stf->df", n2_all, ggate, preferred_element_type=F32)
-        dup = jnp.einsum("std,stf->df", n2_all, gup, preferred_element_type=F32)
-        dqkv = jnp.einsum("td,te->de", n1, glin, preferred_element_type=F32)
-        dout = jnp.einsum("td,te->de", attn_saved[3], gmb, preferred_element_type=F32)
-        dbias = jnp.sum(glin.astype(F32), 0)
-        ddown = lax.dynamic_slice_in_dim(ddown, pad, share, 0)
-        grads[l] = (ddown, dgate, dup, dqkv, dout, dg1[0], dg2[0], dbias)
-
-    def over_sections(index):
-        pair = jnp.stack([grads[0][index], grads[1][index]]).astype(BF16)
-        return lax.psum_scatter(pair, "section", scatter_dimension=0, tiled=False)
-
-    ddown, dgate, dup, dqkv, dout = (over_sections(i) for i in range(5))
-    ddown = lax.psum(ddown, "ctx").astype(F32)
-    dqkv = lax.psum_scatter(dqkv, "fsdp", scatter_dimension=0, tiled=True)
-    dout = lax.psum_scatter(dout, "fsdp", scatter_dimension=0, tiled=True)
-    dqkv, dout = lax.psum((dqkv, dout), "ctx")
-    gu_grad = jnp.concatenate([dgate.reshape(nz, qd, WIN), dup.reshape(nz, qd, WIN)], 2)
-    gu_grad = lax.psum_scatter(gu_grad, "ctx", scatter_dimension=2, tiled=True)
-    gu_grad = lax.all_to_all(gu_grad, "fsdp", 0, 0)
-    gu_grad = lax.all_gather(gu_grad, "ctx", axis=2, tiled=True).astype(F32)
-
-    def assembled(w):
-        total = jnp.zeros((qd, FF), F32)
-        for i, a in enumerate(starts):
-            total = total.at[:, a : a + WIN].add(w[i])
-        return total
-
-    small_grad = jnp.stack(
-        [jnp.concatenate([g[5].reshape(nz, -1), g[6].reshape(nz, -1), g[7].reshape(nz, -1)], 1) for g in grads]
-    )
-    small_grad = lax.psum(small_grad, ("section", "ctx", "fsdp"))
-    small_grad = lax.dynamic_slice(small_grad, (s, z, 0), (1, 1, small_grad.shape[2]))[0, 0]
+        given[l] = reduce_gradients(fa, fb, q, l)
+    dgate, dup, ddown, dqkv, dout, small_grad = assemble(given)
+    small_grad = small_grad.reshape(-1)
+
+    def mine(first, size):
+        return lax.dynamic_slice_in_dim(small_grad, first + z * size, size, 0)[None]
 
     def by_layer(pair):
         theirs = jnp.where(s == 0, pair[1], pair[0])
@@ -536,13 +935,13 @@
     return (
         by_layer(outs),
         by_layer(gxs),
-        small_grad[None, :qd],
-        small_grad[None, qd : 2 * qd],
-        dqkv.astype(F32)[None],
-        small_grad[None, 2 * qd :],
-        dout.astype(F32)[None],
-        assembled(gu_grad[:, :, :WIN])[None],
-        assembled(gu_grad[:, :, WIN:])[None],
+        mine(0, qd),
+        mine(D, qd),
+        dqkv[None],
+        mine(2 * D, QKV // nz),
+        dout[None],
+        dgate[None],
+        dup[None],
         ddown[None],
     )
 

time: 849 us -> 626 us (0.74)
  waiting for transfers between devices: 252 us -> 1.44 us
  Pallas kernels: 255 us -> 439 us
  blocking collectives: 188 us -> 112 us
  other arithmetic: 51.5 us -> 14.4 us
  local copies, waits for them, and re-layouts: 67.7 us -> 36.3 us
  matrix products: 12.3 us -> 0 us
    pallas_call x0 -> x3, Pallas kernels: none -> 173 us  [the longest x2 164 us: reduce_gradients(): pl.pallas_call(functools.partial(reduce_kernel, layer), out_shape=[jax.Sh...]
    psum x1 -> x0, waiting for transfers between devices: 145 us -> none  [local(): dqkv, dout = lax.psum((dqkv, dout), 'ctx')]
    reduce_scatter x7 -> x0, waiting for transfers between devices: 105 us -> none  [the longest x5 43.5 us: over_sections(): return lax.psum_scatter(pair, 'section', scatter_dimension=0, tiled=False)]
    psum x1 -> x0, blocking collectives: 64.1 us -> none  [local(): small_grad = lax.psum(small_grad, ('section', 'ctx', 'fsdp'))]
    another operation x11 -> x0, other arithmetic: 14.2 us -> none  [the longest x5 12 us: over_sections(): pair = jnp.stack([grads[0][index], grads[1][index]]).astype(BF16)]
    dot_general x10 -> x0, matrix products: 12.3 us -> none  [the longest x2 3.11 us: local(): ddown = jnp.einsum('stf,std->fd', hid, gy_all, preferred_element_type=F32)]
    unnamed x89 -> x28, local copies, waits for them, and re-layouts: 15.8 us -> 3.7 us
    all_to_all x1 -> x0, blocking collectives: 11.4 us -> none  [local(): gu_grad = lax.all_to_all(gu_grad, 'fsdp', 0, 0)]
  transfers between devices with their start and end apart: 15 -> 6, of which waited for: 7 -> 0; matrix products, arithmetic and copies ran while one was open for 10% -> 6% of each run, Pallas kernels for 4% -> 57%
where the time goes in v2:
time: 626 us; the launch traced here: 619 us
  Pallas kernels  439 us (70%)
  blocking collectives  112 us (18%)
  local copies, waits for them, and re-layouts  36.3 us (6%)
  between operations  15.7 us (3%)
  other arithmetic  14.4 us (2%)
    pallas_call x8, Pallas kernels, call(): pl.pallas_call(functools.partial(kernel, n), out_shape=[jax.ShapeDtypeStr...  266 us
    pallas_call x2, Pallas kernels, reduce_gradients(): pl.pallas_call(functools.partial(reduce_kernel, layer), out_shape=[jax.Sh...  164 us
    all_to_all x1, blocking collectives, local(): gu = lax.all_to_all(gu, 'fsdp', 0, 0)  71.1 us
    unnamed x2, blocking collectives  41.2 us
  transfers between devices with their start and end apart: 6, of which 0 were waited for; matrix products, arithmetic and copies ran while one was open for 6% of the time, Pallas kernels for 57%

profile of v2, /device:TPU:0, one launch (start us, length us, event | category | flops | bytes accessed | tf_op | source)
XLA Modules:
  0.0 619.3 jit_solution(1930856991145843074)
XLA Ops:
  7.2 3.2 pad_dynamic-slice_fusion
  12.2 1.5 copy-done.1
  14.9 71.1 %all_to_all.5 = bf16[4,2,224,1280]{3,2,1,0:T(8,128)(2,1)S(1)} all-to-all(bf16[4,2,224,1280]{3,2,1,0:T(8,128)(2,1)S(1)} %pad_maximum_fusion), channel_id=1, replica_groups=mesh['section'=2,'ctx'=16,'fsdp'=4] {'fsdp'}, dimensions={0} | all-to-all | bytes 9175040 | tf_op jit(solution)/shard_map/all_to_all | solution.py:895
  86.0 2.5 copy.21
  90.7 16.4 %all-reduce.2 = s32[16]{0:T(128)S(1)} all-reduce(s32[16]{0:T(128)S(1)} %dynamic-update-slice.1), channel_id=1, replica_groups=mesh['section'=2,'ctx'=16,'fsdp'=4] {'ctx'}, use_global_device_ids=true, to_apply=%add.2 | all-reduce | flops 16 | bytes 128
  108.7 24.7 %all-reduce.1 = bf16[5888]{0:T(1024)(128)(2,1)S(1)} all-reduce(bf16[5888]{0:T(1024)(128)(2,1)S(1)} %dynamic-update-slice), channel_id=2, replica_groups=mesh['section'=2,'ctx'=16,'fsdp'=4] {'section','fsdp'}, use_global_device_ids=true, to_apply=%add.1 | all-reduce | flops 5888 | bytes 23552
  139.4 0.8 pad_maximum_fusion.3
  140.2 0.8 select_bitcast_fusion.3.x_ref
  141.1 0.8 select_bitcast_fusion.1.gy_ref
  141.9 1.3 add_select_fusion.kpos_ref
  143.1 4.8 fusion.1
  147.9 3.9 fusion.3
  151.8 4.5 fusion.2
  156.3 31.2 %attn_fwd.2 = (f32[128,896]{1,0:T(8,128)}, bf16[128,896]{1,0:T(8,128)(2,1)}, bf16[128,896]{1,0:T(8,128)(2,1)}, bf16[128,1792]{1,0:T(8,128)(2,1)}, bf16[16,128,25...) custom-call(f32[128,896]{1,0:T(8,128)} %select_bitcast_fusion.3.x_ref, f32[1,896]{1,0:T(1,128)} %squeeze.88.g1_ref, ...), custom_call_target="tpu_custom_call" | custom-call | flops 10000000000 | bytes 4345856 | tf_op jit(solution)/shard_map/attn_fwd/pallas_call | solution.py:762
  187.6 6.5 %slice_bitcast_fusion = (bf16[896,1280]{1,0:T(8,128)(2,1)}, bf16[896,1280]{1,0:T(8,128)(2,1)}, bf16[896,1280]{1,0:T(8,128)(2,1)}, bf16[896,1280]{1,0:T(8,128)(2,1)}) fusion(bf16[2,2,896,1280]{3,2,1,0:T(8,128)(2,1)} %all-gather.11.cloned.1.call-done), kind=kLoop, calls=%fused_computation.2 | loop fusion | bytes 18350080 | tf_op jit(solution)/shard_map/squeeze | solution.py:908
  194.1 29.9 %ffn_fwd.2 = (f32[128,896]{1,0:T(8,128)}, bf16[4,128,896]{2,1,0:T(8,128)(2,1)}, f32[4,128,1280]{2,1,0:T(8,128)}, f32[4,128,1280]{2,1,0:T(8,128)}) custom-call(bf16[128,896]{1,0:T(8,128)(2,1)} %get-tuple-element.58.n2_ref, f32[128,896]{1,0:T(8,128)} %get-tuple-element.59.mid_ref, bf16[896,1280]{1,0:T(8,128)(2,1)} %get-tuple-element.109.wg_ref, ...), custom_call_target="tpu_custom_call" | custom-call | flops 10000000000 | bytes 7569408 | tf_op jit(solution)/shard_map/ffn_fwd/pallas_call | solution.py:762
  224.0 1.8 convert_convert_fusion.1.x_ref
  225.8 25.8 %attn_fwd.3 = (f32[128,896]{1,0:T(8,128)}, bf16[128,896]{1,0:T(8,128)(2,1)}, bf16[128,896]{1,0:T(8,128)(2,1)}, bf16[128,1792]{1,0:T(8,128)(2,1)}, bf16[16,128,25...) custom-call(f32[128,896]{1,0:T(8,128)} %convert_convert_fusion.1.x_ref, f32[1,896]{1,0:T(1,128)} %squeeze.99.g1_ref, ...), custom_call_target="tpu_custom_call" | custom-call | flops 10000000000 | bytes 4345856 | tf_op jit(solution)/shard_map/attn_fwd/pallas_call | solution.py:762
  251.7 32.0 %ffn_fwd.3 = (f32[128,896]{1,0:T(8,128)}, bf16[4,128,896]{2,1,0:T(8,128)(2,1)}, f32[4,128,1280]{2,1,0:T(8,128)}, f32[4,128,1280]{2,1,0:T(8,128)}) custom-call(bf16[128,896]{1,0:T(8,128)(2,1)} %get-tuple-element.61.n2_ref, f32[128,896]{1,0:T(8,128)} %get-tuple-element.62.mid_ref, bf16[896,1280]{1,0:T(8,128)(2,1)} %get-tuple-element.107.wg_ref, ...), custom_call_target="tpu_custom_call" | custom-call | flops 10000000000 | bytes 7569408 | tf_op jit(solution)/shard_map/ffn_fwd/pallas_call | solution.py:762
  283.7 1.1 select_bitcast_fusion.2
  284.9 39.5 %ffn_bwd.2 = (f32[128,896]{1,0:T(8,128)}, f32[1,896]{1,0:T(1,128)}, bf16[2,4,4,448,128]{4,3,2,1,0:T(8,128)(2,1)}, bf16[2,4,4,400,128]{4,3,2,1,0:T(8,128)(2,1)}) custom-call(f32[128,896]{1,0:T(8,128)} %select_bitcast_fusion.1.gy_ref, f32[128,896]{1,0:T(8,128)} %get-tuple-element.62.mid_ref, f32[1,896]{1,0:T(1,128)} %squeeze.100.g2_ref, ...), custom_call_target="tpu_custom_call" | custom-call | flops 20000000000 | bytes 13962752 | tf_op jit(solution)/shard_map/ffn_bwd/pallas_call | solution.py:762
  324.4 35.3 %attn_bwd.2 = (f32[128,896]{1,0:T(8,128)}, bf16[2,4,2048,128]{3,2,1,0:T(8,128)(2,1)}) custom-call(f32[128,896]{1,0:T(8,128)} %get-tuple-element.67.gm_ref, f32[128,896]{1,0:T(8,128)} %convert_convert_fusion.1.x_ref, f32[1,896]{1,0:T(1,128)} %squeeze.99.g1_ref, bf16[896,1152]{1,0:T(8,128)(2,1)} %bitcast.67, bf16[896,896]{1,0:T(8,128)(2,1)} %bitcast.71, ...), custom_call_target="tpu_custom_call" | custom-call | flops 20000000000 | bytes 6773248 | tf_op jit(solution)/shard_map/attn_bwd/pallas_call | solution.py:762
  359.8 1.8 convert_convert_fusion.gy_ref
  361.6 30.8 %ffn_bwd.3 = (f32[128,896]{1,0:T(8,128)}, f32[1,896]{1,0:T(1,128)}, bf16[2,4,4,448,128]{4,3,2,1,0:T(8,128)(2,1)}, bf16[2,4,4,400,128]{4,3,2,1,0:T(8,128)(2,1)}) custom-call(f32[128,896]{1,0:T(8,128)} %convert_convert_fusion.gy_ref, f32[128,896]{1,0:T(8,128)} %get-tuple-element.59.mid_ref, f32[1,896]{1,0:T(1,128)} %squeeze.89.g2_ref, ...), custom_call_target="tpu_custom_call" | custom-call | flops 20000000000 | bytes 13962752 | tf_op jit(solution)/shard_map/ffn_bwd/pallas_call | solution.py:762
  392.4 40.9 %attn_bwd.3 = (f32[128,896]{1,0:T(8,128)}, bf16[2,4,2048,128]{3,2,1,0:T(8,128)(2,1)}) custom-call(f32[128,896]{1,0:T(8,128)} %get-tuple-element.78.gm_ref, f32[128,896]{1,0:T(8,128)} %select_bitcast_fusion.3.x_ref, f32[1,896]{1,0:T(1,128)} %squeeze.88.g1_ref, bf16[896,1152]{1,0:T(8,128)(2,1)} %bitcast.65, bf16[896,896]{1,0:T(8,128)(2,1)} %bitcast.69, ...), custom_call_target="tpu_custom_call" | custom-call | flops 20000000000 | bytes 6773248 | tf_op jit(solution)/shard_map/attn_bwd/pallas_call | solution.py:762
  433.3 1.1 select_bitcast_fusion
  434.5 83.5 %reduce_0.1 = (bf16[2,4,4,448,128]{4,3,2,1,0:T(8,128)(2,1)}, bf16[2,4,4,400,128]{4,3,2,1,0:T(8,128)(2,1)}, bf16[2,4,4,64,128]{4,3,2,1,0:T(8,128)(2,1)}, bf16[2,4,4,64,128]{4,3,2,1,0:T(8,128)(2,1)}) custom-call(bf16[2,4,4,448,128]{4,3,2,1,0:T(8,128)(2,1)} %get-tuple-element.86.fa_ref, bf16[2,4,4,400,128]{4,3,2,1,0:T(8,128)(2,1)} %get-tuple-element.87.fb_ref, ...), custom_call_target="tpu_custom_call" | custom-call | flops 1000000000 | bytes 41943040 | tf_op jit(solution)/shard_map/reduce_0/pallas_call | solution.py:663
  518.0 80.9 %reduce_1.1 = (bf16[2,4,4,448,128]{4,3,2,1,0:T(8,128)(2,1)}, bf16[2,4,4,400,128]{4,3,2,1,0:T(8,128)(2,1)}, bf16[2,4,4,64,128]{4,3,2,1,0:T(8,128)(2,1)}, bf16[2,4,4,64,128]{4,3,2,1,0:T(8,128)(2,1)}) custom-call(bf16[2,4,4,448,128]{4,3,2,1,0:T(8,128)(2,1)} %get-tuple-element.93.fa_ref, bf16[2,4,4,400,128]{4,3,2,1,0:T(8,128)(2,1)} %get-tuple-element.94.fb_ref, ...), custom_call_target="tpu_custom_call" | custom-call | flops 1000000000 | bytes 41943040 | tf_op jit(solution)/shard_map/reduce_1/pallas_call | solution.py:663
  599.0 8.8 %assemble.1 = (f32[224,4864]{1,0:T(8,128)}, f32[224,4864]{1,0:T(8,128)}, f32[1216,896]{1,0:T(8,128)}, f32[224,1152]{1,0:T(8,128)}, f32[224,896]{1,0:T(8,128)}, /*index=5*/f32[32,128]{1,0:T(8,128)}) custom-call(bf16[2,4,4,448,128]{4,3,2,1,0:T(8,128)(2,1)} %get-tuple-element.89.refs_0_, bf16[2,4,4,400,128]{4,3,2,1,0:T(8,128)(2,1)} %get-tuple-element.90.refs_1_, ...), custom_call_target="tpu_custom_call" | custom-call | tf_op jit(solution)/shard_map/assemble/pallas_call | solution.py:748
  609.2 1.4 fusion.4
  610.6 1.0 maximum_select_fusion
  611.6 1.0 maximum_select_fusion.1
  (72 shorter events, 12.8 us)
Async XLA Ops:
  7.2 136.0 %all-gather.13.cloned.1.call-start = ((), (), s32[]{:S(2)}) async-start(), calls=%async_computation.4 | async-start | bytes 6881280 | tf_op jit(solution)/shard_map/all_gather | solution.py:901
  10.4 1.6 copy-start
  10.5 137.4 %all-gather.9.cloned.1.call-start = ((), (), s32[]{:S(2)}) async-start(), calls=%async_computation.2 | async-start | bytes 3612672 | tf_op jit(solution)/shard_map/all_gather | solution.py:889
  11.2 140.6 %all-gather.7.cloned.1.call-start = ((), (), s32[]{:S(2)}) async-start(), calls=%async_computation.1 | async-start | bytes 4644864 | tf_op jit(solution)/shard_map/all_gather | solution.py:888
  11.9 175.6 %all-gather.11.cloned.1.call-start = ((), (), s32[]{:S(2)}) async-start(), calls=%async_computation.3 | async-start | bytes 13762560 | tf_op jit(solution)/shard_map/all_gather | solution.py:897
  12.0 1.6 copy-start.1
  88.5 0.9 copy-start.10
  88.5 18.7 %copy-start.6 = (bf16[1,288]{1,0:T(2,128)(2,1)S(1)}, bf16[1,288]{1,0:T(2,128)(2,1)}, u32[]{:S(2)}) copy-start(bf16[1,288]{1,0:T(2,128)(2,1)} %param.17) | copy-start | bytes 1732
  88.5 18.7 %copy-start.7 = (bf16[1,224]{1,0:T(2,128)(2,1)S(1)}, bf16[1,224]{1,0:T(2,128)(2,1)}, u32[]{:S(2)}) copy-start(bf16[1,224]{1,0:T(2,128)(2,1)} %param.15) | copy-start | bytes 1348
  88.5 18.7 %copy-start.8 = (bf16[1,224]{1,0:T(2,128)(2,1)S(1)}, bf16[1,224]{1,0:T(2,128)(2,1)}, u32[]{:S(2)}) copy-start(bf16[1,224]{1,0:T(2,128)(2,1)} %param.14) | copy-start | bytes 1348
  88.5 18.7 %copy-start.9 = (u32[128]{0:T(128)S(1)}, u32[128]{0:T(128)}, u32[]{:S(2)}) copy-start(u32[128]{0:T(128)} %constant.75) | copy-start | bytes 1540
  88.5 51.7 %copy-start.4 = (f32[2,1,128,896]{3,2,1,0:T(8,128)S(1)}, f32[2,1,128,896]{3,2,1,0:T(8,128)}, u32[]{:S(2)}) copy-start(f32[2,1,128,896]{3,2,1,0:T(8,128)} %param.11) | copy-start | bytes 2752516
  88.5 52.5 %copy-start.5 = (f32[2,1,128,896]{3,2,1,0:T(8,128)S(1)}, f32[2,1,128,896]{3,2,1,0:T(8,128)}, u32[]{:S(2)}) copy-start(f32[2,1,128,896]{3,2,1,0:T(8,128)} %param.12) | copy-start | bytes 2752516
  251.7 32.1 %copy-start.3 = (f32[128,896]{1,0:T(8,128)S(1)}, f32[128,896]{1,0:T(8,128)}, u32[]{:S(2)}) copy-start(f32[128,896]{1,0:T(8,128)} %get-tuple-element.60) | copy-start | bytes 1376260
  284.8 325.8 %collective-permute-start = (f32[128,896]{1,0:T(8,128)S(1)}, f32[128,896]{1,0:T(8,128)S(1)}, u32[]{:S(2)}, u32[]{:S(2)}) collective-permute-start(f32[128,896]{1,0:T(8,128)S(1)} %get-tuple-element.127), channel_id=1, source_target_pairs={{0,64},{64,0},{1,65},{65,1},{2,66},{66,2},{3,67},{67,3},{4,68},{68... | collective-permute-start | bytes 1376264 | tf_op jit(solution)/shard_map/ppermute | solution.py:932
  392.4 40.9 %copy-start.2 = (f32[128,896]{1,0:T(8,128)S(1)}, f32[128,896]{1,0:T(8,128)}, u32[]{:S(2)}) copy-start(f32[128,896]{1,0:T(8,128)} %get-tuple-element.74) | copy-start | bytes 1376260
  434.4 177.2 %collective-permute-start.1 = (f32[128,896]{1,0:T(8,128)S(1)}, f32[128,896]{1,0:T(8,128)S(1)}, u32[]{:S(2)}, u32[]{:S(2)}) collective-permute-start(f32[128,896]{1,0:T(8,128)S(1)} %get-tuple-element.125), channel_id=1, source_target_pairs={{0,64},{64,0},{1,65},{65,1},{2,66},{66,2},{3,67},{67,3},{4,68},{68... | collective-permute-start | bytes 1376264 | tf_op jit(solution)/shard_map/ppermute | solution.py:932
Sparse Core Ops, SparseCore 0:
  10.6 19.3 all-gather.12
  31.7 54.5 all-gather.8
  88.0 31.6 all-gather.6
  121.3 24.1 all-gather.10

commit v3 on v1

v3 whole, which is shorter than its diff:
```python
import functools
import types

import jax
import jax.numpy as jnp
from jax import lax
from jax.experimental import pallas as pl
from jax.experimental.pallas import tpu as pltpu
from jax.sharding import PartitionSpec as P

D = 896
HEADS = 14
KV_HEADS = 2
HEAD_DIM = 64
GROUP = HEADS // KV_HEADS
FF = 4864
QKV = 1152
EPS = 1e-06
THETA = 1000000.0
LANES = 128
TILES = D // LANES
WIN = 1280
NEG = -1e30
F32 = jnp.float32
BF16 = jnp.bfloat16
MESH = pl.DeviceIdType.MESH
VMEM_LIMIT = 56 * 2**20
UNIT = 16
SIDE = 4
GATE_PER = (5, 4)
DOWN_PER = (8, 9)
Q_PER = (4, 4)
Q_ROWS = 16 * sum(Q_PER) * UNIT


def mm(a, b):
    return jnp.dot(a, b, preferred_element_type=F32)


def mm_nt(a, b):
    return lax.dot_general(a, b, (((1,), (1,)), ((), ())), preferred_element_type=F32)


def mm_tn(a, b):
    return lax.dot_general(a, b, (((0,), (0,)), ((), ())), preferred_element_type=F32)


ORDER = (1, 3, 2)
SMALL = 2 * D + QKV
AXES = (("x", "y"), ("y", "x"))


def push(src, dst, ssem, rsem, axis, to):
    return pltpu.make_async_remote_copy(
        src_ref=src,
        dst_ref=dst,
        send_sem=ssem,
        recv_sem=rsem,
        device_id={axis: to},
        device_id_type=MESH,
    )


def rope(u, cos, sa, sb):
    return u * cos + pltpu.roll(u, 96, 1) * sa + pltpu.roll(u, 32, 1) * sb


def unrope(u, cos, sa, sb):
    return u * cos - pltpu.roll(u, 96, 1) * sa - pltpu.roll(u, 32, 1) * sb


def spread(ref, t, tile_t):
    half = HEAD_DIM
    zero = jnp.zeros((half, LANES), BF16)
    for j in range(2):
        h = 2 * t + j
        slab = tile_t[j * half : (j + 1) * half, :].astype(BF16)
        both = [slab, zero] if h // GROUP == 0 else [zero, slab]
        ref[:, h * LANES : (h + 1) * LANES] = jnp.concatenate(both, 0)


def gathered_tile(wide, t):
    half = HEAD_DIM
    rows = []
    for j in range(2):
        g = (2 * t + j) // GROUP
        rows.append(wide[g * half : (g + 1) * half, j * LANES : (j + 1) * LANES])
    return jnp.concatenate(rows, 0).T


def dealt(a_per, b_per):
    where = [(0, u // a_per, u % a_per) for u in range(16 * a_per)]
    return where + [(1, v // b_per, v % b_per) for v in range(16 * b_per)]


def unit_runs(first, count, per):
    where = dealt(*per)
    found = []
    for i in range(count):
        part, piece, slot = where[first + i]
        if found and found[-1][0] == part and found[-1][1] == piece:
            found[-1][4] += 1
        else:
            found.append([part, piece, slot, i, 1])
    return found


def put_units(refs, section, base, per, first, rows):
    for part, piece, slot, i, m in unit_runs(first, rows.shape[0] // UNIT, per):
        at = base[part] + slot * UNIT
        refs[part][section, piece // SIDE, piece % SIDE, at : at + m * UNIT, :] = rows[i * UNIT : (i + m) * UNIT, :]


class Stages:
    def __init__(self, r):
        self.s = lax.axis_index("section")
        self.c = lax.axis_index("ctx")
        self.nc = lax.axis_size("ctx")
        self.x, self.y = self.c // SIDE, lax.rem(self.c, SIDE)
        self.z = lax.axis_index("fsdp")
        self.nz = lax.axis_size("fsdp")
        self.ssem, self.rsem, self.lsem = r.ssem, r.rsem, r.lsem
        self.used = 0
        self.local_used = 0
        self.sent = []

    def along(self, axis, k):
        own, n = {
            "x": (self.x, SIDE),
            "y": (self.y, SIDE),
            "z": (self.z, self.nz),
            "c": (self.c, self.nc),
        }[axis]
        return lax.rem(own + n + k, n)

    def peer(self, axis, k, section=None):
        if axis == "s":
            return {"section": 1 - self.s}
        if axis == "z":
            to = {"fsdp": self.along("z", k)}
        elif axis == "c":
            to = {"ctx": self.along("c", k)}
        elif axis == "x":
            to = {"ctx": self.along("x", k) * SIDE + self.y}
        else:
            to = {"ctx": self.x * SIDE + self.along("y", k)}
        if section is not None:
            to["section"] = section
        return to

    def hail(self, ids, ring=False):
        bar = pltpu.get_barrier_semaphore()
        for i in ids:
            pl.semaphore_signal(bar, inc=1, device_id=i, device_id_type=MESH)
        self.expected = len(ids)
        if ring:
            def one(k, c):
                pl.semaphore_signal(bar, inc=1, device_id=self.peer("c", k), device_id_type=MESH)
                return c

            lax.fori_loop(1, self.nc, one, 0)
            self.expected += self.nc - 1
        self.bar = bar

    def met(self):
        pl.semaphore_wait(self.bar, self.expected)

    def beside(self):
        return [self.peer("s", 0)]

    def upright(self, both=False):
        ids = [self.peer("z", k) for k in range(1, self.nz)]
        return ids + ([self.peer("z", k, 1 - self.s) for k in range(1, self.nz)] if both else [])

    def flat(self, both=False):
        ids = [self.peer(a, k) for a in "xy" for k in range(1, SIDE)]
        return ids + ([self.peer(a, k, 1 - self.s) for a in "xy" for k in range(1, SIDE)] if both else [])

    def take(self, count):
        self.used += count
        return self.used - count

    def copy(self, src, dst, at, to, recv_at=None):
        return pltpu.make_async_remote_copy(
            src_ref=src,
            dst_ref=dst,
            send_sem=self.ssem.at[at],
            recv_sem=self.rsem.at[at if recv_at is None else recv_at],
            device_id=to,
            device_id_type=MESH,
        )

    def begin(self, copies):
        for c in copies:
            c.start()
        self.sent += copies
        return copies

    def drain(self):
        for c in self.sent:
            c.wait_send()

    def swap(self, src, land):
        return self.begin([self.copy(src.at[1 - self.s], land, self.take(1), self.peer("s", 0))])

    def scatter(self, axis, src, land):
        n = self.nz if axis == "z" else SIDE
        at = self.take(n - 1)
        return self.begin(
            [self.copy(src.at[self.along(axis, k)], land.at[k - 1], at + k - 1, self.peer(axis, k)) for k in range(1, n)]
        )

    def gather(self, axis, ref):
        at = self.take(SIDE - 1)
        mine = ref.at[self.along(axis, 0)]
        return self.begin([self.copy(mine, mine, at + k - 1, self.peer(axis, k)) for k in range(1, SIDE)])

    def deal(self, src, dst, rows):
        at = self.take(self.nz - 1)
        mine = dst.at[self.block(self.z, rows), :]
        return self.begin(
            [
                self.copy(src.at[self.block(self.along("z", k), rows), :], mine, at + k - 1, self.peer("z", k))
                for k in range(1, self.nz)
            ]
        )

    def block(self, i, rows):
        return pl.ds(pl.multiple_of(i * rows, UNIT), rows)

    def hand_over(self, axis, src, dst, layer):
        at = self.take(2 * SIDE)
        mine = dst.at[self.s, self.along(axis, 0)]
        self.begin(
            [
                self.copy(src, mine, at + k, self.peer(axis, k, layer), at + self.s * SIDE + k)
                for k in range(1, SIDE)
            ]
        )
        beside = self.copy(src, mine, at, {"section": layer}, at + self.s * SIDE)

        @pl.when(self.s != layer)
        def _():
            beside.start()

        @pl.when(self.s == layer)
        def _():
            mine[...] = src[...]

        def finish():
            @pl.when(self.s == layer)
            def _():
                for half in range(2):
                    for k in range(0 if half != layer else 1, SIDE):
                        self.copy(src, mine, at, {"section": layer}, at + half * SIDE + k).wait_recv()

            @pl.when(self.s != layer)
            def _():
                beside.wait_send()

        return finish


class Feed:
    def __init__(self, st, layer, source, piece):
        self.st, self.layer, self.source, self.piece = st, layer, source, piece
        self.across = st.take(2 * (st.nz - 1))
        self.own = st.take(2)
        self.passed = st.take(st.nz - 1)
        self.local = st.local_used
        st.local_used += 2

    def out_copies(self):
        st = self.st
        found = []
        for k in ORDER:
            for h in range(2):
                found.append(
                    st.copy(
                        self.source(h, st.along("z", k)), self.piece(st.z, h), self.across + 2 * (k - 1) + h, st.peer("z", k, h)
                    )
                )
        for h in range(2):
            found.append(st.copy(self.source(h, st.z), self.piece(st.z, h), self.own + h, st.peer("s", 0)))
        return found

    def in_place(self):
        st = self.st
        return [
            pltpu.make_async_copy(self.source(h, st.z), self.piece(st.z, h), st.lsem.at[self.local + h]) for h in range(2)
        ]

    def start(self):
        @pl.when(self.st.s == self.layer)
        def _():
            for c in self.in_place() + self.out_copies():
                c.start()

    def pass_on(self, k):
        st = self.st
        p = self.piece(st.along("z", -k), st.s)
        st.copy(p, p, self.across + 2 * (k - 1) + st.s, st.peer("s", 0)).wait_recv()
        st.begin([st.copy(p, p, self.passed + k - 1, st.peer("s", 0))])

    def finish(self):
        st = self.st
        for k in ORDER:
            p = self.piece(st.along("z", -k), 1 - st.s)
            st.copy(p, p, self.passed + k - 1, st.peer("s", 0)).wait_recv()

        @pl.when(st.s == self.layer)
        def _():
            for c in self.in_place():
                c.wait()
            for c in self.out_copies():
                c.wait_send()

        @pl.when(st.s != self.layer)
        def _():
            for h in range(2):
                p = self.piece(st.z, h)
                st.copy(p, p, self.own + h, st.peer("s", 0)).wait_recv()


class FeedDown:
    def __init__(self, st, layer, src, dst):
        self.st, self.layer = st, layer
        share = src.shape[1]
        spare = WIN - share
        odd = lax.rem(st.z, 2)
        place = dst.at[pl.ds(pl.multiple_of(odd * spare, UNIT), share), :]
        dst[pl.ds(pl.multiple_of((1 - odd) * share, UNIT), spare), :] = jnp.zeros((spare, D), BF16)
        self.local = pltpu.make_async_copy(src.at[0], place, st.lsem.at[st.local_used])
        st.local_used += 1
        self.remote = st.copy(src.at[0], place, st.take(1), st.peer("s", 0))

    def start(self):
        @pl.when(self.st.s == self.layer)
        def _():
            self.local.start()
            self.remote.start()

    def finish(self):
        @pl.when(self.st.s == self.layer)
        def _():
            self.local.wait()
            self.remote.wait_send()

        @pl.when(self.st.s != self.layer)
        def _():
            self.remote.wait_recv()


def feed_rows(st, layer, src, dst):
    share = src.shape[1]
    half = share // 2

    def source(h, z_to):
        return src.at[0, h * half : (h + 1) * half, :]

    def piece(z_from, h):
        return dst.at[pl.ds(pl.multiple_of(z_from * share + h * half, UNIT), half), :]

    return Feed(st, layer, source, piece)


def feed_windows(st, layer, gate, up, dst):
    share = gate.shape[1]
    pace = FF // st.nz // (LANES // 2)

    def source(h, z_to):
        start = pl.multiple_of(z_to * pace // 2 * LANES, LANES)
        return (gate, up)[h].at[0, :, pl.ds(start, WIN)]

    def piece(z_from, h):
        return dst.at[h, pl.ds(pl.multiple_of(z_from * share, UNIT), share), :]

    return Feed(st, layer, source, piece)


def arrived(copies):
    for c in copies:
        c.wait_recv()


def add_into(dst, parts):
    def one(i, c):
        total = parts[0][i].astype(F32)
        for p in parts[1:]:
            total = total + p[i].astype(F32)
        dst[i] = total.astype(dst.dtype)
        return c

    lax.fori_loop(0, dst.shape[0], one, 0)


def add_rows(dst, parts):
    total = parts[0][...].astype(F32)
    for p in parts[1:]:
        total = total + p[...].astype(F32)
    dst[...] = total.astype(dst.dtype)


def swapped_sum(st, copies, given, land):
    arrived(copies)
    for i in range(SIDE):
        add_into(land.at[i], [given.at[st.s, i], land.at[i]])


def key_positions(pairs_ref, src, n):
    pair = pairs_ref[src, 0:1, :]
    i = lax.broadcasted_iota(jnp.int32, (LANES, LANES), 0)
    block = LANES // 2
    return jnp.where(i < block, pair * block + i, (2 * n - 1 - pair) * block + i - block)


def hidden_bias(pairs_ref, src, qpos, n):
    hide = jnp.where(key_positions(pairs_ref, src, n) <= qpos, 0.0, NEG)
    return jnp.concatenate([hide, hide], 1)


def row_positions(pairs_ref, me, n):
    pair = pairs_ref[me, 0:1, :]
    i = lax.broadcasted_iota(jnp.int32, (1, LANES), 1)
    block = LANES // 2
    return jnp.where(i < block, pair * block + i, (2 * n - 1 - pair) * block + i - block)


def attn_fwd_kernel(layer, r):
    st = Stages(r)
    n, me = st.nc, st.c
    st.hail(st.beside() + st.upright(True), ring=True)
    first = layer == 0
    x = r.x[...]
    r1 = lax.rsqrt(jnp.mean(x * x, -1, keepdims=True) + EPS)
    unit = x * r1
    if first:
        r.pairs[me] = jnp.broadcast_to(r.pair[...], r.pairs.shape[1:])
        r.parts[st.s, st.z] = r.small_own[...]
    st.met()
    wout = feed_rows(st, layer, r.wout_shard, r.wout)
    gu = feed_windows(st, layer, r.gate_shard, r.up_shard, r.gu)
    down = FeedDown(st, layer, r.down_shard, r.down)
    if first:
        qkv = feed_rows(st, layer, r.wqkv_shard, r.wqkv)
        qkv.start()
        at = st.take(2 * st.nz)
        mine = r.parts.at[st.s, st.z]
        st.begin(
            [st.copy(mine, mine, at + k, st.peer("z", k, st.s), at + st.s * st.nz + k) for k in range(1, st.nz)]
            + [st.copy(mine, mine, at + st.nz + k, st.peer("z", k, 1 - st.s), at + st.s * st.nz + k) for k in range(1, st.nz)]
            + [st.copy(mine, mine, at, st.peer("s", 0), at + st.s * st.nz)]
        )

        def tell(k, c):
            p = r.pairs.at[me]
            push(p, p, r.psem.at[k], r.psem2.at[k], "ctx", lax.rem(me + k, n)).start()
            return c

        lax.fori_loop(1, n, tell, 0)
        block = LANES // 2
        i = lax.broadcasted_iota(jnp.int32, (LANES, LANES), 0)
        pair = r.pairs[me, 0:1, :]
        pos = jnp.where(i < block, pair * block + i, (2 * n - 1 - pair) * block + i - block)
        angle = pos.astype(F32) * r.inverse[...]
        lane = lax.rem(lax.broadcasted_iota(jnp.int32, (LANES, LANES), 1), HEAD_DIM)
        sine = jnp.sin(angle)
        r.cos[...] = jnp.cos(angle)
        r.sa[...] = jnp.where(lane < HEAD_DIM // 2, -sine, 0.0)
        r.sb[...] = jnp.where(lane < HEAD_DIM // 2, 0.0, sine)
        for h in (st.s, 1 - st.s):
            for k in range(st.nz):
                if h is st.s and k == 0:
                    continue
                st.copy(mine, mine, at, st.peer("s", 0), at + h * st.nz + k).wait_recv()
        for h in range(2):
            total = r.parts[h, 0]
            for k in range(1, st.nz):
                total = total + r.parts[h, k]
            r.small[h] = total
        for k in ORDER:
            qkv.pass_on(k)
    wout.start()
    gu.start()
    down.start()
    small = r.small[layer]
    n1 = (unit * small[:, :D]).astype(BF16)
    r.n1[...] = n1
    bias = small[:, 2 * D :]
    if first:
        qkv.finish()
    cos, sa, sb = r.cos[...], r.sa[...], r.sb[...]
    lin = mm(n1, r.wqkv[:, D:]) + bias[:, D:]
    r.kv[me] = jnp.concatenate([rope(lin[:, :LANES], cos, sa, sb), lin[:, LANES:]], 1).astype(BF16)

    def keys_copy(k, src):
        return push(r.kv.at[src], r.kv.at[src], r.csem.at[k], r.csem2.at[k], "ctx", lax.rem(me + k, n))

    def start(k, c):
        keys_copy(k, me).start()
        return c

    lax.fori_loop(1, n, start, 0)
    linq = mm(n1, r.wqkv[:, :D]) + bias[:, :D]
    for t in range(TILES):
        q = rope(linq[:, t * LANES : (t + 1) * LANES], cos, sa, sb) * HEAD_DIM ** (-0.5)
        spread(r.qst, t, q.T)
    r.m_s[...] = jnp.full(r.m_s.shape, NEG, F32)
    r.l_s[...] = jnp.zeros(r.l_s.shape, F32)
    r.acc_s[...] = jnp.zeros(r.acc_s.shape, F32)
    qpos = row_positions(r.pairs, me, n)

    def block(src):
        keys = r.kv[src, :, :LANES]
        vals_t = r.kv[src, :, LANES:].astype(F32).T.astype(BF16)
        hide = hidden_bias(r.pairs, src, qpos, n)
        for t in range(TILES):
            cols = slice(2 * t * LANES, 2 * (t + 1) * LANES)
            s = mm(keys, r.qst[:, cols]) + hide
            m_old = r.m_s[:, cols]
            m_new = jnp.maximum(m_old, jnp.max(s, 0, keepdims=True))
            p = jnp.exp(s - m_new)
            alpha = jnp.exp(m_old - m_new)
            r.m_s[:, cols] = m_new
            r.l_s[:, cols] = r.l_s[:, cols] * alpha + jnp.sum(p, 0, keepdims=True)
            r.acc_s[:, cols] = r.acc_s[:, cols] * alpha + mm(vals_t, p.astype(BF16))

    block(me)

    def step(k, c):
        src = lax.rem(me + n - k, n)
        keys_copy(k, src).wait_recv()
        if first:
            p = r.pairs.at[src]
            push(p, p, r.psem.at[k], r.psem2.at[k], "ctx", lax.rem(me + k, n)).wait_recv()
        block(src)
        return c

    low = 1
    for high, feed, k in ((5, wout, 1), (6, wout, 3), (9, wout, 2), (13, gu, 1), (14, gu, 3)):
        lax.fori_loop(low, high, step, 0)
        feed.pass_on(k)
        low = high
    lax.fori_loop(low, n, step, 0)
    r.lse[...] = r.m_s[...] + jnp.log(r.l_s[...])
    for t in range(TILES):
        cols = slice(2 * t * LANES, 2 * (t + 1) * LANES)
        wide = r.acc_s[:, cols] / r.l_s[:, cols]
        r.att[:, t * LANES : (t + 1) * LANES] = gathered_tile(wide, t).astype(BF16)
    wout.finish()
    mid = x + mm(r.att[...], r.wout[...])
    r.mid[...] = mid
    r2 = lax.rsqrt(jnp.mean(mid * mid, -1, keepdims=True) + EPS)
    r.n2[...] = (mid * r2 * small[:, D : 2 * D]).astype(BF16)
    gu.pass_on(2)
    gu.finish()
    down.finish()
    st.drain()

    def done(k, c):
        keys_copy(k, me).wait_send()
        if first:
            p = r.pairs.at[me]
            push(p, p, r.psem.at[k], r.psem2.at[k], "ctx", lax.rem(me + k, n)).wait_send()
        return c

    lax.fori_loop(1, n, done, 0)


def attn_bwd_kernel(layer, r):
    st = Stages(r)
    n, me = st.nc, st.c
    last = layer == 0
    st.hail(st.beside() + (st.upright() if last else []), ring=True)
    half = HEAD_DIM
    gm = r.gm[...]
    gmb = gm.astype(BF16)
    ga = mm_nt(gmb, r.wout[...])
    for t in range(TILES):
        tile = slice(t * LANES, (t + 1) * LANES)
        ga_t = ga[:, tile].T
        spread(r.gst_s, t, ga_t)
        prod = ga_t * r.att[:, tile].astype(F32).T
        r.delta_s[:, 2 * t * LANES : (2 * t + 1) * LANES] = jnp.sum(prod[:half], 0, keepdims=True)
        r.delta_s[:, (2 * t + 1) * LANES : (2 * t + 2) * LANES] = jnp.sum(prod[half:], 0, keepdims=True)
    r.gq_s[...] = jnp.zeros(r.gq_s.shape, F32)
    qpos = row_positions(r.pairs, me, n)
    st.met()
    f, sl, l1, t1 = (r.fa, r.fb), (r.sla, r.slb), (r.l1a, r.l1b), (r.t1a, r.t1b)
    swaps = [st.swap(f[h], sl[h]) for h in range(2)]
    if last:
        qswap = st.swap(r.q_before, r.sq)

    def block(src):
        keys = r.kv[src, :, :LANES]
        vals = r.kv[src, :, LANES:]
        keys_t = keys.astype(F32).T.astype(BF16)
        hide = hidden_bias(r.pairs, src, qpos, n)
        gk = jnp.zeros((LANES, LANES), F32)
        gv = jnp.zeros((LANES, LANES), F32)
        for t in range(TILES):
            cols = slice(2 * t * LANES, 2 * (t + 1) * LANES)
            qs, gs = r.qst[:, cols], r.gst_s[:, cols]
            p = jnp.exp(mm(keys, qs) + hide - r.lse[:, cols])
            ds = (p * (mm(vals, gs) - r.delta_s[:, cols])).astype(BF16)
            gv = gv + mm_nt(p.astype(BF16), gs)
            gk = gk + mm_nt(ds, qs)
            r.gq_s[:, cols] += mm(keys_t, ds)
        return jnp.concatenate([gk, gv], 1)

    def sum_copy(k):
        return push(r.send_s.at[k], r.land_s.at[k], r.csem.at[k], r.csem2.at[k], "ctx", lax.rem(me + k, n))

    def step(k, c):
        r.send_s[k] = block(lax.rem(me + k, n)).astype(BF16)
        sum_copy(k).start()
        return c

    lax.fori_loop(1, 6, step, 0)
    r1 = [None, None]
    for h in range(2):
        swapped_sum(st, swaps[h], f[h], sl[h])
        r1[h] = st.scatter(AXES[h][0], sl[h], l1[h])
    lax.fori_loop(6, 9, step, 0)
    if last:
        arrived(qswap)
        add_into(r.sq, [r.q_before.at[st.s], r.sq])
        zr = st.scatter("z", r.sq, r.zq)
    lax.fori_loop(9, n, step, 0)
    own = block(me)

    def take(k, total):
        sum_copy(k).wait_recv()
        return total + r.land_s[k].astype(F32)

    own = lax.fori_loop(1, n, take, own)
    cos, sa, sb = r.cos[...], r.sa[...], r.sb[...]
    for t in range(TILES):
        wide = r.gq_s[:, 2 * t * LANES : 2 * (t + 1) * LANES]
        gq = gathered_tile(wide, t) * HEAD_DIM ** (-0.5)
        r.glin_s[:, t * LANES : (t + 1) * LANES] = unrope(gq, cos, sa, sb).astype(BF16)
    r.glin_s[:, D : D + LANES] = unrope(own[:, :LANES], cos, sa, sb).astype(BF16)
    r.glin_s[:, D + LANES :] = own[:, LANES:].astype(BF16)
    gn1 = mm_nt(r.glin_s[...], r.wqkv[...])
    x = r.x[...]
    r1_ = lax.rsqrt(jnp.mean(x * x, -1, keepdims=True) + EPS)
    unit = x * r1_
    dg1 = jnp.sum(gn1 * unit, 0, keepdims=True)
    dz = gn1 * r.small[layer][:, :D]
    r.gx[...] = gm + r1_ * (dz - unit * jnp.mean(dz * unit, -1, keepdims=True))
    dbias = jnp.sum(r.glin_s[...].astype(F32), 0, keepdims=True)
    r.small_s[...] = jnp.zeros(r.small_s.shape, F32)
    row = 0
    for part in (dg1, r.dg2[...], dbias):
        for t in range(part.shape[1] // LANES):
            r.small_s[row : row + 1, :] = part[:, t * LANES : (t + 1) * LANES]
            row += 1
    small = r.small_s[...].astype(BF16)
    share = D // st.nz
    for j in range(0, QKV // LANES + TILES, 8):
        for t in range(j, j + 8):
            if t < QKV // LANES:
                d = mm_tn(r.n1[...], r.glin_s[:, t * LANES : (t + 1) * LANES])
            else:
                u = t - QKV // LANES
                d = mm_tn(r.att[...], gmb[:, u * LANES : (u + 1) * LANES])
            d = d.astype(BF16)
            for i in range(st.nz):
                r.q[j // 8, i, (t % 8) * share : (t % 8 + 1) * share, :] = d[i * share : (i + 1) * share, :]
        for i in range(st.nz):
            r.q[j // 8, i, 8 * share : 8 * share + 2 * UNIT, :] = small if j == 0 else jnp.zeros_like(small)
            r.q[j // 8, i, 8 * share + 2 * UNIT :, :] = jnp.zeros((Q_ROWS - 8 * share - 2 * UNIT, LANES), BF16)
    for h in range(2):
        arrived(r1[h])
        mine = sl[h].at[st.along(AXES[h][0], 0)]
        add_into(t1[h], [mine] + [l1[h].at[k] for k in range(SIDE - 1)])
    if last:
        arrived(zr)
        fold_z(st, r.sq, r.zq, (r.qpa, r.qpb))
    st.drain()

    def done(k, c):
        sum_copy(k).wait_send()
        return c

    lax.fori_loop(1, n, done, 0)


def fold_z(st, sq, zq, out):
    parts = [sq.at[st.z]] + [zq.at[k] for k in range(st.nz - 1)]
    rows = Q_ROWS // 2 // 16
    for h in range(2):
        for i in range(16):
            at = (h * 16 + i) * rows
            total = jnp.zeros((rows, LANES), F32)
            for p in parts:
                total = total + p[at : at + rows, :].astype(F32)
            out[h][i // SIDE, i % SIDE] = total.astype(BF16)


def ffn_fwd_kernel(layer, r):
    st = Stages(r)
    n, me = st.nz, st.z
    carry = layer == 0
    st.hail(st.upright(carry) + (st.beside() if carry else []))
    r.all[me] = r.n2[...]
    st.met()
    at = st.take(2 * n)

    def first(k):
        return st.copy(r.all.at[me], r.all.at[me], at + k, st.peer("z", k))

    def second(k):
        return st.copy(r.send_s.at[k], r.land_s.at[k], at + n + k, st.peer("z", -k))

    for k in ORDER:
        first(k).start()
    if carry:
        qkv = feed_rows(st, 1, r.wqkv_shard, r.wqkv)
        qkv.start()

    def block(src):
        a = r.all[src]
        gate = mm(a, r.gu[0])
        up = mm(a, r.gu[1])
        r.gate[src] = gate
        r.up[src] = up
        hidden = (gate * jax.nn.sigmoid(gate) * up).astype(BF16)
        return mm(hidden, r.down[...])

    r.y[...] = r.mid[...] + block(me)
    for k in ORDER:
        first(k).wait_recv()
        r.send_s[k] = block(st.along("z", -k)).astype(BF16)
        second(k).start()
        if carry and k == 3:
            qkv.pass_on(1)
            qkv.pass_on(3)
    if carry:
        qkv.pass_on(2)
    for k in ORDER:
        second(k).wait_recv()
        r.y[...] += r.land_s[k].astype(F32)
    for k in ORDER:
        first(k).wait_send()
        second(k).wait_send()
    if carry:
        qkv.finish()
    st.drain()


def ffn_bwd_kernel(layer, r):
    st = Stages(r)
    n, me = st.nz, st.z
    carry = layer == 0
    st.hail(st.upright() + (st.beside() + st.flat(True) if carry else []))
    tok = r.gy.shape[0]

    def rows_of(i):
        return pl.ds(pl.multiple_of(i * tok, tok), tok)

    r.all_s[rows_of(me), :] = r.gy[...].astype(BF16)
    st.met()
    at = st.take(2 * n)

    def first(k):
        mine = r.all_s.at[rows_of(me), :]
        return st.copy(mine, mine, at + k, st.peer("z", k))

    def second(k):
        return st.copy(r.send_s.at[k], r.land_s.at[k], at + n + k, st.peer("z", -k))

    for k in ORDER:
        first(k).start()
    if carry:
        rest = Rest(st, (r.t1a, r.t1b), (r.l2a, r.l2b), (r.t2a, r.t2b), (r.g1a, r.g1b), (r.ga, r.gb), 1)

    def block(src):
        rows = rows_of(src)
        gh = mm_nt(r.all_s[rows, :], r.down[...])
        gate, up = r.gate[src], r.up[src]
        sg = jax.nn.sigmoid(gate)
        act = gate * sg
        r.hid_s[rows, :] = (act * up).astype(BF16)
        ggate = (gh * up * sg * (1.0 + gate * (1.0 - sg))).astype(BF16)
        gup = (gh * act).astype(BF16)
        r.ggate_s[rows, :] = ggate
        r.gup_s[rows, :] = gup
        return mm_nt(ggate, r.gu[0]) + mm_nt(gup, r.gu[1])

    r.own_s[...] = block(me)
    for k in ORDER:
        if carry:
            rest.advance()
        first(k).wait_recv()
        r.send_s[k] = block(st.along("z", -k)).astype(BF16)
        second(k).start()

    refs = (r.fa, r.fb)
    share = D // n
    normed = jnp.concatenate([r.n2_all[i] for i in range(n)], 0)
    for section, part in ((0, r.ggate_s), (1, r.gup_s)):
        for j in range(WIN // (2 * LANES)):
            d = mm_tn(normed, part[:, 2 * j * LANES : 2 * (j + 1) * LANES]).astype(BF16)
            for t in (2 * j, 2 * j + 1):
                tile = d[:, (t % 2) * LANES : (t % 2 + 1) * LANES]
                for i in range(n):
                    base = [i * per * UNIT for per in GATE_PER]
                    put_units(refs, section, base, GATE_PER, t * (share // UNIT), tile[i * share : (i + 1) * share, :])
        used = WIN // LANES * (share // UNIT)
        extra = 16 * sum(GATE_PER) - used
        for i in range(n):
            base = [i * per * UNIT for per in GATE_PER]
            put_units(refs, section, base, GATE_PER, used, jnp.zeros((extra * UNIT, LANES), BF16))
    for j in range(WIN // (2 * LANES)):
        cols = slice(2 * j * LANES, 2 * (j + 1) * LANES)
        r.down_s[cols, :] = mm_tn(r.hid_s[:, cols], r.all_s[...]).astype(BF16)
    pad = (WIN - FF // n) * lax.rem(me, 2)
    half = FF // n // 2
    base = [n * per * UNIT for per in GATE_PER]
    for section in range(2):
        rows = r.down_s[pl.ds(pl.multiple_of(pad + section * half, UNIT), half), :]
        for t in range(TILES):
            put_units(refs, section, base, DOWN_PER, t * (half // UNIT), rows[:, t * LANES : (t + 1) * LANES])
        used = TILES * (half // UNIT)
        extra = 16 * sum(DOWN_PER) - used
        put_units(refs, section, base, DOWN_PER, used, jnp.zeros((extra * UNIT, LANES), BF16))

    for k in ORDER:
        second(k).wait_recv()
        r.own_s[...] += r.land_s[k].astype(F32)
    gn2 = r.own_s[...]
    mid = r.mid[...]
    r2 = lax.rsqrt(jnp.mean(mid * mid, -1, keepdims=True) + EPS)
    unit = mid * r2
    r.dg2[...] = jnp.sum(gn2 * unit, 0, keepdims=True)
    dz = gn2 * r.small[layer][:, D : 2 * D]
    r.gm[...] = r.gy[...] + r2 * (dz - unit * jnp.mean(dz * unit, -1, keepdims=True))
    for k in ORDER:
        first(k).wait_send()
        second(k).wait_send()
    if carry:
        rest.finish()
    st.drain()


class Rest:
    def __init__(self, st, t1, l2, t2, g1, out, layer):
        self.st, self.t1, self.l2, self.t2, self.g1, self.out, self.layer = st, t1, l2, t2, g1, out, layer
        self.stage = 0
        self.moving = [st.scatter(AXES[h][1], t1[h], l2[h]) for h in range(2)]

    def advance(self):
        st = self.st
        for h in range(2):
            second = AXES[h][1]
            arrived(self.moving[h])
            mine = self.g1[h].at[st.along(second, 0)]
            if self.stage == 0:
                t2 = self.t2[h]
                add_rows(t2, [self.t1[h].at[st.along(second, 0)]] + [self.l2[h].at[k] for k in range(SIDE - 1)])
                per = GATE_PER[h] * UNIT
                self.moving[h] = st.deal(t2, mine, per)
                mine[st.block(st.z, per), :] = t2[st.block(st.z, per), :]
                mine[st.nz * per :, :] = t2[st.nz * per :, :]
            elif self.stage == 1:
                self.moving[h] = st.gather(second, self.g1[h])
            else:
                self.moving[h] = st.hand_over(AXES[h][0], self.g1[h], self.out[h], self.layer)
        self.stage += 1

    def finish(self):
        for h in range(2):
            self.moving[h]()


def reduce_kernel(layer, r):
    st = Stages(r)
    st.hail(st.beside() + st.upright() + st.flat(True))
    st.met()
    rest = Rest(st, (r.t1a, r.t1b), (r.l2a, r.l2b), (r.t2a, r.t2b), (r.g1a, r.g1b), (r.ga, r.gb), 0)
    qswap = st.swap(r.q0, r.sq)
    qp = {1: (r.q1a, r.q1b), 0: (r.qpa, r.qpb)}
    land = {1: (r.m1a, r.m1b), 0: (r.m0a, r.m0b)}
    land2 = {1: (r.w1a, r.w1b), 0: (r.w0a, r.w0b)}
    part = {1: (r.e1a, r.e1b), 0: (r.e0a, r.e0b)}
    wide = {1: (r.h1a, r.h1b), 0: (r.h0a, r.h0b)}
    out = (r.qa, r.qb)
    moving = {}

    def along_first(l):
        moving[l] = [st.scatter(AXES[h][0], qp[l][h], land[l][h]) for h in range(2)]

    def along_second(l):
        for h in range(2):
            arrived(moving[l][h])
            own = qp[l][h].at[st.along(AXES[h][0], 0)]
            add_into(part[l][h], [own] + [land[l][h].at[k] for k in range(SIDE - 1)])
            moving[l][h] = st.scatter(AXES[h][1], part[l][h], land2[l][h])

    def back_second(l):
        for h in range(2):
            arrived(moving[l][h])
            i = st.along(AXES[h][1], 0)
            add_rows(wide[l][h].at[i], [part[l][h].at[i]] + [land2[l][h].at[k] for k in range(SIDE - 1)])
            moving[l][h] = st.gather(AXES[h][1], wide[l][h])

    def back_first(l):
        for h in range(2):
            arrived(moving[l][h])
            moving[l][h] = st.hand_over(AXES[h][0], wide[l][h], out[h], l)

    along_first(1)
    rest.advance()
    arrived(qswap)
    add_into(r.sq, [r.q0.at[st.s], r.sq])
    zr = st.scatter("z", r.sq, r.zq)
    rest.advance()
    along_second(1)
    rest.advance()
    back_second(1)
    arrived(zr)
    fold_z(st, r.sq, r.zq, qp[0])
    along_first(0)
    back_first(1)
    along_second(0)
    back_second(0)
    back_first(0)
    rest.finish()
    for l in (1, 0):
        for h in range(2):
            moving[l][h]()
    st.drain()


def call(kernel, layer, cid, name, ins, outs, scratch, sems, hbm=(), flops=10**10):
    names = list(ins) + list(outs) + list(scratch)
    dma = pltpu.SemaphoreType.DMA
    counts = dict(ssem=sems, rsem=sems, lsem=8, csem=16, csem2=16, psem=16, psem2=16)

    def body(*refs):
        kernel(layer, types.SimpleNamespace(**dict(zip(names + list(counts), refs))))

    vm = pl.BlockSpec(memory_space=pltpu.VMEM)
    anywhere = pl.BlockSpec(memory_space=pl.ANY)
    made = pl.pallas_call(
        body,
        out_shape=[jax.ShapeDtypeStruct(s, t) for s, t in outs.values()],
        in_specs=[anywhere if k in hbm else vm for k in ins],
        out_specs=[vm] * len(outs),
        scratch_shapes=[pltpu.VMEM(s, t) for s, t in scratch.values()] + [dma((k,)) for k in counts.values()],
        compiler_params=pltpu.CompilerParams(
            collective_id=cid, has_side_effects=True, vmem_limit_bytes=VMEM_LIMIT
        ),
        cost_estimate=pl.CostEstimate(flops=flops, bytes_accessed=20 * 2**20, transcendentals=0),
        name=name,
    )(*ins.values())
    return dict(zip(outs, made))


FA_ROWS = tuple((4 * g + d) * UNIT for g, d in zip(GATE_PER, DOWN_PER))
RQ = Q_ROWS // 2 // 16
SIDES = (SIDE, SIDE)
WIDE = HEADS * LANES


def bf(*shape):
    return (shape, BF16)


def f4(*shape):
    return (shape, F32)


def rest_scratch():
    made = {}
    for h, rows in zip("ab", FA_ROWS):
        made["l2" + h] = bf(SIDE - 1, rows, LANES)
        made["t2" + h] = bf(rows, LANES)
        made["g1" + h] = bf(SIDE, rows, LANES)
    return made


def rest_outs():
    return {"g" + h: bf(2, *SIDES, rows, LANES) for h, rows in zip("ab", FA_ROWS)}


def assemble_kernel(nz, *refs):
    given, outs, held, sem = (refs[:2], refs[2:4]), refs[6:12], refs[12:14] + refs[4:6], refs[14]
    s = lax.axis_index("section")
    for layer in range(2):
        @pl.when(s == layer)
        def _():
            copies = [pltpu.make_async_copy(a, b, sem.at[i]) for i, (a, b) in enumerate(zip(given[layer], held))]
            for c in copies:
                c.start()
            for c in copies:
                c.wait()

    gate_ref, up_ref, down_ref, qkv_ref, out_ref, small_ref = outs
    share = D // nz
    starts = window_starts(nz)

    def units(refs, section, base, per, first, count):
        rows = []
        for part, piece, slot, _, m in unit_runs(first, count, per):
            at = base[part] + slot * UNIT
            rows.append(refs[part][section, piece // SIDE, piece % SIDE, at : at + m * UNIT, :].astype(F32))
        return jnp.concatenate(rows, 0) if len(rows) > 1 else rows[0]

    for section, ref in ((0, gate_ref), (1, up_ref)):
        tiles = {}
        for w, a in enumerate(starts):
            for t in range(WIN // LANES):
                tiles.setdefault(a // LANES + t, []).append((w, t))
        for col, sources in tiles.items():
            total = None
            for w, t in sources:
                base = [w * per * UNIT for per in GATE_PER]
                got = units(held[:2], section, base, GATE_PER, t * (share // UNIT), share // UNIT)
                total = got if total is None else total + got
            ref[:, col * LANES : (col + 1) * LANES] = total
    base = [nz * per * UNIT for per in GATE_PER]
    half = FF // nz // 2
    for section in range(2):
        for t in range(TILES):
            got = units(held[:2], section, base, DOWN_PER, t * (half // UNIT), half // UNIT)
            down_ref[section * half : (section + 1) * half, t * LANES : (t + 1) * LANES] = got
    for t in range(QKV // LANES + TILES):
        got = units(held[2:], t // 8, (0, 0), Q_PER, (t % 8) * (share // UNIT), share // UNIT)
        if t < QKV // LANES:
            qkv_ref[:, t * LANES : (t + 1) * LANES] = got
        else:
            u = t - QKV // LANES
            out_ref[:, u * LANES : (u + 1) * LANES] = got
    small_ref[...] = units(held[2:], 0, (0, 0), Q_PER, 8 * (share // UNIT), 2)


def assemble(zero, one, attn):
    nz = lax.axis_size("fsdp")
    vm = pl.BlockSpec(memory_space=pltpu.VMEM)
    anywhere = pl.BlockSpec(memory_space=pl.ANY)
    share = D // nz
    shapes = [(share, FF), (share, FF), (FF // nz, D), (share, QKV), (share, D), (2 * UNIT, LANES)]
    return pl.pallas_call(
        functools.partial(assemble_kernel, nz),
        out_shape=[jax.ShapeDtypeStruct(a, F32) for a in shapes],
        in_specs=[anywhere] * 4 + [vm] * 2,
        out_specs=[vm] * len(shapes),
        scratch_shapes=[pltpu.VMEM(a.shape, a.dtype) for a in zero] + [pltpu.SemaphoreType.DMA((2,))],
        compiler_params=pltpu.CompilerParams(vmem_limit_bytes=VMEM_LIMIT),
        name="assemble",
    )(*zero, *one, *attn)


def window_starts(n):
    share = FF // n
    return [(i * share // LANES) * LANES for i in range(n)]


def attn_fwd(layer, x, shards, small, pair, pairs, tabs, wqkv):
    n, nz = lax.axis_size("ctx"), lax.axis_size("fsdp")
    tok = x.shape[0]
    ins = dict(x=x, wout_shard=shards["out"], gate_shard=shards["gate"], up_shard=shards["up"], down_shard=shards["down"])
    outs = dict(
        mid=f4(tok, D), n2=bf(tok, D), n1=bf(tok, D), qst=bf(LANES, WIDE), kv=bf(n, tok, 2 * LANES), lse=f4(1, WIDE),
        att=bf(tok, D), wout=bf(D, D), gu=bf(2, D, WIN), down=bf(WIN, D),
    )
    scratch = dict(m_s=f4(1, WIDE), l_s=f4(1, WIDE), acc_s=f4(LANES, WIDE))
    if layer == 0:
        freq = jnp.arange(HEAD_DIM // 2, dtype=F32)
        inverse = jnp.tile(THETA ** (-2.0 * freq / HEAD_DIM), 4)[None, :]
        ins.update(wqkv_shard=shards["qkv"], small_own=small, pair=pair, inverse=inverse)
        outs.update(
            wqkv=bf(D, QKV), small=f4(2, 1, SMALL), pairs=((n, 8, LANES), jnp.int32),
            cos=f4(tok, LANES), sa=f4(tok, LANES), sb=f4(tok, LANES),
        )
        scratch.update(parts=f4(2, nz, 1, SMALL))
    else:
        ins.update(wqkv=wqkv, small=small, pairs=pairs, cos=tabs[0], sa=tabs[1], sb=tabs[2])
    hbm = ("wout_shard", "gate_shard", "up_shard", "down_shard", "wqkv_shard")
    return call(attn_fwd_kernel, layer, 1 + layer, f"attn_fwd_{layer}", ins, outs, scratch, 64, hbm)


def ffn_fwd(layer, a, qkv_shard):
    n = lax.axis_size("fsdp")
    tok = a["n2"].shape[0]
    ins = {k: a[k] for k in ("n2", "mid", "gu", "down")}
    outs = dict(y=f4(tok, D), all=bf(n, tok, D), gate=f4(n, tok, WIN), up=f4(n, tok, WIN))
    if layer == 0:
        ins.update(wqkv_shard=qkv_shard)
        outs.update(wqkv=bf(D, QKV))
    scratch = dict(send_s=bf(n, tok, D), land_s=bf(n, tok, D))
    return call(ffn_fwd_kernel, layer, 3 + layer, f"ffn_fwd_{layer}", ins, outs, scratch, 32, ("wqkv_shard",))


def ffn_bwd(layer, gy, a, f, small, before):
    n = lax.axis_size("fsdp")
    tok = gy.shape[0]
    ins = dict(gy=gy, mid=a["mid"], small=small, gu=a["gu"], down=a["down"], gate=f["gate"], up=f["up"], n2_all=f["all"])
    outs = dict(gm=f4(tok, D), dg2=f4(1, D))
    for h, rows in zip("ab", FA_ROWS):
        outs["f" + h] = bf(2, *SIDES, rows, LANES)
    scratch = dict(
        all_s=bf(n * tok, D), hid_s=bf(n * tok, WIN), ggate_s=bf(n * tok, WIN), gup_s=bf(n * tok, WIN), down_s=bf(WIN, D),
        own_s=f4(tok, D), send_s=bf(n, tok, D), land_s=bf(n, tok, D),
    )
    if layer == 0:
        ins.update(t1a=before["t1a"], t1b=before["t1b"])
        outs.update(rest_outs())
        scratch.update(rest_scratch())
    return call(ffn_bwd_kernel, layer, 5 + layer, f"ffn_bwd_{layer}", ins, outs, scratch, 64, flops=2 * 10**10)


def attn_bwd(layer, x, a, b, wqkv, small, pairs, tabs, before):
    n, nz = lax.axis_size("ctx"), lax.axis_size("fsdp")
    tok = x.shape[0]
    ins = dict(
        gm=b["gm"], dg2=b["dg2"], fa=b["fa"], fb=b["fb"], x=x, wqkv=wqkv, small=small, pairs=pairs,
        cos=tabs[0], sa=tabs[1], sb=tabs[2],
    )
    ins.update({k: a[k] for k in ("wout", "qst", "kv", "lse", "att", "n1")})
    outs = dict(gx=f4(tok, D), q=bf(2, nz, Q_ROWS, LANES))
    scratch = dict(
        gst_s=bf(LANES, WIDE), delta_s=f4(1, WIDE), gq_s=f4(LANES, WIDE), glin_s=bf(tok, QKV), small_s=f4(2 * UNIT, LANES),
        send_s=bf(n, tok, 2 * LANES), land_s=bf(n, tok, 2 * LANES),
    )
    for h, rows in zip("ab", FA_ROWS):
        outs["t1" + h] = bf(SIDE, rows, LANES)
        scratch["sl" + h] = bf(*SIDES, rows, LANES)
        scratch["l1" + h] = bf(SIDE - 1, SIDE, rows, LANES)
    if layer == 0:
        ins.update(q_before=before["q"])
        scratch.update(sq=bf(nz, Q_ROWS, LANES), zq=bf(nz - 1, Q_ROWS, LANES))
        outs.update(qpa=bf(*SIDES, RQ, LANES), qpb=bf(*SIDES, RQ, LANES))
    return call(attn_bwd_kernel, layer, 7 + layer, f"attn_bwd_{layer}", ins, outs, scratch, 32, flops=2 * 10**10)


def reduce_rest(last):
    nz = lax.axis_size("fsdp")
    ins = dict(t1a=last["t1a"], t1b=last["t1b"], q0=last["q"], q1a=last["qpa"], q1b=last["qpb"])
    outs = rest_outs()
    scratch = rest_scratch()
    scratch.update(sq=bf(nz, Q_ROWS, LANES), zq=bf(nz - 1, Q_ROWS, LANES), qpa=bf(*SIDES, RQ, LANES), qpb=bf(*SIDES, RQ, LANES))
    for h in "ab":
        outs["q" + h] = bf(2, *SIDES, RQ, LANES)
        for l in "01":
            scratch["m" + l + h] = bf(SIDE - 1, SIDE, RQ, LANES)
            scratch["w" + l + h] = bf(SIDE - 1, RQ, LANES)
            scratch["e" + l + h] = bf(SIDE, RQ, LANES)
            scratch["h" + l + h] = bf(SIDE, RQ, LANES)
    return call(reduce_kernel, 0, 9, "reduce", ins, outs, scratch, 128)


def local(
    tokens, cotangent, pair_of, attn_gain, ffn_gain, qkv_weight, qkv_bias, out_weight, gate_weight, up_weight, down_weight,
):
    s = lax.axis_index("section")
    z = lax.axis_index("fsdp")
    nz = lax.axis_size("fsdp")
    qd = D // nz
    shards = dict(qkv=qkv_weight, out=out_weight, gate=gate_weight, up=up_weight, down=down_weight)

    def placed(part, size):
        whole = jnp.zeros((1, size), F32)
        return lax.dynamic_update_slice(whole, part.astype(F32), (0, z * part.shape[1]))

    small_own = jnp.concatenate([placed(attn_gain, D), placed(ffn_gain, D), placed(qkv_bias, QKV)], 1)
    pair = jnp.broadcast_to(pair_of.reshape(1, 1), (8, LANES))
    x0 = jnp.where(s == 0, tokens[0, 0], tokens[1, 0])
    a0 = attn_fwd(0, x0, shards, small_own, pair, None, None, None)
    small, pairs, tabs = a0["small"], a0["pairs"], (a0["cos"], a0["sa"], a0["sb"])
    f0 = ffn_fwd(0, a0, qkv_weight)
    x1 = f0["y"].astype(BF16).astype(F32)
    a1 = attn_fwd(1, x1, shards, small, None, pairs, tabs, f0["wqkv"])
    f1 = ffn_fwd(1, a1, None)

    gy = jnp.where(s == 0, cotangent[0, 0], cotangent[1, 0])
    b1 = ffn_bwd(1, gy, a1, f1, small, None)
    c1 = attn_bwd(1, x1, a1, b1, f0["wqkv"], small, pairs, tabs, None)
    gy = c1["gx"].astype(BF16).astype(F32)
    b0 = ffn_bwd(0, gy, a0, f0, small, c1)
    c0 = attn_bwd(0, x0, a0, b0, a0["wqkv"], small, pairs, tabs, c1)
    t = reduce_rest(c0)
    dgate, dup, ddown, dqkv, dout, small_grad = assemble((t["ga"], t["gb"]), (b0["ga"], b0["gb"]), (t["qa"], t["qb"]))
    small_grad = small_grad.reshape(-1)

    def mine(first, size):
        return lax.dynamic_slice_in_dim(small_grad, first + z * size, size, 0)[None]

    def by_layer(pair):
        theirs = jnp.where(s == 0, pair[1], pair[0])
        mine = jnp.where(s == 0, pair[0], pair[1])
        got = lax.ppermute(theirs, "section", [(0, 1), (1, 0)])
        return jnp.where(s == 0, jnp.stack([mine, got]), jnp.stack([got, mine]))[None, :, None]

    return (
        by_layer((f0["y"], f1["y"])),
        by_layer((c0["gx"], c1["gx"])),
        mine(0, qd),
        mine(D, qd),
        dqkv[None],
        mine(2 * D, QKV // nz),
        dout[None],
        dgate[None],
        dup[None],
        ddown[None],
    )


def solution(mesh):
    return jax.shard_map(
        local,
        mesh=mesh,
        in_specs=(
            P(None, "fsdp", "ctx", None),
            P(None, "fsdp", "ctx", None),
            P("ctx"),
            P("section", "fsdp"),
            P("section", "fsdp"),
            P("section", "fsdp", None),
            P("section", "fsdp"),
            P("section", "fsdp", None),
            P("section", "fsdp", None),
            P("section", "fsdp", None),
            P("section", "fsdp", None),
        ),
        out_specs=(
            P("section", None, "fsdp", "ctx", None),
            P("section", None, "fsdp", "ctx", None),
            P("section", "fsdp"),
            P("section", "fsdp"),
            P("section", "fsdp", None),
            P("section", "fsdp"),
            P("section", "fsdp", None),
            P("section", "fsdp", None),
            P("section", "fsdp", None),
            P("section", "fsdp", None),
        ),
        check_vma=False,
    )
```

time: 849 us -> 506 us (0.60)
  waiting for transfers between devices: 252 us -> 0.01 us
  Pallas kernels: 255 us -> 475 us
  blocking collectives: 188 us -> 0 us
  local copies, waits for them, and re-layouts: 67.7 us -> 4.4 us
  other arithmetic: 51.5 us -> 13.4 us
  between operations: 17 us -> 1.92 us
  matrix products: 12.3 us -> 0 us
    pallas_call x8 -> x10, Pallas kernels: 255 us -> 475 us  [the longest x9 465 us: call(): pl.pallas_call(body, out_shape=[jax.ShapeDtypeStruct(s, t) for s, t in ou...]
    psum x1 -> x0, waiting for transfers between devices: 145 us -> none  [local(): dqkv, dout = lax.psum((dqkv, dout), 'ctx')]
    reduce_scatter x7 -> x0, waiting for transfers between devices: 105 us -> none  [the longest x5 43.5 us: over_sections(): return lax.psum_scatter(pair, 'section', scatter_dimension=0, tiled=False)]
    all_to_all x2 -> x0, blocking collectives: 82.5 us -> none  [the longest x1 71.1 us: local(): gu = lax.all_to_all(gu, 'fsdp', 0, 0)]
    psum x1 -> x0, blocking collectives: 64.1 us -> none  [local(): small_grad = lax.psum(small_grad, ('section', 'ctx', 'fsdp'))]
    unnamed x2 -> x0, blocking collectives: 41.2 us -> none
    unnamed x89 -> x6, local copies, waits for them, and re-layouts: 15.8 us -> 0.01 us
    another operation x13 -> x0, other arithmetic: 15.3 us -> none  [the longest x5 12 us: over_sections(): pair = jnp.stack([grads[0][index], grads[1][index]]).astype(BF16)]
  transfers between devices with their start and end apart: 15 -> 2, of which waited for: 7 -> 0; matrix products, arithmetic and copies ran while one was open for 10% -> 1% of each run, Pallas kernels for 4% -> 17%
where the time goes in v3:
time: 506 us; the launch traced here: 497 us
  Pallas kernels  475 us (94%)
  other arithmetic  13.4 us (3%)
    pallas_call x9, Pallas kernels, call(): pl.pallas_call(body, out_shape=[jax.ShapeDtypeStruct(s, t) for s, t in ou...  465 us
  transfers between devices with their start and end apart: 2, of which 0 were waited for; matrix products, arithmetic and copies ran while one was open for 1% of the time, Pallas kernels for 17%

profile of v3, /device:TPU:0, one launch (start us, length us, event | category | flops | bytes accessed | tf_op | source)
XLA Modules:
  0.0 496.8 jit_solution(9634743242676827207)
XLA Ops:
  1.3 0.7 convert_element_type.21
  2.0 0.7 convert_element_type.22
  2.7 0.6 broadcast_in_dim_tile.3.refs_8_
  3.3 0.7 convert_element_type.23
  4.0 2.0 select_bitcast_fusion.3.refs_0_.refs_4_
  5.9 2.0 select_bitcast_fusion.1.refs_0_
  7.9 0.1 dynamic_update_slice.10
  8.0 0.2 dynamic_update_slice.9
  8.2 0.2 dynamic_update_slice.11
  8.4 0.6 pad_maximum_fusion.refs_6_
  9.0 0.6 broadcast_in_dim.38.refs_7_
  9.6 68.9 %attn_fwd_0.1 = (f32[128,896]{1,0:T(8,128)}, bf16[128,896]{1,0:T(8,128)(2,1)}, bf16[128,896]{1,0:T(8,128)(2,1)}, bf16[128,1792]{1,0:T(8,128)(2,1)}, bf16[16,128,...) custom-call(f32[128,896]{1,0:T(8,128)} %select_bitcast_fusion.3.refs, ...), custom_call_target="tpu_custom_call" | custom-call | flops 10000000000 | bytes 20971520 | tf_op jit(solution)/shard_map/attn_fwd_0/pallas_call | solution.py:946
  78.5 40.0 %ffn_fwd_0.1 = (f32[128,896]{1,0:T(8,128)}, bf16[4,128,896]{2,1,0:T(8,128)(2,1)}, f32[4,128,1280]{2,1,0:T(8,128)}, f32[4,128,1280]{2,1,0:T(8,128)}, bf16[896,1152]{1,0:T(8,128)(2,1)}) custom-call(bf16[128,896]{1,0:T(8,128)(2,1)} %get-tuple-element.75.refs_0_, f32[128,896]{1,0:T(8,128)} %get-tuple-element.76.refs_1_, ...), custom_call_target="tpu_custom_call" | custom-call | flops 10000000000 | bytes 20971520 | tf_op jit(solution)/shard_map/ffn_fwd_0/pallas_call | solution.py:946
  118.6 1.8 convert_convert_fusion.1.refs_0_.refs_4_
  120.4 50.2 %attn_fwd_1.1 = (f32[128,896]{1,0:T(8,128)}, bf16[128,896]{1,0:T(8,128)(2,1)}, bf16[128,896]{1,0:T(8,128)(2,1)}, bf16[128,1792]{1,0:T(8,128)(2,1)}, bf16[16,128,...) custom-call(f32[128,896]{1,0:T(8,128)} %convert_convert_fusion.1.ref, ...), custom_call_target="tpu_custom_call" | custom-call | flops 10000000000 | bytes 20971520 | tf_op jit(solution)/shard_map/attn_fwd_1/pallas_call | solution.py:946
  170.6 31.2 %ffn_fwd_1.1 = (f32[128,896]{1,0:T(8,128)}, bf16[4,128,896]{2,1,0:T(8,128)(2,1)}, f32[4,128,1280]{2,1,0:T(8,128)}, f32[4,128,1280]{2,1,0:T(8,128)}) custom-call(bf16[128,896]{1,0:T(8,128)(2,1)} %get-tuple-element.86.refs_0_, f32[128,896]{1,0:T(8,128)} %get-tuple-element.87.refs_1_, bf16[2,896,1280]{2,1,0:T(8,128)(2,1)} %get-tuple-element.88.refs_2_.refs_3_, ...), custom_call_target="tpu_custom_call" | custom-call | flops 10000000000 | bytes 20971520 | tf_op jit(solution)/shard_map/ffn_fwd_1/pallas_call | solution.py:946
  201.8 34.0 %ffn_bwd_1.1 = (f32[128,896]{1,0:T(8,128)}, f32[1,896]{1,0:T(1,128)}, bf16[2,4,4,448,128]{4,3,2,1,0:T(8,128)(2,1)}, bf16[2,4,4,400,128]{4,3,2,1,0:T(8,128)(2,1)}) custom-call(f32[128,896]{1,0:T(8,128)} %select_bitcast_fusion.1.refs_0_, f32[128,896]{1,0:T(8,128)} %get-tuple-element.87.refs_1_, f32[2,1,2944]{2,1,0:T(1,128)} %get-tuple-element.81.refs_6_.refs_2_, ...), custom_call_target="tpu_custom_call" | custom-call | flops 20000000000 | bytes 20971520 | tf_op jit(solution)/shard_map/ffn_bwd_1/pallas_call | solution.py:946
  235.8 52.0 %attn_bwd_1.1 = (f32[128,896]{1,0:T(8,128)}, bf16[2,4,2048,128]{3,2,1,0:T(8,128)(2,1)}, bf16[4,448,128]{2,1,0:T(8,128)(2,1)}, bf16[4,400,128]{2,1,0:T(8,128)(2,1)}) custom-call(f32[128,896]{1,0:T(8,128)} %get-tuple-element.94.refs_0_, f32[1,896]{1,0:T(1,128)} %get-tuple-element.95.refs_1_, bf16[2,4,4,448,128]{4,3,2,1,0:T(8,128)(2,1)} %get-tuple-element.96.refs_2_, ...), custom_call_target="tpu_custom_call" | custom-call | flops 20000000000 | bytes 20971520 | tf_op jit(solution)/shard_map/attn_bwd_1/pallas_call | solution.py:946
  287.8 1.8 convert_convert_fusion.refs_0_
  289.7 56.5 %ffn_bwd_0.1 = (f32[128,896]{1,0:T(8,128)}, f32[1,896]{1,0:T(1,128)}, bf16[2,4,4,448,128]{4,3,2,1,0:T(8,128)(2,1)}, bf16[2,4,4,400,128]{4,3,2,1,0:T(8,128)(2,1)}...) custom-call(f32[128,896]{1,0:T(8,128)} %convert_convert_fusion.refs_0_, ...), custom_call_target="tpu_custom_call" | custom-call | flops 20000000000 | bytes 20971520 | tf_op jit(solution)/shard_map/ffn_bwd_0/pallas_call | solution.py:946
  346.2 55.4 %attn_bwd_0.1 = (f32[128,896]{1,0:T(8,128)}, bf16[2,4,2048,128]{3,2,1,0:T(8,128)(2,1)}, bf16[4,448,128]{2,1,0:T(8,128)(2,1)}, bf16[4,400,128]{2,1,0:T(8,128)(2,1...) custom-call(f32[128,896]{1,0:T(8,128)} %get-tuple-element.110.refs_0_, ...), custom_call_target="tpu_custom_call" | custom-call | flops 20000000000 | bytes 20971520 | tf_op jit(solution)/shard_map/attn_bwd_0/pallas_call | solution.py:946
  401.7 1.1 select_bitcast_fusion
  402.7 1.7 collective-permute-start.1
  404.5 0.1 select_bitcast_fusion.2
  404.5 0.1 collective-permute-start
  404.6 77.1 %reduce.1 = (bf16[2,4,4,448,128]{4,3,2,1,0:T(8,128)(2,1)}, bf16[2,4,4,400,128]{4,3,2,1,0:T(8,128)(2,1)}, bf16[2,4,4,64,128]{4,3,2,1,0:T(8,128)(2,1)}, bf16[2,4,4,64,128]{4,3,2,1,0:T(8,128)(2,1)}) custom-call(bf16[4,448,128]{2,1,0:T(8,128)(2,1)} %get-tuple-element.123.refs_0_, bf16[4,400,128]{2,1,0:T(8,128)(2,1)} %get-tuple-element.124.refs_1_, ...), custom_call_target="tpu_custom_call" | custom-call | flops 10000000000 | bytes 20971520 | tf_op jit(solution)/shard_map/reduce/pallas_call | solution.py:946
  481.8 9.8 %assemble.1 = (f32[224,4864]{1,0:T(8,128)}, f32[224,4864]{1,0:T(8,128)}, f32[1216,896]{1,0:T(8,128)}, f32[224,1152]{1,0:T(8,128)}, f32[224,896]{1,0:T(8,128)}, /*index=5*/f32[32,128]{1,0:T(8,128)}) custom-call(bf16[2,4,4,448,128]{4,3,2,1,0:T(8,128)(2,1)} %get-tuple-element.128.refs_0_, bf16[2,4,4,400,128]{4,3,2,1,0:T(8,128)(2,1)} %get-tuple-element.129.refs_1_, ...), custom_call_target="tpu_custom_call" | custom-call | tf_op jit(solution)/shard_map/assemble/pallas_call | solution.py:1045
  491.6 0.8 dynamic_slice.11
  492.4 0.6 broadcast_in_dim.42
  492.9 1.4 fusion
  494.3 1.0 maximum_select_fusion.1
  495.3 1.0 maximum_select_fusion
  (13 shorter events, 0.0 us)
Async XLA Ops:
  346.2 55.5 %copy-start.1 = (f32[128,896]{1,0:T(8,128)S(1)}, f32[128,896]{1,0:T(8,128)}, u32[]{:S(2)}) copy-start(f32[128,896]{1,0:T(8,128)} %get-tuple-element.104) | copy-start | bytes 1376260
  346.2 58.2 %copy-start = (f32[128,896]{1,0:T(8,128)S(1)}, f32[128,896]{1,0:T(8,128)}, u32[]{:S(2)}) copy-start(f32[128,896]{1,0:T(8,128)} %get-tuple-element.79) | copy-start | bytes 1376260
  346.2 58.2 %copy-start.2 = (f32[128,896]{1,0:T(8,128)S(1)}, f32[128,896]{1,0:T(8,128)}, u32[]{:S(2)}) copy-start(f32[128,896]{1,0:T(8,128)} %get-tuple-element.90) | copy-start | bytes 1376260
  402.7 91.6 %collective-permute-start.1 = (f32[128,896]{1,0:T(8,128)S(1)}, f32[128,896]{1,0:T(8,128)S(1)}, u32[]{:S(2)}, u32[]{:S(2)}) collective-permute-start(f32[128,896]{1,0:T(8,128)S(1)} %get-tuple-element.141), channel_id=1, source_target_pairs={{0,64},{64,0},{1,65},{65,1},{2,66},{66,2},{3,67},{67,3},{4,68},{68... | collective-permute-start | bytes 1376264 | tf_op jit(solution)/shard_map/ppermute | solution.py:1194
  404.5 90.8 %collective-permute-start = (f32[128,896]{1,0:T(8,128)S(1)}, f32[128,896]{1,0:T(8,128)S(1)}, u32[]{:S(2)}, u32[]{:S(2)}) collective-permute-start(f32[128,896]{1,0:T(8,128)S(1)} %get-tuple-element.143), channel_id=1, source_target_pairs={{0,64},{64,0},{1,65},{65,1},{2,66},{66,2},{3,67},{67,3},{4,68},{68... | collective-permute-start | bytes 1376264 | tf_op jit(solution)/shard_map/ppermute | solution.py:1194

commit v4 on v3

v4 whole, which is shorter than its diff:
```python
import functools
import types

import jax
import jax.numpy as jnp
from jax import lax
from jax.experimental import pallas as pl
from jax.experimental.pallas import tpu as pltpu
from jax.sharding import PartitionSpec as P

D = 896
HEADS = 14
KV_HEADS = 2
HEAD_DIM = 64
GROUP = HEADS // KV_HEADS
FF = 4864
QKV = 1152
EPS = 1e-06
THETA = 1000000.0
LANES = 128
TILES = D // LANES
WIN = 1280
NEG = -1e30
F32 = jnp.float32
BF16 = jnp.bfloat16
MESH = pl.DeviceIdType.MESH
VMEM_LIMIT = 56 * 2**20
UNIT = 16
SIDE = 4
GATE_PER = (5, 4)
DOWN_PER = (8, 9)
Q_PER = (4, 4)
Q_ROWS = 16 * sum(Q_PER) * UNIT


def mm(a, b):
    return jnp.dot(a, b, preferred_element_type=F32)


def mm_nt(a, b):
    return lax.dot_general(a, b, (((1,), (1,)), ((), ())), preferred_element_type=F32)


def mm_tn(a, b):
    return lax.dot_general(a, b, (((0,), (0,)), ((), ())), preferred_element_type=F32)


ORDER = (1, 3, 2)
SMALL = 2 * D + QKV
AXES = (("x", "y"), ("y", "x"))
BATCH = 3
GROUPS = tuple(slice(a, min(a + 2 * LANES, HEADS * HEAD_DIM)) for a in range(0, HEADS * HEAD_DIM, 2 * LANES))


def push(src, dst, ssem, rsem, axis, to):
    return pltpu.make_async_remote_copy(
        src_ref=src,
        dst_ref=dst,
        send_sem=ssem,
        recv_sem=rsem,
        device_id={axis: to},
        device_id_type=MESH,
    )


def rope(u, cos, sa, sb):
    return u * cos + pltpu.roll(u, 96, 1) * sa + pltpu.roll(u, 32, 1) * sb


def unrope(u, cos, sa, sb):
    return u * cos - pltpu.roll(u, 96, 1) * sa - pltpu.roll(u, 32, 1) * sb


def halves(a0, a1):
    lane = lax.broadcasted_iota(jnp.int32, a0.shape, 1) < HEAD_DIM
    low = jnp.where(lane, a0, pltpu.roll(a1, HEAD_DIM, 1))
    high = jnp.where(lane, pltpu.roll(a0, HEAD_DIM, 1), a1)
    return low, high


def spread(ref, t, tile_t):
    half = HEAD_DIM
    zero = jnp.zeros((half, LANES), F32)
    cols = slice(t * LANES, (t + 1) * LANES)
    for g in range(KV_HEADS):
        pair = [tile_t[j * half : (j + 1) * half, :] if (2 * t + j) // GROUP == g else zero for j in range(2)]
        for part, content in enumerate(halves(*pair)):
            ref[part * LANES + g * half : part * LANES + (g + 1) * half, cols] = content.astype(BF16)


def gathered_tile(wide, t):
    half = HEAD_DIM
    rows = []
    for j in range(2):
        g = (2 * t + j) // GROUP
        low = wide[g * half : (g + 1) * half, :]
        high = wide[LANES + g * half : LANES + (g + 1) * half, :]
        rows.append(halves(low, high)[j])
    return jnp.concatenate(rows, 0)


def dealt(a_per, b_per):
    where = [(0, u // a_per, u % a_per) for u in range(16 * a_per)]
    return where + [(1, v // b_per, v % b_per) for v in range(16 * b_per)]


def unit_runs(first, count, per):
    where = dealt(*per)
    found = []
    for i in range(count):
        part, piece, slot = where[first + i]
        if found and found[-1][0] == part and found[-1][1] == piece:
            found[-1][4] += 1
        else:
            found.append([part, piece, slot, i, 1])
    return found


def put_units(refs, section, base, per, first, rows):
    for part, piece, slot, i, m in unit_runs(first, rows.shape[0] // UNIT, per):
        at = base[part] + slot * UNIT
        refs[part][section, piece // SIDE, piece % SIDE, at : at + m * UNIT, :] = rows[i * UNIT : (i + m) * UNIT, :]


class Stages:
    def __init__(self, r):
        self.s = lax.axis_index("section")
        self.c = lax.axis_index("ctx")
        self.nc = lax.axis_size("ctx")
        self.x, self.y = self.c // SIDE, lax.rem(self.c, SIDE)
        self.z = lax.axis_index("fsdp")
        self.nz = lax.axis_size("fsdp")
        self.ssem, self.rsem, self.lsem = r.ssem, r.rsem, r.lsem
        self.used = 0
        self.local_used = 0
        self.sent = []

    def along(self, axis, k):
        own, n = {
            "x": (self.x, SIDE),
            "y": (self.y, SIDE),
            "z": (self.z, self.nz),
            "c": (self.c, self.nc),
        }[axis]
        return lax.rem(own + n + k, n)

    def peer(self, axis, k, section=None):
        if axis == "s":
            return {"section": 1 - self.s}
        if axis == "z":
            to = {"fsdp": self.along("z", k)}
        elif axis == "c":
            to = {"ctx": self.along("c", k)}
        elif axis == "x":
            to = {"ctx": self.along("x", k) * SIDE + self.y}
        else:
            to = {"ctx": self.x * SIDE + self.along("y", k)}
        if section is not None:
            to["section"] = section
        return to

    def hail(self, ids, ring=False):
        bar = pltpu.get_barrier_semaphore()
        for i in ids:
            pl.semaphore_signal(bar, inc=1, device_id=i, device_id_type=MESH)
        self.expected = len(ids)
        if ring:
            def one(k, c):
                pl.semaphore_signal(bar, inc=1, device_id=self.peer("c", k), device_id_type=MESH)
                return c

            lax.fori_loop(1, self.nc, one, 0)
            self.expected += self.nc - 1
        self.bar = bar

    def met(self):
        pl.semaphore_wait(self.bar, self.expected)

    def beside(self):
        return [self.peer("s", 0)]

    def upright(self, both=False):
        ids = [self.peer("z", k) for k in range(1, self.nz)]
        return ids + ([self.peer("z", k, 1 - self.s) for k in range(1, self.nz)] if both else [])

    def flat(self, both=False):
        ids = [self.peer(a, k) for a in "xy" for k in range(1, SIDE)]
        return ids + ([self.peer(a, k, 1 - self.s) for a in "xy" for k in range(1, SIDE)] if both else [])

    def take(self, count):
        self.used += count
        return self.used - count

    def copy(self, src, dst, at, to, recv_at=None):
        return pltpu.make_async_remote_copy(
            src_ref=src,
            dst_ref=dst,
            send_sem=self.ssem.at[at],
            recv_sem=self.rsem.at[at if recv_at is None else recv_at],
            device_id=to,
            device_id_type=MESH,
        )

    def begin(self, copies):
        for c in copies:
            c.start()
        self.sent += copies
        return copies

    def drain(self):
        for c in self.sent:
            c.wait_send()

    def swap(self, src, land):
        return self.begin([self.copy(src.at[1 - self.s], land, self.take(1), self.peer("s", 0))])

    def scatter(self, axis, src, land):
        n = self.nz if axis == "z" else SIDE
        at = self.take(n - 1)
        return self.begin(
            [self.copy(src.at[self.along(axis, k)], land.at[k - 1], at + k - 1, self.peer(axis, k)) for k in range(1, n)]
        )

    def gather(self, axis, ref):
        at = self.take(SIDE - 1)
        mine = ref.at[self.along(axis, 0)]
        return self.begin([self.copy(mine, mine, at + k - 1, self.peer(axis, k)) for k in range(1, SIDE)])

    def deal(self, src, dst, rows):
        at = self.take(self.nz - 1)
        mine = dst.at[self.block(self.z, rows), :]
        return self.begin(
            [
                self.copy(src.at[self.block(self.along("z", k), rows), :], mine, at + k - 1, self.peer("z", k))
                for k in range(1, self.nz)
            ]
        )

    def block(self, i, rows):
        return pl.ds(pl.multiple_of(i * rows, UNIT), rows)

    def aside(self, j):
        x = lax.rem(self.x + (1 - self.s) * j, SIDE)
        y = lax.rem(self.y + self.s * j, SIDE)
        return {"ctx": x * SIDE + y}

    def quarter(self):
        return self.x * (1 - self.s) + self.y * self.s

    def hand_over(self, axis, src, dst, layer):
        at = self.take(2 * SIDE)
        mine = dst.at[self.s, self.along(axis, 0)]
        self.begin(
            [
                self.copy(src, mine, at + k, self.peer(axis, k, layer), at + self.s * SIDE + k)
                for k in range(1, SIDE)
            ]
        )
        beside = self.copy(src, mine, at, {"section": layer}, at + self.s * SIDE)
        within = pltpu.make_async_copy(src, mine, self.lsem.at[self.local_used])
        self.local_used += 1

        @pl.when(self.s != layer)
        def _():
            beside.start()

        @pl.when(self.s == layer)
        def _():
            within.start()

        def finish():
            @pl.when(self.s == layer)
            def _():
                within.wait()
                for half in range(2):
                    for k in range(0 if half != layer else 1, SIDE):
                        self.copy(src, mine, at, {"section": layer}, at + half * SIDE + k).wait_recv()

            @pl.when(self.s != layer)
            def _():
                beside.wait_send()

        return finish


class Feed:
    def __init__(self, st, layer, sources, piece, band):
        self.st, self.layer, self.sources, self.piece, self.band = st, layer, sources, piece, band
        steps = st.nz - 1
        self.across = st.take(2 * steps)
        self.sideways = st.take((SIDE - 1) * steps)
        self.passed = st.take(steps)
        self.own = st.take(2)

    def beside(self, h):
        b = self.band(self.st.z, h)
        return self.st.copy(b, b, self.own + h, self.st.peer("s", 0))

    def send(self, h, k, src):
        st = self.st
        dst = self.piece(st.z, h, (st.x, st.y)[h])
        return st.copy(dst if src is None else src, dst, self.across + 2 * (k - 1) + h, st.peer("z", k, h))

    def start(self):
        st = self.st

        @pl.when(st.s == self.layer)
        def _():
            for k in ORDER:
                for h in range(2):
                    for needed, src in self.sources(h, (st.x, st.y)[h], st.along("z", k)):
                        if needed is None:
                            self.send(h, k, src).start()
                        else:
                            pl.when(needed)(self.send(h, k, src).start)
            for h in range(2):
                self.beside(h).start()

    def relay(self, k):
        st = self.st
        p = self.piece(st.along("z", -k), st.s, st.quarter())
        st.copy(p, p, self.across + 2 * (k - 1) + st.s, st.peer("s", 0)).wait_recv()
        at = self.sideways + (SIDE - 1) * (k - 1) - 1
        st.begin([st.copy(p, p, at + j, st.aside(j)) for j in range(1, SIDE)])

    def collect(self, k):
        st = self.st
        z = st.along("z", -k)
        at = self.sideways + (SIDE - 1) * (k - 1) - 1
        for j in range(1, SIDE):
            p = self.piece(z, st.s, lax.rem(st.quarter() + SIDE - j, SIDE))
            st.copy(p, p, at + j, st.aside(j)).wait_recv()
        b = self.band(z, st.s)
        st.begin([st.copy(b, b, self.passed + k - 1, st.peer("s", 0))])

    def finish(self):
        st = self.st
        for k in ORDER:
            b = self.band(st.along("z", -k), 1 - st.s)
            st.copy(b, b, self.passed + k - 1, st.peer("s", 0)).wait_recv()

        @pl.when(st.s == self.layer)
        def _():
            for h in range(2):
                for k in ORDER:
                    self.send(h, k, None).wait_send()
                self.beside(h).wait_send()

        @pl.when(st.s != self.layer)
        def _():
            for h in range(2):
                self.beside(h).wait_recv()


class FeedDown:
    def __init__(self, st, layer, src, dst):
        self.st, self.layer = st, layer
        share = src.shape[1]
        spare = WIN - share
        odd = lax.rem(st.z, 2)
        place = dst.at[pl.ds(pl.multiple_of(odd * spare, UNIT), share), :]
        dst[pl.ds(pl.multiple_of((1 - odd) * share, UNIT), spare), :] = jnp.zeros((spare, D), BF16)
        self.local = pltpu.make_async_copy(src.at[0], place, st.lsem.at[st.local_used])
        st.local_used += 1
        self.remote = st.copy(src.at[0], place, st.take(1), st.peer("s", 0))

    def start(self):
        @pl.when(self.st.s == self.layer)
        def _():
            self.local.start()
            self.remote.start()

    def finish(self):
        @pl.when(self.st.s == self.layer)
        def _():
            self.local.wait()
            self.remote.wait_send()

        @pl.when(self.st.s != self.layer)
        def _():
            self.remote.wait_recv()


class Local:
    def __init__(self, st, layer, pairs):
        self.st, self.layer = st, layer
        self.copies = [pltpu.make_async_copy(a, b, st.lsem.at[st.local_used + i]) for i, (a, b) in enumerate(pairs)]
        st.local_used += len(pairs)

        @pl.when(st.s == layer)
        def _():
            for c in self.copies:
                c.start()

    def wait(self):
        @pl.when(self.st.s == self.layer)
        def _():
            for c in self.copies:
                c.wait()


def half_rows(z, h, share):
    return pl.ds(pl.multiple_of(z * share + h * (share // 2), UNIT), share // 2)


def feed_attention(st, layer, qkv, out, dst):
    share = qkv.shape[1]
    rows = st.block(st.z, share)
    local = Local(st, layer, [(qkv.at[0], dst.at[rows, :QKV]), (out.at[0], dst.at[rows, QKV:])])
    width = (QKV + D) // SIDE

    def piece(z, h, q):
        return dst.at[half_rows(z, h, share), pl.ds(pl.multiple_of(q * width, LANES), width)]

    def band(z, h):
        return dst.at[half_rows(z, h, share), :]

    return local, Feed(st, layer, lambda h, q, z_to: [(None, None)], piece, band)


def feed_windows(st, layer, gate, up, dst):
    share = gate.shape[1]
    pace = FF // st.nz // (LANES // 2)
    width = WIN // 2

    def window(z):
        return pl.multiple_of(z * pace // 2 * LANES, LANES)

    rows = st.block(st.z, share)
    local = Local(st, layer, [(w.at[0, :, pl.ds(window(st.z), WIN)], dst.at[i, rows, :]) for i, w in enumerate((gate, up))])

    def sources(h, q, z_to):
        at = pl.multiple_of(window(z_to) + lax.rem(q, 2) * width, LANES)
        part = slice(h * (share // 2), (h + 1) * (share // 2))
        return [(q < 2, gate.at[0, part, pl.ds(at, width)]), (q >= 2, up.at[0, part, pl.ds(at, width)])]

    def piece(z, h, q):
        return dst.at[q // 2, half_rows(z, h, share), pl.ds(pl.multiple_of(lax.rem(q, 2) * width, LANES), width)]

    def band(z, h):
        return dst.at[:, half_rows(z, h, share), :]

    return local, Feed(st, layer, sources, piece, band)


def arrived(copies):
    for c in copies:
        c.wait_recv()


def add_into(dst, parts):
    def one(i, c):
        total = parts[0][i].astype(F32)
        for p in parts[1:]:
            total = total + p[i].astype(F32)
        dst[i] = total.astype(dst.dtype)
        return c

    lax.fori_loop(0, dst.shape[0], one, 0)


def add_rows(dst, parts):
    total = parts[0][...].astype(F32)
    for p in parts[1:]:
        total = total + p[...].astype(F32)
    dst[...] = total.astype(dst.dtype)


def swapped_sum(st, copies, given, land):
    arrived(copies)
    for i in range(SIDE):
        add_into(land.at[i], [given.at[st.s, i], land.at[i]])


def sides(tile, chosen):
    half = HEAD_DIM
    low, high = tile[:half], tile[half:]
    zero = jnp.zeros_like(low)
    below = jnp.concatenate([jnp.where(chosen, low, zero), jnp.where(chosen, zero, high)], 1)
    return jnp.concatenate([jnp.concatenate([zero, low], 1), below], 0).astype(BF16)


def sides_t(tile_t, chosen):
    lane = lax.broadcasted_iota(jnp.int32, tile_t.shape, 1) < HEAD_DIM
    upper = jnp.where(jnp.logical_or(lane, jnp.logical_not(chosen)), 0.0, pltpu.roll(tile_t, HEAD_DIM, 1))
    lower = jnp.where(jnp.logical_or(lane, jnp.logical_not(chosen)), tile_t, 0.0)
    return jnp.concatenate([upper, lower], 0).astype(BF16)


def own_sides(tile):
    low, high = tile[:HEAD_DIM], tile[HEAD_DIM:]
    zero = jnp.zeros_like(low)
    rows = [[zero, low], [low, zero], [zero, high]]
    return jnp.concatenate([jnp.concatenate(p, 1) for p in rows], 0).astype(BF16)


def own_bias(width):
    key = lax.broadcasted_iota(jnp.int32, (HEAD_DIM, width), 0)
    query = lax.rem(lax.broadcasted_iota(jnp.int32, (HEAD_DIM, width), 1), HEAD_DIM)
    return jnp.where(key <= query, 0.0, NEG)


def earlier(pairs_ref, src, me, width):
    return pairs_ref[src, 0:1, :width] < pairs_ref[me, 0:1, :width]


def col_max(a):
    return jnp.max(a, 0, keepdims=True)


def col_sum(a):
    return jnp.sum(a, 0, keepdims=True)


def attn_fwd_kernel(layer, r):
    st = Stages(r)
    n, me = st.nc, st.c
    st.hail(st.beside() + st.upright(True), ring=True)
    first = layer == 0
    r.load()
    if first:
        wa_local, wa = feed_attention(st, layer, r.wqkv_shard, r.wout_shard, r.wa)
    gu_local, gu = feed_windows(st, layer, r.gate_shard, r.up_shard, r.gu)
    down = FeedDown(st, layer, r.down_shard, r.down)
    r.need("x")
    x = r.x[...]
    r1 = lax.rsqrt(jnp.mean(x * x, -1, keepdims=True) + EPS)
    unit = x * r1
    if first:
        r.need("pair", "small_own", "inverse")
        r.pairs[me] = jnp.broadcast_to(r.pair[...], r.pairs.shape[1:])
        r.parts[st.s, st.z] = r.small_own[...]
        wa_local.wait()
    gu_local.wait()
    st.met()
    if first:
        wa.start()
        at = st.take(2 * st.nz)
        mine = r.parts.at[st.s, st.z]
        st.begin(
            [st.copy(mine, mine, at + k, st.peer("z", k, st.s), at + st.s * st.nz + k) for k in range(1, st.nz)]
            + [st.copy(mine, mine, at + st.nz + k, st.peer("z", k, 1 - st.s), at + st.s * st.nz + k) for k in range(1, st.nz)]
            + [st.copy(mine, mine, at, st.peer("s", 0), at + st.s * st.nz)]
        )

        def tell(k, c):
            p = r.pairs.at[me]
            push(p, p, r.psem.at[k], r.psem2.at[k], "ctx", lax.rem(me + k, n)).start()
            return c

        lax.fori_loop(1, n, tell, 0)
        block = LANES // 2
        i = lax.broadcasted_iota(jnp.int32, (LANES, LANES), 0)
        pair = r.pairs[me, 0:1, :LANES]
        pos = jnp.where(i < block, pair * block + i, (2 * n - 1 - pair) * block + i - block)
        angle = pos.astype(F32) * r.inverse[...]
        lane = lax.rem(lax.broadcasted_iota(jnp.int32, (LANES, LANES), 1), HEAD_DIM)
        sine = jnp.sin(angle)
        r.cos[...] = jnp.cos(angle)
        r.sa[...] = jnp.where(lane < HEAD_DIM // 2, -sine, 0.0)
        r.sb[...] = jnp.where(lane < HEAD_DIM // 2, 0.0, sine)
        r.flush("cos", "sa", "sb")
        for h in (st.s, 1 - st.s):
            for k in range(st.nz):
                if h is st.s and k == 0:
                    continue
                st.copy(mine, mine, at, st.peer("s", 0), at + h * st.nz + k).wait_recv()
        for h in range(2):
            total = r.parts[h, 0]
            for k in range(1, st.nz):
                total = total + r.parts[h, k]
            r.small[h] = total
        r.flush("small")
        for k in ORDER:
            wa.relay(k)
    gu.start()
    down.start()
    if first:
        for k in ORDER:
            wa.collect(k)
    else:
        r.need("small", "pairs", "cos", "sa", "sb")
    small = r.small[layer]
    n1_f = unit * small[:, :D]
    n1 = n1_f.astype(BF16)
    bias = small[:, 2 * D :]
    if first:
        wa.finish()
        r.flush("wa")
    else:
        r.need("wa")
    cos, sa, sb = r.cos[...], r.sa[...], r.sb[...]
    lin = mm(n1, r.wa[:, D:QKV]) + bias[:, D:]
    r.kv[me] = jnp.concatenate([rope(lin[:, :LANES], cos, sa, sb), lin[:, LANES:]], 1).astype(BF16)

    def keys_copy(k, src):
        return push(r.kv.at[src], r.kv.at[src], r.csem.at[k], r.csem2.at[k], "ctx", lax.rem(me + k, n))

    def start(k, c):
        keys_copy(k, me).start()
        return c

    lax.fori_loop(1, n, start, 0)
    linq = mm(n1, r.wa[:, :D]) + bias[:, :D]
    for t in range(TILES):
        tile = slice(t * LANES, (t + 1) * LANES)
        q = rope(linq[:, tile], cos, sa, sb) * HEAD_DIM ** (-0.5)
        spread(r.qst, t, q.T)
        r.n1t[tile, :] = n1_f[:, tile].T.astype(BF16)
    r.flush("qst", "n1t")
    for k in ORDER[:2]:
        gu.relay(k)
    half = HEAD_DIM
    own_k = own_sides(r.kv[me, :, :LANES].astype(F32))
    own_vt = own_sides(r.kv[me, :, LANES:].astype(F32)).astype(F32).T.astype(BF16)
    for cols in GROUPS:
        width = cols.stop - cols.start
        bias = own_bias(width)
        sc = mm(own_k, r.qst[:, cols])
        s_a, s_l, s_h = sc[:half], sc[half : 2 * half] + bias, sc[2 * half :] + bias
        m_lo = col_max(s_l)
        m_hi = jnp.maximum(col_max(s_a), col_max(s_h))
        p_a, p_l, p_h = jnp.exp(s_a - m_hi), jnp.exp(s_l - m_lo), jnp.exp(s_h - m_hi)
        r.m_s[0:1, cols], r.m_s[1:2, cols] = m_lo, m_hi
        r.l_s[0:1, cols], r.l_s[1:2, cols] = col_sum(p_l), col_sum(p_a) + col_sum(p_h)
        r.acc_s[:, cols] = mm(own_vt, jnp.concatenate([p_a, p_l, p_h], 0).astype(BF16))

    def step(i, c):
        kx, vt, sel = [], [], []
        for j in range(BATCH):
            k = i * BATCH + 1 + j
            src = lax.rem(me + n - k, n)
            keys_copy(k, src).wait_recv()
            if first:
                p = r.pairs.at[src]
                push(p, p, r.psem.at[k], r.psem2.at[k], "ctx", lax.rem(me + k, n)).wait_recv()
            sel.append(src)
            chosen = earlier(r.pairs, src, me, LANES)
            kx.append(sides(r.kv[src, :, :LANES].astype(F32), chosen))
            vt.append(sides_t(r.kv[src, :, LANES:].astype(F32).T, chosen))
        kx = jnp.concatenate(kx, 0)
        vt = jnp.concatenate(vt, 1)
        for cols in GROUPS:
            width = cols.stop - cols.start
            sc = mm(kx, r.qst[:, cols])
            m_lo, m_hi = r.m_s[0:1, cols], r.m_s[1:2, cols]
            n_lo, n_hi = m_lo, m_hi
            chosen = [earlier(r.pairs, src, me, width) for src in sel]
            for j in range(BATCH):
                top = col_max(sc[(2 * j + 1) * half : (2 * j + 2) * half])
                n_hi = jnp.maximum(n_hi, col_max(sc[2 * j * half : (2 * j + 1) * half]))
                n_hi = jnp.where(chosen[j], n_hi, jnp.maximum(n_hi, top))
                n_lo = jnp.where(chosen[j], jnp.maximum(n_lo, top), n_lo)
            a_lo, a_hi = jnp.exp(m_lo - n_lo), jnp.exp(m_hi - n_hi)
            l_lo, l_hi = r.l_s[0:1, cols] * a_lo, r.l_s[1:2, cols] * a_hi
            ps = []
            for j in range(BATCH):
                p_a = jnp.exp(sc[2 * j * half : (2 * j + 1) * half] - n_hi)
                p_s = jnp.exp(sc[(2 * j + 1) * half : (2 * j + 2) * half] - jnp.where(chosen[j], n_lo, n_hi))
                total = col_sum(p_s)
                l_hi = l_hi + col_sum(p_a) + jnp.where(chosen[j], 0.0, total)
                l_lo = l_lo + jnp.where(chosen[j], total, 0.0)
                ps += [p_a.astype(BF16), p_s.astype(BF16)]
            r.m_s[0:1, cols], r.m_s[1:2, cols] = n_lo, n_hi
            r.l_s[0:1, cols], r.l_s[1:2, cols] = l_lo, l_hi
            new = mm(vt, jnp.concatenate(ps, 0))
            r.acc_s[:LANES, cols] = r.acc_s[:LANES, cols] * a_lo + new[:LANES]
            r.acc_s[LANES:, cols] = r.acc_s[LANES:, cols] * a_hi + new[LANES:]
        return c

    lax.fori_loop(0, 1, step, 0)
    gu.relay(2)
    lax.fori_loop(1, 3, step, 0)
    for k in ORDER[:2]:
        gu.collect(k)
    lax.fori_loop(3, (n - 1) // BATCH, step, 0)
    gu.collect(2)
    r.flush("kv")
    if first:
        r.flush("pairs")
    r.lse[...] = r.m_s[...] + jnp.log(r.l_s[...])
    for t in range(TILES):
        cols = slice(t * LANES, (t + 1) * LANES)
        wide = jnp.concatenate([r.acc_s[:LANES, cols] / r.l_s[0:1, cols], r.acc_s[LANES:, cols] / r.l_s[1:2, cols]], 0)
        tile_t = gathered_tile(wide, t)
        r.attt[cols, :] = tile_t.astype(BF16)
        r.att_s[:, cols] = tile_t.T.astype(BF16)
    r.flush("lse", "attt")
    mid = x + mm(r.att_s[...], r.wa[:, QKV:])
    r.mid[...] = mid
    r2 = lax.rsqrt(jnp.mean(mid * mid, -1, keepdims=True) + EPS)
    r.n2[...] = (mid * r2 * small[:, D : 2 * D]).astype(BF16)
    r.flush("mid", "n2")
    gu.finish()
    down.finish()
    r.flush("gu", "down")
    st.drain()

    def done(k, c):
        keys_copy(k, me).wait_send()
        if first:
            p = r.pairs.at[me]
            push(p, p, r.psem.at[k], r.psem2.at[k], "ctx", lax.rem(me + k, n)).wait_send()
        return c

    lax.fori_loop(1, n, done, 0)
    r.close()


class Attention:
    def __init__(self, st):
        self.st = st

    def columns(self, src, dst):
        st = self.st
        share = dst.shape[0]
        at = st.take(st.nz - 1)
        mine = dst.at[:, pl.ds(pl.multiple_of(st.z * LANES, LANES), LANES)]
        moving = st.begin(
            [
                st.copy(src.at[st.block(st.along("z", k), share), :], mine, at + k - 1, st.peer("z", k))
                for k in range(1, st.nz)
            ]
        )
        mine[...] = src[st.block(st.z, share), :]
        return moving

    def whole(self, dst):
        st = self.st
        rows = dst.shape[0] // st.nz
        at = st.take(st.nz - 1)
        mine = dst.at[pl.ds(pl.multiple_of(st.z * rows, UNIT), rows), :]
        return st.begin([st.copy(mine, mine, at + k - 1, st.peer("z", k)) for k in range(1, st.nz)])

    def begin(self, glin, small, all_glin, all_small):
        st = self.st
        tok = glin.shape[0]
        all_glin[st.block(st.z, tok), :] = glin[...]
        all_small[st.block(st.z, 2 * UNIT), :] = small[...]
        return self.whole(all_glin) + self.whole(all_small)

    def swap(self, moving, n1z, all_glin, all_small, dout, made, land):
        st = self.st
        arrived(moving)
        share = n1z.shape[0]
        per = 8
        for j in range(0, QKV // LANES, 2):
            cols = slice(j * LANES, min(j + 2, QKV // LANES) * LANES)
            d = mm(n1z[...], all_glin[:, cols]).astype(BF16)
            for t in range(j, min(j + 2, QKV // LANES)):
                made[t // per, (t % per) * share : (t % per + 1) * share, :] = d[:, (t - j) * LANES : (t - j + 1) * LANES]
        made[1, share : 8 * share, :] = dout[...]
        small = jnp.zeros((2 * UNIT, LANES), F32)
        for i in range(st.nz):
            small = small + all_small[i * 2 * UNIT : (i + 1) * 2 * UNIT, :]
        made[0, 8 * share : 8 * share + 2 * UNIT, :] = small.astype(BF16)
        made[0, 8 * share + 2 * UNIT :, :] = jnp.zeros((Q_ROWS - 8 * share - 2 * UNIT, LANES), BF16)
        made[1, 8 * share :, :] = jnp.zeros((Q_ROWS - 8 * share, LANES), BF16)
        return st.swap(made, land)

    def fold(self, moving, made, land, out):
        st = self.st
        arrived(moving)
        rows = Q_ROWS // 2 // 16
        for h in range(2):
            for i in range(16):
                at = slice((h * 16 + i) * rows, (h * 16 + i + 1) * rows)
                total = made[st.s, at, :].astype(F32) + land[at, :].astype(F32)
                out[h][i // SIDE, i % SIDE] = total.astype(BF16)


def attn_bwd_kernel(layer, r):
    st = Stages(r)
    n, me = st.nc, st.c
    last = layer == 0
    st.hail(st.upright() + (st.beside() if last else []), ring=True)
    r.load()
    half = HEAD_DIM
    r.need("gm")
    gm = r.gm[...]
    gmb = gm.astype(BF16)
    tok = gm.shape[0]
    r.all_gm[st.block(st.z, tok), :] = gmb
    sl, l1, t1 = (r.sla, r.slb), (r.l1a, r.l1b), (r.t1a, r.t1b)
    r.need("sla", "slb", "attt", "n1t")
    st.met()
    r1 = [st.scatter(AXES[h][0], sl[h], l1[h]) for h in range(2)]
    attention = Attention(st)
    out_factors = attention.whole(r.all_gm) + attention.columns(r.attt, r.attz)
    qkv_factor = attention.columns(r.n1t, r.n1z)
    if last:
        r.need("glin1", "gsmall1", "n1z1", "dout1")
        before = attention.begin(r.glin1, r.gsmall1, r.all_glin, r.all_small)
    r.need("wa", "qst", "lse", "kv", "pairs")
    ga = mm_nt(gmb, r.wa[:, QKV:])
    for t in range(TILES):
        tile = slice(t * LANES, (t + 1) * LANES)
        ga_t = ga[:, tile].T
        spread(r.gst_s, t, ga_t)
        prod = ga_t * r.attt[tile, :].astype(F32)
        low, high = halves(col_sum(prod[:half]), col_sum(prod[half:]))
        r.delta_s[0:1, tile], r.delta_s[1:2, tile] = low, high

    def own_block():
        keys, vals = r.kv[me, :, :LANES].astype(F32), r.kv[me, :, LANES:].astype(F32)
        kx, vx = own_sides(keys), own_sides(vals)
        kt = kx.astype(F32).T.astype(BF16)
        rows = slice(0, 3 * half)
        for cols in GROUPS:
            bias = own_bias(cols.stop - cols.start)
            sc = mm(kx, r.qst[:, cols])
            dp = mm(vx, r.gst_s[:, cols])
            lo, hi = (r.lse[0:1, cols], r.delta_s[0:1, cols]), (r.lse[1:2, cols], r.delta_s[1:2, cols])
            parts = [(sc[:half], hi), (sc[half : 2 * half] + bias, lo), (sc[2 * half :] + bias, hi)]
            for i, (part, (lse, delta)) in enumerate(parts):
                p = jnp.exp(part - lse)
                at = slice(i * half, (i + 1) * half)
                r.p_s[at, cols] = p.astype(BF16)
                r.ds_s[at, cols] = (p * (dp[at] - delta)).astype(BF16)
            r.gq_s[:, cols] = mm(kt, r.ds_s[rows, cols])
        made = []
        for w, q in ((r.ds_s, r.qst), (r.p_s, r.gst_s)):
            e = mm_nt(w[rows, :], q[...])
            low = e[:half, LANES:] + e[half : 2 * half, :LANES]
            made.append(jnp.concatenate([low, e[2 * half :, LANES:]], 0))
        return jnp.concatenate(made, 1)

    def sum_copy(k):
        return push(r.send_s.at[k], r.land_s.at[k], r.csem.at[k], r.csem2.at[k], "ctx", lax.rem(me + k, n))

    def step(i, c):
        kx, vx, kt, sel = [], [], [], []
        for j in range(BATCH):
            src = lax.rem(me + i * BATCH + 1 + j, n)
            sel.append(src)
            chosen = earlier(r.pairs, src, me, LANES)
            keys = r.kv[src, :, :LANES].astype(F32)
            kx.append(sides(keys, chosen))
            vx.append(sides(r.kv[src, :, LANES:].astype(F32), chosen))
            kt.append(sides_t(keys.T, chosen))
        kx, vx, kt = jnp.concatenate(kx, 0), jnp.concatenate(vx, 0), jnp.concatenate(kt, 1)
        rows = slice(0, 2 * BATCH * half)
        for cols in GROUPS:
            width = cols.stop - cols.start
            sc = mm(kx, r.qst[:, cols])
            dp = mm(vx, r.gst_s[:, cols])
            for j in range(BATCH):
                chosen = earlier(r.pairs, sel[j], me, width)
                for part in range(2):
                    lse, delta = r.lse[1:2, cols], r.delta_s[1:2, cols]
                    if part:
                        lse = jnp.where(chosen, r.lse[0:1, cols], lse)
                        delta = jnp.where(chosen, r.delta_s[0:1, cols], delta)
                    at = slice((2 * j + part) * half, (2 * j + part + 1) * half)
                    p = jnp.exp(sc[at] - lse)
                    r.p_s[at, cols] = p.astype(BF16)
                    r.ds_s[at, cols] = (p * (dp[at] - delta)).astype(BF16)
            r.gq_s[:, cols] += mm(kt, r.ds_s[rows, cols])
        ek = mm_nt(r.ds_s[rows, :], r.qst[...])
        ev = mm_nt(r.p_s[rows, :], r.gst_s[...])
        for j in range(BATCH):
            chosen = earlier(r.pairs, sel[j], me, LANES)
            k = i * BATCH + 1 + j
            for e, lanes in ((ek, slice(0, LANES)), (ev, slice(LANES, 2 * LANES))):
                top = e[2 * j * half : (2 * j + 1) * half]
                low = e[(2 * j + 1) * half : (2 * j + 2) * half]
                r.send_s[k, :half, lanes] = (top[:, LANES:] + jnp.where(chosen, low[:, :LANES], 0.0)).astype(BF16)
                r.send_s[k, half:, lanes] = jnp.where(chosen, 0.0, low[:, LANES:]).astype(BF16)
            sum_copy(k).start()
        return c

    own = own_block()
    lax.fori_loop(0, 3, step, 0)
    arrived(out_factors)
    share = D // st.nz
    for j in range(0, TILES, 2):
        cols = slice(j * LANES, min(j + 2, TILES) * LANES)
        d = mm(r.attz[...], r.all_gm[:, cols]).astype(BF16)
        for t in range(j, min(j + 2, TILES)):
            r.dout[t * share : (t + 1) * share, :] = d[:, (t - j) * LANES : (t - j + 1) * LANES]
    r.flush("dout")
    if last:
        qswap = attention.swap(before, r.n1z1, r.all_glin, r.all_small, r.dout1, r.qv, r.ql)
    lax.fori_loop(3, (n - 1) // BATCH, step, 0)
    if last:
        attention.fold(qswap, r.qv, r.ql, (r.qpa, r.qpb))
        r.flush("qpa", "qpb")
    arrived(qkv_factor)
    r.flush("n1z")

    def take(k, total):
        sum_copy(k).wait_recv()
        return total + r.land_s[k].astype(F32)

    own = lax.fori_loop(1, n, take, own)
    r.need("cos", "sa", "sb", "x", "small", "dg2")
    cos, sa, sb = r.cos[...], r.sa[...], r.sb[...]
    for t in range(TILES):
        gq = gathered_tile(r.gq_s[:, t * LANES : (t + 1) * LANES], t).T * HEAD_DIM ** (-0.5)
        r.glin[:, t * LANES : (t + 1) * LANES] = unrope(gq, cos, sa, sb).astype(BF16)
    r.glin[:, D : D + LANES] = unrope(own[:, :LANES], cos, sa, sb).astype(BF16)
    r.glin[:, D + LANES :] = own[:, LANES:].astype(BF16)
    r.flush("glin")
    gn1 = mm_nt(r.glin[...], r.wa[:, :QKV])
    x = r.x[...]
    r1_ = lax.rsqrt(jnp.mean(x * x, -1, keepdims=True) + EPS)
    unit = x * r1_
    dz = gn1 * r.small[layer][:, :D]
    r.gx[...] = gm + r1_ * (dz - unit * jnp.mean(dz * unit, -1, keepdims=True))
    r.flush("gx")
    dg1 = col_sum(gn1 * unit)
    dbias = col_sum(r.glin[...].astype(F32))
    r.gsmall[...] = jnp.zeros(r.gsmall.shape, F32)
    row = 0
    for part in (dg1, r.dg2[...], dbias):
        for t in range(part.shape[1] // LANES):
            r.gsmall[row : row + 1, :] = part[:, t * LANES : (t + 1) * LANES]
            row += 1
    r.flush("gsmall")
    for h in range(2):
        arrived(r1[h])
        mine = sl[h].at[st.along(AXES[h][0], 0)]
        add_into(t1[h], [mine] + [l1[h].at[k] for k in range(SIDE - 1)])
    r.flush("t1a", "t1b")
    st.drain()

    def done(k, c):
        sum_copy(k).wait_send()
        return c

    lax.fori_loop(1, n, done, 0)
    r.close()


def ffn_fwd_kernel(layer, r):
    st = Stages(r)
    n, me = st.nz, st.z
    carry = layer == 0
    st.hail(st.upright(carry) + (st.beside() + st.flat() if carry else []))
    r.load()
    if carry:
        wa_local, wa = feed_attention(st, 1, r.wqkv_shard, r.wout_shard, r.wa)
    r.need("n2")
    r.all[me] = r.n2[...]
    st.met()
    at = st.take(2 * n)

    def first(k):
        return st.copy(r.all.at[me], r.all.at[me], at + k, st.peer("z", k))

    def second(k):
        return st.copy(r.send_s.at[k], r.land_s.at[k], at + n + k, st.peer("z", -k))

    for k in ORDER:
        first(k).start()
    if carry:
        wa_local.wait()
        wa.start()
    r.need("gu", "down", "mid")

    def block(src):
        a = r.all[src]
        gate = mm(a, r.gu[0])
        up = mm(a, r.gu[1])
        r.gate[src] = gate
        r.up[src] = up
        hidden = (gate * jax.nn.sigmoid(gate) * up).astype(BF16)
        return mm(hidden, r.down[...])

    r.y[...] = r.mid[...] + block(me)
    for k in ORDER:
        first(k).wait_recv()
        r.send_s[k] = block(st.along("z", -k)).astype(BF16)
        second(k).start()
        if carry and k == 3:
            wa.relay(1)
            wa.relay(3)
    r.flush("all", "gate", "up")
    if carry:
        wa.relay(2)
        for k in ORDER:
            wa.collect(k)
    for k in ORDER:
        second(k).wait_recv()
        r.y[...] += r.land_s[k].astype(F32)
    r.flush("y")
    for k in ORDER:
        first(k).wait_send()
        second(k).wait_send()
    if carry:
        wa.finish()
        r.flush("wa")
    st.drain()
    r.close()


def ffn_bwd_kernel(layer, r):
    st = Stages(r)
    n, me = st.nz, st.z
    carry = layer == 0
    st.hail(st.upright() + st.beside() + (st.flat(True) if carry else []))
    r.load()
    tok = r.gy.shape[0]

    def rows_of(i):
        return pl.ds(pl.multiple_of(i * tok, tok), tok)

    r.need("gy")
    r.all_s[rows_of(me), :] = r.gy[...].astype(BF16)
    st.met()
    at = st.take(2 * n)

    def first(k):
        mine = r.all_s.at[rows_of(me), :]
        return st.copy(mine, mine, at + k, st.peer("z", k))

    def second(k):
        return st.copy(r.send_s.at[k], r.land_s.at[k], at + n + k, st.peer("z", -k))

    for k in ORDER:
        first(k).start()
    if carry:
        r.need("t1a", "t1b")
        rest = Rest(st, (r.t1a, r.t1b), (r.l2a, r.l2b), (r.t2a, r.t2b), (r.g1a, r.g1b), (r.ga, r.gb), 1)
    r.need("down", "gate", "up", "gu")

    def block(src):
        rows = rows_of(src)
        gh = mm_nt(r.all_s[rows, :], r.down[...])
        gate, up = r.gate[src], r.up[src]
        sg = jax.nn.sigmoid(gate)
        act = gate * sg
        r.hid_s[rows, :] = (act * up).astype(BF16)
        ggate = (gh * up * sg * (1.0 + gate * (1.0 - sg))).astype(BF16)
        gup = (gh * act).astype(BF16)
        r.g_s[0, rows, :] = ggate
        r.g_s[1, rows, :] = gup
        return mm_nt(ggate, r.gu[0]) + mm_nt(gup, r.gu[1])

    r.own_s[...] = block(me)
    for k in ORDER:
        if carry:
            rest.advance()
        first(k).wait_recv()
        r.send_s[k] = block(st.along("z", -k)).astype(BF16)
        second(k).start()

    refs = (r.fa, r.fb)
    share = D // n
    for j in range(WIN // (2 * LANES)):
        cols = slice(2 * j * LANES, 2 * (j + 1) * LANES)
        r.down_s[cols, :] = mm_tn(r.hid_s[:, cols], r.all_s[...]).astype(BF16)
    pad = (WIN - FF // n) * lax.rem(me, 2)
    half = FF // n // 2
    base = [n * per * UNIT for per in GATE_PER]
    for section in range(2):
        rows = r.down_s[pl.ds(pl.multiple_of(pad + section * half, UNIT), half), :]
        for t in range(TILES):
            put_units(refs, section, base, DOWN_PER, t * (half // UNIT), rows[:, t * LANES : (t + 1) * LANES])
        used = TILES * (half // UNIT)
        extra = 16 * sum(DOWN_PER) - used
        put_units(refs, section, base, DOWN_PER, used, jnp.zeros((extra * UNIT, LANES), BF16))
    r.need("n2_all")
    normed = jnp.concatenate([r.n2_all[i] for i in range(n)], 0)

    def product(section):
        for j in range(WIN // (2 * LANES)):
            d = mm_tn(normed, r.g_s[section, :, 2 * j * LANES : 2 * (j + 1) * LANES]).astype(BF16)
            for t in (2 * j, 2 * j + 1):
                tile = d[:, (t % 2) * LANES : (t % 2 + 1) * LANES]
                for i in range(n):
                    base = [i * per * UNIT for per in GATE_PER]
                    put_units(refs, section, base, GATE_PER, t * (share // UNIT), tile[i * share : (i + 1) * share, :])
        used = WIN // LANES * (share // UNIT)
        extra = 16 * sum(GATE_PER) - used
        for i in range(n):
            base = [i * per * UNIT for per in GATE_PER]
            put_units(refs, section, base, GATE_PER, used, jnp.zeros((extra * UNIT, LANES), BF16))

    product(1 - st.s)
    swaps = [st.swap(refs[h], (r.sla, r.slb)[h]) for h in range(2)]
    product(st.s)
    for k in ORDER:
        second(k).wait_recv()
        r.own_s[...] += r.land_s[k].astype(F32)
    gn2 = r.own_s[...]
    r.need("mid", "small")
    mid = r.mid[...]
    r2 = lax.rsqrt(jnp.mean(mid * mid, -1, keepdims=True) + EPS)
    unit = mid * r2
    r.dg2[...] = col_sum(gn2 * unit)
    dz = gn2 * r.small[layer][:, D : 2 * D]
    r.gm[...] = r.gy[...] + r2 * (dz - unit * jnp.mean(dz * unit, -1, keepdims=True))
    r.flush("dg2", "gm")
    for h in range(2):
        swapped_sum(st, swaps[h], refs[h], (r.sla, r.slb)[h])
    r.flush("sla", "slb")
    for k in ORDER:
        first(k).wait_send()
        second(k).wait_send()
    if carry:
        rest.finish()
    st.drain()
    r.close()


class Rest:
    def __init__(self, st, t1, l2, t2, g1, out, layer):
        self.st, self.t1, self.l2, self.t2, self.g1, self.out, self.layer = st, t1, l2, t2, g1, out, layer
        self.stage = 0
        self.moving = [st.scatter(AXES[h][1], t1[h], l2[h]) for h in range(2)]

    def advance(self):
        st = self.st
        for h in range(2):
            second = AXES[h][1]
            arrived(self.moving[h])
            mine = self.g1[h].at[st.along(second, 0)]
            if self.stage == 0:
                t2 = self.t2[h]
                add_rows(t2, [self.t1[h].at[st.along(second, 0)]] + [self.l2[h].at[k] for k in range(SIDE - 1)])
                per = GATE_PER[h] * UNIT
                self.moving[h] = st.deal(t2, mine, per)
                mine[st.block(st.z, per), :] = t2[st.block(st.z, per), :]
                mine[st.nz * per :, :] = t2[st.nz * per :, :]
            elif self.stage == 1:
                self.moving[h] = st.gather(second, self.g1[h])
            else:
                self.moving[h] = st.hand_over(AXES[h][0], self.g1[h], self.out[h], self.layer)
        self.stage += 1

    def finish(self):
        for h in range(2):
            self.moving[h]()


def reduce_kernel(layer, r):
    st = Stages(r)
    st.hail(st.beside() + st.upright() + st.flat(True))
    r.load()
    r.need("t1a", "t1b", "q1a", "q1b", "glin", "gsmall")
    qp = {1: (r.q1a, r.q1b), 0: (r.qpa, r.qpb)}
    land = {1: (r.m1a, r.m1b), 0: (r.m0a, r.m0b)}
    land2 = {1: (r.w1a, r.w1b), 0: (r.w0a, r.w0b)}
    part = {1: (r.e1a, r.e1b), 0: (r.e0a, r.e0b)}
    wide = {1: (r.h1a, r.h1b), 0: (r.h0a, r.h0b)}
    out = (r.qa, r.qb)
    moving = {}

    def along_first(l):
        moving[l] = [st.scatter(AXES[h][0], qp[l][h], land[l][h]) for h in range(2)]

    def along_second(l):
        for h in range(2):
            arrived(moving[l][h])
            own = qp[l][h].at[st.along(AXES[h][0], 0)]
            add_into(part[l][h], [own] + [land[l][h].at[k] for k in range(SIDE - 1)])
            moving[l][h] = st.scatter(AXES[h][1], part[l][h], land2[l][h])

    def back_second(l):
        for h in range(2):
            arrived(moving[l][h])
            i = st.along(AXES[h][1], 0)
            add_rows(wide[l][h].at[i], [part[l][h].at[i]] + [land2[l][h].at[k] for k in range(SIDE - 1)])
            moving[l][h] = st.gather(AXES[h][1], wide[l][h])

    def back_first(l):
        for h in range(2):
            arrived(moving[l][h])
            moving[l][h] = st.hand_over(AXES[h][0], wide[l][h], out[h], l)

    st.met()
    attention = Attention(st)
    factors = attention.begin(r.glin, r.gsmall, r.all_glin, r.all_small)
    rest = Rest(st, (r.t1a, r.t1b), (r.l2a, r.l2b), (r.t2a, r.t2b), (r.g1a, r.g1b), (r.ga, r.gb), 0)
    along_first(1)
    rest.advance()
    along_second(1)
    rest.advance()
    back_second(1)
    rest.advance()
    r.need("n1z", "dout")
    qswap = attention.swap(factors, r.n1z, r.all_glin, r.all_small, r.dout, r.qv, r.ql)
    attention.fold(qswap, r.qv, r.ql, qp[0])
    along_first(0)
    back_first(1)
    along_second(0)
    back_second(0)
    back_first(0)
    rest.finish()
    for l in (1, 0):
        for h in range(2):
            moving[l][h]()
    st.drain()
    r.close()


class Refs(types.SimpleNamespace):
    def load(self):
        for c in self.coming.values():
            c.start()

    def need(self, *names):
        for k in names:
            if k not in self.here:
                self.coming[k].wait()
                self.here.add(k)

    def flush(self, *names):
        for k in names:
            self.going[k].start()
            self.gone.add(k)

    def close(self):
        self.need(*self.coming)
        self.flush(*[k for k in self.going if k not in self.gone])
        for c in self.going.values():
            c.wait()


def call(kernel, layer, cid, name, ins, outs, scratch, sems, hbm=(), flops=10**10):
    staged = [k for k in ins if k not in hbm]
    made = [k for k in outs if k not in hbm]
    dma = pltpu.SemaphoreType.DMA
    counts = dict(ssem=sems, rsem=sems, lsem=12, csem=16, csem2=16, psem=16, psem2=16, isem=len(staged), osem=len(made))
    places = [pltpu.VMEM(ins[k].shape, ins[k].dtype) for k in staged] + [pltpu.VMEM(*outs[k]) for k in made]
    names = ["in_" + k for k in ins] + ["out_" + k for k in outs] + staged + made + list(scratch) + list(counts)

    def body(*refs):
        r = Refs(**dict(zip(names, refs)))
        for k in hbm:
            if k in ins or k in outs:
                setattr(r, k, getattr(r, ("in_" if k in ins else "out_") + k))
        r.here, r.gone = set(), set()
        r.coming = {
            k: pltpu.make_async_copy(getattr(r, "in_" + k), getattr(r, k), r.isem.at[i]) for i, k in enumerate(staged)
        }
        r.going = {
            k: pltpu.make_async_copy(getattr(r, k), getattr(r, "out_" + k), r.osem.at[i]) for i, k in enumerate(made)
        }
        kernel(layer, r)

    anywhere = pl.BlockSpec(memory_space=pl.ANY)
    got = pl.pallas_call(
        body,
        out_shape=[jax.ShapeDtypeStruct(s, t) for s, t in outs.values()],
        in_specs=[anywhere] * len(ins),
        out_specs=[anywhere] * len(outs),
        scratch_shapes=places + [pltpu.VMEM(s, t) for s, t in scratch.values()] + [dma((k,)) for k in counts.values()],
        compiler_params=pltpu.CompilerParams(
            collective_id=cid, has_side_effects=True, vmem_limit_bytes=VMEM_LIMIT
        ),
        cost_estimate=pl.CostEstimate(flops=flops, bytes_accessed=20 * 2**20, transcendentals=0),
        name=name,
    )(*ins.values())
    return dict(zip(outs, got))


FA_ROWS = tuple((4 * g + d) * UNIT for g, d in zip(GATE_PER, DOWN_PER))
RQ = Q_ROWS // 2 // 16
SIDES = (SIDE, SIDE)
WIDE = HEADS * HEAD_DIM


def bf(*shape):
    return (shape, BF16)


def f4(*shape):
    return (shape, F32)


def rest_scratch():
    made = {}
    for h, rows in zip("ab", FA_ROWS):
        made["l2" + h] = bf(SIDE - 1, rows, LANES)
        made["t2" + h] = bf(rows, LANES)
        made["g1" + h] = bf(SIDE, rows, LANES)
    return made


def rest_outs():
    return {"g" + h: bf(2, *SIDES, rows, LANES) for h, rows in zip("ab", FA_ROWS)}


def assemble_kernel(nz, *refs):
    given, results, held, outs, sem, osem = (refs[:2], refs[2:4]), refs[6:12], refs[12:14] + refs[4:6], refs[14:20], refs[20], refs[21]
    s = lax.axis_index("section")
    copies = [pltpu.make_async_copy(a, b, osem.at[i]) for i, (a, b) in enumerate(zip(outs, results))]
    for layer in range(2):
        @pl.when(s == layer)
        def _():
            moving = [pltpu.make_async_copy(a, b, sem.at[i]) for i, (a, b) in enumerate(zip(given[layer], held))]
            for c in moving:
                c.start()
            for c in moving:
                c.wait()

    gate_ref, up_ref, down_ref, qkv_ref, out_ref, small_ref = outs
    share = D // nz
    starts = window_starts(nz)

    def units(refs, section, base, per, first, count):
        rows = []
        for part, piece, slot, _, m in unit_runs(first, count, per):
            at = base[part] + slot * UNIT
            rows.append(refs[part][section, piece // SIDE, piece % SIDE, at : at + m * UNIT, :].astype(F32))
        return jnp.concatenate(rows, 0) if len(rows) > 1 else rows[0]

    for section, ref in ((0, gate_ref), (1, up_ref)):
        tiles = {}
        for w, a in enumerate(starts):
            for t in range(WIN // LANES):
                tiles.setdefault(a // LANES + t, []).append((w, t))
        for col, sources in tiles.items():
            total = None
            for w, t in sources:
                base = [w * per * UNIT for per in GATE_PER]
                got = units(held[:2], section, base, GATE_PER, t * (share // UNIT), share // UNIT)
                total = got if total is None else total + got
            ref[:, col * LANES : (col + 1) * LANES] = total
        copies[section].start()
    base = [nz * per * UNIT for per in GATE_PER]
    half = FF // nz // 2
    for section in range(2):
        for t in range(TILES):
            got = units(held[:2], section, base, DOWN_PER, t * (half // UNIT), half // UNIT)
            down_ref[section * half : (section + 1) * half, t * LANES : (t + 1) * LANES] = got
    copies[2].start()
    for t in range(QKV // LANES + TILES):
        got = units(held[2:], t // 8, (0, 0), Q_PER, (t % 8) * (share // UNIT), share // UNIT)
        if t < QKV // LANES:
            qkv_ref[:, t * LANES : (t + 1) * LANES] = got
        else:
            u = t - QKV // LANES
            out_ref[:, u * LANES : (u + 1) * LANES] = got
    small_ref[...] = units(held[2:], 0, (0, 0), Q_PER, 8 * (share // UNIT), 2)
    for c in copies[3:]:
        c.start()
    for c in copies:
        c.wait()


def assemble(zero, one, attn):
    nz = lax.axis_size("fsdp")
    vm = pl.BlockSpec(memory_space=pltpu.VMEM)
    anywhere = pl.BlockSpec(memory_space=pl.ANY)
    share = D // nz
    shapes = [(share, FF), (share, FF), (FF // nz, D), (share, QKV), (share, D), (2 * UNIT, LANES)]
    return pl.pallas_call(
        functools.partial(assemble_kernel, nz),
        out_shape=[jax.ShapeDtypeStruct(a, F32) for a in shapes],
        in_specs=[anywhere] * 4 + [vm] * 2,
        out_specs=[anywhere] * len(shapes),
        scratch_shapes=[pltpu.VMEM(a.shape, a.dtype) for a in zero]
        + [pltpu.VMEM(a, F32) for a in shapes]
        + [pltpu.SemaphoreType.DMA((2,)), pltpu.SemaphoreType.DMA((len(shapes),))],
        compiler_params=pltpu.CompilerParams(vmem_limit_bytes=VMEM_LIMIT),
        name="assemble",
    )(*zero, *one, *attn)


def window_starts(n):
    share = FF // n
    return [(i * share // LANES) * LANES for i in range(n)]


def attn_fwd(layer, x, shards, small, pair, pairs, tabs, wa):
    n, nz = lax.axis_size("ctx"), lax.axis_size("fsdp")
    tok = x.shape[0]
    ins = dict(x=x)
    outs = dict(
        mid=f4(tok, D), n2=bf(tok, D), n1t=bf(D, tok), qst=bf(2 * LANES, WIDE), kv=bf(n, tok, 2 * LANES), lse=f4(2, WIDE),
        attt=bf(D, tok), gu=bf(2, D, WIN), down=bf(WIN, D),
    )
    scratch = dict(m_s=f4(2, WIDE), l_s=f4(2, WIDE), acc_s=f4(2 * LANES, WIDE), att_s=bf(tok, D))
    if layer == 0:
        freq = jnp.arange(HEAD_DIM // 2, dtype=F32)
        inverse = jnp.tile(THETA ** (-2.0 * freq / HEAD_DIM), 4)[None, :]
        ins.update(small_own=small, pair=pair, inverse=inverse, wqkv_shard=shards["qkv"], wout_shard=shards["out"])
        outs.update(
            wa=bf(D, QKV + D), small=f4(2, 1, SMALL), pairs=((n, 8, 2 * LANES), jnp.int32),
            cos=f4(tok, LANES), sa=f4(tok, LANES), sb=f4(tok, LANES),
        )
        scratch.update(parts=f4(2, nz, 1, SMALL))
    else:
        ins.update(small=small, cos=tabs[0], sa=tabs[1], sb=tabs[2], wa=wa, pairs=pairs)
    ins.update(gate_shard=shards["gate"], up_shard=shards["up"], down_shard=shards["down"])
    hbm = ("wout_shard", "gate_shard", "up_shard", "down_shard", "wqkv_shard")
    return call(attn_fwd_kernel, layer, 1 + layer, f"attn_fwd_{layer}", ins, outs, scratch, 64, hbm)


def ffn_fwd(layer, a, shards):
    n = lax.axis_size("fsdp")
    tok = a["n2"].shape[0]
    ins = {k: a[k] for k in ("n2", "gu", "down", "mid")}
    outs = dict(y=f4(tok, D), all=bf(n, tok, D), gate=f4(n, tok, WIN), up=f4(n, tok, WIN))
    if layer == 0:
        ins.update(wqkv_shard=shards["qkv"], wout_shard=shards["out"])
        outs.update(wa=bf(D, QKV + D))
    scratch = dict(send_s=bf(n, tok, D), land_s=bf(n, tok, D))
    return call(ffn_fwd_kernel, layer, 3 + layer, f"ffn_fwd_{layer}", ins, outs, scratch, 32, ("wqkv_shard", "wout_shard"))


def ffn_bwd(layer, gy, a, f, small, before):
    n = lax.axis_size("fsdp")
    tok = gy.shape[0]
    ins = dict(gy=gy)
    outs = dict(gm=f4(tok, D), dg2=f4(1, D))
    scratch = dict(
        all_s=bf(n * tok, D), hid_s=bf(n * tok, WIN), g_s=bf(2, n * tok, WIN), down_s=bf(WIN, D),
        own_s=f4(tok, D), send_s=bf(n, tok, D), land_s=bf(n, tok, D),
    )
    for h, rows in zip("ab", FA_ROWS):
        scratch["f" + h] = bf(2, *SIDES, rows, LANES)
        outs["sl" + h] = bf(*SIDES, rows, LANES)
    if layer == 0:
        ins.update(t1a=before["t1a"], t1b=before["t1b"])
        outs.update(rest_outs())
        scratch.update(rest_scratch())
    ins.update(down=a["down"], gate=f["gate"], up=f["up"], gu=a["gu"], n2_all=f["all"], mid=a["mid"], small=small)
    return call(ffn_bwd_kernel, layer, 5 + layer, f"ffn_bwd_{layer}", ins, outs, scratch, 64, ("ga", "gb"), 2 * 10**10)


def attn_bwd(layer, x, a, b, wa, small, pairs, tabs, before):
    n, nz = lax.axis_size("ctx"), lax.axis_size("fsdp")
    tok = x.shape[0]
    share = D // nz
    ins = dict(gm=b["gm"], sla=b["sla"], slb=b["slb"])
    ins.update({k: a[k] for k in ("attt", "n1t")})
    if layer == 0:
        ins.update(glin1=before["glin"], gsmall1=before["gsmall"], n1z1=before["n1z"], dout1=before["dout"])
    ins.update({k: a[k] for k in ("qst", "lse", "kv")})
    ins.update(wa=wa, pairs=pairs, cos=tabs[0], sa=tabs[1], sb=tabs[2], x=x, small=small, dg2=b["dg2"])
    outs = dict(
        gx=f4(tok, D), glin=bf(tok, QKV), gsmall=f4(2 * UNIT, LANES), n1z=bf(share, nz * tok), dout=bf(TILES * share, LANES)
    )
    scratch = dict(
        gst_s=bf(2 * LANES, WIDE), delta_s=f4(2, WIDE), gq_s=f4(2 * LANES, WIDE), all_gm=bf(nz * tok, D), attz=bf(share, nz * tok),
        p_s=bf(2 * BATCH * HEAD_DIM, WIDE), ds_s=bf(2 * BATCH * HEAD_DIM, WIDE),
        send_s=bf(n, tok, 2 * LANES), land_s=bf(n, tok, 2 * LANES),
    )
    for h, rows in zip("ab", FA_ROWS):
        outs["t1" + h] = bf(SIDE, rows, LANES)
        scratch["l1" + h] = bf(SIDE - 1, SIDE, rows, LANES)
    if layer == 0:
        scratch.update(attention_scratch(tok))
        outs.update(qpa=bf(*SIDES, RQ, LANES), qpb=bf(*SIDES, RQ, LANES))
    return call(attn_bwd_kernel, layer, 7 + layer, f"attn_bwd_{layer}", ins, outs, scratch, 48, flops=2 * 10**10)


def attention_scratch(tok):
    nz = lax.axis_size("fsdp")
    return dict(all_glin=bf(nz * tok, QKV), all_small=f4(nz * 2 * UNIT, LANES), qv=bf(2, Q_ROWS, LANES), ql=bf(Q_ROWS, LANES))


def reduce_rest(last):
    ins = dict(glin=last["glin"], gsmall=last["gsmall"], t1a=last["t1a"], t1b=last["t1b"], q1a=last["qpa"], q1b=last["qpb"])
    ins.update(n1z=last["n1z"], dout=last["dout"])
    outs = rest_outs()
    scratch = rest_scratch()
    scratch.update(attention_scratch(last["glin"].shape[0]))
    scratch.update(qpa=bf(*SIDES, RQ, LANES), qpb=bf(*SIDES, RQ, LANES))
    for h in "ab":
        outs["q" + h] = bf(2, *SIDES, RQ, LANES)
        for l in "01":
            scratch["m" + l + h] = bf(SIDE - 1, SIDE, RQ, LANES)
            scratch["w" + l + h] = bf(SIDE - 1, RQ, LANES)
            scratch["e" + l + h] = bf(SIDE, RQ, LANES)
            scratch["h" + l + h] = bf(SIDE, RQ, LANES)
    return call(reduce_kernel, 0, 9, "reduce", ins, outs, scratch, 128, ("ga", "gb", "qa", "qb"))


def local(
    tokens, cotangent, pair_of, attn_gain, ffn_gain, qkv_weight, qkv_bias, out_weight, gate_weight, up_weight, down_weight,
):
    s = lax.axis_index("section")
    z = lax.axis_index("fsdp")
    nz = lax.axis_size("fsdp")
    qd = D // nz
    shards = dict(qkv=qkv_weight, out=out_weight, gate=gate_weight, up=up_weight, down=down_weight)

    def placed(part, size):
        whole = jnp.zeros((1, size), F32)
        return lax.dynamic_update_slice(whole, part.astype(F32), (0, z * part.shape[1]))

    small_own = jnp.concatenate([placed(attn_gain, D), placed(ffn_gain, D), placed(qkv_bias, QKV)], 1)
    pair = jnp.broadcast_to(pair_of.reshape(1, 1), (8, 2 * LANES))
    x0 = jnp.where(s == 0, tokens[0, 0], tokens[1, 0])
    a0 = attn_fwd(0, x0, shards, small_own, pair, None, None, None)
    small, pairs, tabs = a0["small"], a0["pairs"], (a0["cos"], a0["sa"], a0["sb"])
    f0 = ffn_fwd(0, a0, shards)
    x1 = f0["y"].astype(BF16).astype(F32)
    a1 = attn_fwd(1, x1, shards, small, None, pairs, tabs, f0["wa"])
    f1 = ffn_fwd(1, a1, None)

    gy = jnp.where(s == 0, cotangent[0, 0], cotangent[1, 0])
    b1 = ffn_bwd(1, gy, a1, f1, small, None)
    c1 = attn_bwd(1, x1, a1, b1, f0["wa"], small, pairs, tabs, None)
    gy = c1["gx"].astype(BF16).astype(F32)
    b0 = ffn_bwd(0, gy, a0, f0, small, c1)
    c0 = attn_bwd(0, x0, a0, b0, a0["wa"], small, pairs, tabs, c1)
    t = reduce_rest(c0)
    dgate, dup, ddown, dqkv, dout, small_grad = assemble((t["ga"], t["gb"]), (b0["ga"], b0["gb"]), (t["qa"], t["qb"]))
    small_grad = small_grad.reshape(-1)

    def mine(first, size):
        return lax.dynamic_slice_in_dim(small_grad, first + z * size, size, 0)[None]

    def by_layer(pair):
        theirs = jnp.where(s == 0, pair[1], pair[0])
        mine = jnp.where(s == 0, pair[0], pair[1])
        got = lax.ppermute(theirs, "section", [(0, 1), (1, 0)])
        return jnp.where(s == 0, jnp.stack([mine, got]), jnp.stack([got, mine]))[None, :, None]

    return (
        by_layer((f0["y"], f1["y"])),
        by_layer((c0["gx"], c1["gx"])),
        mine(0, qd),
        mine(D, qd),
        dqkv[None],
        mine(2 * D, QKV // nz),
        dout[None],
        dgate[None],
        dup[None],
        ddown[None],
    )


def solution(mesh):
    return jax.shard_map(
        local,
        mesh=mesh,
        in_specs=(
            P(None, "fsdp", "ctx", None),
            P(None, "fsdp", "ctx", None),
            P("ctx"),
            P("section", "fsdp"),
            P("section", "fsdp"),
            P("section", "fsdp", None),
            P("section", "fsdp"),
            P("section", "fsdp", None),
            P("section", "fsdp", None),
            P("section", "fsdp", None),
            P("section", "fsdp", None),
        ),
        out_specs=(
            P("section", None, "fsdp", "ctx", None),
            P("section", None, "fsdp", "ctx", None),
            P("section", "fsdp"),
            P("section", "fsdp"),
            P("section", "fsdp", None),
            P("section", "fsdp"),
            P("section", "fsdp", None),
            P("section", "fsdp", None),
            P("section", "fsdp", None),
            P("section", "fsdp", None),
        ),
        check_vma=False,
    )
```

time: 506 us -> 449 us (0.89)
  Pallas kernels: 475 us -> 423 us
    pallas_call x9, Pallas kernels: 465 us -> 413 us  [call(): pl.pallas_call(body, out_shape=[jax.ShapeDtypeStruct(s, t) for s, t in ou...]
  transfers between devices with their start and end apart: 2 -> 2, of which waited for: 0 -> 0; matrix products, arithmetic and copies ran while one was open for 1% -> 1% of each run, Pallas kernels for 17% -> 20%
where the time goes in v4:
time: 449 us; the launch traced here: 443 us
  Pallas kernels  423 us (94%)
  other arithmetic  13.4 us (3%)
    pallas_call x9, Pallas kernels, call(): pl.pallas_call(body, out_shape=[jax.ShapeDtypeStruct(s, t) for s, t in ou...  413 us
    pallas_call x1, Pallas kernels, assemble(): pl.pallas_call(functools.partial(assemble_kernel, nz), out_shape=[jax.Sha...  9.85 us
  transfers between devices with their start and end apart: 2, of which 0 were waited for; matrix products, arithmetic and copies ran while one was open for 1% of the time, Pallas kernels for 20%

profile of v4, /device:TPU:0, one launch (start us, length us, event | category | flops | bytes accessed | tf_op | source)
XLA Modules:
  0.0 442.7 jit_solution(6947392357763730130)
XLA Ops:
  1.3 0.7 convert_element_type.21
  2.0 0.7 convert_element_type.22
  2.7 0.6 broadcast_in_dim_tile.3.refs_3_
  3.3 0.7 convert_element_type.23
  4.0 2.0 select_bitcast_fusion.3.refs_0_.refs_17_
  5.9 2.0 select_bitcast_fusion.1.refs_0_
  7.9 0.1 dynamic_update_slice.10
  8.0 0.2 dynamic_update_slice.9
  8.2 0.2 dynamic_update_slice.11
  8.4 0.6 pad_maximum_fusion.refs_1_
  9.0 0.6 broadcast_in_dim.38.refs_2_
  9.6 59.0 %attn_fwd_0.1 = (f32[128,896]{1,0:T(8,128)}, bf16[128,896]{1,0:T(8,128)(2,1)}, bf16[896,128]{1,0:T(8,128)(2,1)}, bf16[256,896]{1,0:T(8,128)(2,1)}, bf16[16,128,2...) custom-call(f32[128,896]{1,0:T(8,128)} %select_bitcast_fusion.3.refs, ...), custom_call_target="tpu_custom_call" | custom-call | flops 10000000000 | bytes 20971520 | tf_op jit(solution)/shard_map/attn_fwd_0/pallas_call | solution.py:1244
  68.6 40.1 %ffn_fwd_0.1 = (f32[128,896]{1,0:T(8,128)}, bf16[4,128,896]{2,1,0:T(8,128)(2,1)}, f32[4,128,1280]{2,1,0:T(8,128)}, f32[4,128,1280]{2,1,0:T(8,128)}, bf16[896,2048]{1,0:T(8,128)(2,1)}) custom-call(bf16[128,896]{1,0:T(8,128)(2,1)} %get-tuple-element.79.refs_0_, bf16[2,896,1280]{2,1,0:T(8,128)(2,1)} %get-tuple-element.80.refs_1_.refs_6_, ...), custom_call_target="tpu_custom_call" | custom-call | flops 10000000000 | bytes 20971520 | tf_op jit(solution)/shard_map/ffn_fwd_0/pallas_call | solution.py:1244
  108.7 1.8 convert_convert_fusion.1.refs_0_.refs_13_
  110.5 35.6 %attn_fwd_1.1 = (f32[128,896]{1,0:T(8,128)}, bf16[128,896]{1,0:T(8,128)(2,1)}, bf16[896,128]{1,0:T(8,128)(2,1)}, bf16[256,896]{1,0:T(8,128)(2,1)}, bf16[16,128,2...) custom-call(f32[128,896]{1,0:T(8,128)} %convert_convert_fusion.1.ref, ...), custom_call_target="tpu_custom_call" | custom-call | flops 10000000000 | bytes 20971520 | tf_op jit(solution)/shard_map/attn_fwd_1/pallas_call | solution.py:1244
  146.1 26.9 %ffn_fwd_1.1 = (f32[128,896]{1,0:T(8,128)}, bf16[4,128,896]{2,1,0:T(8,128)(2,1)}, f32[4,128,1280]{2,1,0:T(8,128)}, f32[4,128,1280]{2,1,0:T(8,128)}) custom-call(bf16[128,896]{1,0:T(8,128)(2,1)} %get-tuple-element.90.refs_0_, bf16[2,896,1280]{2,1,0:T(8,128)(2,1)} %get-tuple-element.91.refs_1_.refs_4_, bf16[1280,896]{1,0:T(8,128)(2,1)} %get-tuple-element.92.refs_2_.refs_1_, ...), custom_call_target="tpu_custom_call" | custom-call | flops 10000000000 | bytes 20971520 | tf_op jit(solution)/shard_map/ffn_fwd_1/pallas_call | solution.py:1244
  173.0 30.0 %ffn_bwd_1.1 = (f32[128,896]{1,0:T(8,128)}, f32[1,896]{1,0:T(1,128)}, bf16[4,4,448,128]{3,2,1,0:T(8,128)(2,1)}, bf16[4,4,400,128]{3,2,1,0:T(8,128)(2,1)}) custom-call(f32[128,896]{1,0:T(8,128)} %select_bitcast_fusion.1.refs_0_, bf16[1280,896]{1,0:T(8,128)(2,1)} %get-tuple-element.92.refs_2_.refs_1_, f32[4,128,1280]{2,1,0:T(8,128)} %get-tuple-element.95.refs_2_, ...), custom_call_target="tpu_custom_call" | custom-call | flops 20000000000 | bytes 20971520 | tf_op jit(solution)/shard_map/ffn_bwd_1/pallas_call | solution.py:1244
  203.0 45.8 %attn_bwd_1.1 = (f32[128,896]{1,0:T(8,128)}, bf16[128,1152]{1,0:T(8,128)(2,1)}, f32[32,128]{1,0:T(8,128)}, bf16[224,512]{1,0:T(8,128)(2,1)}, bf16[1568,128]{1,0:...) custom-call(f32[128,896]{1,0:T(8,128)} %get-tuple-element.98.refs_0_, ...), custom_call_target="tpu_custom_call" | custom-call | flops 20000000000 | bytes 20971520 | tf_op jit(solution)/shard_map/attn_bwd_1/pallas_call | solution.py:1244
  248.8 1.8 convert_convert_fusion.refs_0_
  250.6 48.2 %ffn_bwd_0.1 = (f32[128,896]{1,0:T(8,128)}, f32[1,896]{1,0:T(1,128)}, bf16[4,4,448,128]{3,2,1,0:T(8,128)(2,1)}, bf16[4,4,400,128]{3,2,1,0:T(8,128)(2,1)}, bf16[2...) custom-call(f32[128,896]{1,0:T(8,128)} %convert_convert_fusion.refs_0_, ...), custom_call_target="tpu_custom_call" | custom-call | flops 20000000000 | bytes 20971520 | tf_op jit(solution)/shard_map/ffn_bwd_0/pallas_call | solution.py:1244
  298.8 50.0 %attn_bwd_0.1 = (f32[128,896]{1,0:T(8,128)}, bf16[128,1152]{1,0:T(8,128)(2,1)}, f32[32,128]{1,0:T(8,128)}, bf16[224,512]{1,0:T(8,128)(2,1)}, bf16[1568,128]{1,0:...) custom-call(f32[128,896]{1,0:T(8,128)} %get-tuple-element.113.refs_0, ...), custom_call_target="tpu_custom_call" | custom-call | flops 20000000000 | bytes 20971520 | tf_op jit(solution)/shard_map/attn_bwd_0/pallas_call | solution.py:1244
  348.9 1.1 select_bitcast_fusion
  349.9 0.1 collective-permute-start.1
  350.1 0.1 select_bitcast_fusion.2
  350.1 0.6 collective-permute-start
  350.7 77.2 %reduce.1 = (bf16[2,4,4,448,128]{4,3,2,1,0:T(8,128)(2,1)}, bf16[2,4,4,400,128]{4,3,2,1,0:T(8,128)(2,1)}, bf16[2,4,4,64,128]{4,3,2,1,0:T(8,128)(2,1)}, bf16[2,4,4,64,128]{4,3,2,1,0:T(8,128)(2,1)}) custom-call(bf16[128,1152]{1,0:T(8,128)(2,1)} %get-tuple-element.128.refs_0_, f32[32,128]{1,0:T(8,128)} %get-tuple-element.129.refs_1_, ...), custom_call_target="tpu_custom_call" | custom-call | flops 10000000000 | bytes 20971520 | tf_op jit(solution)/shard_map/reduce/pallas_call | solution.py:1244
  427.9 9.8 %assemble.1 = (f32[224,4864]{1,0:T(8,128)}, f32[224,4864]{1,0:T(8,128)}, f32[1216,896]{1,0:T(8,128)}, f32[224,1152]{1,0:T(8,128)}, f32[224,896]{1,0:T(8,128)}, /*index=5*/f32[32,128]{1,0:T(8,128)}) custom-call(bf16[2,4,4,448,128]{4,3,2,1,0:T(8,128)(2,1)} %get-tuple-element.136.refs_0_, bf16[2,4,4,400,128]{4,3,2,1,0:T(8,128)(2,1)} %get-tuple-element.137.refs_1_, ...), custom_call_target="tpu_custom_call" | custom-call | tf_op jit(solution)/shard_map/assemble/pallas_call | solution.py:1350
  437.8 0.8 dynamic_slice.11
  438.6 0.6 broadcast_in_dim.42
  439.1 1.4 fusion
  440.6 1.0 maximum_select_fusion.1
  441.6 1.0 maximum_select_fusion
  (13 shorter events, 0.0 us)
Async XLA Ops:
  298.8 50.1 %copy-start.1 = (f32[128,896]{1,0:T(8,128)S(1)}, f32[128,896]{1,0:T(8,128)}, u32[]{:S(2)}) copy-start(f32[128,896]{1,0:T(8,128)} %get-tuple-element.107) | copy-start | bytes 1376260
  298.8 51.3 %copy-start = (f32[128,896]{1,0:T(8,128)S(1)}, f32[128,896]{1,0:T(8,128)}, u32[]{:S(2)}) copy-start(f32[128,896]{1,0:T(8,128)} %get-tuple-element.83) | copy-start | bytes 1376260
  298.8 51.3 %copy-start.2 = (f32[128,896]{1,0:T(8,128)S(1)}, f32[128,896]{1,0:T(8,128)}, u32[]{:S(2)}) copy-start(f32[128,896]{1,0:T(8,128)} %get-tuple-element.94) | copy-start | bytes 1376260
  349.9 90.6 %collective-permute-start.1 = (f32[128,896]{1,0:T(8,128)S(1)}, f32[128,896]{1,0:T(8,128)S(1)}, u32[]{:S(2)}, u32[]{:S(2)}) collective-permute-start(f32[128,896]{1,0:T(8,128)S(1)} %get-tuple-element.149), channel_id=1, source_target_pairs={{0,64},{64,0},{1,65},{65,1},{2,66},{66,2},{3,67},{67,3},{4,68},{68... | collective-permute-start | bytes 1376264 | tf_op jit(solution)/shard_map/ppermute | solution.py:1513
  350.1 91.4 %collective-permute-start = (f32[128,896]{1,0:T(8,128)S(1)}, f32[128,896]{1,0:T(8,128)S(1)}, u32[]{:S(2)}, u32[]{:S(2)}) collective-permute-start(f32[128,896]{1,0:T(8,128)S(1)} %get-tuple-element.151), channel_id=1, source_target_pairs={{0,64},{64,0},{1,65},{65,1},{2,66},{66,2},{3,67},{67,3},{4,68},{68... | collective-permute-start | bytes 1376264 | tf_op jit(solution)/shard_map/ppermute | solution.py:1513

commit v5 on v4

--- a/solution.py
+++ b/solution.py
@@ -24,7 +24,7 @@
 F32 = jnp.float32
 BF16 = jnp.bfloat16
 MESH = pl.DeviceIdType.MESH
-VMEM_LIMIT = 56 * 2**20
+VMEM_LIMIT = 60 * 2**20
 UNIT = 16
 SIDE = 4
 GATE_PER = (5, 4)
@@ -512,83 +512,171 @@
     return jnp.sum(a, 0, keepdims=True)
 
 
-def attn_fwd_kernel(layer, r):
+class View:
+    def __init__(self, r, layer):
+        self.r, self.layer = r, layer
+
+    def named(self, k):
+        own = k + str(self.layer)
+        return own if hasattr(self.r, own) else k
+
+    def __getattr__(self, k):
+        return getattr(self.r, self.named(k))
+
+    def need(self, *names):
+        self.r.need(*[self.named(k) for k in names])
+
+    def flush(self, *names):
+        self.r.flush(*[self.named(k) for k in names])
+
+
+def forward_kernel(_, r):
     st = Stages(r)
     n, me = st.nc, st.c
     st.hail(st.beside() + st.upright(True), ring=True)
-    first = layer == 0
     r.load()
-    if first:
-        wa_local, wa = feed_attention(st, layer, r.wqkv_shard, r.wout_shard, r.wa)
-    gu_local, gu = feed_windows(st, layer, r.gate_shard, r.up_shard, r.gu)
-    down = FeedDown(st, layer, r.down_shard, r.down)
-    r.need("x")
+    wa, gu, down = [None, None], [None, None], [None, None]
+    for l in range(2):
+        v = View(r, l)
+        wa[l] = feed_attention(st, l, r.qkv_shard, r.out_shard, v.wa)
+        gu[l] = feed_windows(st, l, r.gate_shard, r.up_shard, v.gu)
+        down[l] = FeedDown(st, l, r.down_shard, v.down)
+    r.need("pair", "small_own", "inverse", "x0")
+    r.pairs[me] = jnp.broadcast_to(r.pair[...], r.pairs.shape[1:])
+    r.parts[st.s, st.z] = r.small_own[...]
+    wa[0][0].wait()
+    st.met()
+    wa[0][1].start()
+    at = st.take(2 * st.nz)
+    mine = r.parts.at[st.s, st.z]
+    st.begin(
+        [st.copy(mine, mine, at + k, st.peer("z", k, st.s), at + st.s * st.nz + k) for k in range(1, st.nz)]
+        + [st.copy(mine, mine, at + st.nz + k, st.peer("z", k, 1 - st.s), at + st.s * st.nz + k) for k in range(1, st.nz)]
+        + [st.copy(mine, mine, at, st.peer("s", 0), at + st.s * st.nz)]
+    )
+
+    def tell(k, c):
+        p = r.pairs.at[me]
+        push(p, p, r.psem.at[k], r.psem2.at[k], "ctx", lax.rem(me + k, n)).start()
+        return c
+
+    lax.fori_loop(1, n, tell, 0)
+    block = LANES // 2
+    i = lax.broadcasted_iota(jnp.int32, (LANES, LANES), 0)
+    pair = r.pairs[me, 0:1, :LANES]
+    pos = jnp.where(i < block, pair * block + i, (2 * n - 1 - pair) * block + i - block)
+    angle = pos.astype(F32) * r.inverse[...]
+    lane = lax.rem(lax.broadcasted_iota(jnp.int32, (LANES, LANES), 1), HEAD_DIM)
+    sine = jnp.sin(angle)
+    r.cos[...] = jnp.cos(angle)
+    r.sa[...] = jnp.where(lane < HEAD_DIM // 2, -sine, 0.0)
+    r.sb[...] = jnp.where(lane < HEAD_DIM // 2, 0.0, sine)
+    r.flush("cos", "sa", "sb")
+    for h in (st.s, 1 - st.s):
+        for k in range(st.nz):
+            if h is st.s and k == 0:
+                continue
+            st.copy(mine, mine, at, st.peer("s", 0), at + h * st.nz + k).wait_recv()
+    for h in range(2):
+        total = r.parts[h, 0]
+        for k in range(1, st.nz):
+            total = total + r.parts[h, k]
+        r.small[h] = total
+    r.flush("small")
+    for k in ORDER:
+        wa[0][1].relay(k)
+    gu[0][0].wait()
+    gu[0][1].start()
+    down[0].start()
+    for k in ORDER:
+        wa[0][1].collect(k)
+
+    def begin_next():
+        wa[1][0].wait()
+        wa[1][1].start()
+        gu[1][0].wait()
+        gu[1][1].start()
+        down[1].start()
+
+    def relays(*steps):
+        def go():
+            for feed, name, k in steps:
+                getattr(feed, name)(k)
+
+        return go
+
+    g0, w1, g1 = gu[0][1], wa[1][1], gu[1][1]
+    wa[0][1].finish()
+    v = View(r, 0)
+    v.flush("wa")
+    attention_forward(
+        st, v, 0,
+        (
+            relays((g0, "relay", 1), (g0, "relay", 3)),
+            relays((g0, "relay", 2)),
+            begin_next,
+            relays((g0, "collect", 1), (g0, "collect", 3)),
+            relays((g0, "collect", 2)),
+        ),
+    )
+
+    def ready_0():
+        g0.finish()
+        down[0].finish()
+        v.flush("gu", "down")
+
+    ffn_forward(
+        st, v, ready_0,
+        (
+            relays((w1, "relay", 1), (w1, "relay", 3)),
+            relays((w1, "relay", 2), (g1, "relay", 1)),
+            relays((g1, "relay", 3), (g1, "relay", 2), (w1, "collect", 1), (w1, "collect", 3)),
+            relays((w1, "collect", 2), (g1, "collect", 1), (g1, "collect", 3), (g1, "collect", 2)),
+        ),
+    )
+    r.x1[...] = r.y0[...].astype(BF16).astype(F32)
+    r.flush("y0", "x1")
+    r.need("gy")
+    tok = r.gy.shape[0]
+    rows = st.block(st.z, tok)
+    r.gy_all[rows, :] = r.gy[...].astype(BF16)
+    at = st.take(st.nz - 1)
+    mine_gy = r.gy_all.at[rows, :]
+    gy_moving = st.begin([st.copy(mine_gy, mine_gy, at + k - 1, st.peer("z", k)) for k in range(1, st.nz)])
+    w1.finish()
+    v = View(r, 1)
+    v.flush("wa")
+    nothing = lambda: None
+    attention_forward(st, v, 1, (nothing,) * 5)
+
+    def ready_1():
+        g1.finish()
+        down[1].finish()
+        v.flush("gu", "down")
+
+    ffn_forward(st, v, ready_1, (nothing,) * 4)
+    r.flush("y1")
+    arrived(gy_moving)
+    r.flush("gy_all")
+    st.drain()
+
+    def done(k, c):
+        p = r.pairs.at[me]
+        push(p, p, r.psem.at[k], r.psem2.at[k], "ctx", lax.rem(me + k, n)).wait_send()
+        return c
+
+    lax.fori_loop(1, n, done, 0)
+    r.close()
+
+
+def attention_forward(st, r, layer, between):
+    n, me = st.nc, st.c
     x = r.x[...]
     r1 = lax.rsqrt(jnp.mean(x * x, -1, keepdims=True) + EPS)
-    unit = x * r1
-    if first:
-        r.need("pair", "small_own", "inverse")
-        r.pairs[me] = jnp.broadcast_to(r.pair[...], r.pairs.shape[1:])
-        r.parts[st.s, st.z] = r.small_own[...]
-        wa_local.wait()
-    gu_local.wait()
-    st.met()
-    if first:
-        wa.start()
-        at = st.take(2 * st.nz)
-        mine = r.parts.at[st.s, st.z]
-        st.begin(
-            [st.copy(mine, mine, at + k, st.peer("z", k, st.s), at + st.s * st.nz + k) for k in range(1, st.nz)]
-            + [st.copy(mine, mine, at + st.nz + k, st.peer("z", k, 1 - st.s), at + st.s * st.nz + k) for k in range(1, st.nz)]
-            + [st.copy(mine, mine, at, st.peer("s", 0), at + st.s * st.nz)]
-        )
-
-        def tell(k, c):
-            p = r.pairs.at[me]
-            push(p, p, r.psem.at[k], r.psem2.at[k], "ctx", lax.rem(me + k, n)).start()
-            return c
-
-        lax.fori_loop(1, n, tell, 0)
-        block = LANES // 2
-        i = lax.broadcasted_iota(jnp.int32, (LANES, LANES), 0)
-        pair = r.pairs[me, 0:1, :LANES]
-        pos = jnp.where(i < block, pair * block + i, (2 * n - 1 - pair) * block + i - block)
-        angle = pos.astype(F32) * r.inverse[...]
-        lane = lax.rem(lax.broadcasted_iota(jnp.int32, (LANES, LANES), 1), HEAD_DIM)
-        sine = jnp.sin(angle)
-        r.cos[...] = jnp.cos(angle)
-        r.sa[...] = jnp.where(lane < HEAD_DIM // 2, -sine, 0.0)
-        r.sb[...] = jnp.where(lane < HEAD_DIM // 2, 0.0, sine)
-        r.flush("cos", "sa", "sb")
-        for h in (st.s, 1 - st.s):
-            for k in range(st.nz):
-                if h is st.s and k == 0:
-                    continue
-                st.copy(mine, mine, at, st.peer("s", 0), at + h * st.nz + k).wait_recv()
-        for h in range(2):
-            total = r.parts[h, 0]
-            for k in range(1, st.nz):
-                total = total + r.parts[h, k]
-            r.small[h] = total
-        r.flush("small")
-        for k in ORDER:
-            wa.relay(k)
-    gu.start()
-    down.start()
-    if first:
-        for k in ORDER:
-            wa.collect(k)
-    else:
-        r.need("small", "pairs", "cos", "sa", "sb")
     small = r.small[layer]
-    n1_f = unit * small[:, :D]
+    n1_f = x * r1 * small[:, :D]
     n1 = n1_f.astype(BF16)
     bias = small[:, 2 * D :]
-    if first:
-        wa.finish()
-        r.flush("wa")
-    else:
-        r.need("wa")
     cos, sa, sb = r.cos[...], r.sa[...], r.sb[...]
     lin = mm(n1, r.wa[:, D:QKV]) + bias[:, D:]
     r.kv[me] = jnp.concatenate([rope(lin[:, :LANES], cos, sa, sb), lin[:, LANES:]], 1).astype(BF16)
@@ -608,8 +696,7 @@
         spread(r.qst, t, q.T)
         r.n1t[tile, :] = n1_f[:, tile].T.astype(BF16)
     r.flush("qst", "n1t")
-    for k in ORDER[:2]:
-        gu.relay(k)
+    between[0]()
     half = HEAD_DIM
     own_k = own_sides(r.kv[me, :, :LANES].astype(F32))
     own_vt = own_sides(r.kv[me, :, LANES:].astype(F32)).astype(F32).T.astype(BF16)
@@ -631,7 +718,7 @@
             k = i * BATCH + 1 + j
             src = lax.rem(me + n - k, n)
             keys_copy(k, src).wait_recv()
-            if first:
+            if layer == 0:
                 p = r.pairs.at[src]
                 push(p, p, r.psem.at[k], r.psem2.at[k], "ctx", lax.rem(me + k, n)).wait_recv()
             sel.append(src)
@@ -669,14 +756,15 @@
         return c
 
     lax.fori_loop(0, 1, step, 0)
-    gu.relay(2)
-    lax.fori_loop(1, 3, step, 0)
-    for k in ORDER[:2]:
-        gu.collect(k)
-    lax.fori_loop(3, (n - 1) // BATCH, step, 0)
-    gu.collect(2)
+    between[1]()
+    lax.fori_loop(1, 2, step, 0)
+    between[2]()
+    lax.fori_loop(2, 4, step, 0)
+    between[3]()
+    lax.fori_loop(4, (n - 1) // BATCH, step, 0)
+    between[4]()
     r.flush("kv")
-    if first:
+    if layer == 0:
         r.flush("pairs")
     r.lse[...] = r.m_s[...] + jnp.log(r.l_s[...])
     for t in range(TILES):
@@ -689,22 +777,53 @@
     mid = x + mm(r.att_s[...], r.wa[:, QKV:])
     r.mid[...] = mid
     r2 = lax.rsqrt(jnp.mean(mid * mid, -1, keepdims=True) + EPS)
-    r.n2[...] = (mid * r2 * small[:, D : 2 * D]).astype(BF16)
-    r.flush("mid", "n2")
-    gu.finish()
-    down.finish()
-    r.flush("gu", "down")
-    st.drain()
+    r.all[st.z] = (mid * r2 * small[:, D : 2 * D]).astype(BF16)
+    r.flush("mid")
 
     def done(k, c):
         keys_copy(k, me).wait_send()
-        if first:
-            p = r.pairs.at[me]
-            push(p, p, r.psem.at[k], r.psem2.at[k], "ctx", lax.rem(me + k, n)).wait_send()
         return c
 
     lax.fori_loop(1, n, done, 0)
-    r.close()
+
+
+def ffn_forward(st, r, ready, between):
+    n, me = st.nz, st.z
+    at = st.take(2 * n)
+
+    def first(k):
+        return st.copy(r.all.at[me], r.all.at[me], at + k, st.peer("z", k))
+
+    def second(k):
+        return st.copy(r.send_s.at[k], r.land_s.at[k], at + n + k, st.peer("z", -k))
+
+    for k in ORDER:
+        first(k).start()
+    ready()
+
+    def block(src):
+        a = r.all[src]
+        gate = mm(a, r.gu[0])
+        up = mm(a, r.gu[1])
+        r.gate[src] = gate.astype(BF16)
+        r.up[src] = up.astype(BF16)
+        hidden = (gate * jax.nn.sigmoid(gate) * up).astype(BF16)
+        return mm(hidden, r.down[...])
+
+    r.y[...] = r.mid[...] + block(me)
+    for i, k in enumerate(ORDER):
+        between[i]()
+        first(k).wait_recv()
+        r.send_s[k] = block(st.along("z", -k)).astype(BF16)
+        second(k).start()
+    r.flush("all", "gate", "up")
+    between[3]()
+    for k in ORDER:
+        second(k).wait_recv()
+        r.y[...] += r.land_s[k].astype(F32)
+    for k in ORDER:
+        first(k).wait_send()
+        second(k).wait_send()
 
 
 class Attention:
@@ -769,341 +888,6 @@
                 out[h][i // SIDE, i % SIDE] = total.astype(BF16)
 
 
-def attn_bwd_kernel(layer, r):
-    st = Stages(r)
-    n, me = st.nc, st.c
-    last = layer == 0
-    st.hail(st.upright() + (st.beside() if last else []), ring=True)
-    r.load()
-    half = HEAD_DIM
-    r.need("gm")
-    gm = r.gm[...]
-    gmb = gm.astype(BF16)
-    tok = gm.shape[0]
-    r.all_gm[st.block(st.z, tok), :] = gmb
-    sl, l1, t1 = (r.sla, r.slb), (r.l1a, r.l1b), (r.t1a, r.t1b)
-    r.need("sla", "slb", "attt", "n1t")
-    st.met()
-    r1 = [st.scatter(AXES[h][0], sl[h], l1[h]) for h in range(2)]
-    attention = Attention(st)
-    out_factors = attention.whole(r.all_gm) + attention.columns(r.attt, r.attz)
-    qkv_factor = attention.columns(r.n1t, r.n1z)
-    if last:
-        r.need("glin1", "gsmall1", "n1z1", "dout1")
-        before = attention.begin(r.glin1, r.gsmall1, r.all_glin, r.all_small)
-    r.need("wa", "qst", "lse", "kv", "pairs")
-    ga = mm_nt(gmb, r.wa[:, QKV:])
-    for t in range(TILES):
-        tile = slice(t * LANES, (t + 1) * LANES)
-        ga_t = ga[:, tile].T
-        spread(r.gst_s, t, ga_t)
-        prod = ga_t * r.attt[tile, :].astype(F32)
-        low, high = halves(col_sum(prod[:half]), col_sum(prod[half:]))
-        r.delta_s[0:1, tile], r.delta_s[1:2, tile] = low, high
-
-    def own_block():
-        keys, vals = r.kv[me, :, :LANES].astype(F32), r.kv[me, :, LANES:].astype(F32)
-        kx, vx = own_sides(keys), own_sides(vals)
-        kt = kx.astype(F32).T.astype(BF16)
-        rows = slice(0, 3 * half)
-        for cols in GROUPS:
-            bias = own_bias(cols.stop - cols.start)
-            sc = mm(kx, r.qst[:, cols])
-            dp = mm(vx, r.gst_s[:, cols])
-            lo, hi = (r.lse[0:1, cols], r.delta_s[0:1, cols]), (r.lse[1:2, cols], r.delta_s[1:2, cols])
-            parts = [(sc[:half], hi), (sc[half : 2 * half] + bias, lo), (sc[2 * half :] + bias, hi)]
-            for i, (part, (lse, delta)) in enumerate(parts):
-                p = jnp.exp(part - lse)
-                at = slice(i * half, (i + 1) * half)
-                r.p_s[at, cols] = p.astype(BF16)
-                r.ds_s[at, cols] = (p * (dp[at] - delta)).astype(BF16)
-            r.gq_s[:, cols] = mm(kt, r.ds_s[rows, cols])
-        made = []
-        for w, q in ((r.ds_s, r.qst), (r.p_s, r.gst_s)):
-            e = mm_nt(w[rows, :], q[...])
-            low = e[:half, LANES:] + e[half : 2 * half, :LANES]
-            made.append(jnp.concatenate([low, e[2 * half :, LANES:]], 0))
-        return jnp.concatenate(made, 1)
-
-    def sum_copy(k):
-        return push(r.send_s.at[k], r.land_s.at[k], r.csem.at[k], r.csem2.at[k], "ctx", lax.rem(me + k, n))
-
-    def step(i, c):
-        kx, vx, kt, sel = [], [], [], []
-        for j in range(BATCH):
-            src = lax.rem(me + i * BATCH + 1 + j, n)
-            sel.append(src)
-            chosen = earlier(r.pairs, src, me, LANES)
-            keys = r.kv[src, :, :LANES].astype(F32)
-            kx.append(sides(keys, chosen))
-            vx.append(sides(r.kv[src, :, LANES:].astype(F32), chosen))
-            kt.append(sides_t(keys.T, chosen))
-        kx, vx, kt = jnp.concatenate(kx, 0), jnp.concatenate(vx, 0), jnp.concatenate(kt, 1)
-        rows = slice(0, 2 * BATCH * half)
-        for cols in GROUPS:
-            width = cols.stop - cols.start
-            sc = mm(kx, r.qst[:, cols])
-            dp = mm(vx, r.gst_s[:, cols])
-            for j in range(BATCH):
-                chosen = earlier(r.pairs, sel[j], me, width)
-                for part in range(2):
-                    lse, delta = r.lse[1:2, cols], r.delta_s[1:2, cols]
-                    if part:
-                        lse = jnp.where(chosen, r.lse[0:1, cols], lse)
-                        delta = jnp.where(chosen, r.delta_s[0:1, cols], delta)
-                    at = slice((2 * j + part) * half, (2 * j + part + 1) * half)
-                    p = jnp.exp(sc[at] - lse)
-                    r.p_s[at, cols] = p.astype(BF16)
-                    r.ds_s[at, cols] = (p * (dp[at] - delta)).astype(BF16)
-            r.gq_s[:, cols] += mm(kt, r.ds_s[rows, cols])
-        ek = mm_nt(r.ds_s[rows, :], r.qst[...])
-        ev = mm_nt(r.p_s[rows, :], r.gst_s[...])
-        for j in range(BATCH):
-            chosen = earlier(r.pairs, sel[j], me, LANES)
-            k = i * BATCH + 1 + j
-            for e, lanes in ((ek, slice(0, LANES)), (ev, slice(LANES, 2 * LANES))):
-                top = e[2 * j * half : (2 * j + 1) * half]
-                low = e[(2 * j + 1) * half : (2 * j + 2) * half]
-                r.send_s[k, :half, lanes] = (top[:, LANES:] + jnp.where(chosen, low[:, :LANES], 0.0)).astype(BF16)
-                r.send_s[k, half:, lanes] = jnp.where(chosen, 0.0, low[:, LANES:]).astype(BF16)
-            sum_copy(k).start()
-        return c
-
-    own = own_block()
-    lax.fori_loop(0, 3, step, 0)
-    arrived(out_factors)
-    share = D // st.nz
-    for j in range(0, TILES, 2):
-        cols = slice(j * LANES, min(j + 2, TILES) * LANES)
-        d = mm(r.attz[...], r.all_gm[:, cols]).astype(BF16)
-        for t in range(j, min(j + 2, TILES)):
-            r.dout[t * share : (t + 1) * share, :] = d[:, (t - j) * LANES : (t - j + 1) * LANES]
-    r.flush("dout")
-    if last:
-        qswap = attention.swap(before, r.n1z1, r.all_glin, r.all_small, r.dout1, r.qv, r.ql)
-    lax.fori_loop(3, (n - 1) // BATCH, step, 0)
-    if last:
-        attention.fold(qswap, r.qv, r.ql, (r.qpa, r.qpb))
-        r.flush("qpa", "qpb")
-    arrived(qkv_factor)
-    r.flush("n1z")
-
-    def take(k, total):
-        sum_copy(k).wait_recv()
-        return total + r.land_s[k].astype(F32)
-
-    own = lax.fori_loop(1, n, take, own)
-    r.need("cos", "sa", "sb", "x", "small", "dg2")
-    cos, sa, sb = r.cos[...], r.sa[...], r.sb[...]
-    for t in range(TILES):
-        gq = gathered_tile(r.gq_s[:, t * LANES : (t + 1) * LANES], t).T * HEAD_DIM ** (-0.5)
-        r.glin[:, t * LANES : (t + 1) * LANES] = unrope(gq, cos, sa, sb).astype(BF16)
-    r.glin[:, D : D + LANES] = unrope(own[:, :LANES], cos, sa, sb).astype(BF16)
-    r.glin[:, D + LANES :] = own[:, LANES:].astype(BF16)
-    r.flush("glin")
-    gn1 = mm_nt(r.glin[...], r.wa[:, :QKV])
-    x = r.x[...]
-    r1_ = lax.rsqrt(jnp.mean(x * x, -1, keepdims=True) + EPS)
-    unit = x * r1_
-    dz = gn1 * r.small[layer][:, :D]
-    r.gx[...] = gm + r1_ * (dz - unit * jnp.mean(dz * unit, -1, keepdims=True))
-    r.flush("gx")
-    dg1 = col_sum(gn1 * unit)
-    dbias = col_sum(r.glin[...].astype(F32))
-    r.gsmall[...] = jnp.zeros(r.gsmall.shape, F32)
-    row = 0
-    for part in (dg1, r.dg2[...], dbias):
-        for t in range(part.shape[1] // LANES):
-            r.gsmall[row : row + 1, :] = part[:, t * LANES : (t + 1) * LANES]
-            row += 1
-    r.flush("gsmall")
-    for h in range(2):
-        arrived(r1[h])
-        mine = sl[h].at[st.along(AXES[h][0], 0)]
-        add_into(t1[h], [mine] + [l1[h].at[k] for k in range(SIDE - 1)])
-    r.flush("t1a", "t1b")
-    st.drain()
-
-    def done(k, c):
-        sum_copy(k).wait_send()
-        return c
-
-    lax.fori_loop(1, n, done, 0)
-    r.close()
-
-
-def ffn_fwd_kernel(layer, r):
-    st = Stages(r)
-    n, me = st.nz, st.z
-    carry = layer == 0
-    st.hail(st.upright(carry) + (st.beside() + st.flat() if carry else []))
-    r.load()
-    if carry:
-        wa_local, wa = feed_attention(st, 1, r.wqkv_shard, r.wout_shard, r.wa)
-    r.need("n2")
-    r.all[me] = r.n2[...]
-    st.met()
-    at = st.take(2 * n)
-
-    def first(k):
-        return st.copy(r.all.at[me], r.all.at[me], at + k, st.peer("z", k))
-
-    def second(k):
-        return st.copy(r.send_s.at[k], r.land_s.at[k], at + n + k, st.peer("z", -k))
-
-    for k in ORDER:
-        first(k).start()
-    if carry:
-        wa_local.wait()
-        wa.start()
-    r.need("gu", "down", "mid")
-
-    def block(src):
-        a = r.all[src]
-        gate = mm(a, r.gu[0])
-        up = mm(a, r.gu[1])
-        r.gate[src] = gate
-        r.up[src] = up
-        hidden = (gate * jax.nn.sigmoid(gate) * up).astype(BF16)
-        return mm(hidden, r.down[...])
-
-    r.y[...] = r.mid[...] + block(me)
-    for k in ORDER:
-        first(k).wait_recv()
-        r.send_s[k] = block(st.along("z", -k)).astype(BF16)
-        second(k).start()
-        if carry and k == 3:
-            wa.relay(1)
-            wa.relay(3)
-    r.flush("all", "gate", "up")
-    if carry:
-        wa.relay(2)
-        for k in ORDER:
-            wa.collect(k)
-    for k in ORDER:
-        second(k).wait_recv()
-        r.y[...] += r.land_s[k].astype(F32)
-    r.flush("y")
-    for k in ORDER:
-        first(k).wait_send()
-        second(k).wait_send()
-    if carry:
-        wa.finish()
-        r.flush("wa")
-    st.drain()
-    r.close()
-
-
-def ffn_bwd_kernel(layer, r):
-    st = Stages(r)
-    n, me = st.nz, st.z
-    carry = layer == 0
-    st.hail(st.upright() + st.beside() + (st.flat(True) if carry else []))
-    r.load()
-    tok = r.gy.shape[0]
-
-    def rows_of(i):
-        return pl.ds(pl.multiple_of(i * tok, tok), tok)
-
-    r.need("gy")
-    r.all_s[rows_of(me), :] = r.gy[...].astype(BF16)
-    st.met()
-    at = st.take(2 * n)
-
-    def first(k):
-        mine = r.all_s.at[rows_of(me), :]
-        return st.copy(mine, mine, at + k, st.peer("z", k))
-
-    def second(k):
-        return st.copy(r.send_s.at[k], r.land_s.at[k], at + n + k, st.peer("z", -k))
-
-    for k in ORDER:
-        first(k).start()
-    if carry:
-        r.need("t1a", "t1b")
-        rest = Rest(st, (r.t1a, r.t1b), (r.l2a, r.l2b), (r.t2a, r.t2b), (r.g1a, r.g1b), (r.ga, r.gb), 1)
-    r.need("down", "gate", "up", "gu")
-
-    def block(src):
-        rows = rows_of(src)
-        gh = mm_nt(r.all_s[rows, :], r.down[...])
-        gate, up = r.gate[src], r.up[src]
-        sg = jax.nn.sigmoid(gate)
-        act = gate * sg
-        r.hid_s[rows, :] = (act * up).astype(BF16)
-        ggate = (gh * up * sg * (1.0 + gate * (1.0 - sg))).astype(BF16)
-        gup = (gh * act).astype(BF16)
-        r.g_s[0, rows, :] = ggate
-        r.g_s[1, rows, :] = gup
-        return mm_nt(ggate, r.gu[0]) + mm_nt(gup, r.gu[1])
-
-    r.own_s[...] = block(me)
-    for k in ORDER:
-        if carry:
-            rest.advance()
-        first(k).wait_recv()
-        r.send_s[k] = block(st.along("z", -k)).astype(BF16)
-        second(k).start()
-
-    refs = (r.fa, r.fb)
-    share = D // n
-    for j in range(WIN // (2 * LANES)):
-        cols = slice(2 * j * LANES, 2 * (j + 1) * LANES)
-        r.down_s[cols, :] = mm_tn(r.hid_s[:, cols], r.all_s[...]).astype(BF16)
-    pad = (WIN - FF // n) * lax.rem(me, 2)
-    half = FF // n // 2
-    base = [n * per * UNIT for per in GATE_PER]
-    for section in range(2):
-        rows = r.down_s[pl.ds(pl.multiple_of(pad + section * half, UNIT), half), :]
-        for t in range(TILES):
-            put_units(refs, section, base, DOWN_PER, t * (half // UNIT), rows[:, t * LANES : (t + 1) * LANES])
-        used = TILES * (half // UNIT)
-        extra = 16 * sum(DOWN_PER) - used
-        put_units(refs, section, base, DOWN_PER, used, jnp.zeros((extra * UNIT, LANES), BF16))
-    r.need("n2_all")
-    normed = jnp.concatenate([r.n2_all[i] for i in range(n)], 0)
-
-    def product(section):
-        for j in range(WIN // (2 * LANES)):
-            d = mm_tn(normed, r.g_s[section, :, 2 * j * LANES : 2 * (j + 1) * LANES]).astype(BF16)
-            for t in (2 * j, 2 * j + 1):
-                tile = d[:, (t % 2) * LANES : (t % 2 + 1) * LANES]
-                for i in range(n):
-                    base = [i * per * UNIT for per in GATE_PER]
-                    put_units(refs, section, base, GATE_PER, t * (share // UNIT), tile[i * share : (i + 1) * share, :])
-        used = WIN // LANES * (share // UNIT)
-        extra = 16 * sum(GATE_PER) - used
-        for i in range(n):
-            base = [i * per * UNIT for per in GATE_PER]
-            put_units(refs, section, base, GATE_PER, used, jnp.zeros((extra * UNIT, LANES), BF16))
-
-    product(1 - st.s)
-    swaps = [st.swap(refs[h], (r.sla, r.slb)[h]) for h in range(2)]
-    product(st.s)
-    for k in ORDER:
-        second(k).wait_recv()
-        r.own_s[...] += r.land_s[k].astype(F32)
-    gn2 = r.own_s[...]
-    r.need("mid", "small")
-    mid = r.mid[...]
-    r2 = lax.rsqrt(jnp.mean(mid * mid, -1, keepdims=True) + EPS)
-    unit = mid * r2
-    r.dg2[...] = col_sum(gn2 * unit)
-    dz = gn2 * r.small[layer][:, D : 2 * D]
-    r.gm[...] = r.gy[...] + r2 * (dz - unit * jnp.mean(dz * unit, -1, keepdims=True))
-    r.flush("dg2", "gm")
-    for h in range(2):
-        swapped_sum(st, swaps[h], refs[h], (r.sla, r.slb)[h])
-    r.flush("sla", "slb")
-    for k in ORDER:
-        first(k).wait_send()
-        second(k).wait_send()
-    if carry:
-        rest.finish()
-    st.drain()
-    r.close()
-
-
 class Rest:
     def __init__(self, st, t1, l2, t2, g1, out, layer):
         self.st, self.t1, self.l2, self.t2, self.g1, self.out, self.layer = st, t1, l2, t2, g1, out, layer
@@ -1129,68 +913,361 @@
                 self.moving[h] = st.hand_over(AXES[h][0], self.g1[h], self.out[h], self.layer)
         self.stage += 1
 
+    def landed(self):
+        for h in range(2):
+            arrived(self.moving[h])
+
     def finish(self):
         for h in range(2):
             self.moving[h]()
 
 
-def reduce_kernel(layer, r):
+class Few:
+    def __init__(self, st, r, tag):
+        self.st = st
+
+        def both(name):
+            return tuple(getattr(r, name + tag + h) for h in "ab")
+
+        self.qp, self.land, self.part, self.land2, self.wide = both("qp"), both("qm"), both("qe"), both("qw"), both("qh")
+        self.moving = [st.scatter(AXES[h][0], self.qp[h], self.land[h]) for h in range(2)]
+
+    def second_sum(self):
+        st = self.st
+        for h in range(2):
+            arrived(self.moving[h])
+            own = self.qp[h].at[st.along(AXES[h][0], 0)]
+            add_into(self.part[h], [own] + [self.land[h].at[k] for k in range(SIDE - 1)])
+            self.moving[h] = st.scatter(AXES[h][1], self.part[h], self.land2[h])
+
+    def first_gather(self):
+        st = self.st
+        for h in range(2):
+            arrived(self.moving[h])
+            i = st.along(AXES[h][1], 0)
+            add_rows(self.wide[h].at[i], [self.part[h].at[i]] + [self.land2[h].at[k] for k in range(SIDE - 1)])
+            self.moving[h] = st.gather(AXES[h][1], self.wide[h])
+
+    def landed(self):
+        for h in range(2):
+            arrived(self.moving[h])
+
+
+def backward_kernel(layer, r):
+    st = Stages(r)
+    n, me = st.nz, st.z
+    carry = layer == 0
+    ids = st.upright() + st.beside()
+    if carry:
+        ids += [st.peer(a, k, 1 - st.s) for a in "xy" for k in range(1, SIDE)]
+    st.hail(ids, ring=True)
+    r.load()
+    tok = r.gy.shape[0]
+
+    def rows_of(i):
+        return pl.ds(pl.multiple_of(i * tok, tok), tok)
+
+    r.need("gy")
+    gyb = r.gy[...].astype(BF16)
+    gy = gyb.astype(F32) if carry else r.gy[...]
+    if carry:
+        r.all_s[rows_of(me), :] = gyb
+    else:
+        r.need("all_s")
+    st.met()
+    at = st.take(2 * n)
+
+    def first(k):
+        mine = r.all_s.at[rows_of(me), :]
+        return st.copy(mine, mine, at + k, st.peer("z", k))
+
+    def second(k):
+        return st.copy(r.send_s.at[k], r.land_s.at[k], at + n + k, st.peer("z", -k))
+
+    if carry:
+        for k in ORDER:
+            first(k).start()
+        r.need("p1a", "p1b")
+        rest = Rest(st, (r.p1a, r.p1b), (r.l2a, r.l2b), (r.t2a, r.t2b), (r.g1a, r.g1b), (r.ga, r.gb), 1)
+    r.need("down", "gate", "up", "gu")
+
+    def block(src):
+        rows = rows_of(src)
+        gh = mm_nt(r.all_s[rows, :], r.down[...])
+        gate, up = r.gate[src].astype(F32), r.up[src].astype(F32)
+        sg = jax.nn.sigmoid(gate)
+        act = gate * sg
+        r.hid_s[rows, :] = (act * up).astype(BF16)
+        ggate = (gh * up * sg * (1.0 + gate * (1.0 - sg))).astype(BF16)
+        gup = (gh * act).astype(BF16)
+        r.g_s[0, rows, :] = ggate
+        r.g_s[1, rows, :] = gup
+        return mm_nt(ggate, r.gu[0]) + mm_nt(gup, r.gu[1])
+
+    r.own_s[...] = block(me)
+    for k in ORDER:
+        if carry:
+            rest.advance()
+            first(k).wait_recv()
+        r.send_s[k] = block(st.along("z", -k)).astype(BF16)
+        second(k).start()
+
+    refs = (r.fa, r.fb)
+    share = D // n
+    for j in range(WIN // (2 * LANES)):
+        cols = slice(2 * j * LANES, 2 * (j + 1) * LANES)
+        r.down_s[cols, :] = mm_tn(r.hid_s[:, cols], r.all_s[...]).astype(BF16)
+    pad = (WIN - FF // n) * lax.rem(me, 2)
+    half = FF // n // 2
+    base = [n * per * UNIT for per in GATE_PER]
+    for section in range(2):
+        rows = r.down_s[pl.ds(pl.multiple_of(pad + section * half, UNIT), half), :]
+        for t in range(TILES):
+            put_units(refs, section, base, DOWN_PER, t * (half // UNIT), rows[:, t * LANES : (t + 1) * LANES])
+        used = TILES * (half // UNIT)
+        extra = 16 * sum(DOWN_PER) - used
+        put_units(refs, section, base, DOWN_PER, used, jnp.zeros((extra * UNIT, LANES), BF16))
+    r.need("n2_all")
+    normed = jnp.concatenate([r.n2_all[i] for i in range(n)], 0)
+
+    def product(section):
+        for j in range(WIN // (2 * LANES)):
+            d = mm_tn(normed, r.g_s[section, :, 2 * j * LANES : 2 * (j + 1) * LANES]).astype(BF16)
+            for t in (2 * j, 2 * j + 1):
+                tile = d[:, (t % 2) * LANES : (t % 2 + 1) * LANES]
+                for i in range(n):
+                    base = [i * per * UNIT for per in GATE_PER]
+                    put_units(refs, section, base, GATE_PER, t * (share // UNIT), tile[i * share : (i + 1) * share, :])
+        used = WIN // LANES * (share // UNIT)
+        extra = 16 * sum(GATE_PER) - used
+        for i in range(n):
+            base = [i * per * UNIT for per in GATE_PER]
+            put_units(refs, section, base, GATE_PER, used, jnp.zeros((extra * UNIT, LANES), BF16))
+
+    product(1 - st.s)
+    swaps = [st.swap(refs[h], (r.sla, r.slb)[h]) for h in range(2)]
+    product(st.s)
+    for k in ORDER:
+        second(k).wait_recv()
+        r.own_s[...] += r.land_s[k].astype(F32)
+    gn2 = r.own_s[...]
+    r.need("mid", "small")
+    mid = r.mid[...]
+    r2 = lax.rsqrt(jnp.mean(mid * mid, -1, keepdims=True) + EPS)
+    unit = mid * r2
+    dg2 = col_sum(gn2 * unit)
+    dz = gn2 * r.small[layer][:, D : 2 * D]
+    gm = gy + r2 * (dz - unit * jnp.mean(dz * unit, -1, keepdims=True))
+    r.gm_s[...] = gm
+    for k in ORDER:
+        if carry:
+            first(k).wait_send()
+        second(k).wait_send()
+    attention_backward(st, r, layer, gm, dg2, refs, swaps, rest if carry else None)
+
+
+def attention_backward(st, r, layer, gm, dg2, refs, swaps, rest):
+    n, me = st.nc, st.c
+    last = layer == 0
+    half = HEAD_DIM
+    gmb = gm.astype(BF16)
+    tok = gm.shape[0]
+    r.all_gm[st.block(st.z, tok), :] = gmb
+    sl, l1, t1 = (r.sla, r.slb), (r.l1a, r.l1b), (r.t1a, r.t1b)
+    r.need("attt", "n1t")
+    attention = Attention(st)
+    size = 2 * BATCH * half
+    pr, ds, gst = r.g_s.at[0, :size, :WIDE], r.g_s.at[1, :size, :WIDE], r.hid_s.at[: 2 * LANES, :WIDE]
+    out_factors = attention.whole(r.all_gm) + attention.columns(r.attt, r.attz)
+    qkv_factor = attention.columns(r.n1t, r.n1z)
+    if last:
+        r.need("glin1", "gsmall1", "n1z1", "dout1")
+        before = attention.begin(r.glin1, r.gsmall1, r.all_glin, r.all_small)
+    r1 = []
+    for h in range(2):
+        swapped_sum(st, swaps[h], refs[h], sl[h])
+        r1.append(st.scatter(AXES[h][0], sl[h], l1[h]))
+    r.need("wa", "qst", "lse", "kv", "pairs")
+    ga = mm_nt(gmb, r.wa[:, QKV:])
+    for t in range(TILES):
+        tile = slice(t * LANES, (t + 1) * LANES)
+        ga_t = ga[:, tile].T
+        spread(gst, t, ga_t)
+        prod = ga_t * r.attt[tile, :].astype(F32)
+        low, high = halves(col_sum(prod[:half]), col_sum(prod[half:]))
+        r.delta_s[0:1, tile], r.delta_s[1:2, tile] = low, high
+
+    def own_block():
+        keys, vals = r.kv[me, :, :LANES].astype(F32), r.kv[me, :, LANES:].astype(F32)
+        kx, vx = own_sides(keys), own_sides(vals)
+        kt = kx.astype(F32).T.astype(BF16)
+        rows = slice(0, 3 * half)
+        for cols in GROUPS:
+            bias = own_bias(cols.stop - cols.start)
+            sc = mm(kx, r.qst[:, cols])
+            dp = mm(vx, gst[:, cols])
+            lo, hi = (r.lse[0:1, cols], r.delta_s[0:1, cols]), (r.lse[1:2, cols], r.delta_s[1:2, cols])
+            parts = [(sc[:half], hi), (sc[half : 2 * half] + bias, lo), (sc[2 * half :] + bias, hi)]
+            for i, (part, (lse, delta)) in enumerate(parts):
+                p = jnp.exp(part - lse)
+                at = slice(i * half, (i + 1) * half)
+                pr[at, cols] = p.astype(BF16)
+                ds[at, cols] = (p * (dp[at] - delta)).astype(BF16)
+            r.gq_s[:, cols] = mm(kt, ds[rows, cols])
+        made = []
+        for w, q in ((ds, r.qst), (pr, gst)):
+            e = mm_nt(w[rows, :], q[...])
+            low = e[:half, LANES:] + e[half : 2 * half, :LANES]
+            made.append(jnp.concatenate([low, e[2 * half :, LANES:]], 0))
+        return jnp.concatenate(made, 1)
+
+    def sum_copy(k):
+        return push(r.send_k.at[k], r.land_k.at[k], r.csem.at[k], r.csem2.at[k], "ctx", lax.rem(me + k, n))
+
+    def step(i):
+        kx, vx, kt, sel = [], [], [], []
+        for j in range(BATCH):
+            src = lax.rem(me + i * BATCH + 1 + j, n)
+            sel.append(src)
+            chosen = earlier(r.pairs, src, me, LANES)
+            keys = r.kv[src, :, :LANES].astype(F32)
+            kx.append(sides(keys, chosen))
+            vx.append(sides(r.kv[src, :, LANES:].astype(F32), chosen))
+            kt.append(sides_t(keys.T, chosen))
+        kx, vx, kt = jnp.concatenate(kx, 0), jnp.concatenate(vx, 0), jnp.concatenate(kt, 1)
+        rows = slice(0, 2 * BATCH * half)
+        for cols in GROUPS:
+            width = cols.stop - cols.start
+            sc = mm(kx, r.qst[:, cols])
+            dp = mm(vx, gst[:, cols])
+            for j in range(BATCH):
+                chosen = earlier(r.pairs, sel[j], me, width)
+                for part in range(2):
+                    lse, delta = r.lse[1:2, cols], r.delta_s[1:2, cols]
+                    if part:
+                        lse = jnp.where(chosen, r.lse[0:1, cols], lse)
+                        delta = jnp.where(chosen, r.delta_s[0:1, cols], delta)
+                    at = slice((2 * j + part) * half, (2 * j + part + 1) * half)
+                    p = jnp.exp(sc[at] - lse)
+                    pr[at, cols] = p.astype(BF16)
+                    ds[at, cols] = (p * (dp[at] - delta)).astype(BF16)
+            r.gq_s[:, cols] += mm(kt, ds[rows, cols])
+        ek = mm_nt(ds[rows, :], r.qst[...])
+        ev = mm_nt(pr[rows, :], gst[...])
+        for j in range(BATCH):
+            chosen = earlier(r.pairs, sel[j], me, LANES)
+            k = i * BATCH + 1 + j
+            for e, lanes in ((ek, slice(0, LANES)), (ev, slice(LANES, 2 * LANES))):
+                top = e[2 * j * half : (2 * j + 1) * half]
+                low = e[(2 * j + 1) * half : (2 * j + 2) * half]
+                r.send_k[k, :half, lanes] = (top[:, LANES:] + jnp.where(chosen, low[:, :LANES], 0.0)).astype(BF16)
+                r.send_k[k, half:, lanes] = jnp.where(chosen, 0.0, low[:, LANES:]).astype(BF16)
+            sum_copy(k).start()
+
+    own = own_block()
+    for i in range(3):
+        step(i)
+    arrived(out_factors)
+    share = D // st.nz
+    for j in range(0, TILES, 2):
+        cols = slice(j * LANES, min(j + 2, TILES) * LANES)
+        d = mm(r.attz[...], r.all_gm[:, cols]).astype(BF16)
+        for t in range(j, min(j + 2, TILES)):
+            r.dout[t * share : (t + 1) * share, :] = d[:, (t - j) * LANES : (t - j + 1) * LANES]
+    r.flush("dout")
+    if last:
+        rest.finish()
+        qswap = attention.swap(before, r.n1z1, r.all_glin, r.all_small, r.dout1, r.qv, r.ql)
+    for i in range(3, (n - 1) // BATCH):
+        step(i)
+    arrived(qkv_factor)
+    r.flush("n1z")
+    if last:
+        attention.fold(qswap, r.qv, r.ql, (r.qpa, r.qpb))
+        few = Few(st, r, "")
+        for h in range(2):
+            arrived(r1[h])
+            mine = sl[h].at[st.along(AXES[h][0], 0)]
+            add_into(t1[h], [mine] + [l1[h].at[k] for k in range(SIDE - 1)])
+        own_rest = Rest(st, t1, (r.l2c, r.l2d), (r.t2c, r.t2d), (r.g1c, r.g1d), None, 0)
+
+    def take(k, total):
+        sum_copy(k).wait_recv()
+        return total + r.land_k[k].astype(F32)
+
+    own = lax.fori_loop(1, n, take, own)
+    if last:
+        few.second_sum()
+        own_rest.advance()
+    r.need("cos", "sa", "sb", "x", "small")
+    cos, sa, sb = r.cos[...], r.sa[...], r.sb[...]
+    for t in range(TILES):
+        gq = gathered_tile(r.gq_s[:, t * LANES : (t + 1) * LANES], t).T * HEAD_DIM ** (-0.5)
+        r.glin[:, t * LANES : (t + 1) * LANES] = unrope(gq, cos, sa, sb).astype(BF16)
+    r.glin[:, D : D + LANES] = unrope(own[:, :LANES], cos, sa, sb).astype(BF16)
+    r.glin[:, D + LANES :] = own[:, LANES:].astype(BF16)
+    r.flush("glin")
+    gn1 = mm_nt(r.glin[...], r.wa[:, :QKV])
+    x = r.x[...]
+    r1_ = lax.rsqrt(jnp.mean(x * x, -1, keepdims=True) + EPS)
+    unit = x * r1_
+    dz = gn1 * r.small[layer][:, :D]
+    r.gx[...] = r.gm_s[...] + r1_ * (dz - unit * jnp.mean(dz * unit, -1, keepdims=True))
+    r.flush("gx")
+    dg1 = col_sum(gn1 * unit)
+    dbias = col_sum(r.glin[...].astype(F32))
+    r.gsmall[...] = jnp.zeros(r.gsmall.shape, F32)
+    row = 0
+    for part in (dg1, dg2, dbias):
+        for t in range(part.shape[1] // LANES):
+            r.gsmall[row : row + 1, :] = part[:, t * LANES : (t + 1) * LANES]
+            row += 1
+    r.flush("gsmall")
+    if last:
+        few.first_gather()
+        own_rest.advance()
+        own_rest.landed()
+        few.landed()
+    else:
+        for h in range(2):
+            arrived(r1[h])
+            mine = sl[h].at[st.along(AXES[h][0], 0)]
+            add_into(t1[h], [mine] + [l1[h].at[k] for k in range(SIDE - 1)])
+    st.drain()
+
+    def done(k, c):
+        sum_copy(k).wait_send()
+        return c
+
+    lax.fori_loop(1, n, done, 0)
+    r.close()
+
+
+def reduce_kernel(_, r):
     st = Stages(r)
     st.hail(st.beside() + st.upright() + st.flat(True))
     r.load()
-    r.need("t1a", "t1b", "q1a", "q1b", "glin", "gsmall")
-    qp = {1: (r.q1a, r.q1b), 0: (r.qpa, r.qpb)}
-    land = {1: (r.m1a, r.m1b), 0: (r.m0a, r.m0b)}
-    land2 = {1: (r.w1a, r.w1b), 0: (r.w0a, r.w0b)}
-    part = {1: (r.e1a, r.e1b), 0: (r.e0a, r.e0b)}
-    wide = {1: (r.h1a, r.h1b), 0: (r.h0a, r.h0b)}
-    out = (r.qa, r.qb)
-    moving = {}
-
-    def along_first(l):
-        moving[l] = [st.scatter(AXES[h][0], qp[l][h], land[l][h]) for h in range(2)]
-
-    def along_second(l):
-        for h in range(2):
-            arrived(moving[l][h])
-            own = qp[l][h].at[st.along(AXES[h][0], 0)]
-            add_into(part[l][h], [own] + [land[l][h].at[k] for k in range(SIDE - 1)])
-            moving[l][h] = st.scatter(AXES[h][1], part[l][h], land2[l][h])
-
-    def back_second(l):
-        for h in range(2):
-            arrived(moving[l][h])
-            i = st.along(AXES[h][1], 0)
-            add_rows(wide[l][h].at[i], [part[l][h].at[i]] + [land2[l][h].at[k] for k in range(SIDE - 1)])
-            moving[l][h] = st.gather(AXES[h][1], wide[l][h])
-
-    def back_first(l):
-        for h in range(2):
-            arrived(moving[l][h])
-            moving[l][h] = st.hand_over(AXES[h][0], wide[l][h], out[h], l)
-
+    r.need("glin", "gsmall")
+    attention = Attention(st)
     st.met()
-    attention = Attention(st)
     factors = attention.begin(r.glin, r.gsmall, r.all_glin, r.all_small)
-    rest = Rest(st, (r.t1a, r.t1b), (r.l2a, r.l2b), (r.t2a, r.t2b), (r.g1a, r.g1b), (r.ga, r.gb), 0)
-    along_first(1)
-    rest.advance()
-    along_second(1)
-    rest.advance()
-    back_second(1)
-    rest.advance()
+    r.need("g1a", "g1b", "h1a", "h1b")
+    last = []
+    for h in range(2):
+        last.append(st.hand_over(AXES[h][0], (r.g1a, r.g1b)[h], (r.ga, r.gb)[h], 0))
+    for h in range(2):
+        last.append(st.hand_over(AXES[h][0], (r.h1a, r.h1b)[h], (r.qa, r.qb)[h], 1))
     r.need("n1z", "dout")
     qswap = attention.swap(factors, r.n1z, r.all_glin, r.all_small, r.dout, r.qv, r.ql)
-    attention.fold(qswap, r.qv, r.ql, qp[0])
-    along_first(0)
-    back_first(1)
-    along_second(0)
-    back_second(0)
-    back_first(0)
-    rest.finish()
-    for l in (1, 0):
-        for h in range(2):
-            moving[l][h]()
+    attention.fold(qswap, r.qv, r.ql, (r.qpa, r.qpb))
+    few = Few(st, r, "")
+    few.second_sum()
+    few.first_gather()
+    for h in range(2):
+        arrived(few.moving[h])
+        last.append(st.hand_over(AXES[h][0], few.wide[h], (r.qa, r.qb)[h], 0))
+    for finish in last:
+        finish()
     st.drain()
     r.close()
 
@@ -1222,7 +1299,9 @@
     staged = [k for k in ins if k not in hbm]
     made = [k for k in outs if k not in hbm]
     dma = pltpu.SemaphoreType.DMA
-    counts = dict(ssem=sems, rsem=sems, lsem=12, csem=16, csem2=16, psem=16, psem2=16, isem=len(staged), osem=len(made))
+    counts = dict(ssem=sems, rsem=sems, lsem=16, csem=16, csem2=16, psem=16, psem2=16, isem=len(staged), osem=len(made))
+    if name == "forward":
+        counts.update(csem1=16, csem21=16)
     places = [pltpu.VMEM(ins[k].shape, ins[k].dtype) for k in staged] + [pltpu.VMEM(*outs[k]) for k in made]
     names = ["in_" + k for k in ins] + ["out_" + k for k in outs] + staged + made + list(scratch) + list(counts)
 
@@ -1365,110 +1444,105 @@
     return [(i * share // LANES) * LANES for i in range(n)]
 
 
-def attn_fwd(layer, x, shards, small, pair, pairs, tabs, wa):
+def forward(x, gy, shards, small, pair):
     n, nz = lax.axis_size("ctx"), lax.axis_size("fsdp")
     tok = x.shape[0]
-    ins = dict(x=x)
+    freq = jnp.arange(HEAD_DIM // 2, dtype=F32)
+    inverse = jnp.tile(THETA ** (-2.0 * freq / HEAD_DIM), 4)[None, :]
+    ins = dict(small_own=small, pair=pair, inverse=inverse, x0=x, gy=gy)
+    hbm = {k + "_shard": v for k, v in shards.items()}
+    ins.update(hbm)
     outs = dict(
-        mid=f4(tok, D), n2=bf(tok, D), n1t=bf(D, tok), qst=bf(2 * LANES, WIDE), kv=bf(n, tok, 2 * LANES), lse=f4(2, WIDE),
-        attt=bf(D, tok), gu=bf(2, D, WIN), down=bf(WIN, D),
+        small=f4(2, 1, SMALL), pairs=((n, 8, 2 * LANES), jnp.int32), cos=f4(tok, LANES), sa=f4(tok, LANES), sb=f4(tok, LANES),
+        x1=f4(tok, D), gy_all=bf(nz * tok, D),
     )
-    scratch = dict(m_s=f4(2, WIDE), l_s=f4(2, WIDE), acc_s=f4(2 * LANES, WIDE), att_s=bf(tok, D))
-    if layer == 0:
-        freq = jnp.arange(HEAD_DIM // 2, dtype=F32)
-        inverse = jnp.tile(THETA ** (-2.0 * freq / HEAD_DIM), 4)[None, :]
-        ins.update(small_own=small, pair=pair, inverse=inverse, wqkv_shard=shards["qkv"], wout_shard=shards["out"])
-        outs.update(
-            wa=bf(D, QKV + D), small=f4(2, 1, SMALL), pairs=((n, 8, 2 * LANES), jnp.int32),
-            cos=f4(tok, LANES), sa=f4(tok, LANES), sb=f4(tok, LANES),
+    scratch = dict(m_s=f4(2, WIDE), l_s=f4(2, WIDE), acc_s=f4(2 * LANES, WIDE), att_s=bf(tok, D), parts=f4(2, nz, 1, SMALL))
+    for l in "01":
+        each = dict(
+            mid=f4(tok, D), n1t=bf(D, tok), qst=bf(2 * LANES, WIDE), kv=bf(n, tok, 2 * LANES), lse=f4(2, WIDE),
+            attt=bf(D, tok), gu=bf(2, D, WIN), down=bf(WIN, D), wa=bf(D, QKV + D),
+            y=f4(tok, D), all=bf(nz, tok, D), gate=bf(nz, tok, WIN), up=bf(nz, tok, WIN),
         )
-        scratch.update(parts=f4(2, nz, 1, SMALL))
-    else:
-        ins.update(small=small, cos=tabs[0], sa=tabs[1], sb=tabs[2], wa=wa, pairs=pairs)
-    ins.update(gate_shard=shards["gate"], up_shard=shards["up"], down_shard=shards["down"])
-    hbm = ("wout_shard", "gate_shard", "up_shard", "down_shard", "wqkv_shard")
-    return call(attn_fwd_kernel, layer, 1 + layer, f"attn_fwd_{layer}", ins, outs, scratch, 64, hbm)
-
-
-def ffn_fwd(layer, a, shards):
-    n = lax.axis_size("fsdp")
-    tok = a["n2"].shape[0]
-    ins = {k: a[k] for k in ("n2", "gu", "down", "mid")}
-    outs = dict(y=f4(tok, D), all=bf(n, tok, D), gate=f4(n, tok, WIN), up=f4(n, tok, WIN))
-    if layer == 0:
-        ins.update(wqkv_shard=shards["qkv"], wout_shard=shards["out"])
-        outs.update(wa=bf(D, QKV + D))
-    scratch = dict(send_s=bf(n, tok, D), land_s=bf(n, tok, D))
-    return call(ffn_fwd_kernel, layer, 3 + layer, f"ffn_fwd_{layer}", ins, outs, scratch, 32, ("wqkv_shard", "wout_shard"))
-
-
-def ffn_bwd(layer, gy, a, f, small, before):
-    n = lax.axis_size("fsdp")
+        outs.update({k + l: v for k, v in each.items()})
+        scratch.update({"send_s" + l: bf(nz, tok, D), "land_s" + l: bf(nz, tok, D)})
+    return call(forward_kernel, 0, 1, "forward", ins, outs, scratch, 160, tuple(hbm))
+
+
+def backward(layer, gy, f, before):
+    n, nz = lax.axis_size("ctx"), lax.axis_size("fsdp")
     tok = gy.shape[0]
+    share = D // nz
+    own = {k: f[k + str(layer)] for k in ("down", "gate", "up", "gu", "all", "mid", "attt", "n1t", "qst", "lse", "kv", "wa")}
     ins = dict(gy=gy)
-    outs = dict(gm=f4(tok, D), dg2=f4(1, D))
-    scratch = dict(
-        all_s=bf(n * tok, D), hid_s=bf(n * tok, WIN), g_s=bf(2, n * tok, WIN), down_s=bf(WIN, D),
-        own_s=f4(tok, D), send_s=bf(n, tok, D), land_s=bf(n, tok, D),
-    )
-    for h, rows in zip("ab", FA_ROWS):
-        scratch["f" + h] = bf(2, *SIDES, rows, LANES)
-        outs["sl" + h] = bf(*SIDES, rows, LANES)
-    if layer == 0:
-        ins.update(t1a=before["t1a"], t1b=before["t1b"])
-        outs.update(rest_outs())
-        scratch.update(rest_scratch())
-    ins.update(down=a["down"], gate=f["gate"], up=f["up"], gu=a["gu"], n2_all=f["all"], mid=a["mid"], small=small)
-    return call(ffn_bwd_kernel, layer, 5 + layer, f"ffn_bwd_{layer}", ins, outs, scratch, 64, ("ga", "gb"), 2 * 10**10)
-
-
-def attn_bwd(layer, x, a, b, wa, small, pairs, tabs, before):
-    n, nz = lax.axis_size("ctx"), lax.axis_size("fsdp")
-    tok = x.shape[0]
-    share = D // nz
-    ins = dict(gm=b["gm"], sla=b["sla"], slb=b["slb"])
-    ins.update({k: a[k] for k in ("attt", "n1t")})
-    if layer == 0:
-        ins.update(glin1=before["glin"], gsmall1=before["gsmall"], n1z1=before["n1z"], dout1=before["dout"])
-    ins.update({k: a[k] for k in ("qst", "lse", "kv")})
-    ins.update(wa=wa, pairs=pairs, cos=tabs[0], sa=tabs[1], sb=tabs[2], x=x, small=small, dg2=b["dg2"])
     outs = dict(
         gx=f4(tok, D), glin=bf(tok, QKV), gsmall=f4(2 * UNIT, LANES), n1z=bf(share, nz * tok), dout=bf(TILES * share, LANES)
     )
     scratch = dict(
-        gst_s=bf(2 * LANES, WIDE), delta_s=f4(2, WIDE), gq_s=f4(2 * LANES, WIDE), all_gm=bf(nz * tok, D), attz=bf(share, nz * tok),
-        p_s=bf(2 * BATCH * HEAD_DIM, WIDE), ds_s=bf(2 * BATCH * HEAD_DIM, WIDE),
-        send_s=bf(n, tok, 2 * LANES), land_s=bf(n, tok, 2 * LANES),
+        hid_s=bf(nz * tok, WIN), g_s=bf(2, nz * tok, WIN), down_s=bf(WIN, D), gm_s=f4(tok, D),
+        own_s=f4(tok, D), send_s=bf(nz, tok, D), land_s=bf(nz, tok, D),
+        delta_s=f4(2, WIDE), gq_s=f4(2 * LANES, WIDE), all_gm=bf(nz * tok, D), attz=bf(share, nz * tok),
+        send_k=bf(n, tok, 2 * LANES), land_k=bf(n, tok, 2 * LANES),
     )
     for h, rows in zip("ab", FA_ROWS):
-        outs["t1" + h] = bf(SIDE, rows, LANES)
+        scratch["f" + h] = bf(2, *SIDES, rows, LANES)
+        scratch["sl" + h] = bf(*SIDES, rows, LANES)
         scratch["l1" + h] = bf(SIDE - 1, SIDE, rows, LANES)
     if layer == 0:
+        scratch["all_s"] = bf(nz * tok, D)
+        ins.update(p1a=before["t1a"], p1b=before["t1b"])
+        scratch.update(rest_scratch())
+        outs.update(rest_outs())
+    else:
+        ins["all_s"] = f["gy_all"]
+    ins.update(down=own["down"], gate=own["gate"], up=own["up"], gu=own["gu"], n2_all=own["all"], mid=own["mid"])
+    ins["small"] = f["small"]
+    ins.update({k: own[k] for k in ("attt", "n1t")})
+    if layer == 0:
+        ins.update(glin1=before["glin"], gsmall1=before["gsmall"], n1z1=before["n1z"], dout1=before["dout"])
         scratch.update(attention_scratch(tok))
-        outs.update(qpa=bf(*SIDES, RQ, LANES), qpb=bf(*SIDES, RQ, LANES))
-    return call(attn_bwd_kernel, layer, 7 + layer, f"attn_bwd_{layer}", ins, outs, scratch, 48, flops=2 * 10**10)
+        scratch.update(few_scratch())
+        scratch.update(t1a=bf(SIDE, FA_ROWS[0], LANES), t1b=bf(SIDE, FA_ROWS[1], LANES))
+        for h, rows in zip("cd", FA_ROWS):
+            scratch["l2" + h] = bf(SIDE - 1, rows, LANES)
+            scratch["t2" + h] = bf(rows, LANES)
+            outs["g1" + h] = bf(SIDE, rows, LANES)
+        for h in "ab":
+            outs["qh" + h] = bf(SIDE, RQ, LANES)
+    else:
+        outs.update(t1a=bf(SIDE, FA_ROWS[0], LANES), t1b=bf(SIDE, FA_ROWS[1], LANES))
+    ins.update({k: own[k] for k in ("qst", "lse", "kv", "wa")})
+    ins.update({k: f[k] for k in ("pairs", "cos", "sa", "sb")})
+    ins["x"] = f["x" + str(layer)] if layer else before["x0"]
+    return call(backward_kernel, layer, 2 + layer, f"backward_{layer}", ins, outs, scratch, 112, ("ga", "gb"), 3 * 10**10)
 
 
 def attention_scratch(tok):
     nz = lax.axis_size("fsdp")
-    return dict(all_glin=bf(nz * tok, QKV), all_small=f4(nz * 2 * UNIT, LANES), qv=bf(2, Q_ROWS, LANES), ql=bf(Q_ROWS, LANES))
+    return dict(
+        all_glin=bf(nz * tok, QKV), all_small=f4(nz * 2 * UNIT, LANES), qv=bf(2, Q_ROWS, LANES), ql=bf(Q_ROWS, LANES),
+        qpa=bf(*SIDES, RQ, LANES), qpb=bf(*SIDES, RQ, LANES),
+    )
+
+
+def few_scratch():
+    made = {}
+    for h in "ab":
+        made["qm" + h] = bf(SIDE - 1, SIDE, RQ, LANES)
+        made["qw" + h] = bf(SIDE - 1, RQ, LANES)
+        made["qe" + h] = bf(SIDE, RQ, LANES)
+    return made
 
 
 def reduce_rest(last):
-    ins = dict(glin=last["glin"], gsmall=last["gsmall"], t1a=last["t1a"], t1b=last["t1b"], q1a=last["qpa"], q1b=last["qpb"])
+    ins = dict(glin=last["glin"], gsmall=last["gsmall"], g1a=last["g1c"], g1b=last["g1d"], h1a=last["qha"], h1b=last["qhb"])
     ins.update(n1z=last["n1z"], dout=last["dout"])
     outs = rest_outs()
-    scratch = rest_scratch()
-    scratch.update(attention_scratch(last["glin"].shape[0]))
-    scratch.update(qpa=bf(*SIDES, RQ, LANES), qpb=bf(*SIDES, RQ, LANES))
+    scratch = attention_scratch(last["glin"].shape[0])
+    scratch.update(few_scratch())
     for h in "ab":
         outs["q" + h] = bf(2, *SIDES, RQ, LANES)
-        for l in "01":
-            scratch["m" + l + h] = bf(SIDE - 1, SIDE, RQ, LANES)
-            scratch["w" + l + h] = bf(SIDE - 1, RQ, LANES)
-            scratch["e" + l + h] = bf(SIDE, RQ, LANES)
-            scratch["h" + l + h] = bf(SIDE, RQ, LANES)
-    return call(reduce_kernel, 0, 9, "reduce", ins, outs, scratch, 128, ("ga", "gb", "qa", "qb"))
+        scratch["qh" + h] = bf(SIDE, RQ, LANES)
+    return call(reduce_kernel, 0, 9, "reduce", ins, outs, scratch, 96, ("ga", "gb", "qa", "qb"))
 
 
 def local(
@@ -1487,21 +1561,12 @@
     small_own = jnp.concatenate([placed(attn_gain, D), placed(ffn_gain, D), placed(qkv_bias, QKV)], 1)
     pair = jnp.broadcast_to(pair_of.reshape(1, 1), (8, 2 * LANES))
     x0 = jnp.where(s == 0, tokens[0, 0], tokens[1, 0])
-    a0 = attn_fwd(0, x0, shards, small_own, pair, None, None, None)
-    small, pairs, tabs = a0["small"], a0["pairs"], (a0["cos"], a0["sa"], a0["sb"])
-    f0 = ffn_fwd(0, a0, shards)
-    x1 = f0["y"].astype(BF16).astype(F32)
-    a1 = attn_fwd(1, x1, shards, small, None, pairs, tabs, f0["wa"])
-    f1 = ffn_fwd(1, a1, None)
-
     gy = jnp.where(s == 0, cotangent[0, 0], cotangent[1, 0])
-    b1 = ffn_bwd(1, gy, a1, f1, small, None)
-    c1 = attn_bwd(1, x1, a1, b1, f0["wa"], small, pairs, tabs, None)
-    gy = c1["gx"].astype(BF16).astype(F32)
-    b0 = ffn_bwd(0, gy, a0, f0, small, c1)
-    c0 = attn_bwd(0, x0, a0, b0, a0["wa"], small, pairs, tabs, c1)
+    f = forward(x0, gy, shards, small_own, pair)
+    c1 = backward(1, gy, f, None)
+    c0 = backward(0, c1["gx"], f, dict(c1, x0=x0))
     t = reduce_rest(c0)
-    dgate, dup, ddown, dqkv, dout, small_grad = assemble((t["ga"], t["gb"]), (b0["ga"], b0["gb"]), (t["qa"], t["qb"]))
+    dgate, dup, ddown, dqkv, dout, small_grad = assemble((t["ga"], t["gb"]), (c0["ga"], c0["gb"]), (t["qa"], t["qb"]))
     small_grad = small_grad.reshape(-1)
 
     def mine(first, size):
@@ -1514,7 +1579,7 @@
         return jnp.where(s == 0, jnp.stack([mine, got]), jnp.stack([got, mine]))[None, :, None]
 
     return (
-        by_layer((f0["y"], f1["y"])),
+        by_layer((f["y0"], f["y1"])),
         by_layer((c0["gx"], c1["gx"])),
         mine(0, qd),
         mine(D, qd),

time: 449 us -> 378 us (0.84)
  Pallas kernels: 423 us -> 358 us
    pallas_call x9 -> x4, Pallas kernels: 413 us -> 348 us  [call(): pl.pallas_call(body, out_shape=[jax.ShapeDtypeStruct(s, t) for s, t in ou...]
  transfers between devices with their start and end apart: 2 -> 2, of which waited for: 0 -> 0; matrix products, arithmetic and copies ran while one was open for 1% -> 1% of each run, Pallas kernels for 20% -> 59%
where the time goes in v5:
time: 378 us; the launch traced here: 373 us
  Pallas kernels  358 us (95%)
  other arithmetic  9.39 us (2%)
  local copies, waits for them, and re-layouts  4.43 us (1%)
    pallas_call x4, Pallas kernels, call(): pl.pallas_call(body, out_shape=[jax.ShapeDtypeStruct(s, t) for s, t in ou...  348 us
    pallas_call x1, Pallas kernels, assemble(): pl.pallas_call(functools.partial(assemble_kernel, nz), out_shape=[jax.Sha...  9.85 us
  transfers between devices with their start and end apart: 2, of which 0 were waited for; matrix products, arithmetic and copies ran while one was open for 1% of the time, Pallas kernels for 59%

profile of v5, /device:TPU:0, one launch (start us, length us, event | category | flops | bytes accessed | tf_op | source)
XLA Modules:
  0.0 373.5 jit_solution(16432602259789109661)
XLA Ops:
  1.3 0.7 convert_element_type.9
  2.0 0.7 convert_element_type.10
  2.7 0.6 broadcast_in_dim_tile.3.refs_2_
  3.3 0.7 convert_element_type.11
  4.0 0.1 dynamic_update_slice.10
  4.1 0.2 dynamic_update_slice.9
  4.3 0.2 dynamic_update_slice.11
  4.5 0.6 pad_maximum_fusion.refs_0_
  5.1 2.4 select_bitcast_fusion.2
  7.5 0.6 broadcast_in_dim.38.refs_1_
  8.1 135.8 %forward.1 = (f32[2,1,2944]{2,1,0:T(1,128)}, s32[16,8,256]{2,1,0:T(8,128)}, f32[128,128]{1,0:T(8,128)}, f32[128,128]{1,0:T(8,128)}, f32[128,128]{1,0:T(8,128)}, ...) custom-call(f32[1,2944]{1,0:T(1,128)} %pad_maximum_fusion.refs_0_, ...), custom_call_target="tpu_custom_call" | custom-call | flops 10000000000 | bytes 20971520 | tf_op jit(solution)/shard_map/forward/pallas_call | solution.py:1323
  144.0 1.2 select_bitcast_fusion.1
  145.2 0.1 collective-permute-start
  145.3 64.5 %backward_1.1 = (f32[128,896]{1,0:T(8,128)}, bf16[128,1152]{1,0:T(8,128)(2,1)}, f32[32,128]{1,0:T(8,128)}, bf16[224,512]{1,0:T(8,128)(2,1)}, bf16[1568,128]{1,0:...) custom-call(f32[128,896]{1,0:T(8,128)} %get-tuple-element.138.refs_4_.refs_0_, ...), custom_call_target="tpu_custom_call" | custom-call | flops 30000001024 | bytes 20971520 | tf_op jit(solution)/shard_map/backward_1/pallas_call | solution.py:1323
  209.8 0.0 copy-start
  209.8 100.6 %backward_0.1 = (f32[128,896]{1,0:T(8,128)}, bf16[128,1152]{1,0:T(8,128)(2,1)}, f32[32,128]{1,0:T(8,128)}, bf16[224,512]{1,0:T(8,128)(2,1)}, bf16[1568,128]{1,0:...) custom-call(f32[128,896]{1,0:T(8,128)} %get-tuple-element.92.refs_0_, ...), custom_call_target="tpu_custom_call" | custom-call | flops 30000001024 | bytes 20971520 | tf_op jit(solution)/shard_map/backward_0/pallas_call | solution.py:1323
  310.5 0.0 copy-done
  310.5 1.1 select_bitcast_fusion
  311.5 0.3 collective-permute-start.1
  311.8 46.9 %reduce.1 = (bf16[2,4,4,448,128]{4,3,2,1,0:T(8,128)(2,1)}, bf16[2,4,4,400,128]{4,3,2,1,0:T(8,128)(2,1)}, bf16[2,4,4,64,128]{4,3,2,1,0:T(8,128)(2,1)}, bf16[2,4,4,64,128]{4,3,2,1,0:T(8,128)(2,1)}) custom-call(bf16[128,1152]{1,0:T(8,128)(2,1)} %get-tuple-element.112.refs_0_, f32[32,128]{1,0:T(8,128)} %get-tuple-element.113.refs_1_, ...), custom_call_target="tpu_custom_call" | custom-call | flops 10000000000 | bytes 20971520 | tf_op jit(solution)/shard_map/reduce/pallas_call | solution.py:1323
  358.7 9.8 %assemble.1 = (f32[224,4864]{1,0:T(8,128)}, f32[224,4864]{1,0:T(8,128)}, f32[1216,896]{1,0:T(8,128)}, f32[224,1152]{1,0:T(8,128)}, f32[224,896]{1,0:T(8,128)}, /*index=5*/f32[32,128]{1,0:T(8,128)}) custom-call(bf16[2,4,4,448,128]{4,3,2,1,0:T(8,128)(2,1)} %get-tuple-element.120.refs_0_, bf16[2,4,4,400,128]{4,3,2,1,0:T(8,128)(2,1)} %get-tuple-element.121.refs_1_, ...), custom_call_target="tpu_custom_call" | custom-call | tf_op jit(solution)/shard_map/assemble/pallas_call | solution.py:1429
  368.6 0.8 dynamic_slice.11
  369.3 0.6 broadcast_in_dim.42
  369.9 1.4 fusion
  371.3 0.0 collective-permute-done
  371.3 1.0 maximum_select_fusion
  372.3 0.0 collective-permute-done.1
  372.3 1.0 maximum_select_fusion.1
  (5 shorter events, 0.0 us)
Async XLA Ops:
  145.2 226.1 %collective-permute-start = (f32[128,896]{1,0:T(8,128)S(1)}, f32[128,896]{1,0:T(8,128)S(1)}, u32[]{:S(2)}, u32[]{:S(2)}) collective-permute-start(f32[128,896]{1,0:T(8,128)S(1)} %get-tuple-element.135), channel_id=1, source_target_pairs={{0,64},{64,0},{1,65},{65,1},{2,66},{66,2},{3,67},{67,3},{4,68},{68... | collective-permute-start | bytes 1376264 | tf_op jit(solution)/shard_map/ppermute | solution.py:1578
  209.8 100.7 %copy-start = (f32[128,896]{1,0:T(8,128)S(1)}, f32[128,896]{1,0:T(8,128)}, u32[]{:S(2)}) copy-start(f32[128,896]{1,0:T(8,128)} %get-tuple-element.92.refs_0_) | copy-start | bytes 1376260
  311.5 60.8 %collective-permute-start.1 = (f32[128,896]{1,0:T(8,128)S(1)}, f32[128,896]{1,0:T(8,128)S(1)}, u32[]{:S(2)}, u32[]{:S(2)}) collective-permute-start(f32[128,896]{1,0:T(8,128)S(1)} %get-tuple-element.133), channel_id=1, source_target_pairs={{0,64},{64,0},{1,65},{65,1},{2,66},{66,2},{3,67},{67,3},{4,68},{68... | collective-permute-start | bytes 1376264 | tf_op jit(solution)/shard_map/ppermute | solution.py:1578

commit v6 on v5

--- a/solution.py
+++ b/solution.py
@@ -3,6 +3,7 @@
 
 import jax
 import jax.numpy as jnp
+import numpy as np
 from jax import lax
 from jax.experimental import pallas as pl
 from jax.experimental.pallas import tpu as pltpu
@@ -247,9 +248,11 @@
     def quarter(self):
         return self.x * (1 - self.s) + self.y * self.s
 
-    def hand_over(self, axis, src, dst, layer):
+    def hand_over(self, axis, src, dst, layer, part=None):
         at = self.take(2 * SIDE)
         mine = dst.at[self.s, self.along(axis, 0)]
+        if part is not None:
+            src, mine = src.at[part], mine.at[part]
         self.begin(
             [
                 self.copy(src, mine, at + k, self.peer(axis, k, layer), at + self.s * SIDE + k)
@@ -381,6 +384,25 @@
             self.remote.wait_recv()
 
 
+class Delivery:
+    def __init__(self, st, layer, src, out):
+        self.st, self.layer = st, layer
+        mine = out.at[st.s]
+        self.within = pltpu.make_async_copy(src, mine, st.lsem.at[st.local_used])
+        st.local_used += 1
+        self.over = st.copy(src, mine, st.take(1), st.peer("s", 0))
+        pl.when(st.s == layer)(self.within.start)
+        pl.when(st.s != layer)(self.over.start)
+
+    def finish(self):
+        @pl.when(self.st.s == self.layer)
+        def _():
+            self.within.wait()
+            self.over.wait_recv()
+
+        pl.when(self.st.s != self.layer)(self.over.wait_send)
+
+
 class Local:
     def __init__(self, st, layer, pairs):
         self.st, self.layer = st, layer
@@ -541,9 +563,15 @@
         wa[l] = feed_attention(st, l, r.qkv_shard, r.out_shard, v.wa)
         gu[l] = feed_windows(st, l, r.gate_shard, r.up_shard, v.gu)
         down[l] = FeedDown(st, l, r.down_shard, v.down)
-    r.need("pair", "small_own", "inverse", "x0")
-    r.pairs[me] = jnp.broadcast_to(r.pair[...], r.pairs.shape[1:])
-    r.parts[st.s, st.z] = r.small_own[...]
+    r.need("inverse", "x0")
+    r.pairs[me] = jnp.full(r.pairs.shape[1:], r.pair[0], jnp.int32)
+    at = 0
+    for part, size in ((r.attn_gain, D), (r.ffn_gain, D), (r.qkv_bias, QKV)):
+        share = part.shape[1]
+        line = jnp.concatenate([part[...].astype(F32), jnp.zeros((1, size - share), F32)], 1)
+        line = pltpu.roll(jnp.broadcast_to(line, (8, size)), st.z * share, 1)
+        r.parts[st.s, st.z, :, at : at + size] = line[:1]
+        at += size
     wa[0][0].wait()
     st.met()
     wa[0][1].start()
@@ -635,7 +663,8 @@
         ),
     )
     r.x1[...] = r.y0[...].astype(BF16).astype(F32)
-    r.flush("y0", "x1")
+    r.flush("x1")
+    done_0 = Delivery(st, 0, r.y0, r.layer_out)
     r.need("gy")
     tok = r.gy.shape[0]
     rows = st.block(st.z, tok)
@@ -655,9 +684,11 @@
         v.flush("gu", "down")
 
     ffn_forward(st, v, ready_1, (nothing,) * 4)
-    r.flush("y1")
+    done_1 = Delivery(st, 1, r.y1, r.layer_out)
     arrived(gy_moving)
     r.flush("gy_all")
+    done_0.finish()
+    done_1.finish()
     st.drain()
 
     def done(k, c):
@@ -801,21 +832,31 @@
         first(k).start()
     ready()
 
-    def block(src):
-        a = r.all[src]
+    tok = r.mid.shape[0]
+
+    def block(sources):
+        a = jnp.concatenate([r.all[i] for i in sources], 0) if len(sources) > 1 else r.all[sources[0]]
         gate = mm(a, r.gu[0])
         up = mm(a, r.gu[1])
-        r.gate[src] = gate.astype(BF16)
-        r.up[src] = up.astype(BF16)
+        for j, i in enumerate(sources):
+            r.gate[i] = gate[j * tok : (j + 1) * tok].astype(BF16)
+            r.up[i] = up[j * tok : (j + 1) * tok].astype(BF16)
         hidden = (gate * jax.nn.sigmoid(gate) * up).astype(BF16)
         return mm(hidden, r.down[...])
 
-    r.y[...] = r.mid[...] + block(me)
-    for i, k in enumerate(ORDER):
-        between[i]()
-        first(k).wait_recv()
-        r.send_s[k] = block(st.along("z", -k)).astype(BF16)
+    r.y[...] = r.mid[...] + block([me])
+    between[0]()
+    first(1).wait_recv()
+    first(3).wait_recv()
+    both = block([st.along("z", -1), st.along("z", -3)]).astype(BF16)
+    for i, k in enumerate((1, 3)):
+        r.send_s[k] = both[i * tok : (i + 1) * tok]
         second(k).start()
+    between[1]()
+    first(2).wait_recv()
+    r.send_s[2] = block([st.along("z", -2)]).astype(BF16)
+    second(2).start()
+    between[2]()
     r.flush("all", "gate", "up")
     between[3]()
     for k in ORDER:
@@ -844,11 +885,11 @@
         mine[...] = src[st.block(st.z, share), :]
         return moving
 
-    def whole(self, dst):
+    def whole(self, dst, cols=slice(None)):
         st = self.st
         rows = dst.shape[0] // st.nz
         at = st.take(st.nz - 1)
-        mine = dst.at[pl.ds(pl.multiple_of(st.z * rows, UNIT), rows), :]
+        mine = dst.at[pl.ds(pl.multiple_of(st.z * rows, UNIT), rows), cols]
         return st.begin([st.copy(mine, mine, at + k - 1, st.peer("z", k)) for k in range(1, st.nz)])
 
     def begin(self, glin, small, all_glin, all_small):
@@ -910,16 +951,17 @@
             elif self.stage == 1:
                 self.moving[h] = st.gather(second, self.g1[h])
             else:
-                self.moving[h] = st.hand_over(AXES[h][0], self.g1[h], self.out[h], self.layer)
+                self.moving[h] = st.hand_over(AXES[h][0], self.g1[h], self.out[h], self.layer, slice(0, SIDE // 2))
         self.stage += 1
 
-    def landed(self):
-        for h in range(2):
-            arrived(self.moving[h])
+    def second_half(self):
+        self.ends = self.moving + [
+            self.st.hand_over(AXES[h][0], self.g1[h], self.out[h], self.layer, slice(SIDE // 2, SIDE)) for h in range(2)
+        ]
 
     def finish(self):
-        for h in range(2):
-            self.moving[h]()
+        for end in self.ends:
+            end()
 
 
 class Few:
@@ -948,9 +990,10 @@
             add_rows(self.wide[h].at[i], [self.part[h].at[i]] + [self.land2[h].at[k] for k in range(SIDE - 1)])
             self.moving[h] = st.gather(AXES[h][1], self.wide[h])
 
-    def landed(self):
+    def hand_over(self, out, layer):
         for h in range(2):
             arrived(self.moving[h])
+        return [self.st.hand_over(AXES[h][0], self.wide[h], out[h], layer) for h in range(2)]
 
 
 def backward_kernel(layer, r):
@@ -970,6 +1013,7 @@
     r.need("gy")
     gyb = r.gy[...].astype(BF16)
     gy = gyb.astype(F32) if carry else r.gy[...]
+    above = None
     if carry:
         r.all_s[rows_of(me), :] = gyb
     else:
@@ -987,41 +1031,69 @@
     if carry:
         for k in ORDER:
             first(k).start()
+        above = Delivery(st, 1, r.gy, r.input_grad)
         r.need("p1a", "p1b")
         rest = Rest(st, (r.p1a, r.p1b), (r.l2a, r.l2b), (r.t2a, r.t2b), (r.g1a, r.g1b), (r.ga, r.gb), 1)
     r.need("down", "gate", "up", "gu")
 
-    def block(src):
-        rows = rows_of(src)
-        gh = mm_nt(r.all_s[rows, :], r.down[...])
-        gate, up = r.gate[src].astype(F32), r.up[src].astype(F32)
+    def block(sources):
+        def stacked(ref):
+            parts = [ref[rows_of(i), :] for i in sources]
+            return jnp.concatenate(parts, 0) if len(parts) > 1 else parts[0]
+
+        def picked(ref):
+            parts = [ref[i].astype(F32) for i in sources]
+            return jnp.concatenate(parts, 0) if len(parts) > 1 else parts[0]
+
+        def keep(ref, value):
+            for j, i in enumerate(sources):
+                ref[rows_of(i), :] = value[j * tok : (j + 1) * tok]
+
+        gh = mm_nt(stacked(r.all_s), r.down[...])
+        gate, up = picked(r.gate), picked(r.up)
         sg = jax.nn.sigmoid(gate)
         act = gate * sg
-        r.hid_s[rows, :] = (act * up).astype(BF16)
+        keep(r.hid_s, (act * up).astype(BF16))
         ggate = (gh * up * sg * (1.0 + gate * (1.0 - sg))).astype(BF16)
         gup = (gh * act).astype(BF16)
-        r.g_s[0, rows, :] = ggate
-        r.g_s[1, rows, :] = gup
+        keep(r.g_s.at[0], ggate)
+        keep(r.g_s.at[1], gup)
         return mm_nt(ggate, r.gu[0]) + mm_nt(gup, r.gu[1])
 
-    r.own_s[...] = block(me)
-    for k in ORDER:
-        if carry:
-            rest.advance()
-            first(k).wait_recv()
-        r.send_s[k] = block(st.along("z", -k)).astype(BF16)
+    r.own_s[...] = block([me])
+    if carry:
+        rest.advance()
+        first(1).wait_recv()
+        first(3).wait_recv()
+    both = block([st.along("z", -1), st.along("z", -3)]).astype(BF16)
+    for i, k in enumerate((1, 3)):
+        r.send_s[k] = both[i * tok : (i + 1) * tok]
         second(k).start()
-
+    if carry:
+        rest.advance()
+        first(2).wait_recv()
+    r.send_s[2] = block([st.along("z", -2)]).astype(BF16)
+    second(2).start()
+    if carry:
+        rest.advance()
+
+    late = [
+        pltpu.make_async_copy(r.wa.at[:, :QKV], r.gu.at[0, :, :QKV], st.lsem.at[st.local_used]),
+        pltpu.make_async_copy(r.wa.at[:, QKV:], r.gu.at[1, :, :D], st.lsem.at[st.local_used + 1]),
+    ]
+    st.local_used += 2
+    for c in late:
+        c.start()
     refs = (r.fa, r.fb)
     share = D // n
     for j in range(WIN // (2 * LANES)):
         cols = slice(2 * j * LANES, 2 * (j + 1) * LANES)
-        r.down_s[cols, :] = mm_tn(r.hid_s[:, cols], r.all_s[...]).astype(BF16)
+        r.down[cols, :] = mm_tn(r.hid_s[:, cols], r.all_s[...]).astype(BF16)
     pad = (WIN - FF // n) * lax.rem(me, 2)
     half = FF // n // 2
     base = [n * per * UNIT for per in GATE_PER]
     for section in range(2):
-        rows = r.down_s[pl.ds(pl.multiple_of(pad + section * half, UNIT), half), :]
+        rows = r.down[pl.ds(pl.multiple_of(pad + section * half, UNIT), half), :]
         for t in range(TILES):
             put_units(refs, section, base, DOWN_PER, t * (half // UNIT), rows[:, t * LANES : (t + 1) * LANES])
         used = TILES * (half // UNIT)
@@ -1045,6 +1117,8 @@
             put_units(refs, section, base, GATE_PER, used, jnp.zeros((extra * UNIT, LANES), BF16))
 
     product(1 - st.s)
+    if carry:
+        rest.second_half()
     swaps = [st.swap(refs[h], (r.sla, r.slb)[h]) for h in range(2)]
     product(st.s)
     for k in ORDER:
@@ -1063,10 +1137,10 @@
         if carry:
             first(k).wait_send()
         second(k).wait_send()
-    attention_backward(st, r, layer, gm, dg2, refs, swaps, rest if carry else None)
-
-
-def attention_backward(st, r, layer, gm, dg2, refs, swaps, rest):
+    attention_backward(st, r, layer, gm, dg2, refs, swaps, rest if carry else None, above, late)
+
+
+def attention_backward(st, r, layer, gm, dg2, refs, swaps, rest, above, late):
     n, me = st.nc, st.c
     last = layer == 0
     half = HEAD_DIM
@@ -1087,8 +1161,10 @@
     for h in range(2):
         swapped_sum(st, swaps[h], refs[h], sl[h])
         r1.append(st.scatter(AXES[h][0], sl[h], l1[h]))
-    r.need("wa", "qst", "lse", "kv", "pairs")
-    ga = mm_nt(gmb, r.wa[:, QKV:])
+    r.need("qst", "lse", "kv", "pairs")
+    for c in late:
+        c.wait()
+    ga = mm_nt(gmb, r.gu[1, :, :D])
     for t in range(TILES):
         tile = slice(t * LANES, (t + 1) * LANES)
         ga_t = ga[:, tile].T
@@ -1174,60 +1250,85 @@
         d = mm(r.attz[...], r.all_gm[:, cols]).astype(BF16)
         for t in range(j, min(j + 2, TILES)):
             r.dout[t * share : (t + 1) * share, :] = d[:, (t - j) * LANES : (t - j + 1) * LANES]
-    r.flush("dout")
+    if not last:
+        r.flush("dout")
     if last:
-        rest.finish()
         qswap = attention.swap(before, r.n1z1, r.all_glin, r.all_small, r.dout1, r.qv, r.ql)
     for i in range(3, (n - 1) // BATCH):
         step(i)
     arrived(qkv_factor)
-    r.flush("n1z")
     if last:
+        rest.finish()
         attention.fold(qswap, r.qv, r.ql, (r.qpa, r.qpb))
         few = Few(st, r, "")
         for h in range(2):
             arrived(r1[h])
             mine = sl[h].at[st.along(AXES[h][0], 0)]
             add_into(t1[h], [mine] + [l1[h].at[k] for k in range(SIDE - 1)])
-        own_rest = Rest(st, t1, (r.l2c, r.l2d), (r.t2c, r.t2d), (r.g1c, r.g1d), None, 0)
-
-    def take(k, total):
-        sum_copy(k).wait_recv()
-        return total + r.land_k[k].astype(F32)
-
-    own = lax.fori_loop(1, n, take, own)
-    if last:
-        few.second_sum()
-        own_rest.advance()
+        own_rest = Rest(st, t1, (r.l2c, r.l2d), (r.t2c, r.t2d), (r.g1c, r.g1d), (r.ha, r.hb), 0)
+        glin = r.zglin.at[st.block(st.z, tok), :]
+    else:
+        r.flush("n1z")
+        glin = r.glin
     r.need("cos", "sa", "sb", "x", "small")
     cos, sa, sb = r.cos[...], r.sa[...], r.sb[...]
     for t in range(TILES):
         gq = gathered_tile(r.gq_s[:, t * LANES : (t + 1) * LANES], t).T * HEAD_DIM ** (-0.5)
-        r.glin[:, t * LANES : (t + 1) * LANES] = unrope(gq, cos, sa, sb).astype(BF16)
-    r.glin[:, D : D + LANES] = unrope(own[:, :LANES], cos, sa, sb).astype(BF16)
-    r.glin[:, D + LANES :] = own[:, LANES:].astype(BF16)
-    r.flush("glin")
-    gn1 = mm_nt(r.glin[...], r.wa[:, :QKV])
+        glin[:, t * LANES : (t + 1) * LANES] = unrope(gq, cos, sa, sb).astype(BF16)
+    if last:
+        factors = attention.whole(r.zglin, slice(0, D))
+        few.second_sum()
+        own_rest.advance()
+
+    def take(k, total):
+        sum_copy(k).wait_recv()
+        return total + r.land_k[k].astype(F32)
+
+    own = lax.fori_loop(1, n, take, own)
+    glin[:, D : D + LANES] = unrope(own[:, :LANES], cos, sa, sb).astype(BF16)
+    glin[:, D + LANES :] = own[:, LANES:].astype(BF16)
+    if last:
+        factors += attention.whole(r.zglin, slice(D, QKV))
+    else:
+        r.flush("glin")
+    gn1 = mm_nt(glin[...], r.gu[0, :, :QKV])
     x = r.x[...]
     r1_ = lax.rsqrt(jnp.mean(x * x, -1, keepdims=True) + EPS)
     unit = x * r1_
-    dz = gn1 * r.small[layer][:, :D]
-    r.gx[...] = r.gm_s[...] + r1_ * (dz - unit * jnp.mean(dz * unit, -1, keepdims=True))
-    r.flush("gx")
     dg1 = col_sum(gn1 * unit)
-    dbias = col_sum(r.glin[...].astype(F32))
-    r.gsmall[...] = jnp.zeros(r.gsmall.shape, F32)
+    dbias = col_sum(glin[...].astype(F32))
+    gsmall = r.zsmall.at[st.block(st.z, 2 * UNIT), :] if last else r.gsmall
+    gsmall[...] = jnp.zeros(gsmall.shape, F32)
     row = 0
     for part in (dg1, dg2, dbias):
         for t in range(part.shape[1] // LANES):
-            r.gsmall[row : row + 1, :] = part[:, t * LANES : (t + 1) * LANES]
+            gsmall[row : row + 1, :] = part[:, t * LANES : (t + 1) * LANES]
             row += 1
-    r.flush("gsmall")
     if last:
+        factors += attention.whole(r.zsmall)
+        own_rest.advance()
         few.first_gather()
+    else:
+        r.flush("gsmall")
+    dz = gn1 * r.small[layer][:, :D]
+    r.gx[...] = r.gm_s[...] + r1_ * (dz - unit * jnp.mean(dz * unit, -1, keepdims=True))
+    if last:
+        below = Delivery(st, 0, r.gx, r.input_grad)
+        out = (r.qa, r.qb)
+        zswap = attention.swap(factors, r.n1z, r.zglin, r.zsmall, r.dout, r.zv, r.zl)
         own_rest.advance()
-        own_rest.landed()
-        few.landed()
+        ends = few.hand_over(out, 1)
+        attention.fold(zswap, r.zv, r.zl, (r.qp0a, r.qp0b))
+        few = Few(st, r, "0")
+        few.second_sum()
+        own_rest.second_half()
+        few.first_gather()
+        ends += few.hand_over(out, 0)
+        own_rest.finish()
+        for end in ends:
+            end()
+        above.finish()
+        below.finish()
     else:
         for h in range(2):
             arrived(r1[h])
@@ -1243,35 +1344,6 @@
     r.close()
 
 
-def reduce_kernel(_, r):
-    st = Stages(r)
-    st.hail(st.beside() + st.upright() + st.flat(True))
-    r.load()
-    r.need("glin", "gsmall")
-    attention = Attention(st)
-    st.met()
-    factors = attention.begin(r.glin, r.gsmall, r.all_glin, r.all_small)
-    r.need("g1a", "g1b", "h1a", "h1b")
-    last = []
-    for h in range(2):
-        last.append(st.hand_over(AXES[h][0], (r.g1a, r.g1b)[h], (r.ga, r.gb)[h], 0))
-    for h in range(2):
-        last.append(st.hand_over(AXES[h][0], (r.h1a, r.h1b)[h], (r.qa, r.qb)[h], 1))
-    r.need("n1z", "dout")
-    qswap = attention.swap(factors, r.n1z, r.all_glin, r.all_small, r.dout, r.qv, r.ql)
-    attention.fold(qswap, r.qv, r.ql, (r.qpa, r.qpb))
-    few = Few(st, r, "")
-    few.second_sum()
-    few.first_gather()
-    for h in range(2):
-        arrived(few.moving[h])
-        last.append(st.hand_over(AXES[h][0], few.wide[h], (r.qa, r.qb)[h], 0))
-    for finish in last:
-        finish()
-    st.drain()
-    r.close()
-
-
 class Refs(types.SimpleNamespace):
     def load(self):
         for c in self.coming.values():
@@ -1295,35 +1367,39 @@
             c.wait()
 
 
-def call(kernel, layer, cid, name, ins, outs, scratch, sems, hbm=(), flops=10**10):
-    staged = [k for k in ins if k not in hbm]
+def call(kernel, layer, cid, name, ins, outs, scratch, sems, hbm=(), flops=10**10, picked=(), whole=(), scalars=()):
+    staged = [k for k in ins if k not in hbm + whole + scalars]
     made = [k for k in outs if k not in hbm]
     dma = pltpu.SemaphoreType.DMA
-    counts = dict(ssem=sems, rsem=sems, lsem=16, csem=16, csem2=16, psem=16, psem2=16, isem=len(staged), osem=len(made))
+    counts = dict(ssem=sems, rsem=sems, lsem=20, csem=16, csem2=16, psem=16, psem2=16, isem=len(staged), osem=len(made))
     if name == "forward":
         counts.update(csem1=16, csem21=16)
-    places = [pltpu.VMEM(ins[k].shape, ins[k].dtype) for k in staged] + [pltpu.VMEM(*outs[k]) for k in made]
+    places = [pltpu.VMEM(ins[k].shape[2 if k in picked else 0 :], ins[k].dtype) for k in staged] + [pltpu.VMEM(*outs[k]) for k in made]
     names = ["in_" + k for k in ins] + ["out_" + k for k in outs] + staged + made + list(scratch) + list(counts)
 
     def body(*refs):
         r = Refs(**dict(zip(names, refs)))
-        for k in hbm:
+        for k in hbm + whole + scalars:
             if k in ins or k in outs:
                 setattr(r, k, getattr(r, ("in_" if k in ins else "out_") + k))
         r.here, r.gone = set(), set()
-        r.coming = {
-            k: pltpu.make_async_copy(getattr(r, "in_" + k), getattr(r, k), r.isem.at[i]) for i, k in enumerate(staged)
-        }
+        def source(k):
+            ref = getattr(r, "in_" + k)
+            return ref.at[lax.axis_index("section"), 0] if k in picked else ref
+
+        r.coming = {k: pltpu.make_async_copy(source(k), getattr(r, k), r.isem.at[i]) for i, k in enumerate(staged)}
         r.going = {
             k: pltpu.make_async_copy(getattr(r, k), getattr(r, "out_" + k), r.osem.at[i]) for i, k in enumerate(made)
         }
         kernel(layer, r)
 
     anywhere = pl.BlockSpec(memory_space=pl.ANY)
+    places_in = {k: pl.BlockSpec(memory_space=pltpu.VMEM) for k in whole}
+    places_in.update({k: pl.BlockSpec(memory_space=pltpu.SMEM) for k in scalars})
     got = pl.pallas_call(
         body,
         out_shape=[jax.ShapeDtypeStruct(s, t) for s, t in outs.values()],
-        in_specs=[anywhere] * len(ins),
+        in_specs=[places_in.get(k, anywhere) for k in ins],
         out_specs=[anywhere] * len(outs),
         scratch_shapes=places + [pltpu.VMEM(s, t) for s, t in scratch.values()] + [dma((k,)) for k in counts.values()],
         compiler_params=pltpu.CompilerParams(
@@ -1335,6 +1411,7 @@
     return dict(zip(outs, got))
 
 
+FAR = ("ga", "gb", "ha", "hb", "qa", "qb", "input_grad", "wa")
 FA_ROWS = tuple((4 * g + d) * UNIT for g, d in zip(GATE_PER, DOWN_PER))
 RQ = Q_ROWS // 2 // 16
 SIDES = (SIDE, SIDE)
@@ -1363,7 +1440,7 @@
 
 
 def assemble_kernel(nz, *refs):
-    given, results, held, outs, sem, osem = (refs[:2], refs[2:4]), refs[6:12], refs[12:14] + refs[4:6], refs[14:20], refs[20], refs[21]
+    given, results, held, outs, sem, osem = (refs[:2], refs[2:4]), refs[6:14], refs[14:16] + refs[4:6], refs[16:24], refs[24], refs[25]
     s = lax.axis_index("section")
     copies = [pltpu.make_async_copy(a, b, osem.at[i]) for i, (a, b) in enumerate(zip(outs, results))]
     for layer in range(2):
@@ -1375,7 +1452,7 @@
             for c in moving:
                 c.wait()
 
-    gate_ref, up_ref, down_ref, qkv_ref, out_ref, small_ref = outs
+    gate_ref, up_ref, down_ref, qkv_ref, out_ref = outs[:5]
     share = D // nz
     starts = window_starts(nz)
 
@@ -1413,7 +1490,15 @@
         else:
             u = t - QKV // LANES
             out_ref[:, u * LANES : (u + 1) * LANES] = got
-    small_ref[...] = units(held[2:], 0, (0, 0), Q_PER, 8 * (share // UNIT), 2)
+    small = units(held[2:], 0, (0, 0), Q_PER, 8 * (share // UNIT), 2)
+    z = lax.axis_index("fsdp")
+    row = 0
+    for ref, size in zip(outs[5:], (D, D, QKV)):
+        tiles = size // LANES
+        line = jnp.concatenate([small[row + t : row + t + 1, :] for t in range(tiles)], 1)
+        part = size // nz
+        ref[...] = pltpu.roll(jnp.broadcast_to(line, (8, size)), lax.rem(size - z * part, size), 1)[:1, :part]
+        row += tiles
     for c in copies[3:]:
         c.start()
     for c in copies:
@@ -1425,7 +1510,7 @@
     vm = pl.BlockSpec(memory_space=pltpu.VMEM)
     anywhere = pl.BlockSpec(memory_space=pl.ANY)
     share = D // nz
-    shapes = [(share, FF), (share, FF), (FF // nz, D), (share, QKV), (share, D), (2 * UNIT, LANES)]
+    shapes = [(share, FF), (share, FF), (FF // nz, D), (share, QKV), (share, D), (1, share), (1, share), (1, QKV // nz)]
     return pl.pallas_call(
         functools.partial(assemble_kernel, nz),
         out_shape=[jax.ShapeDtypeStruct(a, F32) for a in shapes],
@@ -1444,41 +1529,40 @@
     return [(i * share // LANES) * LANES for i in range(n)]
 
 
-def forward(x, gy, shards, small, pair):
+def forward(tokens, cotangent, shards, gains, pair_of):
     n, nz = lax.axis_size("ctx"), lax.axis_size("fsdp")
-    tok = x.shape[0]
-    freq = jnp.arange(HEAD_DIM // 2, dtype=F32)
-    inverse = jnp.tile(THETA ** (-2.0 * freq / HEAD_DIM), 4)[None, :]
-    ins = dict(small_own=small, pair=pair, inverse=inverse, x0=x, gy=gy)
+    tok = tokens.shape[2]
+    freq = np.arange(HEAD_DIM // 2, dtype=np.float64)
+    inverse = jnp.asarray(np.tile(THETA ** (-2.0 * freq / HEAD_DIM), 4)[None, :].astype(np.float32))
+    ins = dict(gains, pair=pair_of, inverse=inverse, x0=tokens, gy=cotangent)
     hbm = {k + "_shard": v for k, v in shards.items()}
     ins.update(hbm)
     outs = dict(
         small=f4(2, 1, SMALL), pairs=((n, 8, 2 * LANES), jnp.int32), cos=f4(tok, LANES), sa=f4(tok, LANES), sb=f4(tok, LANES),
-        x1=f4(tok, D), gy_all=bf(nz * tok, D),
+        x1=f4(tok, D), gy_all=bf(nz * tok, D), layer_out=f4(2, tok, D),
     )
     scratch = dict(m_s=f4(2, WIDE), l_s=f4(2, WIDE), acc_s=f4(2 * LANES, WIDE), att_s=bf(tok, D), parts=f4(2, nz, 1, SMALL))
     for l in "01":
         each = dict(
             mid=f4(tok, D), n1t=bf(D, tok), qst=bf(2 * LANES, WIDE), kv=bf(n, tok, 2 * LANES), lse=f4(2, WIDE),
             attt=bf(D, tok), gu=bf(2, D, WIN), down=bf(WIN, D), wa=bf(D, QKV + D),
-            y=f4(tok, D), all=bf(nz, tok, D), gate=bf(nz, tok, WIN), up=bf(nz, tok, WIN),
+            all=bf(nz, tok, D), gate=bf(nz, tok, WIN), up=bf(nz, tok, WIN),
         )
         outs.update({k + l: v for k, v in each.items()})
-        scratch.update({"send_s" + l: bf(nz, tok, D), "land_s" + l: bf(nz, tok, D)})
-    return call(forward_kernel, 0, 1, "forward", ins, outs, scratch, 160, tuple(hbm))
+        scratch.update({"y" + l: f4(tok, D), "send_s" + l: bf(nz, tok, D), "land_s" + l: bf(nz, tok, D)})
+    return call(forward_kernel, 0, 1, "forward", ins, outs, scratch, 160, tuple(hbm) + ("layer_out",), picked=("x0", "gy"), whole=tuple(gains), scalars=("pair",))
 
 
 def backward(layer, gy, f, before):
     n, nz = lax.axis_size("ctx"), lax.axis_size("fsdp")
-    tok = gy.shape[0]
+    tok = gy.shape[-2]
     share = D // nz
     own = {k: f[k + str(layer)] for k in ("down", "gate", "up", "gu", "all", "mid", "attt", "n1t", "qst", "lse", "kv", "wa")}
     ins = dict(gy=gy)
-    outs = dict(
-        gx=f4(tok, D), glin=bf(tok, QKV), gsmall=f4(2 * UNIT, LANES), n1z=bf(share, nz * tok), dout=bf(TILES * share, LANES)
-    )
+    outs = {}
+    factors = dict(n1z=bf(share, nz * tok), dout=bf(TILES * share, LANES))
     scratch = dict(
-        hid_s=bf(nz * tok, WIN), g_s=bf(2, nz * tok, WIN), down_s=bf(WIN, D), gm_s=f4(tok, D),
+        hid_s=bf(nz * tok, WIN), g_s=bf(2, nz * tok, WIN), gm_s=f4(tok, D),
         own_s=f4(tok, D), send_s=bf(nz, tok, D), land_s=bf(nz, tok, D),
         delta_s=f4(2, WIDE), gq_s=f4(2 * LANES, WIDE), all_gm=bf(nz * tok, D), attz=bf(share, nz * tok),
         send_k=bf(n, tok, 2 * LANES), land_k=bf(n, tok, 2 * LANES),
@@ -1488,103 +1572,62 @@
         scratch["sl" + h] = bf(*SIDES, rows, LANES)
         scratch["l1" + h] = bf(SIDE - 1, SIDE, rows, LANES)
     if layer == 0:
+        scratch["gx"] = f4(tok, D)
+        outs["input_grad"] = f4(2, tok, D)
         scratch["all_s"] = bf(nz * tok, D)
         ins.update(p1a=before["t1a"], p1b=before["t1b"])
         scratch.update(rest_scratch())
         outs.update(rest_outs())
     else:
         ins["all_s"] = f["gy_all"]
+        outs["gx"] = f4(tok, D)
     ins.update(down=own["down"], gate=own["gate"], up=own["up"], gu=own["gu"], n2_all=own["all"], mid=own["mid"])
     ins["small"] = f["small"]
     ins.update({k: own[k] for k in ("attt", "n1t")})
     if layer == 0:
         ins.update(glin1=before["glin"], gsmall1=before["gsmall"], n1z1=before["n1z"], dout1=before["dout"])
-        scratch.update(attention_scratch(tok))
-        scratch.update(few_scratch())
+        scratch.update(factors)
+        scratch.update(all_glin=bf(nz * tok, QKV), all_small=f4(nz * 2 * UNIT, LANES), qv=bf(2, Q_ROWS, LANES), ql=bf(Q_ROWS, LANES))
+        scratch.update(zglin=bf(nz * tok, QKV), zsmall=f4(nz * 2 * UNIT, LANES), zv=bf(2, Q_ROWS, LANES), zl=bf(Q_ROWS, LANES))
         scratch.update(t1a=bf(SIDE, FA_ROWS[0], LANES), t1b=bf(SIDE, FA_ROWS[1], LANES))
-        for h, rows in zip("cd", FA_ROWS):
+        for g, h, rows in zip("ab", "cd", FA_ROWS):
             scratch["l2" + h] = bf(SIDE - 1, rows, LANES)
             scratch["t2" + h] = bf(rows, LANES)
-            outs["g1" + h] = bf(SIDE, rows, LANES)
-        for h in "ab":
-            outs["qh" + h] = bf(SIDE, RQ, LANES)
+            scratch["g1" + h] = bf(SIDE, rows, LANES)
+            outs["h" + g] = bf(2, *SIDES, rows, LANES)
+            outs["q" + g] = bf(2, *SIDES, RQ, LANES)
+            for tag in ("", "0"):
+                scratch["qp" + tag + g] = bf(*SIDES, RQ, LANES)
+                scratch["qm" + tag + g] = bf(SIDE - 1, SIDE, RQ, LANES)
+                scratch["qw" + tag + g] = bf(SIDE - 1, RQ, LANES)
+                scratch["qe" + tag + g] = bf(SIDE, RQ, LANES)
+                scratch["qh" + tag + g] = bf(SIDE, RQ, LANES)
     else:
-        outs.update(t1a=bf(SIDE, FA_ROWS[0], LANES), t1b=bf(SIDE, FA_ROWS[1], LANES))
+        outs.update(factors)
+        outs.update(glin=bf(tok, QKV), gsmall=f4(2 * UNIT, LANES), t1a=bf(SIDE, FA_ROWS[0], LANES), t1b=bf(SIDE, FA_ROWS[1], LANES))
     ins.update({k: own[k] for k in ("qst", "lse", "kv", "wa")})
     ins.update({k: f[k] for k in ("pairs", "cos", "sa", "sb")})
     ins["x"] = f["x" + str(layer)] if layer else before["x0"]
-    return call(backward_kernel, layer, 2 + layer, f"backward_{layer}", ins, outs, scratch, 112, ("ga", "gb"), 3 * 10**10)
-
-
-def attention_scratch(tok):
-    nz = lax.axis_size("fsdp")
-    return dict(
-        all_glin=bf(nz * tok, QKV), all_small=f4(nz * 2 * UNIT, LANES), qv=bf(2, Q_ROWS, LANES), ql=bf(Q_ROWS, LANES),
-        qpa=bf(*SIDES, RQ, LANES), qpb=bf(*SIDES, RQ, LANES),
-    )
-
-
-def few_scratch():
-    made = {}
-    for h in "ab":
-        made["qm" + h] = bf(SIDE - 1, SIDE, RQ, LANES)
-        made["qw" + h] = bf(SIDE - 1, RQ, LANES)
-        made["qe" + h] = bf(SIDE, RQ, LANES)
-    return made
-
-
-def reduce_rest(last):
-    ins = dict(glin=last["glin"], gsmall=last["gsmall"], g1a=last["g1c"], g1b=last["g1d"], h1a=last["qha"], h1b=last["qhb"])
-    ins.update(n1z=last["n1z"], dout=last["dout"])
-    outs = rest_outs()
-    scratch = attention_scratch(last["glin"].shape[0])
-    scratch.update(few_scratch())
-    for h in "ab":
-        outs["q" + h] = bf(2, *SIDES, RQ, LANES)
-        scratch["qh" + h] = bf(SIDE, RQ, LANES)
-    return call(reduce_kernel, 0, 9, "reduce", ins, outs, scratch, 96, ("ga", "gb", "qa", "qb"))
+    return call(backward_kernel, layer, 2 + layer, f"backward_{layer}", ins, outs, scratch, 240, FAR, 3 * 10**10, ("x",) if layer == 0 else ("gy",))
 
 
 def local(
     tokens, cotangent, pair_of, attn_gain, ffn_gain, qkv_weight, qkv_bias, out_weight, gate_weight, up_weight, down_weight,
 ):
-    s = lax.axis_index("section")
-    z = lax.axis_index("fsdp")
-    nz = lax.axis_size("fsdp")
-    qd = D // nz
     shards = dict(qkv=qkv_weight, out=out_weight, gate=gate_weight, up=up_weight, down=down_weight)
 
-    def placed(part, size):
-        whole = jnp.zeros((1, size), F32)
-        return lax.dynamic_update_slice(whole, part.astype(F32), (0, z * part.shape[1]))
-
-    small_own = jnp.concatenate([placed(attn_gain, D), placed(ffn_gain, D), placed(qkv_bias, QKV)], 1)
-    pair = jnp.broadcast_to(pair_of.reshape(1, 1), (8, 2 * LANES))
-    x0 = jnp.where(s == 0, tokens[0, 0], tokens[1, 0])
-    gy = jnp.where(s == 0, cotangent[0, 0], cotangent[1, 0])
-    f = forward(x0, gy, shards, small_own, pair)
-    c1 = backward(1, gy, f, None)
-    c0 = backward(0, c1["gx"], f, dict(c1, x0=x0))
-    t = reduce_rest(c0)
-    dgate, dup, ddown, dqkv, dout, small_grad = assemble((t["ga"], t["gb"]), (c0["ga"], c0["gb"]), (t["qa"], t["qb"]))
-    small_grad = small_grad.reshape(-1)
-
-    def mine(first, size):
-        return lax.dynamic_slice_in_dim(small_grad, first + z * size, size, 0)[None]
-
-    def by_layer(pair):
-        theirs = jnp.where(s == 0, pair[1], pair[0])
-        mine = jnp.where(s == 0, pair[0], pair[1])
-        got = lax.ppermute(theirs, "section", [(0, 1), (1, 0)])
-        return jnp.where(s == 0, jnp.stack([mine, got]), jnp.stack([got, mine]))[None, :, None]
-
+    gains = dict(attn_gain=attn_gain, ffn_gain=ffn_gain, qkv_bias=qkv_bias)
+    f = forward(tokens, cotangent, shards, gains, pair_of)
+    c1 = backward(1, cotangent, f, None)
+    c0 = backward(0, c1["gx"], f, dict(c1, x0=tokens))
+    dgate, dup, ddown, dqkv, dout, dg1, dg2, dbias = assemble((c0["ha"], c0["hb"]), (c0["ga"], c0["gb"]), (c0["qa"], c0["qb"]))
     return (
-        by_layer((f["y0"], f["y1"])),
-        by_layer((c0["gx"], c1["gx"])),
-        mine(0, qd),
-        mine(D, qd),
+        f["layer_out"][None, :, None],
+        c0["input_grad"][None, :, None],
+        dg1,
+        dg2,
         dqkv[None],
-        mine(2 * D, QKV // nz),
+        dbias,
         dout[None],
         dgate[None],
         dup[None],

time: 378 us -> 353 us (0.934)
  Pallas kernels: 358 us -> 345 us
  other arithmetic: 9.39 us -> 0 us
    pallas_call x4 -> x3, Pallas kernels: 348 us -> 335 us  [call(): pl.pallas_call(body, out_shape=[jax.ShapeDtypeStruct(s, t) for s, t in ou...]
    select_n x3 -> x0, other arithmetic: 4.41 us -> none  [the longest x1 2.44 us: local(): gy = jnp.where(s == 0, cotangent[0, 0], cotangent[1, 0])]
  transfers between devices with their start and end apart: 2 -> 0, of which waited for: 0 -> 0; matrix products, arithmetic and copies ran while one was open for 1% -> 0% of each run, Pallas kernels for 59% -> 0%
where the time goes in v6:
time: 353 us; the launch traced here: 349 us
  Pallas kernels  345 us (98%)
    pallas_call x3, Pallas kernels, call(): pl.pallas_call(body, out_shape=[jax.ShapeDtypeStruct(s, t) for s, t in ou...  335 us
    pallas_call x1, Pallas kernels, assemble(): pl.pallas_call(functools.partial(assemble_kernel, nz), out_shape=[jax.Sha...  10 us

profile of v6, /device:TPU:0, one launch (start us, length us, event | category | flops | bytes accessed | tf_op | source)
XLA Modules:
  0.0 348.9 jit_solution(3709061091221318492)
XLA Ops:
  1.3 137.1 %forward.1 = (f32[2,1,2944]{2,1,0:T(1,128)}, s32[16,8,256]{2,1,0:T(8,128)}, f32[128,128]{1,0:T(8,128)}, f32[128,128]{1,0:T(8,128)}, f32[128,128]{1,0:T(8,128)}, ...) custom-call(bf16[1,224]{1,0:T(2,128)(2,1)} %refs_0_.2, ...), custom_call_target="tpu_custom_call" | custom-call | flops 10000000000 | bytes 20971520 | tf_op jit(solution)/shard_map/forward/pallas_call | solution.py:1399
  138.4 67.4 %backward_1.1 = (f32[128,896]{1,0:T(8,128)}, bf16[224,512]{1,0:T(8,128)(2,1)}, bf16[1568,128]{1,0:T(8,128)(2,1)}, bf16[128,1152]{1,0:T(8,128)(2,1)}, f32[32,128]...) custom-call(f32[2,1,128,896]{3,2,1,0:T(8,128)} %refs_0_.3, ...), custom_call_target="tpu_custom_call" | custom-call | flops 30000001024 | bytes 20971520 | tf_op jit(solution)/shard_map/backward_1/pallas_call | solution.py:1399
  205.8 130.9 %backward_0.1 = (f32[2,128,896]{2,1,0:T(8,128)}, bf16[2,4,4,448,128]{4,3,2,1,0:T(8,128)(2,1)}, bf16[2,4,4,400,128]{4,3,2,1,0:T(8,128)(2,1)}, bf16[2,4,4,448,128]...) custom-call(f32[128,896]{1,0:T(8,128)} %get-tuple-element.84.refs_0_, ...), custom_call_target="tpu_custom_call" | custom-call | flops 30000001024 | bytes 20971520 | tf_op jit(solution)/shard_map/backward_0/pallas_call | solution.py:1399
  336.7 0.0 copy-start
  336.7 0.0 copy-start.1
  336.7 10.0 %assemble.1 = (f32[224,4864]{1,0:T(8,128)}, f32[224,4864]{1,0:T(8,128)}, f32[1216,896]{1,0:T(8,128)}, f32[224,1152]{1,0:T(8,128)}, f32[224,896]{1,0:T(8,128)}, /...) custom-call(bf16[2,4,4,448,128]{4,3,2,1,0:T(8,128)(2,1)} %get-tuple-element.104.refs_0_, ...), custom_call_target="tpu_custom_call" | custom-call | tf_op jit(solution)/shard_map/assemble/pallas_call | solution.py:1514
  346.7 0.0 copy-done
  346.7 0.9 copy.27
  347.7 0.0 copy-done.1
  347.7 0.9 copy.28
Async XLA Ops:
  336.7 10.1 %copy-start = (f32[2,128,896]{2,1,0:T(8,128)S(1)}, f32[2,128,896]{2,1,0:T(8,128)}, u32[]{:S(2)}) copy-start(f32[2,128,896]{2,1,0:T(8,128)} %get-tuple-element.64) | copy-start | bytes 2752516
  336.7 11.0 %copy-start.1 = (f32[2,128,896]{2,1,0:T(8,128)S(1)}, f32[2,128,896]{2,1,0:T(8,128)}, u32[]{:S(2)}) copy-start(f32[2,128,896]{2,1,0:T(8,128)} %get-tuple-element.103) | copy-start | bytes 2752516

commit v7 on v6

--- a/solution.py
+++ b/solution.py
@@ -249,41 +249,90 @@
         return self.x * (1 - self.s) + self.y * self.s
 
     def hand_over(self, axis, src, dst, layer, part=None):
-        at = self.take(2 * SIDE)
-        mine = dst.at[self.s, self.along(axis, 0)]
+        return Handover(self, axis, src, dst, layer, part)
+
+
+class Handover:
+    def __init__(self, st, axis, src, dst, layer, part=None):
+        self.st, self.axis, self.layer = st, axis, layer
+        self.at = st.take(2 * SIDE)
+        mine = dst.at[st.s, st.along(axis, 0)]
         if part is not None:
             src, mine = src.at[part], mine.at[part]
-        self.begin(
-            [
-                self.copy(src, mine, at + k, self.peer(axis, k, layer), at + self.s * SIDE + k)
-                for k in range(1, SIDE)
-            ]
+        self.src, self.mine, self.dst, self.part = src, mine, dst, part
+        st.begin(
+            [st.copy(src, mine, self.at + k, st.peer(axis, k, layer), self.at + st.s * SIDE + k) for k in (1, SIDE - 1)]
         )
-        beside = self.copy(src, mine, at, {"section": layer}, at + self.s * SIDE)
-        within = pltpu.make_async_copy(src, mine, self.lsem.at[self.local_used])
-        self.local_used += 1
-
-        @pl.when(self.s != layer)
+        self.beside = st.copy(src, mine, self.at, {"section": layer}, self.at + st.s * SIDE)
+        self.within = pltpu.make_async_copy(src, mine, st.lsem.at[st.local_used])
+        st.local_used += 1
+        pl.when(st.s != layer)(self.beside.start)
+        pl.when(st.s == layer)(self.within.start)
+
+    def arrival(self, half, k):
+        return self.st.copy(self.src, self.mine, self.at, {"section": self.layer}, self.at + half * SIDE + k)
+
+    def passing(self, half):
+        st = self.st
+        way = 1 - 2 * half
+        p = self.dst.at[half, st.along(self.axis, -way)]
+        if self.part is not None:
+            p = p.at[self.part]
+        at = self.at + half * SIDE + 2
+        return st.copy(p, p, at, st.peer(self.axis, way), at)
+
+    def relay(self):
+        @pl.when(self.st.s == self.layer)
         def _():
-            beside.start()
-
-        @pl.when(self.s == layer)
+            for half, k in ((0, 1), (1, SIDE - 1)):
+                self.arrival(half, k).wait_recv()
+                self.passing(half).start()
+
+    def finish(self):
+        @pl.when(self.st.s == self.layer)
         def _():
-            within.start()
-
-        def finish():
-            @pl.when(self.s == layer)
-            def _():
-                within.wait()
-                for half in range(2):
-                    for k in range(0 if half != layer else 1, SIDE):
-                        self.copy(src, mine, at, {"section": layer}, at + half * SIDE + k).wait_recv()
-
-            @pl.when(self.s != layer)
-            def _():
-                beside.wait_send()
-
-        return finish
+            self.within.wait()
+            for half, k in ((0, SIDE - 1), (1, 1), (0, 2), (1, 2), (1 - self.layer, 0)):
+                self.arrival(half, k).wait_recv()
+            for half in range(2):
+                self.passing(half).wait_send()
+
+        pl.when(self.st.s != self.layer)(self.beside.wait_send)
+
+
+class Scatter:
+    def __init__(self, st, axis, src, land):
+        self.st, self.axis, self.src, self.land = st, axis, src, land
+        self.at = st.take(6)
+        low, high = slice(0, SIDE // 2), slice(SIDE // 2, SIDE)
+        far = src.at[st.along(axis, 2)]
+        self.through = [
+            self.send(far.at[low], land.at[2, low], 0, 1),
+            self.send(far.at[high], land.at[2, high], 1, -1),
+        ]
+        self.straight = [
+            self.send(src.at[st.along(axis, 1), high], land.at[0, high], 2, 1),
+            self.send(src.at[st.along(axis, -1), low], land.at[1, low], 3, -1),
+        ]
+        st.begin(self.through + self.straight)
+
+    def send(self, src, dst, i, way):
+        return self.st.copy(src, dst, self.at + i, self.st.peer(self.axis, way))
+
+    def pass_on(self):
+        st = self.st
+        low, high = slice(0, SIDE // 2), slice(SIDE // 2, SIDE)
+        self.late = []
+        for i, (part, way) in enumerate(((low, 1), (high, -1))):
+            self.through[i].wait_recv()
+            mine = self.src.at[st.along(self.axis, way), part]
+            add_into(mine, [mine, self.land.at[2, part]])
+            self.late.append(self.send(mine, self.land.at[i, part], 4 + i, way))
+        st.begin(self.late)
+
+    def sum_into(self, out):
+        arrived(self.straight + self.late)
+        add_into(out, [self.src.at[self.st.along(self.axis, 0)], self.land.at[0], self.land.at[1]])
 
 
 class Feed:
@@ -950,18 +999,25 @@
                 mine[st.nz * per :, :] = t2[st.nz * per :, :]
             elif self.stage == 1:
                 self.moving[h] = st.gather(second, self.g1[h])
-            else:
-                self.moving[h] = st.hand_over(AXES[h][0], self.g1[h], self.out[h], self.layer, slice(0, SIDE // 2))
+        if self.stage == 2:
+            self.ends = []
+            self.open = []
+            self.give(slice(0, SIDE // 2))
         self.stage += 1
 
-    def second_half(self):
-        self.ends = self.moving + [
-            self.st.hand_over(AXES[h][0], self.g1[h], self.out[h], self.layer, slice(SIDE // 2, SIDE)) for h in range(2)
-        ]
+    def give(self, part):
+        made = [self.st.hand_over(AXES[h][0], self.g1[h], self.out[h], self.layer, part) for h in range(2)]
+        self.ends += made
+        self.open += made
+
+    def relay(self):
+        for one in self.open:
+            one.relay()
+        self.open = []
 
     def finish(self):
-        for end in self.ends:
-            end()
+        for one in self.ends:
+            one.finish()
 
 
 class Few:
@@ -1074,7 +1130,11 @@
         first(2).wait_recv()
     r.send_s[2] = block([st.along("z", -2)]).astype(BF16)
     second(2).start()
+    attention = Attention(st)
+    before = None
     if carry:
+        r.need("glin1", "gsmall1")
+        before = attention.begin(r.glin1, r.gsmall1, r.all_glin, r.all_small)
         rest.advance()
 
     late = [
@@ -1117,8 +1177,6 @@
             put_units(refs, section, base, GATE_PER, used, jnp.zeros((extra * UNIT, LANES), BF16))
 
     product(1 - st.s)
-    if carry:
-        rest.second_half()
     swaps = [st.swap(refs[h], (r.sla, r.slb)[h]) for h in range(2)]
     product(st.s)
     for k in ORDER:
@@ -1137,10 +1195,10 @@
         if carry:
             first(k).wait_send()
         second(k).wait_send()
-    attention_backward(st, r, layer, gm, dg2, refs, swaps, rest if carry else None, above, late)
-
-
-def attention_backward(st, r, layer, gm, dg2, refs, swaps, rest, above, late):
+    attention_backward(st, r, layer, gm, dg2, refs, swaps, rest if carry else None, above, late, attention, before)
+
+
+def attention_backward(st, r, layer, gm, dg2, refs, swaps, rest, above, late, attention, before):
     n, me = st.nc, st.c
     last = layer == 0
     half = HEAD_DIM
@@ -1149,18 +1207,14 @@
     r.all_gm[st.block(st.z, tok), :] = gmb
     sl, l1, t1 = (r.sla, r.slb), (r.l1a, r.l1b), (r.t1a, r.t1b)
     r.need("attt", "n1t")
-    attention = Attention(st)
     size = 2 * BATCH * half
     pr, ds, gst = r.g_s.at[0, :size, :WIDE], r.g_s.at[1, :size, :WIDE], r.hid_s.at[: 2 * LANES, :WIDE]
     out_factors = attention.whole(r.all_gm) + attention.columns(r.attt, r.attz)
     qkv_factor = attention.columns(r.n1t, r.n1z)
-    if last:
-        r.need("glin1", "gsmall1", "n1z1", "dout1")
-        before = attention.begin(r.glin1, r.gsmall1, r.all_glin, r.all_small)
     r1 = []
     for h in range(2):
         swapped_sum(st, swaps[h], refs[h], sl[h])
-        r1.append(st.scatter(AXES[h][0], sl[h], l1[h]))
+        r1.append(Scatter(st, AXES[h][0], sl[h], l1[h]))
     r.need("qst", "lse", "kv", "pairs")
     for c in late:
         c.wait()
@@ -1241,35 +1295,24 @@
             sum_copy(k).start()
 
     own = own_block()
-    for i in range(3):
+    for i in range((n - 1) // BATCH):
         step(i)
-    arrived(out_factors)
-    share = D // st.nz
-    for j in range(0, TILES, 2):
-        cols = slice(j * LANES, min(j + 2, TILES) * LANES)
-        d = mm(r.attz[...], r.all_gm[:, cols]).astype(BF16)
-        for t in range(j, min(j + 2, TILES)):
-            r.dout[t * share : (t + 1) * share, :] = d[:, (t - j) * LANES : (t - j + 1) * LANES]
-    if not last:
-        r.flush("dout")
-    if last:
-        qswap = attention.swap(before, r.n1z1, r.all_glin, r.all_small, r.dout1, r.qv, r.ql)
-    for i in range(3, (n - 1) // BATCH):
-        step(i)
-    arrived(qkv_factor)
-    if last:
-        rest.finish()
-        attention.fold(qswap, r.qv, r.ql, (r.qpa, r.qpb))
-        few = Few(st, r, "")
-        for h in range(2):
-            arrived(r1[h])
-            mine = sl[h].at[st.along(AXES[h][0], 0)]
-            add_into(t1[h], [mine] + [l1[h].at[k] for k in range(SIDE - 1)])
-        own_rest = Rest(st, t1, (r.l2c, r.l2d), (r.t2c, r.t2d), (r.g1c, r.g1d), (r.ha, r.hb), 0)
-        glin = r.zglin.at[st.block(st.z, tok), :]
-    else:
-        r.flush("n1z")
-        glin = r.glin
+        if i == 0:
+            for one in r1:
+                one.pass_on()
+        if i == 1 and last:
+            rest.relay()
+
+    def out_gradient():
+        arrived(out_factors)
+        share = D // st.nz
+        for j in range(0, TILES, 2):
+            cols = slice(j * LANES, min(j + 2, TILES) * LANES)
+            d = mm(r.attz[...], r.all_gm[:, cols]).astype(BF16)
+            for t in range(j, min(j + 2, TILES)):
+                r.dout[t * share : (t + 1) * share, :] = d[:, (t - j) * LANES : (t - j + 1) * LANES]
+
+    glin = r.zglin.at[st.block(st.z, tok), :] if last else r.glin
     r.need("cos", "sa", "sb", "x", "small")
     cos, sa, sb = r.cos[...], r.sa[...], r.sb[...]
     for t in range(TILES):
@@ -1277,8 +1320,18 @@
         glin[:, t * LANES : (t + 1) * LANES] = unrope(gq, cos, sa, sb).astype(BF16)
     if last:
         factors = attention.whole(r.zglin, slice(0, D))
-        few.second_sum()
-        own_rest.advance()
+        r.need("n1z1", "dout1")
+        qswap = attention.swap(before, r.n1z1, r.all_glin, r.all_small, r.dout1, r.qv, r.ql)
+        for h in range(2):
+            r1[h].sum_into(t1[h])
+        own_rest = Rest(st, t1, (r.l2c, r.l2d), (r.t2c, r.t2d), (r.g1c, r.g1d), (r.ha, r.hb), 0)
+        rest.give(slice(2, 3))
+        attention.fold(qswap, r.qv, r.ql, (r.qpa, r.qpb))
+        few = Few(st, r, "")
+    else:
+        out_gradient()
+        arrived(qkv_factor)
+        r.flush("dout", "n1z")
 
     def take(k, total):
         sum_copy(k).wait_recv()
@@ -1289,6 +1342,8 @@
     glin[:, D + LANES :] = own[:, LANES:].astype(BF16)
     if last:
         factors += attention.whole(r.zglin, slice(D, QKV))
+        own_rest.advance()
+        few.second_sum()
     else:
         r.flush("glin")
     gn1 = mm_nt(glin[...], r.gu[0, :, :QKV])
@@ -1308,6 +1363,8 @@
         factors += attention.whole(r.zsmall)
         own_rest.advance()
         few.first_gather()
+        rest.relay()
+        rest.give(slice(3, 4))
     else:
         r.flush("gsmall")
     dz = gn1 * r.small[layer][:, :D]
@@ -1315,25 +1372,35 @@
     if last:
         below = Delivery(st, 0, r.gx, r.input_grad)
         out = (r.qa, r.qb)
+        out_gradient()
+        arrived(qkv_factor)
+        own_rest.advance()
         zswap = attention.swap(factors, r.n1z, r.zglin, r.zsmall, r.dout, r.zv, r.zl)
-        own_rest.advance()
+        attention.fold(zswap, r.zv, r.zl, (r.qp0a, r.qp0b))
+        last_few = Few(st, r, "0")
         ends = few.hand_over(out, 1)
-        attention.fold(zswap, r.zv, r.zl, (r.qp0a, r.qp0b))
-        few = Few(st, r, "0")
-        few.second_sum()
-        own_rest.second_half()
-        few.first_gather()
-        ends += few.hand_over(out, 0)
+        rest.relay()
+        own_rest.relay()
+        last_few.second_sum()
+        own_rest.give(slice(2, SIDE))
+        for end in ends:
+            end.relay()
+        last_few.first_gather()
+        own_rest.relay()
+        final = last_few.hand_over(out, 0)
+        rest.finish()
+        for end in final:
+            end.relay()
+        for end in ends:
+            end.finish()
         own_rest.finish()
-        for end in ends:
-            end()
+        for end in final:
+            end.finish()
         above.finish()
         below.finish()
     else:
         for h in range(2):
-            arrived(r1[h])
-            mine = sl[h].at[st.along(AXES[h][0], 0)]
-            add_into(t1[h], [mine] + [l1[h].at[k] for k in range(SIDE - 1)])
+            r1[h].sum_into(t1[h])
     st.drain()
 
     def done(k, c):
@@ -1608,7 +1675,7 @@
     ins.update({k: own[k] for k in ("qst", "lse", "kv", "wa")})
     ins.update({k: f[k] for k in ("pairs", "cos", "sa", "sb")})
     ins["x"] = f["x" + str(layer)] if layer else before["x0"]
-    return call(backward_kernel, layer, 2 + layer, f"backward_{layer}", ins, outs, scratch, 240, FAR, 3 * 10**10, ("x",) if layer == 0 else ("gy",))
+    return call(backward_kernel, layer, 2 + layer, f"backward_{layer}", ins, outs, scratch, 256, FAR, 3 * 10**10, ("x",) if layer == 0 else ("gy",))
 
 
 def local(

time: 353 us -> 340 us (0.963)
  Pallas kernels: 345 us -> 333 us
    pallas_call x3, Pallas kernels: 335 us -> 323 us  [call(): pl.pallas_call(body, out_shape=[jax.ShapeDtypeStruct(s, t) for s, t in ou...]
where the time goes in v7:
time: 340 us; the launch traced here: 336 us
  Pallas kernels  333 us (98%)
    pallas_call x3, Pallas kernels, call(): pl.pallas_call(body, out_shape=[jax.ShapeDtypeStruct(s, t) for s, t in ou...  323 us
    pallas_call x1, Pallas kernels, assemble(): pl.pallas_call(functools.partial(assemble_kernel, nz), out_shape=[jax.Sha...  10 us

profile of v7, /device:TPU:0, one launch (start us, length us, event | category | flops | bytes accessed | tf_op | source)
XLA Modules:
  0.0 336.2 jit_solution(9836256175753970185)
XLA Ops:
  1.3 137.1 %forward.1 = (f32[2,1,2944]{2,1,0:T(1,128)}, s32[16,8,256]{2,1,0:T(8,128)}, f32[128,128]{1,0:T(8,128)}, f32[128,128]{1,0:T(8,128)}, f32[128,128]{1,0:T(8,128)}, ...) custom-call(bf16[1,224]{1,0:T(2,128)(2,1)} %refs_0_.2, ...), custom_call_target="tpu_custom_call" | custom-call | flops 10000000000 | bytes 20971520 | tf_op jit(solution)/shard_map/forward/pallas_call | solution.py:1466
  138.4 63.2 %backward_1.1 = (f32[128,896]{1,0:T(8,128)}, bf16[224,512]{1,0:T(8,128)(2,1)}, bf16[1568,128]{1,0:T(8,128)(2,1)}, bf16[128,1152]{1,0:T(8,128)(2,1)}, f32[32,128]...) custom-call(f32[2,1,128,896]{3,2,1,0:T(8,128)} %refs_0_.3, ...), custom_call_target="tpu_custom_call" | custom-call | flops 30000001024 | bytes 20971520 | tf_op jit(solution)/shard_map/backward_1/pallas_call | solution.py:1466
  201.6 122.4 %backward_0.1 = (f32[2,128,896]{2,1,0:T(8,128)}, bf16[2,4,4,448,128]{4,3,2,1,0:T(8,128)(2,1)}, bf16[2,4,4,400,128]{4,3,2,1,0:T(8,128)(2,1)}, bf16[2,4,4,448,128]...) custom-call(f32[128,896]{1,0:T(8,128)} %get-tuple-element.84.refs_0_, ...), custom_call_target="tpu_custom_call" | custom-call | flops 30000001024 | bytes 20971520 | tf_op jit(solution)/shard_map/backward_0/pallas_call | solution.py:1466
  324.0 0.0 copy-start
  324.0 0.0 copy-start.1
  324.0 10.0 %assemble.1 = (f32[224,4864]{1,0:T(8,128)}, f32[224,4864]{1,0:T(8,128)}, f32[1216,896]{1,0:T(8,128)}, f32[224,1152]{1,0:T(8,128)}, f32[224,896]{1,0:T(8,128)}, /...) custom-call(bf16[2,4,4,448,128]{4,3,2,1,0:T(8,128)(2,1)} %get-tuple-element.104.refs_0_, ...), custom_call_target="tpu_custom_call" | custom-call | tf_op jit(solution)/shard_map/assemble/pallas_call | solution.py:1581
  334.0 0.0 copy-done
  334.0 0.9 copy.27
  335.0 0.0 copy-done.1
  335.0 0.9 copy.28
Async XLA Ops:
  324.0 10.1 %copy-start = (f32[2,128,896]{2,1,0:T(8,128)S(1)}, f32[2,128,896]{2,1,0:T(8,128)}, u32[]{:S(2)}) copy-start(f32[2,128,896]{2,1,0:T(8,128)} %get-tuple-element.64) | copy-start | bytes 2752516
  324.0 11.0 %copy-start.1 = (f32[2,128,896]{2,1,0:T(8,128)S(1)}, f32[2,128,896]{2,1,0:T(8,128)}, u32[]{:S(2)}) copy-start(f32[2,128,896]{2,1,0:T(8,128)} %get-tuple-element.103) | copy-start | bytes 2752516

commit v8 on v7

--- a/solution.py
+++ b/solution.py
@@ -353,6 +353,12 @@
         dst = self.piece(st.z, h, (st.x, st.y)[h])
         return st.copy(dst if src is None else src, dst, self.across + 2 * (k - 1) + h, st.peer("z", k, h))
 
+    def start_beside(self):
+        @pl.when(self.st.s == self.layer)
+        def _():
+            for h in range(2):
+                self.beside(h).start()
+
     def start(self):
         st = self.st
 
@@ -365,8 +371,6 @@
                             self.send(h, k, src).start()
                         else:
                             pl.when(needed)(self.send(h, k, src).start)
-            for h in range(2):
-                self.beside(h).start()
 
     def relay(self, k):
         st = self.st
@@ -478,15 +482,21 @@
     share = qkv.shape[1]
     rows = st.block(st.z, share)
     local = Local(st, layer, [(qkv.at[0], dst.at[rows, :QKV]), (out.at[0], dst.at[rows, QKV:])])
-    width = (QKV + D) // SIDE
-
-    def piece(z, h, q):
-        return dst.at[half_rows(z, h, share), pl.ds(pl.multiple_of(q * width, LANES), width)]
-
-    def band(z, h):
-        return dst.at[half_rows(z, h, share), :]
-
-    return local, Feed(st, layer, lambda h, q, z_to: [(None, None)], piece, band)
+    whole = QKV + D
+    split = whole // 4 * 3
+
+    def feed(low, high):
+        width = (high - low) // SIDE
+
+        def piece(z, h, q):
+            return dst.at[half_rows(z, h, share), pl.ds(pl.multiple_of(low + q * width, LANES), width)]
+
+        def band(z, h):
+            return dst.at[half_rows(z, h, share), low:high]
+
+        return Feed(st, layer, lambda h, q, z_to: [(None, None)], piece, band)
+
+    return local, feed(0, split), feed(split, whole)
 
 
 def feed_windows(st, layer, gate, up, dst):
@@ -512,6 +522,30 @@
         return dst.at[:, half_rows(z, h, share), :]
 
     return local, Feed(st, layer, sources, piece, band)
+
+
+class Ring:
+    def __init__(self, st, place, rows):
+        self.st, self.place, self.rows = st, place, rows
+        self.at = st.take(4)
+        mine = place(st.z, 0, rows)
+        self.near = st.begin([self.send(mine, i, way) for i, way in enumerate((1, -1))])
+
+    def send(self, ref, i, way):
+        return self.st.copy(ref, ref, self.at + i, self.st.peer("z", way))
+
+    def pass_on(self):
+        st, half = self.st, self.rows // 2
+        arrived(self.near)
+        self.far = st.begin(
+            [
+                self.send(self.place(st.along("z", -1), 0, half), 2, 1),
+                self.send(self.place(st.along("z", 1), half, half), 3, -1),
+            ]
+        )
+
+    def finish(self):
+        arrived(self.far)
 
 
 def arrived(copies):
@@ -624,6 +658,7 @@
     wa[0][0].wait()
     st.met()
     wa[0][1].start()
+    wa[0][1].start_beside()
     at = st.take(2 * st.nz)
     mine = r.parts.at[st.s, st.z]
     st.begin(
@@ -662,17 +697,21 @@
     r.flush("small")
     for k in ORDER:
         wa[0][1].relay(k)
+    wa[0][2].start()
     gu[0][0].wait()
     gu[0][1].start()
-    down[0].start()
     for k in ORDER:
         wa[0][1].collect(k)
+    wa[0][2].start_beside()
+    gu[0][1].start_beside()
+    down[0].start()
 
     def begin_next():
         wa[1][0].wait()
-        wa[1][1].start()
         gu[1][0].wait()
-        gu[1][1].start()
+        for feed in (wa[1][1], wa[1][2], gu[1][1]):
+            feed.start()
+            feed.start_beside()
         down[1].start()
 
     def relays(*steps):
@@ -682,18 +721,23 @@
 
         return go
 
-    g0, w1, g1 = gu[0][1], wa[1][1], gu[1][1]
+    g0, w0, w1, w2, g1 = gu[0][1], wa[0][2], wa[1][1], wa[1][2], gu[1][1]
     wa[0][1].finish()
     v = View(r, 0)
-    v.flush("wa")
+
+    def out_ready():
+        g0.collect(2)
+        w0.finish()
+        v.flush("wa")
+
     attention_forward(
         st, v, 0,
         (
-            relays((g0, "relay", 1), (g0, "relay", 3)),
-            relays((g0, "relay", 2)),
+            relays((w0, "relay", 1), (w0, "relay", 3), (w0, "relay", 2), (g0, "relay", 1), (g0, "relay", 3)),
+            relays((g0, "relay", 2), (w0, "collect", 1), (w0, "collect", 3), (w0, "collect", 2)),
             begin_next,
             relays((g0, "collect", 1), (g0, "collect", 3)),
-            relays((g0, "collect", 2)),
+            out_ready,
         ),
     )
 
@@ -706,9 +750,12 @@
         st, v, ready_0,
         (
             relays((w1, "relay", 1), (w1, "relay", 3)),
-            relays((w1, "relay", 2), (g1, "relay", 1)),
+            relays((w1, "relay", 2), (w2, "relay", 1), (w2, "relay", 3), (w2, "relay", 2), (g1, "relay", 1)),
             relays((g1, "relay", 3), (g1, "relay", 2), (w1, "collect", 1), (w1, "collect", 3)),
-            relays((w1, "collect", 2), (g1, "collect", 1), (g1, "collect", 3), (g1, "collect", 2)),
+            relays(
+                (w1, "collect", 2), (w2, "collect", 1), (w2, "collect", 3), (w2, "collect", 2),
+                (g1, "collect", 1), (g1, "collect", 3), (g1, "collect", 2),
+            ),
         ),
     )
     r.x1[...] = r.y0[...].astype(BF16).astype(F32)
@@ -722,6 +769,7 @@
     mine_gy = r.gy_all.at[rows, :]
     gy_moving = st.begin([st.copy(mine_gy, mine_gy, at + k - 1, st.peer("z", k)) for k in range(1, st.nz)])
     w1.finish()
+    w2.finish()
     v = View(r, 1)
     v.flush("wa")
     nothing = lambda: None
@@ -869,19 +917,14 @@
 
 def ffn_forward(st, r, ready, between):
     n, me = st.nz, st.z
-    at = st.take(2 * n)
-
-    def first(k):
-        return st.copy(r.all.at[me], r.all.at[me], at + k, st.peer("z", k))
+    tok = r.mid.shape[0]
+    at = st.take(n)
 
     def second(k):
-        return st.copy(r.send_s.at[k], r.land_s.at[k], at + n + k, st.peer("z", -k))
-
-    for k in ORDER:
-        first(k).start()
+        return st.copy(r.send_s.at[k], r.land_s.at[k], at + k, st.peer("z", -k))
+
+    ring = Ring(st, lambda z, row, rows: r.all.at[z, row : row + rows, :], tok)
     ready()
-
-    tok = r.mid.shape[0]
 
     def block(sources):
         a = jnp.concatenate([r.all[i] for i in sources], 0) if len(sources) > 1 else r.all[sources[0]]
@@ -895,14 +938,13 @@
 
     r.y[...] = r.mid[...] + block([me])
     between[0]()
-    first(1).wait_recv()
-    first(3).wait_recv()
+    ring.pass_on()
     both = block([st.along("z", -1), st.along("z", -3)]).astype(BF16)
     for i, k in enumerate((1, 3)):
         r.send_s[k] = both[i * tok : (i + 1) * tok]
         second(k).start()
     between[1]()
-    first(2).wait_recv()
+    ring.finish()
     r.send_s[2] = block([st.along("z", -2)]).astype(BF16)
     second(2).start()
     between[2]()
@@ -912,7 +954,6 @@
         second(k).wait_recv()
         r.y[...] += r.land_s[k].astype(F32)
     for k in ORDER:
-        first(k).wait_send()
         second(k).wait_send()
 
 
@@ -1077,16 +1118,11 @@
     st.met()
     at = st.take(2 * n)
 
-    def first(k):
-        mine = r.all_s.at[rows_of(me), :]
-        return st.copy(mine, mine, at + k, st.peer("z", k))
-
     def second(k):
         return st.copy(r.send_s.at[k], r.land_s.at[k], at + n + k, st.peer("z", -k))
 
     if carry:
-        for k in ORDER:
-            first(k).start()
+        ring = Ring(st, lambda z, row, rows: r.all_s.at[pl.ds(pl.multiple_of(z * tok + row, UNIT), rows), :], tok)
         above = Delivery(st, 1, r.gy, r.input_grad)
         r.need("p1a", "p1b")
         rest = Rest(st, (r.p1a, r.p1b), (r.l2a, r.l2b), (r.t2a, r.t2b), (r.g1a, r.g1b), (r.ga, r.gb), 1)
@@ -1119,15 +1155,14 @@
     r.own_s[...] = block([me])
     if carry:
         rest.advance()
-        first(1).wait_recv()
-        first(3).wait_recv()
+        ring.pass_on()
     both = block([st.along("z", -1), st.along("z", -3)]).astype(BF16)
     for i, k in enumerate((1, 3)):
         r.send_s[k] = both[i * tok : (i + 1) * tok]
         second(k).start()
     if carry:
         rest.advance()
-        first(2).wait_recv()
+        ring.finish()
     r.send_s[2] = block([st.along("z", -2)]).astype(BF16)
     second(2).start()
     attention = Attention(st)
@@ -1192,8 +1227,6 @@
     gm = gy + r2 * (dz - unit * jnp.mean(dz * unit, -1, keepdims=True))
     r.gm_s[...] = gm
     for k in ORDER:
-        if carry:
-            first(k).wait_send()
         second(k).wait_send()
     attention_backward(st, r, layer, gm, dg2, refs, swaps, rest if carry else None, above, late, attention, before)
 
@@ -1617,7 +1650,7 @@
         )
         outs.update({k + l: v for k, v in each.items()})
         scratch.update({"y" + l: f4(tok, D), "send_s" + l: bf(nz, tok, D), "land_s" + l: bf(nz, tok, D)})
-    return call(forward_kernel, 0, 1, "forward", ins, outs, scratch, 160, tuple(hbm) + ("layer_out",), picked=("x0", "gy"), whole=tuple(gains), scalars=("pair",))
+    return call(forward_kernel, 0, 1, "forward", ins, outs, scratch, 200, tuple(hbm) + ("layer_out",), picked=("x0", "gy"), whole=tuple(gains), scalars=("pair",))
 
 
 def backward(layer, gy, f, before):

time: 340 us -> 332 us (0.976)
  Pallas kernels: 333 us -> 324 us
    pallas_call x3, Pallas kernels: 323 us -> 314 us  [call(): pl.pallas_call(body, out_shape=[jax.ShapeDtypeStruct(s, t) for s, t in ou...]
where the time goes in v8:
time: 332 us; the launch traced here: 328 us
  Pallas kernels  324 us (98%)
    pallas_call x3, Pallas kernels, call(): pl.pallas_call(body, out_shape=[jax.ShapeDtypeStruct(s, t) for s, t in ou...  314 us
    pallas_call x1, Pallas kernels, assemble(): pl.pallas_call(functools.partial(assemble_kernel, nz), out_shape=[jax.Sha...  10 us

profile of v8, /device:TPU:0, one launch (start us, length us, event | category | flops | bytes accessed | tf_op | source)
XLA Modules:
  0.0 327.6 jit_solution(8332966517857004317)
XLA Ops:
  1.3 131.3 %forward.1 = (f32[2,1,2944]{2,1,0:T(1,128)}, s32[16,8,256]{2,1,0:T(8,128)}, f32[128,128]{1,0:T(8,128)}, f32[128,128]{1,0:T(8,128)}, f32[128,128]{1,0:T(8,128)}, ...) custom-call(bf16[1,224]{1,0:T(2,128)(2,1)} %refs_0_.2, ...), custom_call_target="tpu_custom_call" | custom-call | flops 10000000000 | bytes 20971520 | tf_op jit(solution)/shard_map/forward/pallas_call | solution.py:1499
  132.6 61.1 %backward_1.1 = (f32[128,896]{1,0:T(8,128)}, bf16[224,512]{1,0:T(8,128)(2,1)}, bf16[1568,128]{1,0:T(8,128)(2,1)}, bf16[128,1152]{1,0:T(8,128)(2,1)}, f32[32,128]...) custom-call(f32[2,1,128,896]{3,2,1,0:T(8,128)} %refs_0_.3, ...), custom_call_target="tpu_custom_call" | custom-call | flops 30000001024 | bytes 20971520 | tf_op jit(solution)/shard_map/backward_1/pallas_call | solution.py:1499
  193.7 121.7 %backward_0.1 = (f32[2,128,896]{2,1,0:T(8,128)}, bf16[2,4,4,448,128]{4,3,2,1,0:T(8,128)(2,1)}, bf16[2,4,4,400,128]{4,3,2,1,0:T(8,128)(2,1)}, bf16[2,4,4,448,128]...) custom-call(f32[128,896]{1,0:T(8,128)} %get-tuple-element.84.refs_0_, ...), custom_call_target="tpu_custom_call" | custom-call | flops 30000001024 | bytes 20971520 | tf_op jit(solution)/shard_map/backward_0/pallas_call | solution.py:1499
  315.4 0.0 copy-start
  315.5 0.0 copy-start.1
  315.5 10.0 %assemble.1 = (f32[224,4864]{1,0:T(8,128)}, f32[224,4864]{1,0:T(8,128)}, f32[1216,896]{1,0:T(8,128)}, f32[224,1152]{1,0:T(8,128)}, f32[224,896]{1,0:T(8,128)}, /...) custom-call(bf16[2,4,4,448,128]{4,3,2,1,0:T(8,128)(2,1)} %get-tuple-element.104.refs_0_, ...), custom_call_target="tpu_custom_call" | custom-call | tf_op jit(solution)/shard_map/assemble/pallas_call | solution.py:1614
  325.5 0.0 copy-done
  325.5 0.9 copy.27
  326.4 0.0 copy-done.1
  326.4 0.9 copy.28
Async XLA Ops:
  315.4 10.1 %copy-start = (f32[2,128,896]{2,1,0:T(8,128)S(1)}, f32[2,128,896]{2,1,0:T(8,128)}, u32[]{:S(2)}) copy-start(f32[2,128,896]{2,1,0:T(8,128)} %get-tuple-element.64) | copy-start | bytes 2752516
  315.5 11.0 %copy-start.1 = (f32[2,128,896]{2,1,0:T(8,128)S(1)}, f32[2,128,896]{2,1,0:T(8,128)}, u32[]{:S(2)}) copy-start(f32[2,128,896]{2,1,0:T(8,128)} %get-tuple-element.103) | copy-start | bytes 2752516

commit v9 on v8

--- a/solution.py
+++ b/solution.py
@@ -711,6 +711,9 @@
         gu[1][0].wait()
         for feed in (wa[1][1], wa[1][2], gu[1][1]):
             feed.start()
+
+    def besides_next():
+        for feed in (wa[1][1], wa[1][2], gu[1][1]):
             feed.start_beside()
         down[1].start()
 
@@ -726,36 +729,36 @@
     v = View(r, 0)
 
     def out_ready():
-        g0.collect(2)
         w0.finish()
         v.flush("wa")
 
+    nothing = lambda: None
+    ahead = relays((w0, "relay", 1), (w0, "relay", 3), (w0, "relay", 2), (g0, "relay", 1), (g0, "relay", 3))
     attention_forward(
         st, v, 0,
         (
-            relays((w0, "relay", 1), (w0, "relay", 3), (w0, "relay", 2), (g0, "relay", 1), (g0, "relay", 3)),
+            lambda: (ahead(), begin_next()),
             relays((g0, "relay", 2), (w0, "collect", 1), (w0, "collect", 3), (w0, "collect", 2)),
-            begin_next,
-            relays((g0, "collect", 1), (g0, "collect", 3)),
+            nothing,
+            nothing,
             out_ready,
         ),
     )
 
     def ready_0():
+        relays((g0, "collect", 1), (g0, "collect", 3), (g0, "collect", 2))()
         g0.finish()
         down[0].finish()
         v.flush("gu", "down")
 
+    first = relays((w1, "relay", 1), (w1, "relay", 3), (w1, "relay", 2))
     ffn_forward(
         st, v, ready_0,
         (
-            relays((w1, "relay", 1), (w1, "relay", 3)),
-            relays((w1, "relay", 2), (w2, "relay", 1), (w2, "relay", 3), (w2, "relay", 2), (g1, "relay", 1)),
-            relays((g1, "relay", 3), (g1, "relay", 2), (w1, "collect", 1), (w1, "collect", 3)),
-            relays(
-                (w1, "collect", 2), (w2, "collect", 1), (w2, "collect", 3), (w2, "collect", 2),
-                (g1, "collect", 1), (g1, "collect", 3), (g1, "collect", 2),
-            ),
+            lambda: (besides_next(), first()),
+            relays((w2, "relay", 1), (w2, "relay", 3), (w2, "relay", 2), (g1, "relay", 1), (g1, "relay", 3)),
+            relays((g1, "relay", 2), (w1, "collect", 1), (w1, "collect", 3), (w1, "collect", 2)),
+            relays((w2, "collect", 1), (w2, "collect", 3), (w2, "collect", 2)),
         ),
     )
     r.x1[...] = r.y0[...].astype(BF16).astype(F32)
@@ -772,8 +775,10 @@
     w2.finish()
     v = View(r, 1)
     v.flush("wa")
-    nothing = lambda: None
-    attention_forward(st, v, 1, (nothing,) * 5)
+    attention_forward(
+        st, v, 1,
+        (nothing, relays((g1, "collect", 1)), relays((g1, "collect", 3)), relays((g1, "collect", 2)), nothing),
+    )
 
     def ready_1():
         g1.finish()
@@ -1051,10 +1056,10 @@
         self.ends += made
         self.open += made
 
-    def relay(self):
-        for one in self.open:
+    def relay(self, count=None):
+        for one in self.open[:count]:
             one.relay()
-        self.open = []
+        self.open = self.open[count:] if count else []
 
     def finish(self):
         for one in self.ends:
@@ -1194,6 +1199,8 @@
         used = TILES * (half // UNIT)
         extra = 16 * sum(DOWN_PER) - used
         put_units(refs, section, base, DOWN_PER, used, jnp.zeros((extra * UNIT, LANES), BF16))
+    if carry:
+        rest.give(slice(SIDE // 2, SIDE))
     r.need("n2_all")
     normed = jnp.concatenate([r.n2_all[i] for i in range(n)], 0)
 
@@ -1212,6 +1219,8 @@
             put_units(refs, section, base, GATE_PER, used, jnp.zeros((extra * UNIT, LANES), BF16))
 
     product(1 - st.s)
+    if carry:
+        rest.relay(2)
     swaps = [st.swap(refs[h], (r.sla, r.slb)[h]) for h in range(2)]
     product(st.s)
     for k in ORDER:
@@ -1333,8 +1342,8 @@
         if i == 0:
             for one in r1:
                 one.pass_on()
-        if i == 1 and last:
-            rest.relay()
+            if last:
+                rest.relay()
 
     def out_gradient():
         arrived(out_factors)
@@ -1346,6 +1355,10 @@
                 r.dout[t * share : (t + 1) * share, :] = d[:, (t - j) * LANES : (t - j + 1) * LANES]
 
     glin = r.zglin.at[st.block(st.z, tok), :] if last else r.glin
+    if last:
+        for h in range(2):
+            r1[h].sum_into(t1[h])
+        own_rest = Rest(st, t1, (r.l2c, r.l2d), (r.t2c, r.t2d), (r.g1c, r.g1d), (r.ha, r.hb), 0)
     r.need("cos", "sa", "sb", "x", "small")
     cos, sa, sb = r.cos[...], r.sa[...], r.sb[...]
     for t in range(TILES):
@@ -1355,10 +1368,7 @@
         factors = attention.whole(r.zglin, slice(0, D))
         r.need("n1z1", "dout1")
         qswap = attention.swap(before, r.n1z1, r.all_glin, r.all_small, r.dout1, r.qv, r.ql)
-        for h in range(2):
-            r1[h].sum_into(t1[h])
-        own_rest = Rest(st, t1, (r.l2c, r.l2d), (r.t2c, r.t2d), (r.g1c, r.g1d), (r.ha, r.hb), 0)
-        rest.give(slice(2, 3))
+        own_rest.advance()
         attention.fold(qswap, r.qv, r.ql, (r.qpa, r.qpb))
         few = Few(st, r, "")
     else:
@@ -1396,8 +1406,6 @@
         factors += attention.whole(r.zsmall)
         own_rest.advance()
         few.first_gather()
-        rest.relay()
-        rest.give(slice(3, 4))
     else:
         r.flush("gsmall")
     dz = gn1 * r.small[layer][:, :D]
@@ -1407,19 +1415,17 @@
         out = (r.qa, r.qb)
         out_gradient()
         arrived(qkv_factor)
-        own_rest.advance()
         zswap = attention.swap(factors, r.n1z, r.zglin, r.zsmall, r.dout, r.zv, r.zl)
+        own_rest.relay()
         attention.fold(zswap, r.zv, r.zl, (r.qp0a, r.qp0b))
         last_few = Few(st, r, "0")
+        own_rest.give(slice(SIDE // 2, SIDE))
         ends = few.hand_over(out, 1)
-        rest.relay()
+        last_few.second_sum()
         own_rest.relay()
-        last_few.second_sum()
-        own_rest.give(slice(2, SIDE))
         for end in ends:
             end.relay()
         last_few.first_gather()
-        own_rest.relay()
         final = last_few.hand_over(out, 0)
         rest.finish()
         for end in final:

time: 332 us -> 326 us (0.982)
  Pallas kernels: 324 us -> 317 us
    pallas_call x3, Pallas kernels: 314 us -> 307 us  [call(): pl.pallas_call(body, out_shape=[jax.ShapeDtypeStruct(s, t) for s, t in ou...]
where the time goes in v9:
time: 326 us; the launch traced here: 320 us
  Pallas kernels  317 us (97%)
    pallas_call x3, Pallas kernels, call(): pl.pallas_call(body, out_shape=[jax.ShapeDtypeStruct(s, t) for s, t in ou...  307 us
    pallas_call x1, Pallas kernels, assemble(): pl.pallas_call(functools.partial(assemble_kernel, nz), out_shape=[jax.Sha...  10 us

profile of v9, /device:TPU:0, one launch (start us, length us, event | category | flops | bytes accessed | tf_op | source)
XLA Modules:
  0.0 320.5 jit_solution(17673369223377208781)
XLA Ops:
  1.3 124.7 %forward.1 = (f32[2,1,2944]{2,1,0:T(1,128)}, s32[16,8,256]{2,1,0:T(8,128)}, f32[128,128]{1,0:T(8,128)}, f32[128,128]{1,0:T(8,128)}, f32[128,128]{1,0:T(8,128)}, ...) custom-call(bf16[1,224]{1,0:T(2,128)(2,1)} %refs_0_.2, ...), custom_call_target="tpu_custom_call" | custom-call | flops 10000000000 | bytes 20971520 | tf_op jit(solution)/shard_map/forward/pallas_call | solution.py:1505
  125.9 61.1 %backward_1.1 = (f32[128,896]{1,0:T(8,128)}, bf16[224,512]{1,0:T(8,128)(2,1)}, bf16[1568,128]{1,0:T(8,128)(2,1)}, bf16[128,1152]{1,0:T(8,128)(2,1)}, f32[32,128]...) custom-call(f32[2,1,128,896]{3,2,1,0:T(8,128)} %refs_0_.3, ...), custom_call_target="tpu_custom_call" | custom-call | flops 30000001024 | bytes 20971520 | tf_op jit(solution)/shard_map/backward_1/pallas_call | solution.py:1505
  187.1 121.3 %backward_0.1 = (f32[2,128,896]{2,1,0:T(8,128)}, bf16[2,4,4,448,128]{4,3,2,1,0:T(8,128)(2,1)}, bf16[2,4,4,400,128]{4,3,2,1,0:T(8,128)(2,1)}, bf16[2,4,4,448,128]...) custom-call(f32[128,896]{1,0:T(8,128)} %get-tuple-element.84.refs_0_, ...), custom_call_target="tpu_custom_call" | custom-call | flops 30000001024 | bytes 20971520 | tf_op jit(solution)/shard_map/backward_0/pallas_call | solution.py:1505
  308.4 0.0 copy-start
  308.4 0.0 copy-start.1
  308.4 10.0 %assemble.1 = (f32[224,4864]{1,0:T(8,128)}, f32[224,4864]{1,0:T(8,128)}, f32[1216,896]{1,0:T(8,128)}, f32[224,1152]{1,0:T(8,128)}, f32[224,896]{1,0:T(8,128)}, /...) custom-call(bf16[2,4,4,448,128]{4,3,2,1,0:T(8,128)(2,1)} %get-tuple-element.104.refs_0_, ...), custom_call_target="tpu_custom_call" | custom-call | tf_op jit(solution)/shard_map/assemble/pallas_call | solution.py:1620
  318.4 0.0 copy-done
  318.4 0.9 copy.27
  319.4 0.0 copy-done.1
  319.4 0.9 copy.28
Async XLA Ops:
  308.4 10.1 %copy-start = (f32[2,128,896]{2,1,0:T(8,128)S(1)}, f32[2,128,896]{2,1,0:T(8,128)}, u32[]{:S(2)}) copy-start(f32[2,128,896]{2,1,0:T(8,128)} %get-tuple-element.64) | copy-start | bytes 2752516
  308.4 11.0 %copy-start.1 = (f32[2,128,896]{2,1,0:T(8,128)S(1)}, f32[2,128,896]{2,1,0:T(8,128)}, u32[]{:S(2)}) copy-start(f32[2,128,896]{2,1,0:T(8,128)} %get-tuple-element.103) | copy-start | bytes 2752516

commit v10 on v9

--- a/solution.py
+++ b/solution.py
@@ -1223,6 +1223,11 @@
         rest.relay(2)
     swaps = [st.swap(refs[h], (r.sla, r.slb)[h]) for h in range(2)]
     product(st.s)
+    r1 = []
+    if carry:
+        for h in range(2):
+            swapped_sum(st, swaps[h], refs[h], (r.sla, r.slb)[h])
+            r1.append(Scatter(st, AXES[h][0], (r.sla, r.slb)[h], (r.l1a, r.l1b)[h]))
     for k in ORDER:
         second(k).wait_recv()
         r.own_s[...] += r.land_s[k].astype(F32)
@@ -1237,10 +1242,10 @@
     r.gm_s[...] = gm
     for k in ORDER:
         second(k).wait_send()
-    attention_backward(st, r, layer, gm, dg2, refs, swaps, rest if carry else None, above, late, attention, before)
-
-
-def attention_backward(st, r, layer, gm, dg2, refs, swaps, rest, above, late, attention, before):
+    attention_backward(st, r, layer, gm, dg2, refs, swaps, rest if carry else None, above, late, attention, before, r1)
+
+
+def attention_backward(st, r, layer, gm, dg2, refs, swaps, rest, above, late, attention, before, r1):
     n, me = st.nc, st.c
     last = layer == 0
     half = HEAD_DIM
@@ -1253,10 +1258,10 @@
     pr, ds, gst = r.g_s.at[0, :size, :WIDE], r.g_s.at[1, :size, :WIDE], r.hid_s.at[: 2 * LANES, :WIDE]
     out_factors = attention.whole(r.all_gm) + attention.columns(r.attt, r.attz)
     qkv_factor = attention.columns(r.n1t, r.n1z)
-    r1 = []
-    for h in range(2):
-        swapped_sum(st, swaps[h], refs[h], sl[h])
-        r1.append(Scatter(st, AXES[h][0], sl[h], l1[h]))
+    if not last:
+        for h in range(2):
+            swapped_sum(st, swaps[h], refs[h], sl[h])
+            r1.append(Scatter(st, AXES[h][0], sl[h], l1[h]))
     r.need("qst", "lse", "kv", "pairs")
     for c in late:
         c.wait()
@@ -1548,15 +1553,20 @@
 def assemble_kernel(nz, *refs):
     given, results, held, outs, sem, osem = (refs[:2], refs[2:4]), refs[6:14], refs[14:16] + refs[4:6], refs[16:24], refs[24], refs[25]
     s = lax.axis_index("section")
+
+    def loads(layer, half):
+        return [
+            pltpu.make_async_copy(a.at[half], b.at[half], sem.at[2 * half + i])
+            for i, (a, b) in enumerate(zip(given[layer], held))
+        ]
+
     copies = [pltpu.make_async_copy(a, b, osem.at[i]) for i, (a, b) in enumerate(zip(outs, results))]
     for layer in range(2):
         @pl.when(s == layer)
         def _():
-            moving = [pltpu.make_async_copy(a, b, sem.at[i]) for i, (a, b) in enumerate(zip(given[layer], held))]
-            for c in moving:
-                c.start()
-            for c in moving:
-                c.wait()
+            for half in range(2):
+                for c in loads(layer, half):
+                    c.start()
 
     gate_ref, up_ref, down_ref, qkv_ref, out_ref = outs[:5]
     share = D // nz
@@ -1570,6 +1580,8 @@
         return jnp.concatenate(rows, 0) if len(rows) > 1 else rows[0]
 
     for section, ref in ((0, gate_ref), (1, up_ref)):
+        for c in loads(0, section):
+            c.wait()
         tiles = {}
         for w, a in enumerate(starts):
             for t in range(WIN // LANES):
@@ -1624,7 +1636,7 @@
         out_specs=[anywhere] * len(shapes),
         scratch_shapes=[pltpu.VMEM(a.shape, a.dtype) for a in zero]
         + [pltpu.VMEM(a, F32) for a in shapes]
-        + [pltpu.SemaphoreType.DMA((2,)), pltpu.SemaphoreType.DMA((len(shapes),))],
+        + [pltpu.SemaphoreType.DMA((4,)), pltpu.SemaphoreType.DMA((len(shapes),))],
         compiler_params=pltpu.CompilerParams(vmem_limit_bytes=VMEM_LIMIT),
         name="assemble",
     )(*zero, *one, *attn)

time: 326 us -> 324 us (level)
  no operation moved by 1% of the time
where the time goes in v10:
time: 324 us; the launch traced here: 318 us
  Pallas kernels  315 us (97%)
    pallas_call x3, Pallas kernels, call(): pl.pallas_call(body, out_shape=[jax.ShapeDtypeStruct(s, t) for s, t in ou...  306 us
    pallas_call x1, Pallas kernels, assemble(): pl.pallas_call(functools.partial(assemble_kernel, nz), out_shape=[jax.Sha...  8.96 us

profile of v10, /device:TPU:0, one launch (start us, length us, event | category | flops | bytes accessed | tf_op | source)
XLA Modules:
  0.0 318.0 jit_solution(4800251194144124050)
XLA Ops:
  1.3 124.7 %forward.1 = (f32[2,1,2944]{2,1,0:T(1,128)}, s32[16,8,256]{2,1,0:T(8,128)}, f32[128,128]{1,0:T(8,128)}, f32[128,128]{1,0:T(8,128)}, f32[128,128]{1,0:T(8,128)}, ...) custom-call(bf16[1,224]{1,0:T(2,128)(2,1)} %refs_0_.2, ...), custom_call_target="tpu_custom_call" | custom-call | flops 10000000000 | bytes 20971520 | tf_op jit(solution)/shard_map/forward/pallas_call | solution.py:1510
  125.9 61.1 %backward_1.1 = (f32[128,896]{1,0:T(8,128)}, bf16[224,512]{1,0:T(8,128)(2,1)}, bf16[1568,128]{1,0:T(8,128)(2,1)}, bf16[128,1152]{1,0:T(8,128)(2,1)}, f32[32,128]...) custom-call(f32[2,1,128,896]{3,2,1,0:T(8,128)} %refs_0_.3, ...), custom_call_target="tpu_custom_call" | custom-call | flops 30000001024 | bytes 20971520 | tf_op jit(solution)/shard_map/backward_1/pallas_call | solution.py:1510
  187.1 119.9 %backward_0.1 = (f32[2,128,896]{2,1,0:T(8,128)}, bf16[2,4,4,448,128]{4,3,2,1,0:T(8,128)(2,1)}, bf16[2,4,4,400,128]{4,3,2,1,0:T(8,128)(2,1)}, bf16[2,4,4,448,128]...) custom-call(f32[128,896]{1,0:T(8,128)} %get-tuple-element.84.refs_0_, ...), custom_call_target="tpu_custom_call" | custom-call | flops 30000001024 | bytes 20971520 | tf_op jit(solution)/shard_map/backward_0/pallas_call | solution.py:1510
  306.9 0.0 copy-start
  307.0 0.0 copy-start.1
  307.0 9.0 %assemble.1 = (f32[224,4864]{1,0:T(8,128)}, f32[224,4864]{1,0:T(8,128)}, f32[1216,896]{1,0:T(8,128)}, f32[224,1152]{1,0:T(8,128)}, f32[224,896]{1,0:T(8,128)}, /...) custom-call(bf16[2,4,4,448,128]{4,3,2,1,0:T(8,128)(2,1)} %get-tuple-element.104.refs_0_, ...), custom_call_target="tpu_custom_call" | custom-call | tf_op jit(solution)/shard_map/assemble/pallas_call | solution.py:1632
  315.9 0.0 copy-done
  315.9 0.9 copy.27
  316.9 0.0 copy-done.1
  316.9 0.9 copy.28
Async XLA Ops:
  306.9 9.0 %copy-start = (f32[2,128,896]{2,1,0:T(8,128)S(1)}, f32[2,128,896]{2,1,0:T(8,128)}, u32[]{:S(2)}) copy-start(f32[2,128,896]{2,1,0:T(8,128)} %get-tuple-element.64) | copy-start | bytes 2752516
  307.0 9.9 %copy-start.1 = (f32[2,128,896]{2,1,0:T(8,128)S(1)}, f32[2,128,896]{2,1,0:T(8,128)}, u32[]{:S(2)}) copy-start(f32[2,128,896]{2,1,0:T(8,128)} %get-tuple-element.103) | copy-start | bytes 2752516
